TPU v7x, 128 devices: a whole 4x4x4 slice. The times are simulated.
128 devices in a mesh: rows: 64 (over y, z_lo, x, core), heads: 2 (over z_hi).
Axes of the slice: x: 4, y: 4, z: 4 (z_hi: 2, z_lo: 2; z = z_hi * 2 + z_lo), core: 2. Of those that a mesh axis runs over, the one named last changes fastest.
Arguments:
- tokens: bfloat16 [32768, 768], P('rows'), may hold values from -6 to 6
- cotangent: bfloat16 [32768, 768], P('rows'), may hold values from -6 to 6
- lengths: int32 [64], P('rows'), may hold values from 128 to 512, as said below
- repeats: int32 [64], P('rows'), may hold values from 1 to 4
- query_weight: bfloat16 [2, 768, 768], P(None, None, 'heads'), may hold values from -0.21875 to 0.21875
- query_bias: bfloat16 [2, 768], P(None, 'heads'), may hold values from -1 to 1
- key_weight: bfloat16 [2, 768, 768], P(None, None, 'heads'), may hold values from -0.21875 to 0.21875
- value_weight: bfloat16 [2, 768, 768], P(None, None, 'heads'), may hold values from -0.21875 to 0.21875
- value_bias: bfloat16 [2, 768], P(None, 'heads'), may hold values from -1 to 1
- output_weight: bfloat16 [2, 768, 768], P(None, 'heads'), may hold values from -1.75 to 1.75
- output_bias: bfloat16 [2, 768], replicated, may hold values from -1 to 1
- attn_gain: bfloat16 [2, 768], replicated, may hold values from 0.5 to 1.5
- attn_shift: bfloat16 [2, 768], replicated, may hold values from -1 to 1
- up_weight: bfloat16 [2, 768, 3072], P(None, None, 'heads'), may hold values from -0.21875 to 0.21875
- up_bias: bfloat16 [2, 3072], P(None, 'heads'), may hold values from -1 to 1
- down_weight: bfloat16 [2, 3072, 768], P(None, 'heads'), may hold values from -0.109375 to 0.109375
- down_bias: bfloat16 [2, 768], replicated, may hold values from -1 to 1
- ffn_gain: bfloat16 [2, 768], replicated, may hold values from 0.5 to 1.5
- ffn_shift: bfloat16 [2, 768], replicated, may hold values from -1 to 1
Outputs:
- block_output: bfloat16 [32768, 768], P('rows')
- token_grad: float32 [32768, 768], P('rows')
- grad_query_weight: float32 [2, 768, 768], P(None, None, 'heads')
- grad_query_bias: float32 [2, 768], P(None, 'heads')
- grad_key_weight: float32 [2, 768, 768], P(None, None, 'heads')
- grad_value_weight: float32 [2, 768, 768], P(None, None, 'heads')
- grad_value_bias: float32 [2, 768], P(None, 'heads')
- grad_output_weight: float32 [2, 768, 768], P(None, 'heads')
- grad_output_bias: float32 [2, 768], replicated
- grad_attn_gain: float32 [2, 768], replicated
- grad_attn_shift: float32 [2, 768], replicated
- grad_up_weight: float32 [2, 768, 3072], P(None, None, 'heads')
- grad_up_bias: float32 [2, 3072], P(None, 'heads')
- grad_down_weight: float32 [2, 3072, 768], P(None, 'heads')
- grad_down_bias: float32 [2, 768], replicated
- grad_ffn_gain: float32 [2, 768], replicated
- grad_ffn_shift: float32 [2, 768], replicated
Inputs may be any that keep to these rules, and one draw needn't show every extreme that they name: `lengths`: live tokens stand at the start of a row; some row has exactly 512.
All inputs are finite; a program needn't handle non-finite values.
Results may differ from a plain program's by a relative error of at most 0.028.
The roundings to bfloat16 on the way count: a program that leaves them out, or rounds other values in their place, can miss the bound.
Values sent between devices are 32-bit elements; how exact they have to be, the bound alone decides.
No kernel may reach another device: no remote copies, remote signals or barrier semaphores. Data moves between devices by JAX's collectives and lax.ppermute only.
A program may use at most 192 MiB of HBM per device.

v0:
```python
import jax
import jax.numpy as jnp
from jax import lax
from jax.sharding import PartitionSpec as P

HEAD_DIM = 64


norm_eps = 1e-12


def normalize(summed, gain, shift):
    center = summed - jnp.mean(summed, axis=-1, keepdims=True)
    inverse = lax.rsqrt(jnp.mean(center * center, axis=-1, keepdims=True) + norm_eps)
    scaled = center * inverse
    return (scaled * gain + shift, scaled, inverse)


def normalize_back(gradient, gain, scaled, inverse):
    gained = gradient * gain
    return inverse * (
        gained
        - jnp.mean(gained, axis=-1, keepdims=True)
        - scaled * jnp.mean(gained * scaled, axis=-1, keepdims=True)
    )


def exact_gelu(values):
    return jax.nn.gelu(values, approximate=False)


def split_heads(block):
    return block.reshape(block.shape[0], block.shape[1] // HEAD_DIM, HEAD_DIM)


def score_block(query_row, key_row, length):
    query_heads = split_heads(query_row)
    key_heads = split_heads(key_row)
    scores = jnp.einsum(
        "qhe,khe->hqk", query_heads, key_heads, preferred_element_type=jnp.float32
    ) * HEAD_DIM ** (-0.5)
    valid = jnp.arange(key_row.shape[0]) < length
    return (jnp.where(valid[None, None, :], scores, -1e30), query_heads, key_heads)


def attend_forward(operands):
    query_row, key_row, value_row, length = operands
    scores, query_heads, key_heads = score_block(query_row, key_row, length)
    highest = jnp.max(scores, axis=-1, keepdims=True)
    raised = jnp.exp(scores - highest)
    totals = jnp.sum(raised, axis=-1, keepdims=True)
    probs = (raised / totals).astype(jnp.bfloat16)
    mixture = jnp.einsum(
        "hqk,khe->qhe", probs, split_heads(value_row), preferred_element_type=jnp.float32
    )
    logsum = (highest + jnp.log(totals))[..., 0]
    return (mixture.reshape(query_row.shape[0], -1).astype(jnp.bfloat16), logsum)


def attend_backward(operands):
    query_row, key_row, value_row, grad_row, length, logsum = operands
    scores, query_heads, key_heads = score_block(query_row, key_row, length)
    probs = jnp.exp(scores - logsum[..., None])
    grad_heads = split_heads(grad_row)
    grad_probs = jnp.einsum(
        "qhe,khe->hqk", grad_heads, split_heads(value_row), preferred_element_type=jnp.float32
    )
    inner = jnp.sum(probs * grad_probs, axis=-1, keepdims=True)
    grad_scores = (probs * (grad_probs - inner)).astype(jnp.bfloat16)
    scale = HEAD_DIM ** (-0.5)
    grad_query = (
        jnp.einsum("hqk,khe->qhe", grad_scores, key_heads, preferred_element_type=jnp.float32)
        * scale
    )
    grad_key = (
        jnp.einsum("hqk,qhe->khe", grad_scores, query_heads, preferred_element_type=jnp.float32)
        * scale
    )
    grad_value = jnp.einsum(
        "hqk,qhe->khe", probs.astype(jnp.bfloat16), grad_heads, preferred_element_type=jnp.float32
    )
    width = query_row.shape[1]
    return (
        grad_query.reshape(-1, width),
        grad_key.reshape(-1, width),
        grad_value.reshape(-1, width),
    )


def branch_total(partial_value):
    return lax.psum(partial_value, "heads")


def input_total(partial_value):
    return lax.psum(partial_value, "heads")


def column_sum(values):
    return jnp.sum(values.astype(jnp.float32), axis=0)


def layer_forward(current, lengths, weights):
    (
        query_weight,
        query_bias,
        key_weight,
        value_weight,
        value_bias,
        output_weight,
        output_bias,
        attn_gain,
        attn_shift,
        up_weight,
        up_bias,
        down_weight,
        down_bias,
        ffn_gain,
        ffn_shift,
    ) = weights
    rows_here = lengths.shape[0]
    rounded = current.astype(jnp.bfloat16)
    queries = (
        jnp.dot(rounded, query_weight, preferred_element_type=jnp.float32) + query_bias
    ).astype(jnp.bfloat16)
    key_rows = jnp.dot(rounded, key_weight, preferred_element_type=jnp.float32).astype(jnp.bfloat16)
    value_rows = (
        jnp.dot(rounded, value_weight, preferred_element_type=jnp.float32) + value_bias
    ).astype(jnp.bfloat16)
    width = queries.shape[1]
    mixture, logsum = lax.map(
        attend_forward,
        (
            queries.reshape(rows_here, -1, width),
            key_rows.reshape(rows_here, -1, width),
            value_rows.reshape(rows_here, -1, width),
            lengths,
        ),
    )
    mixture = mixture.reshape(current.shape[0], width)
    attended = (
        branch_total(jnp.dot(mixture, output_weight, preferred_element_type=jnp.float32))
        + output_bias
    )
    hidden, scaled_one, inverse_one = normalize(current + attended, attn_gain, attn_shift)
    hidden_low = hidden.astype(jnp.bfloat16)
    pre_active = jnp.dot(hidden_low, up_weight, preferred_element_type=jnp.float32) + up_bias
    active = exact_gelu(pre_active).astype(jnp.bfloat16)
    ffn_out = (
        branch_total(jnp.dot(active, down_weight, preferred_element_type=jnp.float32)) + down_bias
    )
    output, scaled_two, inverse_two = normalize(hidden + ffn_out, ffn_gain, ffn_shift)
    return (
        output,
        (
            rounded,
            queries,
            key_rows,
            value_rows,
            logsum,
            mixture,
            scaled_one,
            inverse_one,
            hidden_low,
            pre_active,
            active,
            scaled_two,
            inverse_two,
        ),
    )


def layer_backward(gradient, lengths, weights, saved):
    (
        query_weight,
        query_bias,
        key_weight,
        value_weight,
        value_bias,
        output_weight,
        output_bias,
        attn_gain,
        attn_shift,
        up_weight,
        up_bias,
        down_weight,
        down_bias,
        ffn_gain,
        ffn_shift,
    ) = weights
    (
        rounded,
        queries,
        key_rows,
        value_rows,
        logsum,
        mixture,
        scaled_one,
        inverse_one,
        hidden_low,
        pre_active,
        active,
        scaled_two,
        inverse_two,
    ) = saved
    rows_here = lengths.shape[0]
    width = queries.shape[1]
    grad_ffn_gain = jnp.sum(gradient * scaled_two, axis=0)
    grad_ffn_shift = jnp.sum(gradient, axis=0)
    grad_two = normalize_back(gradient, ffn_gain, scaled_two, inverse_two)
    ffn_low = grad_two.astype(jnp.bfloat16)
    grad_down_bias = column_sum(ffn_low)
    grad_down_weight = jnp.einsum("sf,sd->fd", active, ffn_low, preferred_element_type=jnp.float32)
    grad_active = jnp.einsum("sd,fd->sf", ffn_low, down_weight, preferred_element_type=jnp.float32)
    grad_pre = jax.vjp(exact_gelu, pre_active)[1](grad_active)[0]
    pre_low = grad_pre.astype(jnp.bfloat16)
    grad_up_bias = column_sum(pre_low)
    grad_up_weight = jnp.einsum(
        "sd,sf->df", hidden_low, pre_low, preferred_element_type=jnp.float32
    )
    grad_hidden = grad_two + input_total(
        jnp.einsum("sf,df->sd", pre_low, up_weight, preferred_element_type=jnp.float32)
    )
    grad_attn_gain = jnp.sum(grad_hidden * scaled_one, axis=0)
    grad_attn_shift = jnp.sum(grad_hidden, axis=0)
    grad_one = normalize_back(grad_hidden, attn_gain, scaled_one, inverse_one)
    attended_low = grad_one.astype(jnp.bfloat16)
    grad_output_bias = column_sum(attended_low)
    grad_output_weight = jnp.einsum(
        "sc,sd->cd", mixture, attended_low, preferred_element_type=jnp.float32
    )
    grad_mixture = jnp.einsum(
        "sd,cd->sc", attended_low, output_weight, preferred_element_type=jnp.float32
    ).astype(jnp.bfloat16)
    grad_query, grad_key, grad_value = lax.map(
        attend_backward,
        (
            queries.reshape(rows_here, -1, width),
            key_rows.reshape(rows_here, -1, width),
            value_rows.reshape(rows_here, -1, width),
            grad_mixture.reshape(rows_here, -1, width),
            lengths,
            logsum,
        ),
    )
    query_low = grad_query.reshape(-1, width).astype(jnp.bfloat16)
    key_low = grad_key.reshape(-1, width).astype(jnp.bfloat16)
    value_low = grad_value.reshape(-1, width).astype(jnp.bfloat16)
    grad_query_bias = column_sum(query_low)
    grad_value_bias = column_sum(value_low)
    grad_query_weight = jnp.einsum(
        "sd,sc->dc", rounded, query_low, preferred_element_type=jnp.float32
    )
    grad_key_weight = jnp.einsum("sd,sc->dc", rounded, key_low, preferred_element_type=jnp.float32)
    grad_value_weight = jnp.einsum(
        "sd,sc->dc", rounded, value_low, preferred_element_type=jnp.float32
    )
    into_input = jnp.einsum(
        "sc,dc->sd", query_low, query_weight, preferred_element_type=jnp.float32
    )
    into_input = into_input + jnp.einsum(
        "sc,dc->sd", key_low, key_weight, preferred_element_type=jnp.float32
    )
    into_input = into_input + jnp.einsum(
        "sc,dc->sd", value_low, value_weight, preferred_element_type=jnp.float32
    )
    grad_input = grad_one + input_total(into_input)
    return (
        grad_input,
        (
            grad_query_weight,
            grad_query_bias,
            grad_key_weight,
            grad_value_weight,
            grad_value_bias,
            grad_output_weight,
            grad_output_bias,
            grad_attn_gain,
            grad_attn_shift,
            grad_up_weight,
            grad_up_bias,
            grad_down_weight,
            grad_down_bias,
            grad_ffn_gain,
            grad_ffn_shift,
        ),
    )


def whole_sum(parts):
    return lax.psum(
        (
            parts[0],
            parts[1],
            parts[2],
            parts[3],
            parts[4],
            parts[5],
            parts[6],
            parts[7],
            parts[8],
            parts[9],
            parts[10],
            parts[11],
            parts[12],
            parts[13],
            parts[14],
        ),
        "rows",
    )


def local(
    tokens,
    cotangent,
    lengths,
    repeats,
    query_weight,
    query_bias,
    key_weight,
    value_weight,
    value_bias,
    output_weight,
    output_bias,
    attn_gain,
    attn_shift,
    up_weight,
    up_bias,
    down_weight,
    down_bias,
    ffn_gain,
    ffn_shift,
):
    params = (
        query_weight,
        query_bias,
        key_weight,
        value_weight,
        value_bias,
        output_weight,
        output_bias,
        attn_gain,
        attn_shift,
        up_weight,
        up_bias,
        down_weight,
        down_bias,
        ffn_gain,
        ffn_shift,
    )
    layers = query_weight.shape[0]
    rows_here = lengths.shape[0]
    slots = tokens.shape[0]
    seq_len = slots // rows_here
    current = tokens.astype(jnp.float32)
    kept = []
    for layer_index in range(layers):
        current, saved = layer_forward(current, lengths, [item[layer_index] for item in params])
        kept.append(saved)
    block_output = current.astype(jnp.bfloat16)
    positions = jnp.arange(seq_len)
    weighting = (
        jnp.where(positions[None, :] < lengths[:, None], repeats[:, None], 0)
        .astype(jnp.float32)
        .reshape(slots, 1)
    )
    gradient = cotangent.astype(jnp.float32) * weighting
    collected = [None] * layers
    for layer_index in reversed(range(layers)):
        gradient, layer_grads = layer_backward(
            gradient, lengths, [item[layer_index] for item in params], kept[layer_index]
        )
        collected[layer_index] = layer_grads
    stacked = tuple(
        (
            jnp.stack([collected[layer_index][member] for layer_index in range(layers)])
            for member in range(15)
        )
    )
    stacked = whole_sum(stacked)
    return (block_output, gradient) + tuple(stacked)


def solution(mesh):
    in_specs = (
        P("rows", None),
        P("rows", None),
        P("rows"),
        P("rows"),
        P(None, None, "heads"),
        P(None, "heads"),
        P(None, None, "heads"),
        P(None, None, "heads"),
        P(None, "heads"),
        P(None, "heads", None),
        P(),
        P(),
        P(),
        P(None, None, "heads"),
        P(None, "heads"),
        P(None, "heads", None),
        P(),
        P(),
        P(),
    )
    out_specs = (
        P("rows", None),
        P("rows", None),
        P(None, None, "heads"),
        P(None, "heads"),
        P(None, None, "heads"),
        P(None, None, "heads"),
        P(None, "heads"),
        P(None, "heads", None),
        P(),
        P(),
        P(),
        P(None, None, "heads"),
        P(None, "heads"),
        P(None, "heads", None),
        P(),
        P(),
        P(),
    )
    return jax.shard_map(local, mesh=mesh, in_specs=in_specs, out_specs=out_specs, check_vma=False)
```

profile of v0, /device:TPU:0, one launch (start us, length us, event | category | flops | bytes accessed | tf_op | source)
XLA Modules:
  0.0 1283.1 jit_solution(14065210183383057662)
XLA Ops:
  9.5 1.8 convolution_convert_fusion.3
  11.4 2.0 fusion.56
  13.9 1.5 fusion.128
  16.4 1.8 copy-done
  19.4 1.7 fusion.84
  21.4 62.0 %all-reduce.12.cloned.1.call-done = f32[512,768]{1,0:T(8,128)} async-done(((f32[512,768]{1,0:T(8,128)}), f32[512,768]{1,0:T(8,128)}) %all-reduce.12.cloned.1.call-update) | async-done | bytes 1572880 | tf_op jit(solution)/shard_map/psum | solution.py:91
  83.4 1.7 fusion.127
  85.5 11.3 multiply_convert_fusion.3
  97.9 2.5 fusion.35
  101.0 58.5 %all-reduce.14.cloned.1.call-done = f32[512,768]{1,0:T(8,128)} async-done(((f32[512,768]{1,0:T(8,128)}), f32[512,768]{1,0:T(8,128)}) %all-reduce.14.cloned.1.call-update) | async-done | bytes 1572880 | tf_op jit(solution)/shard_map/psum | solution.py:91
  159.5 2.0 fusion.125
  165.1 1.5 fusion.129
  167.5 1.8 copy-done.1
  171.3 1.7 fusion.73
  173.1 58.9 %all-reduce.16.cloned.1.call-done = f32[512,768]{1,0:T(8,128)} async-done(((f32[512,768]{1,0:T(8,128)}), f32[512,768]{1,0:T(8,128)}) %all-reduce.16.cloned.1.call-update) | async-done | bytes 1572880 | tf_op jit(solution)/shard_map/psum | solution.py:91
  232.0 2.1 fusion.124
  234.5 11.3 multiply_convert_fusion.2
  246.9 2.5 fusion.26
  250.2 58.3 %all-reduce.18.cloned.1.call-done = f32[512,768]{1,0:T(8,128)} async-done(((f32[512,768]{1,0:T(8,128)}), f32[512,768]{1,0:T(8,128)}) %all-reduce.18.cloned.1.call-update) | async-done | bytes 1572880 | tf_op jit(solution)/shard_map/psum | solution.py:91
  308.5 2.5 fusion.122
  311.3 1.5 multiply_reduce_fusion.2
  312.8 2.2 convert_reduce_fusion.2
  315.0 5.2 convert_reduce_fusion
  321.3 2.6 fusion.30
  324.2 58.7 %all-reduce.20.cloned.1.call-done = f32[512,768]{1,0:T(8,128)} async-done(((f32[512,768]{1,0:T(8,128)}), f32[512,768]{1,0:T(8,128)}) %all-reduce.20.cloned.1.call-update) | async-done | bytes 1572880 | tf_op jit(solution)/shard_map/psum | solution.py:95
  382.9 3.9 multiply_reduce_fusion.4
  389.3 4.3 multiply_reduce_fusion.1
  393.8 1.9 multiply_convert_fusion.1
  395.7 2.3 convert_reduce_fusion.8
  399.1 1.8 convert_reduce_fusion.6
  402.9 1.8 add_add_fusion.1
  405.1 5.6 convolution_bitcast_fusion
  410.7 3.8 convolution_bitcast_fusion.2
  414.6 1.5 convolution_bitcast_fusion.6
  416.1 1.5 convolution_bitcast_fusion.5
  417.6 46.1 %all-reduce.22.cloned.1.call-done = f32[512,768]{1,0:T(8,128)} async-done(((f32[512,768]{1,0:T(8,128)}), f32[512,768]{1,0:T(8,128)}) %all-reduce.22.cloned.1.call-update) | async-done | bytes 1572880 | tf_op jit(solution)/shard_map/psum | solution.py:95
  463.7 3.5 multiply_reduce_fusion.3
  468.3 5.2 convert_reduce_fusion.1
  474.7 2.6 fusion.39
  477.7 2.8 convolution_bitcast_fusion.4
  480.4 1.5 convolution_bitcast_fusion.7
  482.0 3.8 convolution_bitcast_fusion.1
  485.8 1.6 convolution_bitcast_fusion.3
  487.5 4.6 pad_maximum_fusion
  492.1 44.2 %all-reduce.24.cloned.1.call-done = f32[512,768]{1,0:T(8,128)} async-done(((f32[512,768]{1,0:T(8,128)}), f32[512,768]{1,0:T(8,128)}) %all-reduce.24.cloned.1.call-update) | async-done | bytes 1572880 | tf_op jit(solution)/shard_map/psum | solution.py:95
  536.3 2.8 multiply_reduce_fusion.5
  541.3 4.3 multiply_reduce_fusion
  545.7 1.9 multiply_convert_fusion
  550.0 1.8 convert_reduce_fusion.7
  553.9 1.8 add_add_fusion
  555.8 8.2 pad_maximum_fusion.1
  565.3 1.6 pad_maximum_fusion.2
  567.5 1.6 pad_maximum_fusion.3
  569.5 1.6 pad_maximum_fusion.4
  572.3 1.6 pad_maximum_fusion.5
  575.4 279.9 %all-reduce = (f32[2,384]{1,0:T(2,128)}, f32[2,384]{1,0:T(2,128)}, f32[2,768]{1,0:T(2,128)}, f32[2,768]{1,0:T(2,128)}, f32[2,768]{1,0:T(2,128)}, /*index=5*/f32[...) all-reduce(f32[2,384]{1,0:T(2,128)S(1)} %pad_maximum_fusion.13, ...), channel_id=1, replica_groups=mesh['rows'=64,'heads'=2] {'rows'}, use_global_device_ids=true, to_apply=%region_33.34 | all-reduce | flops 13824 | bytes 110592 | tf_op jit(solution)/shard_map/psum | solution.py:290
  855.2 2.7 add.397
  858.0 393.4 %all-reduce.28.cloned.1.call-done = (f32[2,768,384]{1,2,0:T(8,128)}, f32[2,768,384]{1,2,0:T(8,128)}, f32[2,768,384]{1,2,0:T(8,128)}, f32[2,384,768]{2,1,0:T(8,12...) async-done(((f32[2,768,384]{1,2,0:T(8,128)}, f32[2,768,384]{1,2,0:T(8,128)}, f32[2,768,384]{1,2,0:T(8,128)}, f32[2,384,768]{2,1,0:T(8,128)}, ...) | async-done | bytes 28311568 | tf_op jit(solution)/shard_map/psum | solution.py:290
  1251.4 3.0 copy.47
  1254.4 3.0 copy.48
  1257.4 3.0 copy.49
  1260.5 3.4 copy.77
  1263.9 8.5 copy.78
  1272.3 3.7 copy.79
  (384 shorter events, 36.3 us)
Async XLA Ops:
  7.2 6.2 copy-start.7
  7.2 6.2 copy-start.45
  7.2 76.2 %all-reduce.12.cloned.1.call-start = ((), (), s32[]{:S(2)}) async-start(), calls=%async_computation | async-start | bytes 3145728 | tf_op jit(solution)/shard_map/psum | solution.py:91
  11.4 4.1 copy-start.34
  19.4 64.1 %copy-start.37 = (bf16[6,64,512]{2,1,0:T(8,128)(2,1)}, bf16[6,64,512]{2,1,0:T(8,128)(2,1)S(1)}, u32[]{:S(2)}) copy-start(bf16[6,64,512]{2,1,0:T(8,128)(2,1)S(1)} %fusion.71) | copy-start | bytes 1179652
  21.2 138.3 %all-reduce.14.cloned.1.call-start = ((), (), s32[]{:S(2)}) async-start(), calls=%async_computation.1 | async-start | bytes 3145728 | tf_op jit(solution)/shard_map/psum | solution.py:91
  21.4 138.1 %copy-start.67 = (f32[768]{0:T(1024)}, f32[768]{0:T(1024)S(1)}, u32[]{:S(2)}) copy-start(f32[768]{0:T(1024)S(1)} %get-tuple-element.231) | copy-start | bytes 9220
  21.4 138.1 %copy-start.92 = (f32[768]{0:T(1024)}, f32[768]{0:T(1024)S(1)}, u32[]{:S(2)}) copy-start(f32[768]{0:T(1024)S(1)} %get-tuple-element.163) | copy-start | bytes 9220
  21.4 287.0 %copy-start.94 = (f32[768]{0:T(1024)}, f32[768]{0:T(1024)S(1)}, u32[]{:S(2)}) copy-start(f32[768]{0:T(1024)S(1)} %get-tuple-element.162) | copy-start | bytes 9220
  21.4 365.4 %copy-start.69 = (f32[768]{0:T(1024)}, f32[768]{0:T(1024)S(1)}, u32[]{:S(2)}) copy-start(f32[768]{0:T(1024)S(1)} %get-tuple-element.232) | copy-start | bytes 9220
  85.1 74.4 %copy-start.71 = (f32[512]{0:T(512)}, f32[512]{0:T(512)S(1)}, u32[]{:S(2)}) copy-start(f32[512]{0:T(512)S(1)} %broadcast_multiply_fusion.11) | copy-start | bytes 6148
  85.1 12.8 slice-start.9
  85.5 74.0 %copy-start.77 = (f32[512]{0:T(512)}, f32[512]{0:T(512)S(1)}, u32[]{:S(2)}) copy-start(f32[512]{0:T(512)S(1)} %add_rsqrt_fusion.3) | copy-start | bytes 6148
  85.5 12.4 slice-start.10
  100.5 131.5 %all-reduce.16.cloned.1.call-start = ((), (), s32[]{:S(2)}) async-start(), calls=%async_computation.2 | async-start | bytes 3145728 | tf_op jit(solution)/shard_map/psum | solution.py:91
  101.0 131.0 %copy-start.61 = (f32[768]{0:T(1024)}, f32[768]{0:T(1024)S(1)}, u32[]{:S(2)}) copy-start(f32[768]{0:T(1024)S(1)} %get-tuple-element.233) | copy-start | bytes 9220
  161.5 70.6 %copy-start.63 = (f32[512]{0:T(512)}, f32[512]{0:T(512)S(1)}, u32[]{:S(2)}) copy-start(f32[512]{0:T(512)S(1)} %broadcast_multiply_fusion.10) | copy-start | bytes 6148
  161.8 70.2 %copy-start.73 = (f32[512]{0:T(512)}, f32[512]{0:T(512)S(1)}, u32[]{:S(2)}) copy-start(f32[512]{0:T(512)S(1)} %add_rsqrt_fusion.2) | copy-start | bytes 6148
  173.0 135.4 %all-reduce.18.cloned.1.call-start = ((), (), s32[]{:S(2)}) async-start(), calls=%async_computation.3 | async-start | bytes 3145728 | tf_op jit(solution)/shard_map/psum | solution.py:91
  232.0 14.9 %slice-start.11 = ((s8[4718592]{0:T(1024)(128)(4,1)}), s8[4194304]{0:T(1024)(128)(4,1)S(1)}, s32[]{:S(2)}) async-start(s8[4718592]{0:T(1024)(128)(4,1)} %bitcast.241), calls=%async_computation.20 | async-start | bytes 8388608
  234.1 11.6 copy-start.2
  234.2 152.7 %copy-start.75 = (f32[512]{0:T(512)}, f32[512]{0:T(512)S(1)}, u32[]{:S(2)}) copy-start(f32[512]{0:T(512)S(1)} %broadcast_multiply_fusion.9) | copy-start | bytes 6148
  234.5 152.3 %copy-start.79 = (f32[512]{0:T(512)}, f32[512]{0:T(512)S(1)}, u32[]{:S(2)}) copy-start(f32[512]{0:T(512)S(1)} %add_rsqrt_fusion.1) | copy-start | bytes 6148
  234.5 12.4 slice-start.12
  249.5 133.4 %all-reduce.20.cloned.1.call-start = ((), (), s32[]{:S(2)}) async-start(), calls=%async_computation.4 | async-start | bytes 3145728 | tf_op jit(solution)/shard_map/psum | solution.py:95
  312.8 8.5 slice-start.13
  315.0 5.2 copy-start.11
  315.0 6.3 slice-start.14
  323.9 139.8 %all-reduce.22.cloned.1.call-start = ((), (), s32[]{:S(2)}) async-start(), calls=%async_computation.5 | async-start | bytes 3145728 | tf_op jit(solution)/shard_map/psum | solution.py:95
  382.9 3.9 copy-start.3
  389.1 4.5 slice-start.2
  389.3 4.6 slice-start.3
  404.7 131.5 %all-reduce.24.cloned.1.call-start = ((), (), s32[]{:S(2)}) async-start(), calls=%async_computation.6 | async-start | bytes 3145728 | tf_op jit(solution)/shard_map/psum | solution.py:95
  405.0 5.7 copy-start.4
  405.0 5.6 copy-start.70
  405.1 5.6 copy-start.76
  405.1 5.6 copy-start.80
  405.1 5.6 copy-start.95
  405.1 5.6 copy-start.114
  414.6 49.1 %copy-start.62 = (f32[768]{0:T(1024)S(1)}, f32[768]{0:T(1024)}, u32[]{:S(2)}) copy-start(f32[768]{0:T(1024)} %copy-done.61) | copy-start | bytes 9220
  414.6 49.1 %copy-start.64 = (f32[512]{0:T(512)S(1)}, f32[512]{0:T(512)}, u32[]{:S(2)}) copy-start(f32[512]{0:T(512)} %copy-done.63) | copy-start | bytes 6148
  414.6 49.1 %copy-start.74 = (f32[512]{0:T(512)S(1)}, f32[512]{0:T(512)}, u32[]{:S(2)}) copy-start(f32[512]{0:T(512)} %copy-done.73) | copy-start | bytes 6148
  463.7 4.6 copy-start.117
  463.7 4.6 copy-start.118
  467.2 7.5 slice-start.15
  468.3 5.2 copy-start.12
  468.3 6.4 slice-start.16
  477.3 377.9 %all-reduce.26.cloned.1.call-start = ((), (), s32[]{:S(2)}) async-start(), calls=%async_computation.7 | async-start | bytes 3145728 | tf_op jit(solution)/shard_map/psum | solution.py:95
  477.6 4.3 copy-start.13
  477.6 4.3 copy-start.111
  481.9 3.9 copy-start.68
  481.9 3.9 copy-start.72
  481.9 3.9 copy-start.78
  481.9 3.9 copy-start.93
  481.9 5.5 slice-start.7
  487.5 48.8 %copy-start.14 = (f32[512,768]{1,0:T(8,128)S(1)}, f32[512,768]{1,0:T(8,128)}, u32[]{:S(2)}) copy-start(f32[512,768]{1,0:T(8,128)} %copy-done.12) | copy-start | bytes 4718596
  540.9 4.7 slice-start
  541.3 4.4 slice-start.1
  555.7 8.3 copy-start.8
  555.8 8.3 copy-start.28
  555.8 695.6 %all-reduce.28.cloned.1.call-start = ((), (), s32[]{:S(2)}) async-start(), calls=%async_computation.8 | async-start | bytes 56623104 | tf_op jit(solution)/shard_map/psum | solution.py:290
  1260.5 11.8 slice-start.4
  1263.9 8.5 slice-start.5
  1263.9 8.5 slice-start.6
  (83 other events, 155.4 us)
Sparse Core Ops, SparseCore 0:
  21.3 62.0 all-reduce.11
  100.6 58.8 all-reduce.13
  173.2 58.8 all-reduce.15
  249.6 58.8 all-reduce.17
  324.0 58.8 all-reduce.19
  404.9 58.8 all-reduce.21
  477.4 58.8 all-reduce.23
  555.9 59.0 all-reduce.25
  619.1 632.1 all-reduce.27
where the time goes:
time: 1290 us; the launch traced here: 1280 us
  waiting for transfers between devices  780 us (60%)
  blocking collectives  280 us (22%)
  matrix products  107 us (8%)
  other arithmetic  56.2 us (4%)
  local copies, waits for them, and re-layouts  41.1 us (3%)
  between operations  17.3 us (1%)
    psum x1, waiting for transfers between devices, whole_sum(): lax.psum((parts[0], parts[1], parts[2], parts[3], parts[4], parts[5], par...  393 us
    psum x1, blocking collectives, whole_sum(): lax.psum((parts[0], parts[1], parts[2], parts[3], parts[4], parts[5], par...  280 us
    psum x4, waiting for transfers between devices, branch_total(): return lax.psum(partial_value, 'heads')  238 us
    psum x4, waiting for transfers between devices, input_total(): return lax.psum(partial_value, 'heads')  149 us
    unnamed x282, local copies, waits for them, and re-layouts  40.7 us
  transfers between devices with their start and end apart: 9, of which 8 were waited for; matrix products, arithmetic and copies ran while one was open for 4% of the time, Pallas kernels for 0%

commit v1 on v0

v1 whole, which is shorter than its diff:
```python
import jax
import jax.numpy as jnp
from jax import lax
from jax.experimental import pallas as pl
from jax.experimental.pallas import tpu as pltpu
from jax.sharding import Mesh, PartitionSpec as P

HEAD_DIM = 64
EPS = 1e-12
F32 = jnp.float32
BF16 = jnp.bfloat16
SWAP = ((0, 1), (1, 0))
EDGE0 = ((0, 1), (1, 0), (2, 3), (3, 2))
EDGE1 = ((1, 2), (2, 1), (3, 0), (0, 3))
LINKS = (("x", EDGE0), ("x", EDGE1), ("y", EDGE0), ("y", EDGE1))
PLANE = ("y", "x")


def normalize(summed, gain, shift):
    center = summed - jnp.mean(summed, axis=-1, keepdims=True)
    inverse = lax.rsqrt(jnp.mean(center * center, axis=-1, keepdims=True) + EPS)
    scaled = center * inverse
    return (scaled * gain + shift, scaled, inverse)


def normalize_back(gradient, gain, scaled, inverse):
    gained = gradient * gain
    return inverse * (
        gained
        - jnp.mean(gained, axis=-1, keepdims=True)
        - scaled * jnp.mean(gained * scaled, axis=-1, keepdims=True)
    )


def normal_cdf(values):
    return 0.5 * (1.0 + lax.erf(values * (0.5**0.5)))


def gelu(values):
    return values * normal_cdf(values)


def gelu_slope(values):
    density = jnp.exp(-0.5 * values * values) * 0.3989422804014327
    return normal_cdf(values) + values * density


def dot(left, right):
    return jnp.dot(left, right, preferred_element_type=F32)


def dot_t(left, right):
    return jnp.einsum("sd,fd->sf", left, right, preferred_element_type=F32)


def t_dot(left, right):
    return jnp.einsum("sf,sd->fd", left, right, preferred_element_type=F32)


def split_heads(block):
    return block.reshape(block.shape[0], block.shape[1] // HEAD_DIM, HEAD_DIM)


def masked_scores(queries, keys, length):
    scores = jnp.einsum("qhe,khe->hqk", queries, keys, preferred_element_type=F32) * HEAD_DIM**-0.5
    valid = jnp.arange(keys.shape[0]) < length
    return jnp.where(valid[None, None, :], scores, -1e30)


def attend(queries, keys, values, length):
    scores = masked_scores(split_heads(queries), split_heads(keys), length)
    highest = jnp.max(scores, axis=-1, keepdims=True)
    raised = jnp.exp(scores - highest)
    totals = jnp.sum(raised, axis=-1, keepdims=True)
    probs = (raised / totals).astype(BF16)
    mixture = jnp.einsum("hqk,khe->qhe", probs, split_heads(values), preferred_element_type=F32)
    logsum = highest + jnp.log(totals)
    return mixture.reshape(queries.shape).astype(BF16), logsum


def attend_back(queries, keys, values, grads, length, logsum):
    query_heads, key_heads = split_heads(queries), split_heads(keys)
    grad_heads = split_heads(grads)
    scores = masked_scores(query_heads, key_heads, length)
    probs = jnp.exp(scores - logsum)
    grad_probs = jnp.einsum("qhe,khe->hqk", grad_heads, split_heads(values), preferred_element_type=F32)
    inner = jnp.sum(probs * grad_probs, axis=-1, keepdims=True)
    grad_scores = (probs * (grad_probs - inner)).astype(BF16)
    scale = HEAD_DIM**-0.5
    grad_query = jnp.einsum("hqk,khe->qhe", grad_scores, key_heads, preferred_element_type=F32) * scale
    grad_key = jnp.einsum("hqk,qhe->khe", grad_scores, query_heads, preferred_element_type=F32) * scale
    grad_value = jnp.einsum("hqk,qhe->khe", probs.astype(BF16), grad_heads, preferred_element_type=F32)
    shape = queries.shape
    return tuple(item.reshape(shape).astype(BF16) for item in (grad_query, grad_key, grad_value))


def column_sum(values):
    return jnp.sum(values.astype(F32), axis=0)


def swap(values, axis):
    return lax.ppermute(values, axis, SWAP)


def pair_sum(values):
    return values + swap(values, "h")


def piece(values, index, size):
    return lax.dynamic_slice_in_dim(values, index * size, size, 0)


def in_order(side, mine, other):
    return jnp.concatenate([jnp.where(side == 0, mine, other), jnp.where(side == 0, other, mine)])


def after(values, *earlier):
    return lax.optimization_barrier((values, *earlier))[0]


def sort_kernel(piece_ref, down_ref, up_ref):
    chips, _, _, rows, width = piece_ref.shape
    for i in range(chips):
        down_ref[0, i * rows : (i + 1) * rows, :] = piece_ref[i, 0, 0].astype(BF16)
        up = piece_ref[i, 1, 0].astype(BF16)
        half = rows // 2
        up_ref[0, i * half : (i + 1) * half, :width] = up[:half]
        up_ref[0, i * half : (i + 1) * half, width:] = up[half:]


def sort_weights(gathered):
    chips, _, layers, rows, width = gathered.shape
    step = 4
    units = chips * rows
    return pl.pallas_call(
        sort_kernel,
        grid=(layers, chips // step),
        in_specs=[pl.BlockSpec((step, 2, 1, rows, width), lambda l, i: (i, 0, l, 0, 0))],
        out_specs=[
            pl.BlockSpec((1, step * rows, width), lambda l, i: (l, i, 0)),
            pl.BlockSpec((1, step * rows // 2, units), lambda l, i: (l, i, 0)),
        ],
        out_shape=[
            jax.ShapeDtypeStruct((layers, units, width), BF16),
            jax.ShapeDtypeStruct((layers, width, units), BF16),
        ],
        compiler_params=pltpu.CompilerParams(vmem_limit_bytes=40 * 2**20),
        cost_estimate=pl.CostEstimate(flops=0, bytes_accessed=6 * layers * 2 * units * width, transcendentals=0),
        name="sort_weights",
    )(gathered)


def rows_of(ref):
    chips, _, rows, columns = ref.shape
    return ref[...].reshape(chips * rows, columns)


def place_feed_kernel(down_in, up_in, down_ref, up_ref):
    down_ref[0] = rows_of(down_in)
    up_ref[0] = rows_of(up_in).T


def place_attention_kernel(query_in, key_in, value_in, output_in, query_ref, key_ref, value_ref, output_ref):
    query_ref[0] = rows_of(query_in).T
    key_ref[0] = rows_of(key_in).T
    value_ref[0] = rows_of(value_in).T
    output_ref[0] = rows_of(output_in)


def place_gradients(gathered, width):
    chips, _, rows, _ = gathered.shape
    step = 4
    units, block = chips * rows, step * rows
    half = width // 2

    def feed_in(core):
        return pl.BlockSpec((step, 1, rows, width), lambda l, i: (i, core, 0, 1 - l))

    def attention_in(core, which):
        return pl.BlockSpec((step, 1, rows, half), lambda l, i: (2 * i + which, core, 0, 5 - l))

    limit = pltpu.CompilerParams(vmem_limit_bytes=40 * 2**20)
    down, up = pl.pallas_call(
        place_feed_kernel,
        grid=(2, chips // step),
        in_specs=[feed_in(0), feed_in(1)],
        out_specs=[
            pl.BlockSpec((1, block, width), lambda l, i: (l, i, 0)),
            pl.BlockSpec((1, width, block), lambda l, i: (l, 0, i)),
        ],
        out_shape=[
            jax.ShapeDtypeStruct((2, units, width), F32),
            jax.ShapeDtypeStruct((2, width, units), F32),
        ],
        compiler_params=limit,
        name="place_feed",
    )(gathered, gathered)
    tall = pl.BlockSpec((1, half, block), lambda l, i: (l, i, 0))
    tall_shape = jax.ShapeDtypeStruct((2, width, block), F32)
    query, key, value, output = pl.pallas_call(
        place_attention_kernel,
        grid=(2, 2),
        in_specs=[attention_in(0, 0), attention_in(0, 1), attention_in(1, 0), attention_in(1, 1)],
        out_specs=[tall, tall, tall, pl.BlockSpec((1, block, half), lambda l, i: (l, 0, i))],
        out_shape=[tall_shape, tall_shape, tall_shape, jax.ShapeDtypeStruct((2, block, width), F32)],
        compiler_params=limit,
        name="place_attention",
    )(gathered, gathered, gathered, gathered)
    return query, key, value, output, up, down


def local(
    tokens,
    cotangent,
    lengths,
    repeats,
    query_weight,
    query_bias,
    key_weight,
    value_weight,
    value_bias,
    output_weight,
    output_bias,
    attn_gain,
    attn_shift,
    up_weight,
    up_bias,
    down_weight,
    down_bias,
    ffn_gain,
    ffn_shift,
):
    length = lengths[0]
    side = lax.axis_index("h")
    core = lax.axis_index("c")
    chip = lax.axis_index("y") * 4 + lax.axis_index("x")
    first_core = core == 0
    slots, width = tokens.shape
    half_slots = slots // 2
    units = up_weight.shape[2]
    columns = query_weight.shape[2]

    rows_down, rows_up = units // 16, width // 16
    pieces = []
    for layer in (0, 1):
        up_piece = piece(up_weight[layer], chip, rows_up)
        up_piece = jnp.concatenate([up_piece[:, :width], up_piece[:, width:]])
        pieces.append(jnp.where(first_core, piece(down_weight[layer], chip, rows_down), up_piece).astype(F32))
    gathered = lax.all_gather(swap(jnp.concatenate(pieces), "h"), PLANE + ("c",))
    peer_down, peer_up = sort_weights(gathered.reshape(16, 2, 2, rows_down, width))
    peer_up_bias = swap(up_bias.astype(F32), "h")

    def own_slots(values):
        return piece(values, side, half_slots)

    def attention_in(layer, rounded):
        queries = (dot(rounded, query_weight[layer]) + query_bias[layer]).astype(BF16)
        keys = dot(rounded, key_weight[layer]).astype(BF16)
        values = (dot(rounded, value_weight[layer]) + value_bias[layer]).astype(BF16)
        mixture, logsum = attend(queries, keys, values, length)
        return queries, keys, values, mixture, logsum

    def attention_back(layer, saved, rounded, grad_one_own):
        queries, keys, values, mixture, logsum = saved
        grad_one = 2.0 * in_order(side, *(lambda sent: (sent, swap(sent, "h")))(0.5 * grad_one_own))
        attended_low = grad_one.astype(BF16)
        grad_mixture = dot_t(attended_low, output_weight[layer]).astype(BF16)
        query_low, key_low, value_low = attend_back(queries, keys, values, grad_mixture, length, logsum)
        lows = (query_low, key_low, value_low)

        def into_input(pick):
            return (
                dot_t(pick(query_low), query_weight[layer])
                + dot_t(pick(key_low), key_weight[layer])
                + dot_t(pick(value_low), value_weight[layer])
            )

        small = [jnp.concatenate([column_sum(query_low), column_sum(value_low)]), column_sum(attended_low)]
        return grad_one, lows, attended_low, into_input, small

    def attention_weights_back(saved, rounded, lows, attended_low):
        mixture = saved[3]
        query_low, key_low, value_low = lows
        sent = jnp.concatenate(
            [
                t_dot(jnp.where(first_core, value_low, query_low), rounded),
                t_dot(jnp.where(first_core, mixture, key_low), jnp.where(first_core, attended_low, rounded)),
            ]
        )
        received = swap(sent, "c")
        kept = jnp.concatenate(
            [
                t_dot(jnp.where(first_core, query_low, value_low), rounded),
                t_dot(jnp.where(first_core, key_low, mixture), jnp.where(first_core, rounded, attended_low)),
            ]
        )
        total = kept + received
        return jnp.concatenate([total[:, : width // 2], total[:, width // 2 :]])

    def feed_back(layer, gradient, saved):
        scaled_two, inverse_two, pres, actives, hidden_low, scaled_one, inverse_one = saved
        grad_two = normalize_back(gradient, ffn_gain[layer], scaled_two, inverse_two)
        ffn_low = grad_two.astype(BF16)
        downs, ups = (down_weight[layer], peer_down[layer]), (up_weight[layer], peer_up[layer])
        pre_lows = [
            (dot_t(ffn_low, down) * gelu_slope(pre)).astype(BF16) for down, pre in zip(downs, pres, strict=True)
        ]
        grad_hidden = grad_two + dot_t(pre_lows[0], ups[0]) + dot_t(pre_lows[1], ups[1])
        grad_one = normalize_back(grad_hidden, attn_gain[layer], scaled_one, inverse_one)
        shared = [
            jnp.sum(grad_hidden * scaled_one, axis=0),
            jnp.sum(grad_hidden, axis=0),
            column_sum(ffn_low),
            jnp.sum(gradient * scaled_two, axis=0),
            jnp.sum(gradient, axis=0),
        ]
        biases = [column_sum(item).reshape(-1, width) for item in pre_lows]
        return grad_one, ffn_low, pre_lows, shared, biases

    def feed_weights_back(saved, ffn_low, pre_lows):
        actives, hidden_low = saved[3], saved[4]
        right = jnp.where(first_core, hidden_low, ffn_low)
        sent = jnp.concatenate(
            [t_dot(jnp.where(first_core, pre, act), right) for pre, act in zip(pre_lows, actives)], axis=1
        )
        received = swap(sent, "c")
        right = jnp.where(first_core, ffn_low, hidden_low)
        kept = jnp.concatenate(
            [t_dot(jnp.where(first_core, act, pre), right) for pre, act in zip(pre_lows, actives)], axis=1
        )
        return kept + received

    x1 = tokens.astype(F32)
    att1 = attention_in(0, tokens)
    attended = pair_sum(dot(att1[3], output_weight[0])) + output_bias[0]
    hidden, scaled, inverse = normalize(x1 + attended, attn_gain[0], attn_shift[0])
    hidden_low = hidden.astype(BF16)
    pre = dot(hidden_low, up_weight[0]) + up_bias[0]
    active = gelu(pre).astype(BF16)
    ffn_out = pair_sum(dot(active, down_weight[0])) + down_bias[0]
    x2, scaled_two, inverse_two = normalize(hidden + ffn_out, ffn_gain[0], ffn_shift[0])
    hidden_own = own_slots(hidden_low)
    pre_peer = dot(hidden_own, peer_up[0]) + peer_up_bias[0]
    saved1 = (
        own_slots(scaled_two),
        own_slots(inverse_two),
        (own_slots(pre), pre_peer),
        (own_slots(active), gelu(pre_peer).astype(BF16)),
        hidden_own,
        own_slots(scaled),
        own_slots(inverse),
    )

    x2_low = x2.astype(BF16)
    att2 = attention_in(1, x2_low)
    mixture = att2[3]
    received = swap(dot(piece(mixture, 1 - side, half_slots), output_weight[1]), "h")
    attended = dot(own_slots(mixture), output_weight[1]) + received + output_bias[1]
    hidden, scaled, inverse = normalize(own_slots(x2) + attended, attn_gain[1], attn_shift[1])
    hidden_low = hidden.astype(BF16)
    pre = dot(hidden_low, up_weight[1]) + up_bias[1]
    pre_peer = dot(hidden_low, peer_up[1]) + peer_up_bias[1]
    active, active_peer = gelu(pre).astype(BF16), gelu(pre_peer).astype(BF16)
    ffn_out = dot(active, down_weight[1]) + dot(active_peer, peer_down[1]) + down_bias[1]
    _, scaled_last, inverse_last = normalize(hidden + ffn_out, ffn_gain[1], ffn_shift[1])
    saved2 = (scaled_last, inverse_last, (pre, pre_peer), (active, active_peer), hidden_low, scaled, inverse)

    places = side * half_slots + jnp.arange(half_slots)
    weighting = jnp.where(places < length, repeats[0], 0).astype(F32)[:, None]
    gradient2 = own_slots(cotangent).astype(F32) * weighting
    grad_one_own, ffn_low, pre_lows, shared2, biases2 = feed_back(1, gradient2, saved2)
    grad_one2, lows2, attended_low2, into_input, small_att2 = attention_back(1, att2, x2_low, grad_one_own)
    sent = swap(into_input(lambda item: piece(item, 1 - side, half_slots)), "h")
    feed2 = feed_weights_back(saved2, ffn_low, pre_lows)
    gradient1 = grad_one_own + into_input(own_slots) + sent
    gradient1, feed2 = lax.optimization_barrier((gradient1, feed2))
    feed2 = lax.psum_scatter(feed2, PLANE, tiled=True)

    grad_one_own1, ffn_low, pre_lows, shared1, biases1 = feed_back(0, gradient1, saved1)
    grad_one1, lows1, attended_low1, into_input, small_att1 = attention_back(0, att1, tokens, grad_one_own1)
    feed1 = feed_weights_back(saved1, ffn_low, pre_lows)
    attn2 = attention_weights_back(att2, x2_low, lows2, attended_low2)
    attn1 = attention_weights_back(att1, tokens, lows1, attended_low1)
    rest = lax.psum_scatter(jnp.concatenate([feed1, attn2, attn1], axis=1), PLANE, tiled=True)

    feed2, rest = lax.optimization_barrier((feed2, rest))
    own = jnp.concatenate([feed2[:, :width], rest[:, :width], rest[:, 2 * width :]], axis=1)
    peer = jnp.concatenate([feed2[:, width:], rest[:, width : 2 * width]], axis=1)
    across = lax.ppermute(peer, ("zl", "h"), ((0, 3), (3, 0), (1, 2), (2, 1)))
    peer = swap(peer, "h") + across
    own = own + swap(own, "zl")
    own = jnp.concatenate([own[:, : 2 * width] + peer, own[:, 2 * width :]], axis=1)
    gathered = lax.all_gather(own, PLANE + ("c",)).reshape(16, 2, *own.shape)
    grad_query, grad_key, grad_value, grad_output, grad_up, grad_down = place_gradients(gathered, width)

    token_grad = grad_one1 + pair_sum(into_input(lambda item: item))
    scaled_last = after(scaled_last, token_grad)
    scaled_all = in_order(side, scaled_last, swap(scaled_last, "h"))
    block_output = (scaled_all * ffn_gain[1] + ffn_shift[1]).astype(BF16)
    shared = jnp.stack(shared1 + shared2)
    mine = jnp.concatenate([shared, biases1[0], biases2[0]])
    mine = mine + swap(jnp.concatenate([shared, biases1[1], biases2[1]]), "h")
    small = jnp.concatenate([mine, jnp.stack(small_att1 + small_att2)])
    small = after(small, block_output)
    small = small + swap(small, "c")
    for axis, pairs in LINKS:
        small = small + lax.ppermute(small, axis, pairs)
    small = small + swap(small, "zl")
    bias_rows = units // width
    shared = small[:10].reshape(2, 5, width)
    grad_up_bias = small[10 : 10 + 2 * bias_rows].reshape(2, units)
    attention = small[10 + 2 * bias_rows :].reshape(2, 2, width)

    return (
        block_output,
        token_grad,
        grad_query,
        attention[:, 0, :columns],
        grad_key,
        grad_value,
        attention[:, 0, columns:],
        grad_output,
        attention[:, 1],
        shared[:, 0],
        shared[:, 1],
        grad_up,
        grad_up_bias,
        grad_down,
        shared[:, 2],
        shared[:, 3],
        shared[:, 4],
    )


def solution(mesh):
    fine = Mesh(mesh.devices.reshape(4, 2, 4, 2, 2), ("y", "zl", "x", "c", "h"))
    rows = ("y", "zl", "x", "c")
    in_specs = (
        P(rows, None),
        P(rows, None),
        P(rows),
        P(rows),
        P(None, None, "h"),
        P(None, "h"),
        P(None, None, "h"),
        P(None, None, "h"),
        P(None, "h"),
        P(None, "h", None),
        P(),
        P(),
        P(),
        P(None, None, "h"),
        P(None, "h"),
        P(None, "h", None),
        P(),
        P(),
        P(),
    )
    out_specs = (
        P(rows, None),
        P(rows, None),
        P(None, None, "h"),
        P(None, "h"),
        P(None, None, "h"),
        P(None, None, "h"),
        P(None, "h"),
        P(None, "h", None),
        P(),
        P(),
        P(),
        P(None, None, "h"),
        P(None, "h"),
        P(None, "h", None),
        P(),
        P(),
        P(),
    )
    return jax.shard_map(local, mesh=fine, in_specs=in_specs, out_specs=out_specs, check_vma=False)
```

time: 1290 us -> 682 us (0.53)
  waiting for transfers between devices: 780 us -> 350 us
  blocking collectives: 280 us -> 0 us
  local copies, waits for them, and re-layouts: 41.1 us -> 75.6 us
  starting transfers between devices: 1.35 us -> 34.4 us
  Pallas kernels: 0 us -> 32 us
  matrix products: 107 us -> 84.3 us
  other arithmetic: 56.2 us -> 78.1 us
    psum x9 -> x0, waiting for transfers between devices: 780 us -> none  [the longest x1 393 us: whole_sum(): lax.psum((parts[0], parts[1], parts[2], parts[3], parts[4], parts[5], par...]
    psum x1 -> x0, blocking collectives: 280 us -> none  [whole_sum(): lax.psum((parts[0], parts[1], parts[2], parts[3], parts[4], parts[5], par...]
    ppermute x0 -> x24, waiting for transfers between devices: none -> 251 us  [the longest x19 226 us: swap(): return lax.ppermute(values, axis, SWAP)]
    unnamed x9 -> x6, waiting for transfers between devices: 0.15 us -> 98.9 us
    ppermute x0 -> x24, starting transfers between devices: none -> 34.1 us  [the longest x19 31.7 us: swap(): return lax.ppermute(values, axis, SWAP)]
    pallas_call x0 -> x3, Pallas kernels: none -> 32 us  [the longest x1 15.6 us: place_gradients(): pl.pallas_call(place_feed_kernel, grid=(2, chips // step), in_specs=[feed...]
    concatenate x0 -> x11, other arithmetic: none -> 29.7 us  [the longest x2 14.3 us: feed_weights_back(): jnp.concatenate([t_dot(jnp.where(first_core, pre, act), right) for pre, a...]
    dot_general x48 -> x63, matrix products: 107 us -> 84.3 us  [the longest x19 24.1 us: dot_t(): return jnp.einsum('sd,fd->sf', left, right, preferred_element_type=F32)]
  transfers between devices with their start and end apart: 9 -> 28, of which waited for: 8 -> 18; matrix products, arithmetic and copies ran while one was open for 4% -> 24% of each run, Pallas kernels for 0% -> 0%
where the time goes in v1:
time: 682 us; the launch traced here: 672 us
  waiting for transfers between devices  350 us (51%)
  matrix products  84.3 us (12%)
  other arithmetic  78.1 us (11%)
  local copies, waits for them, and re-layouts  75.6 us (11%)
  starting transfers between devices  34.4 us (5%)
  Pallas kernels  32 us (5%)
  between operations  17.9 us (3%)
    ppermute x19, waiting for transfers between devices, swap(): return lax.ppermute(values, axis, SWAP)  226 us
    unnamed x6, waiting for transfers between devices  98.9 us
    unnamed x362, local copies, waits for them, and re-layouts  54 us
    ppermute x19, starting transfers between devices, swap(): return lax.ppermute(values, axis, SWAP)  31.7 us
    ppermute x4, waiting for transfers between devices, local(): small = small + lax.ppermute(small, axis, pairs)  25.2 us
    dot_general x19, matrix products, dot_t(): return jnp.einsum('sd,fd->sf', left, right, preferred_element_type=F32)  24.1 us
    dot_general x16, matrix products, dot(): return jnp.dot(left, right, preferred_element_type=F32)  22.9 us
    dot_general x16, matrix products, t_dot(): return jnp.einsum('sf,sd->fd', left, right, preferred_element_type=F32)  18.1 us
  transfers between devices with their start and end apart: 28, of which 18 were waited for; matrix products, arithmetic and copies ran while one was open for 24% of the time, Pallas kernels for 0%

profile of v1, /device:TPU:0, one launch (start us, length us, event | category | flops | bytes accessed | tf_op | source)
XLA Modules:
  0.0 672.3 jit_solution(689222423615003709)
XLA Ops:
  7.2 4.1 fusion.256
  12.3 4.1 fusion.255
  19.0 4.0 collective-permute-start.3
  23.0 13.3 %collective-permute-done.3 = f32[192,768]{1,0:T(8,128)S(1)} collective-permute-done((f32[192,768]{1,0:T(8,128)S(1)}, f32[192,768]{1,0:T(8,128)S(1)}, u32[]{:S(2)}, u32[]{:S(2)}) %collective-permute-start.3) | collective-permute-done | bytes 589856 | tf_op jit(solution)/shard_map/ppermute | solution.py:102
  45.1 1.8 copy-done.2
  48.8 3.3 collective-permute-start
  54.6 31.4 %collective-permute-done = f32[512,768]{1,0:T(8,128)S(1)} collective-permute-done((f32[512,768]{1,0:T(8,128)S(1)}, f32[512,768]{1,0:T(8,128)S(1)}, u32[]{:S(2)}, u32[]{:S(2)}) %collective-permute-start) | collective-permute-done | bytes 1572896 | tf_op jit(solution)/shard_map/ppermute | solution.py:102
  87.2 3.0 multiply_convert_fusion.2
  90.2 1.9 slice-done.9
  92.1 2.5 fusion.35
  94.6 3.1 collective-permute-start.1
  99.0 32.3 %collective-permute-done.1 = f32[512,768]{1,0:T(8,128)} collective-permute-done((f32[512,768]{1,0:T(8,128)}, f32[512,768]{1,0:T(8,128)}, u32[]{:S(2)}, u32[]{:S(2)}) %collective-permute-start.1) | collective-permute-done | bytes 1572896 | tf_op jit(solution)/shard_map/ppermute | solution.py:102
  131.3 2.3 fusion.253
  141.4 1.8 copy-done.3
  144.9 2.7 collective-permute-start.2
  150.5 13.3 %collective-permute-done.4 = f32[2,1536]{1,0:T(2,128)} collective-permute-done((f32[2,1536]{1,0:T(2,128)}, f32[2,1536]{1,0:T(2,128)}, u32[]{:S(2)}, u32[]{:S(2)}) %collective-permute-start.4) | collective-permute-done | bytes 12320 | tf_op jit(solution)/shard_map/ppermute | solution.py:102
  167.5 3.6 multiply_convert_fusion.5
  171.2 2.7 fusion.29
  173.9 8.4 %sort_weights.1 = (bf16[2,1536,768]{2,1,0:T(8,128)(2,1)S(1)}, bf16[2,768,1536]{2,1,0:T(8,128)(2,1)S(1)}) custom-call(f32[16,2,2,96,768]{4,3,2,1,0:T(8,128)} %bitcast.280), custom_call_target="tpu_custom_call" | custom-call | bytes 28311552 | tf_op jit(solution)/shard_map/sort_weights/pallas_call | solution.py:135
  186.8 1.8 convert_reduce_fusion.2
  189.6 1.8 convert_reduce_fusion.4
  192.8 3.0 fusion.132
  195.8 6.9 %pad_maximum_fusion = f32[1536,1536]{0,1:T(8,128)} fusion(f32[1536,768]{0,1:T(8,128)S(1)} %fusion.130, f32[1536,768]{0,1:T(8,128)} %fusion.132), kind=kLoop, calls=%fused_computation.2 | loop fusion | flops 2359296 | bytes 18874368 | tf_op jit(solution)/shard_map/concatenate | solution.py:323
  202.8 3.1 fusion.79
  209.0 2.7 collective-permute-start.5
  211.8 2.5 fusion.134
  214.3 16.7 %collective-permute-done.5 = f32[256,768]{1,0:T(8,128)} collective-permute-done((f32[256,768]{1,0:T(8,128)}, f32[256,768]{1,0:T(8,128)}, u32[]{:S(2)}, u32[]{:S(2)}) %collective-permute-start.5) | collective-permute-done | bytes 786464 | tf_op jit(solution)/shard_map/ppermute | solution.py:102
  234.4 4.0 multiply_reduce_fusion.1
  238.4 4.6 multiply_convert_fusion.1
  247.7 1.8 convert_reduce_fusion.6
  249.9 2.4 collective-permute-start.6
  254.0 16.4 %collective-permute-done.6 = f32[256,768]{1,0:T(8,128)S(1)} collective-permute-done((f32[256,768]{1,0:T(8,128)S(1)}, f32[256,768]{1,0:T(8,128)S(1)}, u32[]{:S(2)}, u32[]{:S(2)}) %collective-permute-start.6) | collective-permute-done | bytes 786464 | tf_op jit(solution)/shard_map/ppermute | solution.py:102
  270.9 7.3 %maximum_add_fusion = f32[1536,1536]{0,1:T(8,128)} fusion(f32[1536,1536]{0,1:T(8,128)} %collective-permute-done.7, f32[1536,768]{0,1:T(8,128)S(1)} %fusion.134, f32[1536,768]{0,1:T(8,128)S(1)} %fusion.136), kind=kLoop, calls=%fused_computation.1 | loop fusion | flops 4718592 | bytes 28311552 | tf_op jit(solution)/shard_map/add | solution.py:331
  278.3 9.6 %copy.130 = f32[1536,1536]{1,0:T(8,128)} copy(f32[1536,1536]{0,1:T(8,128)} %maximum_add_fusion) | data formatting | bytes 18874368
  289.0 2.6 fusion.43
  294.1 3.5 convert_reduce_fusion.5
  299.5 1.8 convert_reduce_fusion.3
  302.2 3.1 fusion.122
  305.3 7.4 %pad_maximum_fusion.1 = f32[1536,1536]{0,1:T(8,128)} fusion(f32[1536,768]{0,1:T(8,128)} %fusion.122, f32[1536,768]{0,1:T(8,128)S(1)} %fusion.124), kind=kLoop, calls=%fused_computation.4 | loop fusion | flops 2359296 | bytes 18874368 | tf_op jit(solution)/shard_map/concatenate | solution.py:323
  312.7 3.6 fusion.76
  318.1 2.6 collective-permute-start.8
  323.9 15.4 %collective-permute-done.8 = f32[256,768]{1,0:T(8,128)S(1)} collective-permute-done((f32[256,768]{1,0:T(8,128)S(1)}, f32[256,768]{1,0:T(8,128)S(1)}, u32[]{:S(2)}, u32[]{:S(2)}) %collective-permute-start.8) | collective-permute-done | bytes 786464 | tf_op jit(solution)/shard_map/ppermute | solution.py:102
  339.7 1.9 copy-done.71
  343.6 1.9 multiply_convert_fusion
  349.2 1.8 broadcast_select_fusion.2
  354.1 2.0 maximum_add_fusion.2
  364.7 4.9 maximum_add_fusion.1
  369.7 11.5 %maximum_maximum_fusion = f32[1536,2304]{0,1:T(8,128)} fusion(f32[768,384]{0,1:T(8,128)} %get-tuple-element.108, f32[768,384]{0,1:T(8,128)} %get-tuple-element.107, f32[768,384]{0,1:T(8,128)} %get-tuple-element.106, f32[768,384]{0,1:T(8,128)S(1)} %copy-done.55, f32[1536,1536]{0,1:T(8,128)S(1)} %maximum_add_fusion.1), kind=kLoop, calls=%fused_computation | loop fusion | flops 14155776 | bytes 28311552 | tf_op jit(solution)/shard_map/concatenate | solution.py:384
  381.2 15.2 %copy.132 = f32[1536,2304]{1,0:T(8,128)} copy(f32[1536,2304]{0,1:T(8,128)} %maximum_maximum_fusion) | data formatting | bytes 28311552
  397.8 98.8 %reduce-scatter.9.cloned.1.call-done = f32[96,2304]{1,0:T(8,128)} async-done(((f32[1536,2304]{1,0:T(8,128)}), f32[96,2304]{1,0:T(8,128)}) %reduce-scatter.9.cloned.1.call-update) | async-done | bytes 884752
  501.8 1.7 collective-permute-start.14
  503.8 2.9 collective-permute-start.15
  507.2 17.4 %collective-permute-done.14 = f32[96,2304]{1,0:T(8,128)} collective-permute-done((f32[96,2304]{1,0:T(8,128)}, f32[96,2304]{1,0:T(8,128)}, u32[]{:S(2)}, u32[]{:S(2)}) %collective-permute-start.14) | collective-permute-done | bytes 884768 | tf_op jit(solution)/shard_map/ppermute | solution.py:102
  525.9 12.4 %collective-permute-done.15 = f32[96,1536]{1,0:T(8,128)S(1)} collective-permute-done((f32[96,1536]{1,0:T(8,128)S(1)}, f32[96,1536]{1,0:T(8,128)S(1)}, u32[]{:S(2)}, u32[]{:S(2)}) %collective-permute-start.15) | collective-permute-done | bytes 589856 | tf_op jit(solution)/shard_map/ppermute | solution.py:102
  543.8 36.0 %collective-permute-done.9 = f32[512,768]{1,0:T(8,128)S(1)} collective-permute-done((f32[512,768]{1,0:T(8,128)S(1)}, f32[512,768]{1,0:T(8,128)S(1)}, u32[]{:S(2)}, u32[]{:S(2)}) %collective-permute-start.9) | collective-permute-done | bytes 1572896 | tf_op jit(solution)/shard_map/ppermute | solution.py:102
  582.4 2.9 collective-permute-start.17
  585.4 15.7 %collective-permute-done.17 = f32[14,768]{1,0:T(8,128)S(1)} collective-permute-done((f32[14,768]{1,0:T(8,128)S(1)}, f32[14,768]{1,0:T(8,128)S(1)}, u32[]{:S(2)}, u32[]{:S(2)}) %collective-permute-start.17) | collective-permute-done | bytes 43040 | tf_op jit(solution)/shard_map/ppermute | solution.py:102
  604.6 6.4 collective-permute-done.19
  611.9 6.6 collective-permute-done.20
  618.5 5.9 collective-permute-done.21
  625.3 6.4 collective-permute-done.22
  631.9 4.2 collective-permute-done.23
  641.6 8.0 %place_attention.1 = (f32[2,768,384]{2,1,0:T(8,128)}, f32[2,768,384]{2,1,0:T(8,128)}, f32[2,768,384]{2,1,0:T(8,128)}, f32[2,384,768]{2,1,0:T(8,128)}) custom-call(f32[16,2,96,2304]{3,2,1,0:T(8,128)} %bitcast.270, f32[16,2,96,2304]{3,2,1,0:T(8,128)} %bitcast.271, f32[16,2,96,2304]{3,2,1,0:T(8,128)} %bitcast.272, f32[16,2,96,2304]{3,2,1,0:T(8,128)} %bitcast.273), custom_call_target="tpu_custom_call" | custom-call | tf_op jit(solution)/shard_map/place_attention/pallas_call | solution.py:200
  649.6 15.6 %place_feed.1 = (f32[2,1536,768]{2,1,0:T(8,128)}, f32[2,768,1536]{2,1,0:T(8,128)}) custom-call(f32[16,2,96,2304]{3,2,1,0:T(8,128)} %bitcast.274, f32[16,2,96,2304]{3,2,1,0:T(8,128)} %bitcast.275), custom_call_target="tpu_custom_call" | custom-call | tf_op jit(solution)/shard_map/place_feed/pallas_call | solution.py:183
  (566 shorter events, 109.9 us)
Async XLA Ops:
  7.2 166.7 %all-gather.5.cloned.1.call-start = ((), (), s32[]{:S(2)}) async-start(), calls=%async_computation.2 | async-start | bytes 19464192 | tf_op jit(solution)/shard_map/all_gather | solution.py:249
  16.4 22.1 %copy-start.150 = (bf16[2,384]{1,0:T(2,128)(2,1)S(1)}, bf16[2,384]{1,0:T(2,128)(2,1)}, u32[]{:S(2)}) copy-start(bf16[2,384]{1,0:T(2,128)(2,1)} %param.24) | copy-start | bytes 4612
  16.4 22.7 %copy-start.6 = (bf16[512,768]{1,0:T(8,128)(2,1)S(1)}, bf16[512,768]{1,0:T(8,128)(2,1)}, u32[]{:S(2)}) copy-start(bf16[512,768]{1,0:T(8,128)(2,1)} %param.19) | copy-start | bytes 2359300
  18.9 21.8 %copy-start.72 = (bf16[2,768,384]{2,1,0:T(8,128)(2,1)S(1)}, bf16[2,768,384]{2,1,0:T(8,128)(2,1)}, u32[]{:S(2)}) copy-start(bf16[2,768,384]{2,1,0:T(8,128)(2,1)} %param.26) | copy-start | bytes 3538948
  19.0 17.4 %collective-permute-start.3 = (f32[192,768]{1,0:T(8,128)S(1)}, f32[192,768]{1,0:T(8,128)S(1)}, u32[]{:S(2)}, u32[]{:S(2)}) collective-permute-start(f32[192,768]{1,0:T(8,128)S(1)} %maximum_convert_fusion), channel_id=1, source_target_pairs={{0,1},{1,0},{2,3},{3,2},{4,5},{5,4},{6,7},{7,6},{8,9},{9,8},{10,11... | collective-permute-start | bytes 1769480 | tf_op jit(solution)/shard_map/ppermute | solution.py:102
  37.2 359.3 %reduce-scatter.7.cloned.1.call-start = ((), (), s32[]{:S(2)}) async-start(), calls=%async_computation.4 | async-start | bytes 10027008
  48.1 37.8 %copy-start.88 = (bf16[6,64,512]{2,1,0:T(8,128)(2,1)}, bf16[6,64,512]{2,1,0:T(8,128)(2,1)S(1)}, u32[]{:S(2)}) copy-start(bf16[6,64,512]{2,1,0:T(8,128)(2,1)S(1)} %fusion.112) | copy-start | bytes 1179652
  48.2 39.0 %slice-start.12 = ((s8[4718592]{0:T(1024)(128)(4,1)}), s8[4194304]{0:T(1024)(128)(4,1)S(1)}, s32[]{:S(2)}) async-start(s8[4718592]{0:T(1024)(128)(4,1)} %bitcast.297), calls=%async_computation.18 | async-start | bytes 8388608
  48.8 37.2 %collective-permute-start = (f32[512,768]{1,0:T(8,128)S(1)}, f32[512,768]{1,0:T(8,128)S(1)}, u32[]{:S(2)}, u32[]{:S(2)}) collective-permute-start(f32[512,768]{1,0:T(8,128)S(1)} %fusion.174), channel_id=1, source_target_pairs={{0,1},{1,0},{2,3},{3,2},{4,5},{5,4},{6,7},{7,6},{8,9},{9,8},{10,11... | collective-permute-start | bytes 4718600 | tf_op jit(solution)/shard_map/ppermute | solution.py:102
  53.3 33.3 %copy-start.117 = (f32[768]{0:T(1024)}, f32[768]{0:T(1024)S(1)}, u32[]{:S(2)}) copy-start(f32[768]{0:T(1024)S(1)} %get-tuple-element.74) | copy-start | bytes 9220
  53.9 32.7 %copy-start.104 = (f32[768]{0:T(1024)}, f32[768]{0:T(1024)S(1)}, u32[]{:S(2)}) copy-start(f32[768]{0:T(1024)S(1)} %get-tuple-element.72) | copy-start | bytes 9220
  87.2 44.1 %copy-start.15 = (f32[512,768]{1,0:T(8,128)}, f32[512,768]{1,0:T(8,128)S(1)}, u32[]{:S(2)}) copy-start(f32[512,768]{1,0:T(8,128)S(1)} %get-tuple-element.98) | copy-start | bytes 4718596
  92.1 39.2 %copy-start.105 = (f32[768]{0:T(1024)S(1)}, f32[768]{0:T(1024)}, u32[]{:S(2)}) copy-start(f32[768]{0:T(1024)} %copy-done.104) | copy-start | bytes 9220
  92.1 39.2 %copy-start.118 = (f32[768]{0:T(1024)S(1)}, f32[768]{0:T(1024)}, u32[]{:S(2)}) copy-start(f32[768]{0:T(1024)} %copy-done.117) | copy-start | bytes 9220
  94.6 36.7 %collective-permute-start.1 = (f32[512,768]{1,0:T(8,128)}, f32[512,768]{1,0:T(8,128)}, u32[]{:S(2)}, u32[]{:S(2)}) collective-permute-start(f32[512,768]{1,0:T(8,128)} %fusion.35), channel_id=1, source_target_pairs={{0,1},{1,0},{2,3},{3,2},{4,5},{5,4},{6,7},{7,6},{8,9},{9,8},{10,11... | collective-permute-start | bytes 4718600 | tf_op jit(solution)/shard_map/ppermute | solution.py:102
  99.0 35.0 %copy-start.107 = (f32[768]{0:T(1024)}, f32[768]{0:T(1024)S(1)}, u32[]{:S(2)}) copy-start(f32[768]{0:T(1024)S(1)} %get-tuple-element.168) | copy-start | bytes 9220
  144.4 22.3 %copy-start.59 = (bf16[6,64,512]{2,1,0:T(8,128)(2,1)}, bf16[6,64,512]{2,1,0:T(8,128)(2,1)S(1)}, u32[]{:S(2)}) copy-start(bf16[6,64,512]{2,1,0:T(8,128)(2,1)S(1)} %fusion.111) | copy-start | bytes 1179652
  144.9 20.3 %collective-permute-start.2 = (f32[256,768]{1,0:T(8,128)S(1)}, f32[256,768]{1,0:T(8,128)S(1)}, u32[]{:S(2)}, u32[]{:S(2)}) collective-permute-start(f32[256,768]{1,0:T(8,128)S(1)} %fusion.157), channel_id=1, source_target_pairs={{0,1},{1,0},{2,3},{3,2},{4,5},{5,4},{6,7},{7,6},{8,9},{9,8},{10,11... | collective-permute-start | bytes 2359304 | tf_op jit(solution)/shard_map/ppermute | solution.py:102
  148.2 15.5 %collective-permute-start.4 = (f32[2,1536]{1,0:T(2,128)}, f32[2,1536]{1,0:T(2,128)}, u32[]{:S(2)}, u32[]{:S(2)}) collective-permute-start(f32[2,1536]{1,0:T(2,128)} %convert_element_type.296), channel_id=1, source_target_pairs={{0,1},{1,0},{2,3},{3,2},{4,5},{5,4},{6,7},{7,6},{8,9},{9,8},{10,11... | collective-permute-start | bytes 36872 | tf_op jit(solution)/shard_map/ppermute | solution.py:102
  182.3 23.6 %copy-start = (bf16[2,768,1536]{2,1,0:T(8,128)(2,1)}, bf16[2,768,1536]{2,1,0:T(8,128)(2,1)S(1)}, u32[]{:S(2)}) copy-start(bf16[2,768,1536]{2,1,0:T(8,128)(2,1)S(1)} %get-tuple-element.31) | copy-start | bytes 14155780
  202.8 68.2 %collective-permute-start.7 = (f32[1536,1536]{0,1:T(8,128)}, f32[1536,1536]{0,1:T(8,128)}, u32[]{:S(2)}, u32[]{:S(2)}) collective-permute-start(f32[1536,1536]{0,1:T(8,128)} %pad_maximum_fusion), channel_id=1, source_target_pairs={{0,2},{2,0},{1,3},{3,1},{4,6},{6,4},{5,7},{7,5},{8,10},{10,8},{9,1... | collective-permute-start | bytes 28311560 | tf_op jit(solution)/shard_map/ppermute | solution.py:102
  207.5 26.6 %slice-start.6 = ((s8[6291456]{0:T(1024)(128)(4,1)}), s8[2097152]{0:T(1024)(128)(4,1)S(1)}, s32[]{:S(2)}) async-start(s8[6291456]{0:T(1024)(128)(4,1)} %bitcast.278), calls=%async_computation.12 | async-start | bytes 4194304
  209.0 22.0 %collective-permute-start.5 = (f32[256,768]{1,0:T(8,128)}, f32[256,768]{1,0:T(8,128)}, u32[]{:S(2)}, u32[]{:S(2)}) collective-permute-start(f32[256,768]{1,0:T(8,128)} %get-tuple-element.89), channel_id=1, source_target_pairs={{0,1},{1,0},{2,3},{3,2},{4,5},{5,4},{6,7},{7,6},{8,9},{9,8},{10,11... | collective-permute-start | bytes 2359304 | tf_op jit(solution)/shard_map/ppermute | solution.py:102
  211.7 22.3 %slice-start.7 = ((s8[6291456]{0:T(1024)(128)(4,1)}), s8[4194304]{0:T(1024)(128)(4,1)S(1)}, s32[]{:S(2)}) async-start(s8[6291456]{0:T(1024)(128)(4,1)} %bitcast.278), calls=%async_computation.13 | async-start | bytes 8388608
  249.9 20.6 %collective-permute-start.6 = (f32[256,768]{1,0:T(8,128)S(1)}, f32[256,768]{1,0:T(8,128)S(1)}, u32[]{:S(2)}, u32[]{:S(2)}) collective-permute-start(f32[256,768]{1,0:T(8,128)S(1)} %convolution_add_fusion.2), channel_id=1, source_target_pairs={{0,1},{1,0},{2,3},{3,2},{4,5},{5,4},{6,7},{7,6},{8,9},{9,8},{10,11... | collective-permute-start | bytes 2359304 | tf_op jit(solution)/shard_map/ppermute | solution.py:102
  270.9 21.5 %copy-start.30 = (f32[256,768]{1,0:T(8,128)}, f32[256,768]{1,0:T(8,128)S(1)}, u32[]{:S(2)}) copy-start(f32[256,768]{1,0:T(8,128)S(1)} %fusion.75) | copy-start | bytes 2359300
  287.9 208.7 %reduce-scatter.9.cloned.1.call-start = ((), (), s32[]{:S(2)}) async-start(), calls=%async_computation.5 | async-start | bytes 15040512
  312.6 52.1 %collective-permute-start.11 = (f32[1536,1536]{0,1:T(8,128)}, f32[1536,1536]{0,1:T(8,128)}, u32[]{:S(2)}, u32[]{:S(2)}) collective-permute-start(f32[1536,1536]{0,1:T(8,128)} %pad_maximum_fusion.1), channel_id=1, source_target_pairs={{0,2},{2,0},{1,3},{3,1},{4,6},{6,4},{5,7},{7,5},{8,10},{10,8},{9,1... | collective-permute-start | bytes 28311560 | tf_op jit(solution)/shard_map/ppermute | solution.py:102
  318.1 21.2 %collective-permute-start.8 = (f32[256,768]{1,0:T(8,128)S(1)}, f32[256,768]{1,0:T(8,128)S(1)}, u32[]{:S(2)}, u32[]{:S(2)}) collective-permute-start(f32[256,768]{1,0:T(8,128)S(1)} %multiply_multiply_fusion.4), channel_id=1, source_target_pairs={{0,1},{1,0},{2,3},{3,2},{4,5},{5,4},{6,7},{7,6},{8,9},{9,8},{10,11... | collective-permute-start | bytes 2359304 | tf_op jit(solution)/shard_map/ppermute | solution.py:102
  323.7 30.4 %collective-permute-start.12 = (f32[768,768]{0,1:T(8,128)}, f32[768,768]{0,1:T(8,128)}, u32[]{:S(2)}, u32[]{:S(2)}) collective-permute-start(f32[768,768]{0,1:T(8,128)} %pad_maximum_fusion.2), channel_id=1, source_target_pairs={{0,2},{2,0},{1,3},{3,1},{4,6},{6,4},{5,7},{7,5},{8,10},{10,8},{9,1... | collective-permute-start | bytes 7077896 | tf_op jit(solution)/shard_map/ppermute | solution.py:102
  351.9 11.0 %collective-permute-start.13 = (f32[768,768]{0,1:T(8,128)S(1)}, f32[768,768]{0,1:T(8,128)S(1)}, u32[]{:S(2)}, u32[]{:S(2)}) collective-permute-start(f32[768,768]{0,1:T(8,128)S(1)} %pad_maximum_fusion.3), channel_id=1, source_target_pairs={{0,2},{2,0},{1,3},{3,1},{4,6},{6,4},{5,7},{7,5},{8,10},{10,8},{9,1... | collective-permute-start | bytes 7077896 | tf_op jit(solution)/shard_map/ppermute | solution.py:102
  396.4 245.2 %all-gather.7.cloned.1.call-start = ((), (), s32[]{:S(2)}) async-start(), calls=%async_computation.3 | async-start | bytes 29196288 | tf_op jit(solution)/shard_map/all_gather | solution.py:393
  501.8 22.9 %collective-permute-start.14 = (f32[96,2304]{1,0:T(8,128)}, f32[96,2304]{1,0:T(8,128)}, u32[]{:S(2)}, u32[]{:S(2)}) collective-permute-start(f32[96,2304]{1,0:T(8,128)} %pad_maximum_fusion.4), channel_id=1, source_target_pairs={{0,16},{16,0},{1,17},{17,1},{2,18},{18,2},{3,19},{19,3},{4,20},{20... | collective-permute-start | bytes 2654216 | tf_op jit(solution)/shard_map/ppermute | solution.py:102
  503.8 34.6 %collective-permute-start.15 = (f32[96,1536]{1,0:T(8,128)S(1)}, f32[96,1536]{1,0:T(8,128)S(1)}, u32[]{:S(2)}, u32[]{:S(2)}) collective-permute-start(f32[96,1536]{1,0:T(8,128)S(1)} %copy.112), channel_id=1, source_target_pairs={{0,1},{1,0},{2,3},{3,2},{4,5},{5,4},{6,7},{7,6},{8,9},{9,8},{10,11... | collective-permute-start | bytes 1769480 | tf_op jit(solution)/shard_map/ppermute | solution.py:102
  506.7 31.6 %collective-permute-start.16 = (f32[96,1536]{1,0:T(8,128)S(1)}, f32[96,1536]{1,0:T(8,128)S(1)}, u32[]{:S(2)}, u32[]{:S(2)}) collective-permute-start(f32[96,1536]{1,0:T(8,128)S(1)} %copy.112), channel_id=1, source_target_pairs={{0,17},{17,0},{1,16},{16,1},{2,19},{19,2},{3,18},{18,3},{4,21},{21... | collective-permute-start | bytes 1769480 | tf_op jit(solution)/shard_map/ppermute | solution.py:389
  542.2 37.5 %copy-start.32 = (f32[256,768]{1,0:T(8,128)S(1)}, f32[256,768]{1,0:T(8,128)}, u32[]{:S(2)}) copy-start(f32[256,768]{1,0:T(8,128)} %copy-done.31) | copy-start | bytes 2359300
  542.2 37.5 %copy-start.34 = (f32[256,768]{1,0:T(8,128)S(1)}, f32[256,768]{1,0:T(8,128)}, u32[]{:S(2)}) copy-start(f32[256,768]{1,0:T(8,128)} %copy-done.33) | copy-start | bytes 2359300
  542.8 38.3 %copy-start.36 = (f32[256,768]{1,0:T(8,128)S(1)}, f32[256,768]{1,0:T(8,128)}, u32[]{:S(2)}) copy-start(f32[256,768]{1,0:T(8,128)} %copy-done.35) | copy-start | bytes 2359300
  542.8 39.0 %copy-start.153 = (f32[768]{0:T(1024)S(1)}, f32[768]{0:T(1024)}, u32[]{:S(2)}) copy-start(f32[768]{0:T(1024)} %get-tuple-element.49) | copy-start | bytes 9220
  542.8 39.0 %copy-start.152 = (f32[768]{0:T(1024)S(1)}, f32[768]{0:T(1024)}, u32[]{:S(2)}) copy-start(f32[768]{0:T(1024)} %get-tuple-element.58) | copy-start | bytes 9220
  542.9 39.0 %copy-start.124 = (f32[768]{0:T(1024)S(1)}, f32[768]{0:T(1024)}, u32[]{:S(2)}) copy-start(f32[768]{0:T(1024)} %get-tuple-element.85) | copy-start | bytes 9220
  542.9 39.0 %copy-start.123 = (f32[768]{0:T(1024)S(1)}, f32[768]{0:T(1024)}, u32[]{:S(2)}) copy-start(f32[768]{0:T(1024)} %get-tuple-element.51) | copy-start | bytes 9220
  542.9 39.0 %copy-start.122 = (f32[768]{0:T(1024)S(1)}, f32[768]{0:T(1024)}, u32[]{:S(2)}) copy-start(f32[768]{0:T(1024)} %get-tuple-element.57) | copy-start | bytes 9220
  542.9 39.0 %copy-start.146 = (f32[1536]{0:T(1024)S(1)}, f32[1536]{0:T(1024)}, u32[]{:S(2)}) copy-start(f32[1536]{0:T(1024)} %get-tuple-element.156) | copy-start | bytes 18436
  542.9 39.1 %copy-start.145 = (f32[1536]{0:T(1024)S(1)}, f32[1536]{0:T(1024)}, u32[]{:S(2)}) copy-start(f32[1536]{0:T(1024)} %get-tuple-element.160) | copy-start | bytes 18436
  542.9 39.1 %copy-start.130 = (f32[6,64]{1,0:T(8,128)S(1)}, f32[6,64]{1,0:T(8,128)}, u32[]{:S(2)}) copy-start(f32[6,64]{1,0:T(8,128)} %get-tuple-element.164) | copy-start | bytes 4612
  542.9 39.2 %copy-start.129 = (f32[6,64]{1,0:T(8,128)S(1)}, f32[6,64]{1,0:T(8,128)}, u32[]{:S(2)}) copy-start(f32[6,64]{1,0:T(8,128)} %get-tuple-element.166) | copy-start | bytes 4612
  542.9 39.2 %copy-start.155 = (f32[768]{0:T(1024)S(1)}, f32[768]{0:T(1024)}, u32[]{:S(2)}) copy-start(f32[768]{0:T(1024)} %get-tuple-element.47) | copy-start | bytes 9220
  542.9 39.2 %copy-start.154 = (f32[768]{0:T(1024)S(1)}, f32[768]{0:T(1024)}, u32[]{:S(2)}) copy-start(f32[768]{0:T(1024)} %get-tuple-element.60) | copy-start | bytes 9220
  543.0 39.2 %copy-start.128 = (f32[768]{0:T(1024)S(1)}, f32[768]{0:T(1024)}, u32[]{:S(2)}) copy-start(f32[768]{0:T(1024)} %get-tuple-element.87) | copy-start | bytes 9220
  543.0 39.2 %copy-start.127 = (f32[768]{0:T(1024)S(1)}, f32[768]{0:T(1024)}, u32[]{:S(2)}) copy-start(f32[768]{0:T(1024)} %get-tuple-element.45) | copy-start | bytes 9220
  543.0 39.2 %copy-start.126 = (f32[768]{0:T(1024)S(1)}, f32[768]{0:T(1024)}, u32[]{:S(2)}) copy-start(f32[768]{0:T(1024)} %get-tuple-element.59) | copy-start | bytes 9220
  543.0 39.3 %copy-start.148 = (f32[1536]{0:T(1024)S(1)}, f32[1536]{0:T(1024)}, u32[]{:S(2)}) copy-start(f32[1536]{0:T(1024)} %get-tuple-element.158) | copy-start | bytes 18436
  543.0 42.3 %copy-start.125 = (f32[768]{0:T(1024)S(1)}, f32[768]{0:T(1024)}, u32[]{:S(2)}) copy-start(f32[768]{0:T(1024)} %get-tuple-element.81) | copy-start | bytes 9220
  543.0 42.3 %copy-start.147 = (f32[1536]{0:T(1024)S(1)}, f32[1536]{0:T(1024)}, u32[]{:S(2)}) copy-start(f32[1536]{0:T(1024)} %get-tuple-element.154) | copy-start | bytes 18436
  543.0 36.7 %collective-permute-start.9 = (f32[512,768]{1,0:T(8,128)S(1)}, f32[512,768]{1,0:T(8,128)S(1)}, u32[]{:S(2)}, u32[]{:S(2)}) collective-permute-start(f32[512,768]{1,0:T(8,128)S(1)} %add_add_fusion.1), channel_id=1, source_target_pairs={{0,1},{1,0},{2,3},{3,2},{4,5},{5,4},{6,7},{7,6},{8,9},{9,8},{10,11... | collective-permute-start | bytes 4718600 | tf_op jit(solution)/shard_map/ppermute | solution.py:102
  581.2 20.3 %collective-permute-start.10 = (f32[256,768]{1,0:T(8,128)S(1)}, f32[256,768]{1,0:T(8,128)S(1)}, u32[]{:S(2)}, u32[]{:S(2)}) collective-permute-start(f32[256,768]{1,0:T(8,128)S(1)} %copy-done.36), channel_id=1, source_target_pairs={{0,1},{1,0},{2,3},{3,2},{4,5},{5,4},{6,7},{7,6},{8,9},{9,8},{10,11... | collective-permute-start | bytes 2359304 | tf_op jit(solution)/shard_map/ppermute | solution.py:102
  582.4 18.7 %collective-permute-start.17 = (f32[14,768]{1,0:T(8,128)S(1)}, f32[14,768]{1,0:T(8,128)S(1)}, u32[]{:S(2)}, u32[]{:S(2)}) collective-permute-start(f32[14,768]{1,0:T(8,128)S(1)} %concatenate.102), channel_id=1, source_target_pairs={{0,1},{1,0},{2,3},{3,2},{4,5},{5,4},{6,7},{7,6},{8,9},{9,8},{10,11... | collective-permute-start | bytes 129032 | tf_op jit(solution)/shard_map/ppermute | solution.py:102
  603.2 1.3 collective-permute-start.18
  604.5 6.5 collective-permute-start.19
  611.0 7.5 %collective-permute-start.20 = (f32[18,768]{1,0:T(8,128)S(1)}, f32[18,768]{1,0:T(8,128)S(1)}, u32[]{:S(2)}, u32[]{:S(2)}) collective-permute-start(f32[18,768]{1,0:T(8,128)S(1)} %add.563), channel_id=1, source_target_pairs={{4,8},{8,4},{12,0},{0,12},{5,9},{9,5},{13,1},{1,13},{6,10},{10,6},... | collective-permute-start | bytes 165896 | tf_op jit(solution)/shard_map/ppermute | solution.py:407
  618.4 6.0 collective-permute-start.21
  624.5 7.2 %collective-permute-start.22 = (f32[18,768]{1,0:T(8,128)S(1)}, f32[18,768]{1,0:T(8,128)S(1)}, u32[]{:S(2)}, u32[]{:S(2)}) collective-permute-start(f32[18,768]{1,0:T(8,128)S(1)} %add.565), channel_id=1, source_target_pairs={{32,64},{64,32},{96,0},{0,96},{33,65},{65,33},{97,1},{1,97},{34,66... | collective-permute-start | bytes 165896 | tf_op jit(solution)/shard_map/ppermute | solution.py:407
  631.7 4.4 collective-permute-start.23
  (140 other events, 495.4 us)
Sparse Core Ops, SparseCore 0:
  37.3 78.9 all-gather.4
  288.0 87.8 reduce-scatter.6
  396.5 100.0 reduce-scatter.8
  539.6 97.6 all-gather.6

commit v2 on v1

v2 whole, which is shorter than its diff:
```python
import jax
import jax.numpy as jnp
from jax import lax
from jax.experimental import pallas as pl
from jax.experimental.pallas import tpu as pltpu
from jax.sharding import Mesh, PartitionSpec as P

HEAD_DIM = 64
EPS = 1e-12
F32 = jnp.float32
BF16 = jnp.bfloat16
SWAP = ((0, 1), (1, 0))
EDGE0 = ((0, 1), (1, 0), (2, 3), (3, 2))
EDGE1 = ((1, 2), (2, 1), (3, 0), (0, 3))
LINKS = (("x", EDGE0), ("x", EDGE1), ("y", EDGE0), ("y", EDGE1))
PLANE = ("y", "x")


def normalize(summed, gain, shift):
    center = summed - jnp.mean(summed, axis=-1, keepdims=True)
    inverse = lax.rsqrt(jnp.mean(center * center, axis=-1, keepdims=True) + EPS)
    scaled = center * inverse
    return (scaled * gain + shift, scaled, inverse)


def normalize_back(gradient, gain, scaled, inverse):
    gained = gradient * gain
    return inverse * (
        gained
        - jnp.mean(gained, axis=-1, keepdims=True)
        - scaled * jnp.mean(gained * scaled, axis=-1, keepdims=True)
    )


def normal_cdf(values):
    return 0.5 * (1.0 + lax.erf(values * (0.5**0.5)))


def gelu(values):
    return values * normal_cdf(values)


def gelu_slope(values):
    density = jnp.exp(-0.5 * values * values) * 0.3989422804014327
    return normal_cdf(values) + values * density


def dot(left, right):
    return jnp.dot(left, right, preferred_element_type=F32)


def dot_t(left, right):
    return jnp.einsum("sd,fd->sf", left, right, preferred_element_type=F32)


def t_dot(left, right):
    return jnp.einsum("sf,sd->fd", left, right, preferred_element_type=F32)


def column_sum(values):
    return jnp.sum(values.astype(F32), axis=0)


def swap(values, axis):
    return lax.ppermute(values, axis, SWAP)


def pair_sum(values):
    return values + swap(values, "h")


def piece(values, index, size):
    return lax.dynamic_slice_in_dim(values, index * size, size, 0)


def in_order(side, mine, other):
    return jnp.concatenate([jnp.where(side == 0, mine, other), jnp.where(side == 0, other, mine)])


def together(*values):
    return lax.optimization_barrier(values)


def t_dot_in_kernel(left, right):
    return lax.dot_general(left, right, (((0,), (0,)), ((), ())), preferred_element_type=F32)


LIMIT = pltpu.CompilerParams(vmem_limit_bytes=48 * 2**20)
SCALAR = pl.BlockSpec(memory_space=pltpu.SMEM)


def across_lanes(left, right):
    return lax.dot_general(left, right, (((1,), (1,)), ((), ())), preferred_element_type=F32)


def attend_kernel(
    length_ref,
    slot_ref,
    query_weight,
    query_bias,
    key_weight,
    value_weight,
    value_bias,
    output_weight,
    query_ref,
    key_ref,
    value_ref,
    mixture_ref,
    logsum_ref,
    share_ref,
):
    slots = slot_ref[...]
    query_ref[...] = (dot(slots, query_weight[0]) + query_bias[...]).astype(BF16)
    key_ref[...] = dot(slots, key_weight[0]).astype(BF16)
    value_ref[...] = (dot(slots, value_weight[0]) + value_bias[...]).astype(BF16)
    count = slots.shape[0]
    valid = lax.broadcasted_iota(jnp.int32, (count, count), 0) < length_ref[0]
    for head in range(2):
        cut = slice(head * HEAD_DIM, (head + 1) * HEAD_DIM)
        scores = across_lanes(key_ref[:, cut], query_ref[:, cut]) * HEAD_DIM**-0.5
        scores = jnp.where(valid, scores, -1e30)
        highest = jnp.max(scores, axis=0, keepdims=True)
        raised = jnp.exp(scores - highest)
        totals = jnp.sum(raised, axis=0, keepdims=True)
        probs = (raised * (1.0 / totals)).astype(BF16)
        mixture_ref[:, cut] = t_dot_in_kernel(probs, value_ref[:, cut]).astype(BF16)
        logsum_ref[0, head : head + 1, :] = highest + jnp.log(totals)
    share = dot(mixture_ref[...], output_weight[0])

    @pl.when(pl.program_id(0) == 0)
    def _():
        share_ref[...] = share

    @pl.when(pl.program_id(0) != 0)
    def _():
        share_ref[...] += share


def attend(layer, length, slots, query_weight, query_bias, key_weight, value_weight, value_bias, output_weight):
    count, width = slots.shape
    heads = query_weight.shape[2]
    pair = 2 * HEAD_DIM
    steps = heads // pair
    whole = pl.BlockSpec((count, width), lambda i: (0, 0))
    weight = pl.BlockSpec((1, width, pair), lambda i: (layer, 0, i))
    bias = pl.BlockSpec((1, pair), lambda i: (0, i))
    part = pl.BlockSpec((count, pair), lambda i: (0, i))
    part_shape = jax.ShapeDtypeStruct((count, heads), BF16)
    return pl.pallas_call(
        attend_kernel,
        grid=(steps,),
        in_specs=[SCALAR, whole, weight, bias, weight, weight, bias]
        + [pl.BlockSpec((1, pair, width), lambda i: (layer, i, 0))],
        out_specs=[part] * 4 + [pl.BlockSpec((1, 2, count), lambda i: (i, 0, 0)), whole],
        out_shape=[part_shape] * 4
        + [jax.ShapeDtypeStruct((steps, 2, count), F32), jax.ShapeDtypeStruct((count, width), F32)],
        compiler_params=LIMIT,
        cost_estimate=pl.CostEstimate(
            flops=8 * count * width * heads + 4 * count * count * heads,
            bytes_accessed=8 * width * heads + 8 * count * width,
            transcendentals=count * count * heads // HEAD_DIM,
        ),
        name="attend",
    )(length.reshape(1), slots, query_weight, query_bias, key_weight, value_weight, value_bias, output_weight)


def attend_back_kernel(
    length_ref,
    query_ref,
    key_ref,
    value_ref,
    logsum_ref,
    grad_ref,
    query_weight,
    key_weight,
    value_weight,
    output_weight,
    query_low,
    key_low,
    value_low,
    share_ref,
    query_sum,
    value_sum,
):
    grads = across_lanes(grad_ref[...], output_weight[0]).astype(BF16)
    count = grads.shape[0]
    valid = lax.broadcasted_iota(jnp.int32, (count, count), 0) < length_ref[0]
    scale = HEAD_DIM**-0.5
    for head in range(2):
        cut = slice(head * HEAD_DIM, (head + 1) * HEAD_DIM)
        queries, keys, grad = query_ref[:, cut], key_ref[:, cut], grads[:, cut]
        scores = jnp.where(valid, across_lanes(keys, queries) * scale, -1e30)
        probs = jnp.exp(scores - logsum_ref[0, head : head + 1, :])
        grad_probs = across_lanes(value_ref[:, cut], grad)
        inner = jnp.sum(probs * grad_probs, axis=0, keepdims=True)
        grad_scores = (probs * (grad_probs - inner)).astype(BF16)
        query_low[:, cut] = (t_dot_in_kernel(grad_scores, keys) * scale).astype(BF16)
        key_low[:, cut] = (dot(grad_scores, queries) * scale).astype(BF16)
        value_low[:, cut] = dot(probs.astype(BF16), grad).astype(BF16)
    query_sum[...] = jnp.sum(query_low[...].astype(F32), axis=0, keepdims=True)
    value_sum[...] = jnp.sum(value_low[...].astype(F32), axis=0, keepdims=True)
    share = across_lanes(query_low[...], query_weight[0])
    share += across_lanes(key_low[...], key_weight[0])
    share += across_lanes(value_low[...], value_weight[0])

    @pl.when(pl.program_id(0) == 0)
    def _():
        share_ref[...] = share

    @pl.when(pl.program_id(0) != 0)
    def _():
        share_ref[...] += share


def attend_back(layer, length, saved, attended_low, query_weight, key_weight, value_weight, output_weight):
    queries, keys, values, _, logsum = saved
    count, width = attended_low.shape
    heads = queries.shape[1]
    pair = 2 * HEAD_DIM
    steps = heads // pair
    whole = pl.BlockSpec((count, width), lambda i: (0, 0))
    weight = pl.BlockSpec((1, width, pair), lambda i: (layer, 0, i))
    part = pl.BlockSpec((count, pair), lambda i: (0, i))
    part_shape = jax.ShapeDtypeStruct((count, heads), BF16)
    sums = pl.BlockSpec((1, pair), lambda i: (0, i))
    sums_shape = jax.ShapeDtypeStruct((1, heads), F32)
    return pl.pallas_call(
        attend_back_kernel,
        grid=(steps,),
        in_specs=[SCALAR, part, part, part, pl.BlockSpec((1, 2, count), lambda i: (i, 0, 0)), whole]
        + [weight] * 3
        + [pl.BlockSpec((1, pair, width), lambda i: (layer, i, 0))],
        out_specs=[part] * 3 + [whole, sums, sums],
        out_shape=[part_shape] * 3 + [jax.ShapeDtypeStruct((count, width), F32), sums_shape, sums_shape],
        compiler_params=LIMIT,
        cost_estimate=pl.CostEstimate(
            flops=8 * count * width * heads + 10 * count * count * heads,
            bytes_accessed=8 * width * heads + 8 * count * width,
            transcendentals=count * count * heads // HEAD_DIM,
        ),
        name="attend_back",
    )(length.reshape(1), queries, keys, values, logsum, attended_low, query_weight, key_weight, value_weight, output_weight)


def pieces_kernel(place_ref, down_in, up_in, piece_ref):
    width = piece_ref.shape[2]

    @pl.when(place_ref[1] == 0)
    def _():
        piece_ref[0] = down_in[0].astype(F32)

    @pl.when(place_ref[1] != 0)
    def _():
        half = up_in.shape[1]
        piece_ref[0, :half, :] = up_in[0, :, :width].astype(F32)
        piece_ref[0, half:, :] = up_in[0, :, width:].astype(F32)


def weight_pieces(chip, core, down_weight, up_weight):
    layers, units, width = down_weight.shape
    rows = units // 16
    return pl.pallas_call(
        pieces_kernel,
        grid_spec=pltpu.PrefetchScalarGridSpec(
            num_scalar_prefetch=1,
            grid=(layers,),
            in_specs=[
                pl.BlockSpec((1, rows, width), lambda l, place: (l, place[0], 0)),
                pl.BlockSpec((1, rows // 2, units), lambda l, place: (l, place[0], 0)),
            ],
            out_specs=pl.BlockSpec((1, rows, width), lambda l, place: (l, 0, 0)),
        ),
        out_shape=jax.ShapeDtypeStruct((layers, rows, width), F32),
        compiler_params=LIMIT,
        name="weight_pieces",
    )(jnp.stack([chip, core]), down_weight, up_weight)


def feed_sums_kernel(received, part_ref, act_own, act_peer, pre_own, pre_peer, ffn_low, hidden_low, *refs):
    out_ref = refs[-1]
    width = ffn_low.shape[1]

    def write(own, peer, right):
        for k, left in enumerate((own, peer)):
            total = t_dot_in_kernel(left[...], right[...])
            cut = slice(k * width, (k + 1) * width)
            out_ref[:, cut] = total + refs[0][:, cut] if received else total

    @pl.when(part_ref[0] == 0)
    def _():
        write(act_own, act_peer, ffn_low)

    @pl.when(part_ref[0] != 0)
    def _():
        write(pre_own, pre_peer, hidden_low)


def feed_sums(part, actives, pre_lows, ffn_low, hidden_low, columns, received=None):
    slots, units = actives[0].shape
    width = ffn_low.shape[1]
    block = units // 4
    left = pl.BlockSpec((slots, block), lambda i: (0, i))
    right = pl.BlockSpec((slots, width), lambda i: (0, 0))
    rows = pl.BlockSpec((block, 2 * width), lambda i: (i, 0))
    more = [] if received is None else [received]
    return pl.pallas_call(
        lambda *refs: feed_sums_kernel(bool(more), *refs),
        grid=(4,),
        in_specs=[SCALAR] + [left] * 4 + [right] * 2 + [rows] * len(more),
        out_specs=rows,
        out_shape=jax.ShapeDtypeStruct((units, columns), F32),
        compiler_params=LIMIT,
        cost_estimate=pl.CostEstimate(
            flops=4 * slots * units * width, bytes_accessed=(8 + 8 * len(more)) * units * width, transcendentals=0
        ),
        name="feed_sums",
    )(part.reshape(1), *actives, *pre_lows, ffn_low, hidden_low, *more)


def attention_sums_kernel(received, part_ref, query_ref, key_ref, value_ref, mixture_ref, slot_ref, grad_ref, *refs):
    out_ref = refs[-1]
    second = lax.rem(pl.program_id(0), 2)

    def write(which, left, right):
        @pl.when(2 * part_ref[0] + second == which)
        def _():
            total = t_dot_in_kernel(left[...], right[...])
            out_ref[...] = total + refs[0][...] if received else total

    write(0, query_ref, slot_ref)
    write(1, key_ref, slot_ref)
    write(2, value_ref, slot_ref)
    write(3, mixture_ref, grad_ref)


def attention_sums(part, lows, mixture, rounded, attended_low, received=None, into=None, place=0):
    slots, heads = mixture.shape
    half = rounded.shape[1] // 2
    left = pl.BlockSpec((slots, heads), lambda i: (0, 0))
    right = pl.BlockSpec((slots, half), lambda i: (0, i // 2))
    rows = pl.BlockSpec((heads, half), lambda i: (i, 0))
    more = [] if received is None else [received, into]
    shape = (4 * heads, half) if into is None else into.shape
    return pl.pallas_call(
        lambda *refs: attention_sums_kernel(bool(more), *refs),
        grid=(4,),
        in_specs=[SCALAR] + [left] * 4 + [right] * 2 + ([rows, pl.BlockSpec(memory_space=pl.ANY)] if more else []),
        out_specs=pl.BlockSpec((heads, half), lambda i: (i, place)),
        out_shape=jax.ShapeDtypeStruct(shape, F32),
        input_output_aliases={8: 0} if more else {},
        compiler_params=LIMIT,
        cost_estimate=pl.CostEstimate(flops=8 * slots * heads * half, bytes_accessed=16 * heads * half, transcendentals=0),
        name="attention_sums",
    )(part.reshape(1), *lows, mixture, rounded, attended_low, *more)


def sort_kernel(piece_ref, down_ref, up_ref):
    chips, _, rows, width = piece_ref.shape
    for i in range(chips):
        down_ref[i * rows : (i + 1) * rows, :] = piece_ref[i, 0].astype(BF16)
        up = piece_ref[i, 1].astype(BF16)
        half = rows // 2
        up_ref[i * half : (i + 1) * half, :width] = up[:half]
        up_ref[i * half : (i + 1) * half, width:] = up[half:]


def sort_weights(gathered):
    chips, _, rows, width = gathered.shape
    step = 4
    units = chips * rows
    return pl.pallas_call(
        sort_kernel,
        grid=(chips // step,),
        in_specs=[pl.BlockSpec((step, 2, rows, width), lambda i: (i, 0, 0, 0))],
        out_specs=[
            pl.BlockSpec((step * rows, width), lambda i: (i, 0)),
            pl.BlockSpec((step * rows // 2, units), lambda i: (i, 0)),
        ],
        out_shape=[
            jax.ShapeDtypeStruct((units, width), BF16),
            jax.ShapeDtypeStruct((width, units), BF16),
        ],
        compiler_params=LIMIT,
        cost_estimate=pl.CostEstimate(flops=0, bytes_accessed=12 * units * width, transcendentals=0),
        name="sort_weights",
    )(gathered)


def rows_of(ref):
    chips, _, rows, columns = ref.shape
    return ref[...].reshape(chips * rows, columns)


def place_feed_kernel(down_in, up_in, down_ref, up_ref):
    down_ref[0] = rows_of(down_in)
    up_ref[0] = rows_of(up_in).T


def place_attention_kernel(query_in, key_in, value_in, output_in, query_ref, key_ref, value_ref, output_ref):
    query_ref[0] = rows_of(query_in).T
    key_ref[0] = rows_of(key_in).T
    value_ref[0] = rows_of(value_in).T
    output_ref[0] = rows_of(output_in)


def place_gradients(gathered, width):
    chips, _, rows, _ = gathered.shape
    step = 4
    units, block = chips * rows, step * rows
    half = width // 2

    def feed_in(core):
        return pl.BlockSpec((step, 1, rows, width), lambda l, i: (i, core, 0, 1 - l))

    def attention_in(core, which):
        return pl.BlockSpec((step, 1, rows, half), lambda l, i: (2 * i + which, core, 0, 5 - l))

    limit = pltpu.CompilerParams(vmem_limit_bytes=40 * 2**20)
    down, up = pl.pallas_call(
        place_feed_kernel,
        grid=(2, chips // step),
        in_specs=[feed_in(0), feed_in(1)],
        out_specs=[
            pl.BlockSpec((1, block, width), lambda l, i: (l, i, 0)),
            pl.BlockSpec((1, width, block), lambda l, i: (l, 0, i)),
        ],
        out_shape=[
            jax.ShapeDtypeStruct((2, units, width), F32),
            jax.ShapeDtypeStruct((2, width, units), F32),
        ],
        compiler_params=limit,
        name="place_feed",
    )(gathered, gathered)
    tall = pl.BlockSpec((1, half, block), lambda l, i: (l, i, 0))
    tall_shape = jax.ShapeDtypeStruct((2, width, block), F32)
    query, key, value, output = pl.pallas_call(
        place_attention_kernel,
        grid=(2, 2),
        in_specs=[attention_in(0, 0), attention_in(0, 1), attention_in(1, 0), attention_in(1, 1)],
        out_specs=[tall, tall, tall, pl.BlockSpec((1, block, half), lambda l, i: (l, 0, i))],
        out_shape=[tall_shape, tall_shape, tall_shape, jax.ShapeDtypeStruct((2, block, width), F32)],
        compiler_params=limit,
        name="place_attention",
    )(gathered, gathered, gathered, gathered)
    return query, key, value, output, up, down


def local(
    tokens,
    cotangent,
    lengths,
    repeats,
    query_weight,
    query_bias,
    key_weight,
    value_weight,
    value_bias,
    output_weight,
    output_bias,
    attn_gain,
    attn_shift,
    up_weight,
    up_bias,
    down_weight,
    down_bias,
    ffn_gain,
    ffn_shift,
):
    length = lengths[0]
    side = lax.axis_index("h")
    core = lax.axis_index("c")
    chip = lax.axis_index("y") * 4 + lax.axis_index("x")
    first_core = core == 0
    slots, width = tokens.shape
    half_slots = slots // 2
    units = up_weight.shape[2]
    columns = query_weight.shape[2]

    rows_down = units // 16
    pieces = weight_pieces(chip, core, down_weight, up_weight)
    gathered1, pieces2 = lax.all_gather(swap(pieces[0], "h"), PLANE + ("c",)), pieces[1]
    peer_up_bias = swap(up_bias.astype(F32), "h")

    def own_slots(values):
        return piece(values, side, half_slots)

    def attention_forward(layer, rounded):
        *attention, share = attend(
            layer,
            length,
            rounded,
            query_weight,
            query_bias[layer].astype(F32)[None],
            key_weight,
            value_weight,
            value_bias[layer].astype(F32)[None],
            output_weight,
        )
        return attention, own_slots(share), piece(share, 1 - side, half_slots)

    def attention_back(layer, saved, grad_one_sent, received):
        grad_one = 2.0 * in_order(side, grad_one_sent, received)
        attended_low = grad_one.astype(BF16)
        *lows, share, query_sum, value_sum = attend_back(
            layer, length, saved, attended_low, query_weight, key_weight, value_weight, output_weight
        )
        small = [jnp.concatenate([query_sum[0], value_sum[0]]), column_sum(attended_low)]
        return grad_one, lows, attended_low, share, small

    def feed_back(layer, gradient, saved):
        scaled_two, inverse_two, pres, actives, hidden_low, scaled_one, inverse_one = saved
        grad_two = normalize_back(gradient, ffn_gain[layer], scaled_two, inverse_two)
        ffn_low = grad_two.astype(BF16)
        downs, ups = (down_weight[layer], peer_down[layer]), (up_weight[layer], peer_up[layer])
        pre_lows = [
            (dot_t(ffn_low, down) * gelu_slope(pre)).astype(BF16) for down, pre in zip(downs, pres, strict=True)
        ]
        grad_hidden = grad_two + dot_t(pre_lows[0], ups[0]) + dot_t(pre_lows[1], ups[1])
        grad_one = normalize_back(grad_hidden, attn_gain[layer], scaled_one, inverse_one)
        shared = [
            jnp.sum(grad_hidden * scaled_one, axis=0),
            jnp.sum(grad_hidden, axis=0),
            column_sum(ffn_low),
            jnp.sum(gradient * scaled_two, axis=0),
            jnp.sum(gradient, axis=0),
        ]
        biases = [column_sum(item).reshape(-1, width) for item in pre_lows]
        return grad_one, ffn_low, pre_lows, shared, biases

    def layer_forward(layer, x_own, share, sent, peers):
        attended = share + swap(sent, "h") + output_bias[layer]
        hidden, scaled, inverse = normalize(x_own + attended, attn_gain[layer], attn_shift[layer])
        hidden_low = hidden.astype(BF16)
        pre = dot(hidden_low, up_weight[layer]) + up_bias[layer]
        active = gelu(pre).astype(BF16)
        ffn_out = dot(active, down_weight[layer])
        peer_down, peer_up = peers
        pre_peer = dot(hidden_low, peer_up) + peer_up_bias[layer]
        active_peer = gelu(pre_peer).astype(BF16)
        ffn_out = ffn_out + dot(active_peer, peer_down) + down_bias[layer]
        out, scaled_two, inverse_two = normalize(hidden + ffn_out, ffn_gain[layer], ffn_shift[layer])
        saved = (scaled_two, inverse_two, (pre, pre_peer), (active, active_peer), hidden_low, scaled, inverse)
        return out, saved

    att1, share, sent = attention_forward(0, tokens)
    pieces2, sent = together(pieces2, sent)
    pieces2 = swap(pieces2, "h")
    peers1 = sort_weights(gathered1.reshape(16, 2, rows_down, width))
    x2_own, saved1 = layer_forward(0, own_slots(tokens).astype(F32), share, sent, peers1)
    sent = 0.5 * x2_own
    pieces2, sent = together(pieces2, sent)
    gathered2 = lax.all_gather(pieces2, PLANE + ("c",))
    x2_low = (2.0 * in_order(side, sent, swap(sent, "h"))).astype(BF16)
    att2, share, sent = attention_forward(1, x2_low)
    peers2 = sort_weights(gathered2.reshape(16, 2, rows_down, width))
    _, saved2 = layer_forward(1, x2_own, share, sent, peers2)
    scaled_last = saved2[0]
    mixture = att2[3]
    peer_down, peer_up = (peers1[0], peers2[0]), (peers1[1], peers2[1])

    places = side * half_slots + jnp.arange(half_slots)
    weighting = jnp.where(places < length, repeats[0], 0).astype(F32)[:, None]
    gradient2 = own_slots(cotangent).astype(F32) * weighting
    grad_one_own, ffn_low, pre_lows, shared2, biases2 = feed_back(1, gradient2, saved2)
    sent = 0.5 * grad_one_own
    received = swap(sent, "h")
    feed2_received = swap(feed_sums(1 - core, saved2[3], pre_lows, ffn_low, saved2[4], 2 * width), "c")
    feed2 = feed_sums(core, saved2[3], pre_lows, ffn_low, saved2[4], 2 * width, feed2_received)
    feed2, received = together(feed2, received)
    feed2 = lax.psum_scatter(feed2, PLANE, tiled=True)
    _, lows2, attended_low2, share, small_att2 = attention_back(1, att2, sent, received)
    received = swap(piece(share, 1 - side, half_slots), "h")
    attn2_received = swap(attention_sums(1 - core, lows2, mixture, x2_low, attended_low2), "c")
    gradient1 = grad_one_own + own_slots(share) + received

    grad_one_own1, ffn_low, pre_lows, shared1, biases1 = feed_back(0, gradient1, saved1)
    sent = 0.5 * grad_one_own1
    received = swap(sent, "h")
    feed1_received = swap(feed_sums(1 - core, saved1[3], pre_lows, ffn_low, saved1[4], 2 * width), "c")
    rest = feed_sums(core, saved1[3], pre_lows, ffn_low, saved1[4], 3 * width, feed1_received)
    rest, received = together(rest, received)
    grad_one1, lows1, attended_low1, share, small_att1 = attention_back(0, att1, sent, received)
    attn1_received = swap(attention_sums(1 - core, lows1, att1[3], tokens, attended_low1), "c")
    rest = attention_sums(core, lows2, mixture, x2_low, attended_low2, attn2_received, rest, 4)
    rest = attention_sums(core, lows1, att1[3], tokens, attended_low1, attn1_received, rest, 5)
    rest, feed2 = together(rest, feed2)
    rest = lax.psum_scatter(rest, PLANE, tiled=True)

    def across(own, peer):
        diagonal = lax.ppermute(peer, ("zl", "h"), ((0, 3), (3, 0), (1, 2), (2, 1)))
        peer = swap(peer, "h") + diagonal
        own = own + swap(own, "zl")
        return jnp.concatenate([own[:, :width] + peer, own[:, width:]], axis=1)

    feed2 = across(feed2[:, :width], feed2[:, width:])
    feed2, rest = together(feed2, rest)
    rest = across(jnp.concatenate([rest[:, :width], rest[:, 2 * width :]], axis=1), rest[:, width : 2 * width])
    own = jnp.concatenate([feed2, rest], axis=1)
    gathered = lax.all_gather(own, PLANE + ("c",)).reshape(16, 2, *own.shape)
    grad_query, grad_key, grad_value, grad_output, grad_up, grad_down = place_gradients(gathered, width)

    token_grad = grad_one1 + pair_sum(share)
    scaled_last, token_grad = together(scaled_last, token_grad)
    scaled_all = in_order(side, scaled_last, swap(scaled_last, "h"))
    block_output = (scaled_all * ffn_gain[1] + ffn_shift[1]).astype(BF16)
    shared = jnp.stack(shared1 + shared2)
    mine = jnp.concatenate([shared, biases1[0], biases2[0]])
    mine = mine + swap(jnp.concatenate([shared, biases1[1], biases2[1]]), "h")
    small = jnp.concatenate([mine, jnp.stack(small_att1 + small_att2)])
    small, block_output = together(small, block_output)
    small = small + swap(small, "c")
    for axis, pairs in LINKS:
        small = small + lax.ppermute(small, axis, pairs)
    small = small + swap(small, "zl")
    bias_rows = units // width
    shared = small[:10].reshape(2, 5, width)
    grad_up_bias = small[10 : 10 + 2 * bias_rows].reshape(2, units)
    attention = small[10 + 2 * bias_rows :].reshape(2, 2, width)

    return (
        block_output,
        token_grad,
        grad_query,
        attention[:, 0, :columns],
        grad_key,
        grad_value,
        attention[:, 0, columns:],
        grad_output,
        attention[:, 1],
        shared[:, 0],
        shared[:, 1],
        grad_up,
        grad_up_bias,
        grad_down,
        shared[:, 2],
        shared[:, 3],
        shared[:, 4],
    )


def solution(mesh):
    fine = Mesh(mesh.devices.reshape(4, 2, 4, 2, 2), ("y", "zl", "x", "c", "h"))
    rows = ("y", "zl", "x", "c")
    in_specs = (
        P(rows, None),
        P(rows, None),
        P(rows),
        P(rows),
        P(None, None, "h"),
        P(None, "h"),
        P(None, None, "h"),
        P(None, None, "h"),
        P(None, "h"),
        P(None, "h", None),
        P(),
        P(),
        P(),
        P(None, None, "h"),
        P(None, "h"),
        P(None, "h", None),
        P(),
        P(),
        P(),
    )
    out_specs = (
        P(rows, None),
        P(rows, None),
        P(None, None, "h"),
        P(None, "h"),
        P(None, None, "h"),
        P(None, None, "h"),
        P(None, "h"),
        P(None, "h", None),
        P(),
        P(),
        P(),
        P(None, None, "h"),
        P(None, "h"),
        P(None, "h", None),
        P(),
        P(),
        P(),
    )
    return jax.shard_map(local, mesh=fine, in_specs=in_specs, out_specs=out_specs, check_vma=False)
```

time: 682 us -> 574 us (0.84)
  Pallas kernels: 32 us -> 117 us
  waiting for transfers between devices: 350 us -> 294 us
  other arithmetic: 78.1 us -> 24.2 us
  matrix products: 84.3 us -> 33.6 us
  local copies, waits for them, and re-layouts: 75.6 us -> 35.7 us
  starting transfers between devices: 34.4 us -> 44.4 us
    unnamed x6 -> x5, waiting for transfers between devices: 98.9 us -> 0.08 us
    pallas_call x1 -> x15, Pallas kernels: 8.36 us -> 93.1 us  [the longest x4 26.8 us: feed_sums(): pl.pallas_call(lambda *refs: feed_sums_kernel(bool(more), *refs), grid=(4...]
    reduce_scatter x0 -> x2, waiting for transfers between devices: none -> 80.3 us  [the longest x1 80.3 us: local(): rest = lax.psum_scatter(rest, PLANE, tiled=True)]
    ppermute x19 -> x22, waiting for transfers between devices: 226 us -> 171 us  [swap(): return lax.ppermute(values, axis, SWAP)]
    dot_general x28 -> x0, matrix products: 37.3 us -> none  [the longest x16 18.1 us: t_dot(): return jnp.einsum('sf,sd->fd', left, right, preferred_element_type=F32)]
    concatenate x11 -> x4, other arithmetic: 29.7 us -> 1.03 us  [the longest x1 0.97 us: local(): own = jnp.concatenate([feed2, rest], axis=1)]
    unnamed x362 -> x212, local copies, waits for them, and re-layouts: 54 us -> 27.2 us
    add x15 -> x7, other arithmetic: 21 us -> 4.43 us  [the longest x1 2.9 us: local(): token_grad = grad_one1 + pair_sum(share)]
  transfers between devices with their start and end apart: 28 -> 33, of which waited for: 18 -> 24; matrix products, arithmetic and copies ran while one was open for 24% -> 11% of each run, Pallas kernels for 0% -> 15%
where the time goes in v2:
time: 574 us; the launch traced here: 565 us
  waiting for transfers between devices  294 us (51%)
  Pallas kernels  117 us (20%)
  starting transfers between devices  44.4 us (8%)
  local copies, waits for them, and re-layouts  35.7 us (6%)
  matrix products  33.6 us (6%)
  other arithmetic  24.2 us (4%)
  between operations  16.6 us (3%)
    ppermute x22, waiting for transfers between devices, swap(): return lax.ppermute(values, axis, SWAP)  171 us
    reduce_scatter x1, waiting for transfers between devices, local(): rest = lax.psum_scatter(rest, PLANE, tiled=True)  80.3 us
    ppermute x22, starting transfers between devices, swap(): return lax.ppermute(values, axis, SWAP)  37.3 us
    unnamed x212, local copies, waits for them, and re-layouts  27.2 us
    pallas_call x4, Pallas kernels, feed_sums(): pl.pallas_call(lambda *refs: feed_sums_kernel(bool(more), *refs), grid=(4...  26.8 us
    ppermute x4, waiting for transfers between devices, local(): small = small + lax.ppermute(small, axis, pairs)  24.8 us
    pallas_call x2, Pallas kernels, attend_back(): pl.pallas_call(attend_back_kernel, grid=(steps,), in_specs=[SCALAR, part,...  24.6 us
    pallas_call x2, Pallas kernels, attend(): pl.pallas_call(attend_kernel, grid=(steps,), in_specs=[SCALAR, whole, wei...  19.6 us
  transfers between devices with their start and end apart: 33, of which 24 were waited for; matrix products, arithmetic and copies ran while one was open for 11% of the time, Pallas kernels for 15%

profile of v2, /device:TPU:0, one launch (start us, length us, event | category | flops | bytes accessed | tf_op | source)
XLA Modules:
  0.0 564.9 jit_solution(5323610587623022463)
XLA Ops:
  7.3 2.3 copy-done.1
  12.1 4.0 collective-permute-start.1
  16.0 7.0 %collective-permute-done.1 = f32[96,768]{1,0:T(8,128)S(1)} collective-permute-done((f32[96,768]{1,0:T(8,128)S(1)}, f32[96,768]{1,0:T(8,128)S(1)}, u32[]{:S(2)}, u32[]{:S(2)}) %collective-permute-start.1) | collective-permute-done | bytes 294944 | tf_op jit(solution)/shard_map/ppermute | solution.py:65
  27.1 9.8 %attend.2 = (bf16[512,384]{1,0:T(8,128)(2,1)S(1)}, bf16[512,384]{1,0:T(8,128)(2,1)S(1)}, bf16[512,384]{1,0:T(8,128)(2,1)S(1)}, bf16[512,384]{1,0:T(8,128)(2,1)S(...) custom-call(s32[1]{0:T(128)} %copy.64.length_ref, bf16[512,768]{1,0:T(8,128)(2,1)S(1)} %copy-done, ...), custom_call_target="tpu_custom_call" | custom-call | flops 1610612736 | bytes 5505024 | tf_op jit(solution)/shard_map/attend/pallas_call | solution.py:149
  39.2 3.3 collective-permute-start
  42.9 3.2 collective-permute-start.3
  48.1 13.4 %collective-permute-done.2 = f32[2,1536]{1,0:T(2,128)S(1)} collective-permute-done((f32[2,1536]{1,0:T(2,128)S(1)}, f32[2,1536]{1,0:T(2,128)S(1)}, u32[]{:S(2)}, u32[]{:S(2)}) %collective-permute-start.2) | collective-permute-done | bytes 12320 | tf_op jit(solution)/shard_map/ppermute | solution.py:65
  62.2 1.7 fusion.71
  64.8 3.7 multiply_convert_fusion.3
  68.5 3.5 fusion.11
  72.0 8.9 %all-gather.7.cloned.1.call-done = f32[3072,768]{1,0:T(8,128)} async-done(((f32[96,768]{1,0:T(8,128)}), f32[3072,768]{1,0:T(8,128)}) %all-gather.7.cloned.1.call-update) | async-done | bytes 9437200 | tf_op jit(solution)/shard_map/all_gather | solution.py:481
  81.0 4.4 sort_weights.2
  85.5 2.0 multiply_convert_fusion.2
  91.8 3.2 collective-permute-start.4
  95.0 18.3 %collective-permute-done.4 = f32[256,768]{1,0:T(8,128)S(1)} collective-permute-done((f32[256,768]{1,0:T(8,128)}, f32[256,768]{1,0:T(8,128)S(1)}, u32[]{:S(2)}, u32[]{:S(2)}) %collective-permute-start.4) | collective-permute-done | bytes 786464 | tf_op jit(solution)/shard_map/ppermute | solution.py:65
  116.3 9.8 %attend.3 = (bf16[512,384]{1,0:T(8,128)(2,1)S(1)}, bf16[512,384]{1,0:T(8,128)(2,1)S(1)}, bf16[512,384]{1,0:T(8,128)(2,1)S(1)}, bf16[512,384]{1,0:T(8,128)(2,1)S(...) custom-call(s32[1]{0:T(128)} %copy.64.length_ref, bf16[512,768]{1,0:T(8,128)(2,1)S(1)} %fusion.40.slot_ref.refs_5_, ...), custom_call_target="tpu_custom_call" | custom-call | flops 1610612736 | bytes 5505024 | tf_op jit(solution)/shard_map/attend/pallas_call | solution.py:149
  129.1 2.1 constant_dynamic-slice_fusion.1
  131.2 3.3 collective-permute-start.5
  135.8 16.3 %collective-permute-done.5 = f32[256,768]{1,0:T(8,128)} collective-permute-done((f32[256,768]{1,0:T(8,128)}, f32[256,768]{1,0:T(8,128)}, u32[]{:S(2)}, u32[]{:S(2)}) %collective-permute-start.5) | collective-permute-done | bytes 786464 | tf_op jit(solution)/shard_map/ppermute | solution.py:65
  152.1 2.0 fusion.70
  155.0 3.6 multiply_convert_fusion.1
  158.6 3.3 fusion.5
  162.8 4.4 sort_weights.3
  171.9 1.7 convert_reduce_fusion.2
  174.3 1.8 convert_reduce_fusion.4
  176.1 4.8 feed_sums.4
  182.0 3.4 multiply_reduce_fusion.2
  186.8 3.1 collective-permute-start.7
  190.0 5.9 %collective-permute-done.6.refs_7_ = f32[1536,1536]{1,0:T(8,128)} collective-permute-done((f32[1536,1536]{1,0:T(8,128)}, f32[1536,1536]{1,0:T(8,128)}, u32[]{:S(2)}, u32[]{:S(2)}) %collective-permute-start.6) | collective-permute-done | bytes 9437216 | tf_op jit(solution)/shard_map/ppermute | solution.py:65
  195.9 8.4 %feed_sums.5 = f32[1536,1536]{1,0:T(8,128)} custom-call(s32[1]{0:T(128)} %bitcast.1.refs_0_, bf16[256,1536]{1,0:T(8,128)(2,1)S(1)} %copy-done.5, bf16[256,1536]{1,0:T(8,128)(2,1)S(1)} %get-tuple-element.204.refs_2_, bf16[256,1536]{1,0:T(8,128)(2,1)S(1)} %get-tuple-element.213.refs_3_, bf16[256,1536]{1,0:T(8,128)(2,1)S(1)} %get-tuple-element.217.refs_4_, ...), custom_call_target="tpu_custom_call" | custom-call | flops 1207959552 | bytes 18874368 | tf_op jit(solution)/shard_map/feed_sums/pallas_call | solution.py:306
  204.2 4.1 collective-permute-done.7
  212.1 12.3 %attend_back.2 = (bf16[512,384]{1,0:T(8,128)(2,1)S(1)}, bf16[512,384]{1,0:T(8,128)(2,1)S(1)}, bf16[512,384]{1,0:T(8,128)(2,1)S(1)}, f32[512,768]{1,0:T(8,128)}, ...) custom-call(s32[1]{0:T(128)} %copy.64.length_ref, bf16[512,384]{1,0:T(8,128)(2,1)S(1)} %copy-done.29, ...), custom_call_target="tpu_custom_call" | custom-call | flops 2214592512 | bytes 5505024 | tf_op jit(solution)/shard_map/attend_back/pallas_call | solution.py:227
  225.7 3.2 collective-permute-start.8
  228.9 17.2 %collective-permute-done.8 = f32[256,768]{1,0:T(8,128)S(1)} collective-permute-done((f32[256,768]{1,0:T(8,128)S(1)}, f32[256,768]{1,0:T(8,128)S(1)}, u32[]{:S(2)}, u32[]{:S(2)}) %collective-permute-start.8) | collective-permute-done | bytes 786464 | tf_op jit(solution)/shard_map/ppermute | solution.py:65
  249.8 2.6 convert_reduce_fusion.3
  253.7 5.0 feed_sums.6
  258.8 2.1 fusion.44
  262.4 3.2 collective-permute-start.11
  265.6 3.1 attention_sums.5
  269.0 4.8 collective-permute-done.10.refs_7_
  273.7 8.7 %feed_sums.7.refs_8_ = f32[1536,2304]{1,0:T(8,128)} custom-call(s32[1]{0:T(128)} %bitcast.1.refs_0_, bf16[256,1536]{1,0:T(8,128)(2,1)S(1)} %get-tuple-element.196.refs_1_, bf16[256,1536]{1,0:T(8,128)(2,1)S(1)} %copy-done.3, bf16[256,1536]{1,0:T(8,128)(2,1)S(1)} %get-tuple-element.211.refs_3_, bf16[256,1536]{1,0:T(8,128)(2,1)S(1)} %get-tuple-element.215.refs_4_, ...), custom_call_target="tpu_custom_call" | custom-call | flops 1207959552 | bytes 18874368 | tf_op jit(solution)/shard_map/feed_sums/pallas_call | solution.py:306
  286.5 12.3 %attend_back.3 = (bf16[512,384]{1,0:T(8,128)(2,1)S(1)}, bf16[512,384]{1,0:T(8,128)(2,1)S(1)}, bf16[512,384]{1,0:T(8,128)(2,1)S(1)}, f32[512,768]{1,0:T(8,128)}, ...) custom-call(s32[1]{0:T(128)} %copy.64.length_ref, bf16[512,384]{1,0:T(8,128)(2,1)S(1)} %copy-done.23, ...), custom_call_target="tpu_custom_call" | custom-call | flops 2214592512 | bytes 5505024 | tf_op jit(solution)/shard_map/attend_back/pallas_call | solution.py:227
  298.8 2.0 attention_sums.4
  300.9 3.3 attention_sums.6.refs_8_
  305.4 3.2 attention_sums.7
  311.4 2.1 collective-permute-start.18
  314.2 5.5 collective-permute-done.16
  319.7 8.0 %collective-permute-done.18 = f32[96,768]{1,0:T(8,128)S(1)} collective-permute-done((f32[96,768]{1,0:T(8,128)S(1)}, f32[96,768]{1,0:T(8,128)S(1)}, u32[]{:S(2)}, u32[]{:S(2)}) %collective-permute-start.18) | collective-permute-done | bytes 294944 | tf_op jit(solution)/shard_map/ppermute | solution.py:590
  327.7 80.3 %reduce-scatter.5.cloned.1.call-done = f32[96,2304]{1,0:T(8,128)} async-done(((f32[1536,2304]{1,0:T(8,128)}), f32[96,2304]{1,0:T(8,128)}) %reduce-scatter.5.cloned.1.call-update) | async-done | bytes 884752 | tf_op jit(solution)/shard_map/reduce_scatter | solution.py:587
  409.3 1.7 collective-permute-start.19
  411.0 2.2 collective-permute-start.21
  413.9 11.7 %collective-permute-done.19 = f32[96,1536]{1,0:T(8,128)S(1)} collective-permute-done((f32[96,1536]{1,0:T(8,128)S(1)}, f32[96,1536]{1,0:T(8,128)S(1)}, u32[]{:S(2)}, u32[]{:S(2)}) %collective-permute-start.19) | collective-permute-done | bytes 589856 | tf_op jit(solution)/shard_map/ppermute | solution.py:65
  425.7 7.4 %collective-permute-done.20 = f32[96,768]{1,0:T(8,128)S(1)} collective-permute-done((f32[96,768]{1,0:T(8,128)S(1)}, f32[96,768]{1,0:T(8,128)S(1)}, u32[]{:S(2)}, u32[]{:S(2)}) %collective-permute-start.20) | collective-permute-done | bytes 294944 | tf_op jit(solution)/shard_map/ppermute | solution.py:65
  435.1 36.1 %collective-permute-done.12 = f32[512,768]{1,0:T(8,128)S(1)} collective-permute-done((f32[512,768]{1,0:T(8,128)}, f32[512,768]{1,0:T(8,128)S(1)}, u32[]{:S(2)}, u32[]{:S(2)}) %collective-permute-start.12) | collective-permute-done | bytes 1572896 | tf_op jit(solution)/shard_map/ppermute | solution.py:65
  471.2 2.9 add_add_fusion
  475.6 2.7 collective-permute-start.9
  478.4 15.9 %collective-permute-done.9 = f32[14,768]{1,0:T(8,128)S(1)} collective-permute-done((f32[14,768]{1,0:T(8,128)S(1)}, f32[14,768]{1,0:T(8,128)S(1)}, u32[]{:S(2)}, u32[]{:S(2)}) %collective-permute-start.9) | collective-permute-done | bytes 43040 | tf_op jit(solution)/shard_map/ppermute | solution.py:65
  497.5 6.4 %collective-permute-done.23 = f32[18,768]{1,0:T(8,128)S(1)} collective-permute-done((f32[18,768]{1,0:T(8,128)S(1)}, f32[18,768]{1,0:T(8,128)S(1)}, u32[]{:S(2)}, u32[]{:S(2)}) %collective-permute-start.23) | collective-permute-done | bytes 55328 | tf_op jit(solution)/shard_map/ppermute | solution.py:613
  505.0 6.4 %collective-permute-done.24 = f32[18,768]{1,0:T(8,128)S(1)} collective-permute-done((f32[18,768]{1,0:T(8,128)S(1)}, f32[18,768]{1,0:T(8,128)S(1)}, u32[]{:S(2)}, u32[]{:S(2)}) %collective-permute-start.24) | collective-permute-done | bytes 55328 | tf_op jit(solution)/shard_map/ppermute | solution.py:613
  511.5 5.9 %collective-permute-done.25 = f32[18,768]{1,0:T(8,128)S(1)} collective-permute-done((f32[18,768]{1,0:T(8,128)S(1)}, f32[18,768]{1,0:T(8,128)S(1)}, u32[]{:S(2)}, u32[]{:S(2)}) %collective-permute-start.25) | collective-permute-done | bytes 55328 | tf_op jit(solution)/shard_map/ppermute | solution.py:613
  518.5 6.1 %collective-permute-done.26 = f32[18,768]{1,0:T(8,128)S(1)} collective-permute-done((f32[18,768]{1,0:T(8,128)S(1)}, f32[18,768]{1,0:T(8,128)S(1)}, u32[]{:S(2)}, u32[]{:S(2)}) %collective-permute-start.26) | collective-permute-done | bytes 55328 | tf_op jit(solution)/shard_map/ppermute | solution.py:613
  525.2 3.9 collective-permute-done.27
  534.5 8.0 %place_attention.1 = (f32[2,768,384]{2,1,0:T(8,128)}, f32[2,768,384]{2,1,0:T(8,128)}, f32[2,768,384]{2,1,0:T(8,128)}, f32[2,384,768]{2,1,0:T(8,128)}) custom-call(f32[16,2,96,2304]{3,2,1,0:T(8,128)} %bitcast.102, f32[16,2,96,2304]{3,2,1,0:T(8,128)} %bitcast.103, f32[16,2,96,2304]{3,2,1,0:T(8,128)} %bitcast.104, f32[16,2,96,2304]{3,2,1,0:T(8,128)} %bitcast.105), custom_call_target="tpu_custom_call" | custom-call | tf_op jit(solution)/shard_map/place_attention/pallas_call | solution.py:436
  542.6 15.6 %place_feed.1 = (f32[2,1536,768]{2,1,0:T(8,128)}, f32[2,768,1536]{2,1,0:T(8,128)}) custom-call(f32[16,2,96,2304]{3,2,1,0:T(8,128)} %bitcast.106, f32[16,2,96,2304]{3,2,1,0:T(8,128)} %bitcast.107), custom_call_target="tpu_custom_call" | custom-call | tf_op jit(solution)/shard_map/place_feed/pallas_call | solution.py:419
  (358 shorter events, 69.6 us)
Async XLA Ops:
  7.2 73.8 %all-gather.7.cloned.1.call-start = ((), (), s32[]{:S(2)}) async-start(), calls=%async_computation.4 | async-start | bytes 9732096 | tf_op jit(solution)/shard_map/all_gather | solution.py:481
  9.7 14.8 %copy-start.87 = (bf16[2,384]{1,0:T(2,128)(2,1)S(1)}, bf16[2,384]{1,0:T(2,128)(2,1)}, u32[]{:S(2)}) copy-start(bf16[2,384]{1,0:T(2,128)(2,1)} %param.27) | copy-start | bytes 4612
  9.7 14.8 %copy-start.88 = (bf16[2,384]{1,0:T(2,128)(2,1)S(1)}, bf16[2,384]{1,0:T(2,128)(2,1)}, u32[]{:S(2)}) copy-start(bf16[2,384]{1,0:T(2,128)(2,1)} %param.24) | copy-start | bytes 4612
  9.7 14.8 %copy-start = (bf16[512,768]{1,0:T(8,128)(2,1)S(1)}, bf16[512,768]{1,0:T(8,128)(2,1)}, u32[]{:S(2)}) copy-start(bf16[512,768]{1,0:T(8,128)(2,1)} %refs_5_.3) | copy-start | bytes 2359300
  9.7 14.9 %copy-start.12 = (bf16[2,768,384]{2,1,0:T(8,128)(2,1)S(1)}, bf16[2,768,384]{2,1,0:T(8,128)(2,1)}, u32[]{:S(2)}) copy-start(bf16[2,768,384]{2,1,0:T(8,128)(2,1)} %query_weight.7) | copy-start | bytes 3538948
  12.1 11.0 %collective-permute-start.1 = (f32[96,768]{1,0:T(8,128)S(1)}, f32[96,768]{1,0:T(8,128)S(1)}, u32[]{:S(2)}, u32[]{:S(2)}) collective-permute-start(f32[96,768]{1,0:T(8,128)S(1)} %get-tuple-element.181), channel_id=1, source_target_pairs={{0,1},{1,0},{2,3},{3,2},{4,5},{5,4},{6,7},{7,6},{8,9},{9,8},{10,11... | collective-permute-start | bytes 884744 | tf_op jit(solution)/shard_map/ppermute | solution.py:65
  23.8 139.1 %all-gather.9.cloned.1.call-start = ((), (), s32[]{:S(2)}) async-start(), calls=%async_computation.5 | async-start | bytes 9732096 | tf_op jit(solution)/shard_map/all_gather | solution.py:552
  37.6 26.3 %copy-start.22 = (bf16[512,384]{1,0:T(8,128)(2,1)}, bf16[512,384]{1,0:T(8,128)(2,1)S(1)}, u32[]{:S(2)}) copy-start(bf16[512,384]{1,0:T(8,128)(2,1)S(1)} %get-tuple-element.83.query_ref) | copy-start | bytes 1179652
  37.6 26.3 %copy-start.24 = (bf16[512,384]{1,0:T(8,128)(2,1)}, bf16[512,384]{1,0:T(8,128)(2,1)S(1)}, u32[]{:S(2)}) copy-start(bf16[512,384]{1,0:T(8,128)(2,1)S(1)} %get-tuple-element.84.key_ref) | copy-start | bytes 1179652
  37.6 26.3 %copy-start.34 = (f32[3,2,512]{2,1,0:T(2,128)}, f32[3,2,512]{2,1,0:T(2,128)S(1)}, u32[]{:S(2)}) copy-start(f32[3,2,512]{2,1,0:T(2,128)S(1)} %get-tuple-element.86.logsum_ref) | copy-start | bytes 36868
  37.7 10.4 %copy-start.77 = (bf16[2,768]{1,0:T(2,128)(2,1)S(1)}, bf16[2,768]{1,0:T(2,128)(2,1)}, u32[]{:S(2)}) copy-start(bf16[2,768]{1,0:T(2,128)(2,1)} %param.30) | copy-start | bytes 9220
  39.2 22.9 %collective-permute-start = (f32[256,768]{1,0:T(8,128)S(1)}, f32[256,768]{1,0:T(8,128)}, u32[]{:S(2)}, u32[]{:S(2)}) collective-permute-start(f32[256,768]{1,0:T(8,128)S(1)} %constant_dynamic-slice_fusion.2), channel_id=1, source_target_pairs={{0,1},{1,0},{2,3},{3,2},{4,5},{5,4},{6,7},{7,6},{8,9},{9,8},{10,11... | collective-permute-start | bytes 2359304 | tf_op jit(solution)/shard_map/ppermute | solution.py:65
  42.5 19.0 %collective-permute-start.2 = (f32[2,1536]{1,0:T(2,128)S(1)}, f32[2,1536]{1,0:T(2,128)S(1)}, u32[]{:S(2)}, u32[]{:S(2)}) collective-permute-start(f32[2,1536]{1,0:T(2,128)S(1)} %convert_element_type.141), channel_id=1, source_target_pairs={{0,1},{1,0},{2,3},{3,2},{4,5},{5,4},{6,7},{7,6},{8,9},{9,8},{10,11... | collective-permute-start | bytes 36872 | tf_op jit(solution)/shard_map/ppermute | solution.py:65
  42.9 48.1 %collective-permute-start.3 = (f32[96,768]{1,0:T(8,128)}, f32[96,768]{1,0:T(8,128)S(1)}, u32[]{:S(2)}, u32[]{:S(2)}) collective-permute-start(f32[96,768]{1,0:T(8,128)} %get-tuple-element.71), channel_id=1, source_target_pairs={{0,1},{1,0},{2,3},{3,2},{4,5},{5,4},{6,7},{7,6},{8,9},{9,8},{10,11... | collective-permute-start | bytes 884744 | tf_op jit(solution)/shard_map/ppermute | solution.py:65
  63.9 23.5 %copy-start.62 = (f32[256]{0:T(256)}, f32[256]{0:T(256)S(1)}, u32[]{:S(2)}) copy-start(f32[256]{0:T(256)S(1)} %broadcast_multiply_fusion.12) | copy-start | bytes 3076
  64.2 23.3 %copy-start.78 = (f32[256]{0:T(256)}, f32[256]{0:T(256)S(1)}, u32[]{:S(2)}) copy-start(f32[256]{0:T(256)S(1)} %add_rsqrt_fusion.3) | copy-start | bytes 3076
  89.0 63.1 %copy-start.58 = (f32[256]{0:T(256)}, f32[256]{0:T(256)S(1)}, u32[]{:S(2)}) copy-start(f32[256]{0:T(256)S(1)} %broadcast_multiply_fusion.11) | copy-start | bytes 3076
  89.3 62.8 %copy-start.60 = (f32[256]{0:T(256)}, f32[256]{0:T(256)S(1)}, u32[]{:S(2)}) copy-start(f32[256]{0:T(256)S(1)} %add_rsqrt_fusion.2) | copy-start | bytes 3076
  91.8 216.9 %reduce-scatter.3.cloned.1.call-start = ((), (), s32[]{:S(2)}) async-start(), calls=%async_computation.2 | async-start | bytes 10027008 | tf_op jit(solution)/shard_map/reduce_scatter | solution.py:570
  91.8 21.5 %collective-permute-start.4 = (f32[256,768]{1,0:T(8,128)}, f32[256,768]{1,0:T(8,128)S(1)}, u32[]{:S(2)}, u32[]{:S(2)}) collective-permute-start(f32[256,768]{1,0:T(8,128)} %fusion.62), channel_id=1, source_target_pairs={{0,1},{1,0},{2,3},{3,2},{4,5},{5,4},{6,7},{7,6},{8,9},{9,8},{10,11... | collective-permute-start | bytes 2359304 | tf_op jit(solution)/shard_map/ppermute | solution.py:65
  129.1 25.0 %copy-start.36 = (f32[3,2,512]{2,1,0:T(2,128)}, f32[3,2,512]{2,1,0:T(2,128)S(1)}, u32[]{:S(2)}) copy-start(f32[3,2,512]{2,1,0:T(2,128)S(1)} %get-tuple-element.80.logsum_ref) | copy-start | bytes 36868
  131.2 20.9 %collective-permute-start.5 = (f32[256,768]{1,0:T(8,128)}, f32[256,768]{1,0:T(8,128)}, u32[]{:S(2)}, u32[]{:S(2)}) collective-permute-start(f32[256,768]{1,0:T(8,128)} %constant_dynamic-slice_fusion.1), channel_id=1, source_target_pairs={{0,1},{1,0},{2,3},{3,2},{4,5},{5,4},{6,7},{7,6},{8,9},{9,8},{10,11... | collective-permute-start | bytes 2359304 | tf_op jit(solution)/shard_map/ppermute | solution.py:65
  171.0 10.7 %copy-start.49 = (f32[256,768]{1,0:T(8,128)}, f32[256,768]{1,0:T(8,128)S(1)}, u32[]{:S(2)}) copy-start(f32[256,768]{1,0:T(8,128)S(1)} %get-tuple-element.93) | copy-start | bytes 2359300
  180.9 15.0 %collective-permute-start.6 = (f32[1536,1536]{1,0:T(8,128)}, f32[1536,1536]{1,0:T(8,128)}, u32[]{:S(2)}, u32[]{:S(2)}) collective-permute-start(f32[1536,1536]{1,0:T(8,128)} %feed_sums.4), channel_id=1, source_target_pairs={{0,2},{2,0},{1,3},{3,1},{4,6},{6,4},{5,7},{7,5},{8,10},{10,8},{9,1... | collective-permute-start | bytes 28311560 | tf_op jit(solution)/shard_map/ppermute | solution.py:65
  186.8 21.5 %collective-permute-start.7 = (f32[256,768]{1,0:T(8,128)}, f32[256,768]{1,0:T(8,128)}, u32[]{:S(2)}, u32[]{:S(2)}) collective-permute-start(f32[256,768]{1,0:T(8,128)} %get-tuple-element.159), channel_id=1, source_target_pairs={{0,1},{1,0},{2,3},{3,2},{4,5},{5,4},{6,7},{7,6},{8,9},{9,8},{10,11... | collective-permute-start | bytes 2359304 | tf_op jit(solution)/shard_map/ppermute | solution.py:65
  208.3 199.7 %reduce-scatter.5.cloned.1.call-start = ((), (), s32[]{:S(2)}) async-start(), calls=%async_computation.3 | async-start | bytes 15040512 | tf_op jit(solution)/shard_map/reduce_scatter | solution.py:587
  212.1 40.3 %slice-start.2 = ((s8[4718592]{0:T(1024)(128)(4,1)}), s8[524288]{0:T(1024)(128)(4,1)S(1)}, s32[]{:S(2)}) async-start(s8[4718592]{0:T(1024)(128)(4,1)} %bitcast.100), calls=%async_computation.9 | async-start | bytes 1048576
  224.3 21.8 %copy-start.39 = (f32[256,768]{1,0:T(8,128)S(1)}, f32[256,768]{1,0:T(8,128)}, u32[]{:S(2)}) copy-start(f32[256,768]{1,0:T(8,128)} %copy-done.38) | copy-start | bytes 2359300
  224.3 21.8 %copy-start.51 = (f32[256,768]{1,0:T(8,128)S(1)}, f32[256,768]{1,0:T(8,128)}, u32[]{:S(2)}) copy-start(f32[256,768]{1,0:T(8,128)} %get-tuple-element.160) | copy-start | bytes 2359300
  224.3 21.8 %copy-start.59 = (f32[256]{0:T(256)S(1)}, f32[256]{0:T(256)}, u32[]{:S(2)}) copy-start(f32[256]{0:T(256)} %copy-done.58) | copy-start | bytes 3076
  224.3 21.8 %copy-start.61 = (f32[256]{0:T(256)S(1)}, f32[256]{0:T(256)}, u32[]{:S(2)}) copy-start(f32[256]{0:T(256)} %copy-done.60) | copy-start | bytes 3076
  225.7 26.7 %slice-start.3 = ((s8[4718592]{0:T(1024)(128)(4,1)}), s8[4194304]{0:T(1024)(128)(4,1)S(1)}, s32[]{:S(2)}) async-start(s8[4718592]{0:T(1024)(128)(4,1)} %bitcast.100), calls=%async_computation.10 | async-start | bytes 8388608
  225.7 20.4 %collective-permute-start.8 = (f32[256,768]{1,0:T(8,128)S(1)}, f32[256,768]{1,0:T(8,128)S(1)}, u32[]{:S(2)}, u32[]{:S(2)}) collective-permute-start(f32[256,768]{1,0:T(8,128)S(1)} %constant_dynamic-slice_fusion), channel_id=1, source_target_pairs={{0,1},{1,0},{2,3},{3,2},{4,5},{5,4},{6,7},{7,6},{8,9},{9,8},{10,11... | collective-permute-start | bytes 2359304 | tf_op jit(solution)/shard_map/ppermute | solution.py:65
  258.7 15.0 %collective-permute-start.10 = (f32[1536,1536]{1,0:T(8,128)}, f32[1536,1536]{1,0:T(8,128)}, u32[]{:S(2)}, u32[]{:S(2)}) collective-permute-start(f32[1536,1536]{1,0:T(8,128)} %feed_sums.6), channel_id=1, source_target_pairs={{0,2},{2,0},{1,3},{3,1},{4,6},{6,4},{5,7},{7,5},{8,10},{10,8},{9,1... | collective-permute-start | bytes 28311560 | tf_op jit(solution)/shard_map/ppermute | solution.py:65
  262.4 21.4 %collective-permute-start.11 = (f32[256,768]{1,0:T(8,128)S(1)}, f32[256,768]{1,0:T(8,128)S(1)}, u32[]{:S(2)}, u32[]{:S(2)}) collective-permute-start(f32[256,768]{1,0:T(8,128)S(1)} %multiply_multiply_fusion.4), channel_id=1, source_target_pairs={{0,1},{1,0},{2,3},{3,2},{4,5},{5,4},{6,7},{7,6},{8,9},{9,8},{10,11... | collective-permute-start | bytes 2359304 | tf_op jit(solution)/shard_map/ppermute | solution.py:65
  268.7 32.2 %collective-permute-start.15 = (f32[1536,384]{1,0:T(8,128)}, f32[1536,384]{1,0:T(8,128)S(1)}, u32[]{:S(2)}, u32[]{:S(2)}) collective-permute-start(f32[1536,384]{1,0:T(8,128)} %attention_sums.5), channel_id=1, source_target_pairs={{0,2},{2,0},{1,3},{3,1},{4,6},{6,4},{5,7},{7,5},{8,10},{10,8},{9,1... | collective-permute-start | bytes 7077896 | tf_op jit(solution)/shard_map/ppermute | solution.py:65
  284.0 14.8 %copy-start.47 = (f32[256,768]{1,0:T(8,128)}, f32[256,768]{1,0:T(8,128)S(1)}, u32[]{:S(2)}) copy-start(f32[256,768]{1,0:T(8,128)S(1)} %get-tuple-element.169) | copy-start | bytes 2359300
  300.8 4.6 collective-permute-start.14
  308.7 225.9 %all-gather.11.cloned.1.call-start = ((), (), s32[]{:S(2)}) async-start(), calls=%async_computation.6 | async-start | bytes 29196288 | tf_op jit(solution)/shard_map/all_gather | solution.py:599
  309.7 9.9 %collective-permute-start.16 = (f32[96,768]{1,0:T(8,128)S(1)}, f32[96,768]{1,0:T(8,128)S(1)}, u32[]{:S(2)}, u32[]{:S(2)}) collective-permute-start(f32[96,768]{1,0:T(8,128)S(1)} %get-tuple-element.179), channel_id=1, source_target_pairs={{0,16},{16,0},{1,17},{17,1},{2,18},{18,2},{3,19},{19,3},{4,20},{20... | collective-permute-start | bytes 884744 | tf_op jit(solution)/shard_map/ppermute | solution.py:65
  311.4 16.3 %collective-permute-start.18 = (f32[96,768]{1,0:T(8,128)S(1)}, f32[96,768]{1,0:T(8,128)S(1)}, u32[]{:S(2)}, u32[]{:S(2)}) collective-permute-start(f32[96,768]{1,0:T(8,128)S(1)} %get-tuple-element.180), channel_id=1, source_target_pairs={{0,17},{17,0},{1,16},{16,1},{2,19},{19,2},{3,18},{18,3},{4,21},{21... | collective-permute-start | bytes 884744 | tf_op jit(solution)/shard_map/ppermute | solution.py:590
  313.4 14.2 %collective-permute-start.17 = (f32[96,768]{1,0:T(8,128)S(1)}, f32[96,768]{1,0:T(8,128)S(1)}, u32[]{:S(2)}, u32[]{:S(2)}) collective-permute-start(f32[96,768]{1,0:T(8,128)S(1)} %get-tuple-element.180), channel_id=1, source_target_pairs={{0,1},{1,0},{2,3},{3,2},{4,5},{5,4},{6,7},{7,6},{8,9},{9,8},{10,11... | collective-permute-start | bytes 884744 | tf_op jit(solution)/shard_map/ppermute | solution.py:65
  409.3 16.3 %collective-permute-start.19 = (f32[96,1536]{1,0:T(8,128)S(1)}, f32[96,1536]{1,0:T(8,128)S(1)}, u32[]{:S(2)}, u32[]{:S(2)}) collective-permute-start(f32[96,1536]{1,0:T(8,128)S(1)} %pad_maximum_fusion.1), channel_id=1, source_target_pairs={{0,16},{16,0},{1,17},{17,1},{2,18},{18,2},{3,19},{19,3},{4,20},{20... | collective-permute-start | bytes 1769480 | tf_op jit(solution)/shard_map/ppermute | solution.py:65
  411.0 14.7 %collective-permute-start.21 = (f32[96,768]{1,0:T(8,128)S(1)}, f32[96,768]{1,0:T(8,128)S(1)}, u32[]{:S(2)}, u32[]{:S(2)}) collective-permute-start(f32[96,768]{1,0:T(8,128)S(1)} %get-tuple-element.174), channel_id=1, source_target_pairs={{0,17},{17,0},{1,16},{16,1},{2,19},{19,2},{3,18},{18,3},{4,21},{21... | collective-permute-start | bytes 884744 | tf_op jit(solution)/shard_map/ppermute | solution.py:590
  413.2 19.9 %collective-permute-start.20 = (f32[96,768]{1,0:T(8,128)S(1)}, f32[96,768]{1,0:T(8,128)S(1)}, u32[]{:S(2)}, u32[]{:S(2)}) collective-permute-start(f32[96,768]{1,0:T(8,128)S(1)} %get-tuple-element.174), channel_id=1, source_target_pairs={{0,1},{1,0},{2,3},{3,2},{4,5},{5,4},{6,7},{7,6},{8,9},{9,8},{10,11... | collective-permute-start | bytes 884744 | tf_op jit(solution)/shard_map/ppermute | solution.py:65
  433.2 38.0 %copy-start.46 = (f32[256,768]{1,0:T(8,128)S(1)}, f32[256,768]{1,0:T(8,128)}, u32[]{:S(2)}) copy-start(f32[256,768]{1,0:T(8,128)} %copy-done.45) | copy-start | bytes 2359300
  433.2 38.0 %copy-start.48 = (f32[256,768]{1,0:T(8,128)S(1)}, f32[256,768]{1,0:T(8,128)}, u32[]{:S(2)}) copy-start(f32[256,768]{1,0:T(8,128)} %copy-done.47) | copy-start | bytes 2359300
  434.2 39.9 %copy-start.50 = (f32[256,768]{1,0:T(8,128)S(1)}, f32[256,768]{1,0:T(8,128)}, u32[]{:S(2)}) copy-start(f32[256,768]{1,0:T(8,128)} %copy-done.49) | copy-start | bytes 2359300
  434.2 41.1 %copy-start.70 = (f32[768]{0:T(1024)S(1)}, f32[768]{0:T(1024)}, u32[]{:S(2)}) copy-start(f32[768]{0:T(1024)} %get-tuple-element.123) | copy-start | bytes 9220
  434.2 41.0 %copy-start.69 = (f32[768]{0:T(1024)S(1)}, f32[768]{0:T(1024)}, u32[]{:S(2)}) copy-start(f32[768]{0:T(1024)} %get-tuple-element.129) | copy-start | bytes 9220
  434.3 41.1 %copy-start.71 = (f32[768]{0:T(1024)S(1)}, f32[768]{0:T(1024)}, u32[]{:S(2)}) copy-start(f32[768]{0:T(1024)} %get-tuple-element.153) | copy-start | bytes 9220
  434.3 41.1 %copy-start.86 = (f32[1536]{0:T(1024)S(1)}, f32[1536]{0:T(1024)}, u32[]{:S(2)}) copy-start(f32[1536]{0:T(1024)} %get-tuple-element.212) | copy-start | bytes 18436
  434.3 41.1 %copy-start.85 = (f32[1536]{0:T(1024)S(1)}, f32[1536]{0:T(1024)}, u32[]{:S(2)}) copy-start(f32[1536]{0:T(1024)} %get-tuple-element.216) | copy-start | bytes 18436
  434.3 41.1 %copy-start.91 = (f32[768]{0:T(1024)S(1)}, f32[768]{0:T(1024)}, u32[]{:S(2)}) copy-start(f32[768]{0:T(1024)} %get-tuple-element.119) | copy-start | bytes 9220
  434.3 41.1 %copy-start.90 = (f32[768]{0:T(1024)S(1)}, f32[768]{0:T(1024)}, u32[]{:S(2)}) copy-start(f32[768]{0:T(1024)} %get-tuple-element.131) | copy-start | bytes 9220
  434.3 36.9 %collective-permute-start.12 = (f32[512,768]{1,0:T(8,128)}, f32[512,768]{1,0:T(8,128)S(1)}, u32[]{:S(2)}, u32[]{:S(2)}) collective-permute-start(f32[512,768]{1,0:T(8,128)} %get-tuple-element.92), channel_id=1, source_target_pairs={{0,1},{1,0},{2,3},{3,2},{4,5},{5,4},{6,7},{7,6},{8,9},{9,8},{10,11... | collective-permute-start | bytes 4718600 | tf_op jit(solution)/shard_map/ppermute | solution.py:65
  474.1 20.3 %collective-permute-start.13 = (f32[256,768]{1,0:T(8,128)S(1)}, f32[256,768]{1,0:T(8,128)S(1)}, u32[]{:S(2)}, u32[]{:S(2)}) collective-permute-start(f32[256,768]{1,0:T(8,128)S(1)} %copy-done.50), channel_id=1, source_target_pairs={{0,1},{1,0},{2,3},{3,2},{4,5},{5,4},{6,7},{7,6},{8,9},{9,8},{10,11... | collective-permute-start | bytes 2359304 | tf_op jit(solution)/shard_map/ppermute | solution.py:65
  475.6 18.7 %collective-permute-start.9 = (f32[14,768]{1,0:T(8,128)S(1)}, f32[14,768]{1,0:T(8,128)S(1)}, u32[]{:S(2)}, u32[]{:S(2)}) collective-permute-start(f32[14,768]{1,0:T(8,128)S(1)} %concatenate.38), channel_id=1, source_target_pairs={{0,1},{1,0},{2,3},{3,2},{4,5},{5,4},{6,7},{7,6},{8,9},{9,8},{10,11... | collective-permute-start | bytes 129032 | tf_op jit(solution)/shard_map/ppermute | solution.py:65
  496.1 1.3 collective-permute-start.22
  497.4 6.5 %collective-permute-start.23 = (f32[18,768]{1,0:T(8,128)S(1)}, f32[18,768]{1,0:T(8,128)S(1)}, u32[]{:S(2)}, u32[]{:S(2)}) collective-permute-start(f32[18,768]{1,0:T(8,128)S(1)} %add.412), channel_id=1, source_target_pairs={{0,4},{4,0},{8,12},{12,8},{1,5},{5,1},{9,13},{13,9},{2,6},{6,2},{1... | collective-permute-start | bytes 165896 | tf_op jit(solution)/shard_map/ppermute | solution.py:613
  503.9 7.5 %collective-permute-start.24 = (f32[18,768]{1,0:T(8,128)S(1)}, f32[18,768]{1,0:T(8,128)S(1)}, u32[]{:S(2)}, u32[]{:S(2)}) collective-permute-start(f32[18,768]{1,0:T(8,128)S(1)} %add.413), channel_id=1, source_target_pairs={{4,8},{8,4},{12,0},{0,12},{5,9},{9,5},{13,1},{1,13},{6,10},{10,6},... | collective-permute-start | bytes 165896 | tf_op jit(solution)/shard_map/ppermute | solution.py:613
  511.4 6.0 %collective-permute-start.25 = (f32[18,768]{1,0:T(8,128)S(1)}, f32[18,768]{1,0:T(8,128)S(1)}, u32[]{:S(2)}, u32[]{:S(2)}) collective-permute-start(f32[18,768]{1,0:T(8,128)S(1)} %add.414), channel_id=1, source_target_pairs={{0,32},{32,0},{64,96},{96,64},{1,33},{33,1},{65,97},{97,65},{2,34}... | collective-permute-start | bytes 165896 | tf_op jit(solution)/shard_map/ppermute | solution.py:613
  517.4 7.2 %collective-permute-start.26 = (f32[18,768]{1,0:T(8,128)S(1)}, f32[18,768]{1,0:T(8,128)S(1)}, u32[]{:S(2)}, u32[]{:S(2)}) collective-permute-start(f32[18,768]{1,0:T(8,128)S(1)} %add.415), channel_id=1, source_target_pairs={{32,64},{64,32},{96,0},{0,96},{33,65},{65,33},{97,1},{1,97},{34,66... | collective-permute-start | bytes 165896 | tf_op jit(solution)/shard_map/ppermute | solution.py:613
  524.6 4.4 collective-permute-start.27
  (71 other events, 163.0 us)
Sparse Core Ops, SparseCore 0:
  23.9 57.0 all-gather.6
  91.9 54.9 all-gather.8
  208.5 87.0 reduce-scatter.2
  308.8 99.2 reduce-scatter.4
  434.3 97.6 all-gather.10

commit v3 on v2

--- a/solution.py
+++ b/solution.py
@@ -71,6 +71,29 @@
 
 def piece(values, index, size):
     return lax.dynamic_slice_in_dim(values, index * size, size, 0)
+
+
+def ring_parts(values, axis, dim):
+    place = lax.axis_index(axis)
+    kept = lax.dynamic_index_in_dim(values, place, dim, keepdims=False)
+    received = []
+    for distance in (1, 3, 2):
+        sent = lax.dynamic_index_in_dim(values, lax.rem(place + distance, 4), dim, keepdims=False)
+        pairs = [(start, (start + distance) % 4) for start in range(4)]
+        received.append(lax.ppermute(sent, axis, pairs))
+    return [kept, *received]
+
+
+def plane_sum(values):
+    rows, columns = values.shape
+    values = values.reshape(4, 4, 2, rows // 32, columns)
+    x_first = ring_parts(values[:, :, 0], "x", 1)
+    y_first = ring_parts(values[:, :, 1], "y", 0)
+    parts = together(*x_first, *y_first)
+    x_first = ring_parts(sum(parts[1:4], parts[0]), "y", 0)
+    y_first = ring_parts(sum(parts[5:], parts[4]), "x", 0)
+    parts = together(*x_first, *y_first)
+    return jnp.concatenate([sum(parts[1:4], parts[0]), sum(parts[5:], parts[4])])
 
 
 def in_order(side, mine, other):
@@ -333,21 +356,22 @@
     write(3, mixture_ref, grad_ref)
 
 
-def attention_sums(part, lows, mixture, rounded, attended_low, received=None, into=None, place=0):
+def attention_sums(part, lows, mixture, rounded, attended_low, received=None, columns=None, into=None):
     slots, heads = mixture.shape
     half = rounded.shape[1] // 2
     left = pl.BlockSpec((slots, heads), lambda i: (0, 0))
     right = pl.BlockSpec((slots, half), lambda i: (0, i // 2))
     rows = pl.BlockSpec((heads, half), lambda i: (i, 0))
-    more = [] if received is None else [received, into]
-    shape = (4 * heads, half) if into is None else into.shape
+    more = [item for item in (received, into) if item is not None]
+    place = 0 if into is None else 1
+    shape = (4 * heads, half if columns is None else columns)
     return pl.pallas_call(
-        lambda *refs: attention_sums_kernel(bool(more), *refs),
+        lambda *refs: attention_sums_kernel(received is not None, *refs),
         grid=(4,),
-        in_specs=[SCALAR] + [left] * 4 + [right] * 2 + ([rows, pl.BlockSpec(memory_space=pl.ANY)] if more else []),
+        in_specs=[SCALAR] + [left] * 4 + [right] * 2 + [rows, pl.BlockSpec(memory_space=pl.ANY)][: len(more)],
         out_specs=pl.BlockSpec((heads, half), lambda i: (i, place)),
         out_shape=jax.ShapeDtypeStruct(shape, F32),
-        input_output_aliases={8: 0} if more else {},
+        input_output_aliases={8: 0} if place else {},
         compiler_params=LIMIT,
         cost_estimate=pl.CostEstimate(flops=8 * slots * heads * half, bytes_accessed=16 * heads * half, transcendentals=0),
         name="attention_sums",
@@ -527,8 +551,8 @@
         biases = [column_sum(item).reshape(-1, width) for item in pre_lows]
         return grad_one, ffn_low, pre_lows, shared, biases
 
-    def layer_forward(layer, x_own, share, sent, peers):
-        attended = share + swap(sent, "h") + output_bias[layer]
+    def layer_forward(layer, x_own, share, received, peers):
+        attended = share + received + output_bias[layer]
         hidden, scaled, inverse = normalize(x_own + attended, attn_gain[layer], attn_shift[layer])
         hidden_low = hidden.astype(BF16)
         pre = dot(hidden_low, up_weight[layer]) + up_bias[layer]
@@ -546,14 +570,15 @@
     pieces2, sent = together(pieces2, sent)
     pieces2 = swap(pieces2, "h")
     peers1 = sort_weights(gathered1.reshape(16, 2, rows_down, width))
-    x2_own, saved1 = layer_forward(0, own_slots(tokens).astype(F32), share, sent, peers1)
+    x2_own, saved1 = layer_forward(0, own_slots(tokens).astype(F32), share, swap(sent, "h"), peers1)
     sent = 0.5 * x2_own
     pieces2, sent = together(pieces2, sent)
     gathered2 = lax.all_gather(pieces2, PLANE + ("c",))
     x2_low = (2.0 * in_order(side, sent, swap(sent, "h"))).astype(BF16)
     att2, share, sent = attention_forward(1, x2_low)
     peers2 = sort_weights(gathered2.reshape(16, 2, rows_down, width))
-    _, saved2 = layer_forward(1, x2_own, share, sent, peers2)
+    sent, peer_down, peer_up = together(swap(sent, "h"), *peers2)
+    _, saved2 = layer_forward(1, x2_own, share, sent, (peer_down, peer_up))
     scaled_last = saved2[0]
     mixture = att2[3]
     peer_down, peer_up = (peers1[0], peers2[0]), (peers1[1], peers2[1])
@@ -577,25 +602,25 @@
     sent = 0.5 * grad_one_own1
     received = swap(sent, "h")
     feed1_received = swap(feed_sums(1 - core, saved1[3], pre_lows, ffn_low, saved1[4], 2 * width), "c")
-    rest = feed_sums(core, saved1[3], pre_lows, ffn_low, saved1[4], 3 * width, feed1_received)
+    rest = feed_sums(core, saved1[3], pre_lows, ffn_low, saved1[4], 2 * width, feed1_received)
     rest, received = together(rest, received)
     grad_one1, lows1, attended_low1, share, small_att1 = attention_back(0, att1, sent, received)
+    attn = attention_sums(core, lows2, mixture, x2_low, attended_low2, attn2_received, width)
+    rest, feed2, *lows1 = together(rest, feed2, *lows1)
+    rest = lax.psum_scatter(rest, PLANE, tiled=True)
     attn1_received = swap(attention_sums(1 - core, lows1, att1[3], tokens, attended_low1), "c")
-    rest = attention_sums(core, lows2, mixture, x2_low, attended_low2, attn2_received, rest, 4)
-    rest = attention_sums(core, lows1, att1[3], tokens, attended_low1, attn1_received, rest, 5)
-    rest, feed2 = together(rest, feed2)
-    rest = lax.psum_scatter(rest, PLANE, tiled=True)
-
-    def across(own, peer):
+    attn = attention_sums(core, lows1, att1[3], tokens, attended_low1, attn1_received, width, attn)
+    attn = plane_sum(attn)
+
+    def across(values):
+        own, peer = values[:, :width], values[:, width:]
         diagonal = lax.ppermute(peer, ("zl", "h"), ((0, 3), (3, 0), (1, 2), (2, 1)))
-        peer = swap(peer, "h") + diagonal
-        own = own + swap(own, "zl")
-        return jnp.concatenate([own[:, :width] + peer, own[:, width:]], axis=1)
-
-    feed2 = across(feed2[:, :width], feed2[:, width:])
-    feed2, rest = together(feed2, rest)
-    rest = across(jnp.concatenate([rest[:, :width], rest[:, 2 * width :]], axis=1), rest[:, width : 2 * width])
-    own = jnp.concatenate([feed2, rest], axis=1)
+        return own + swap(own, "zl") + (swap(peer, "h") + diagonal)
+
+    feed2 = across(feed2)
+    attn = attn + swap(attn, "zl")
+    feed2, attn, rest = together(feed2, attn, rest)
+    own = jnp.concatenate([feed2, across(rest), attn], axis=1)
     gathered = lax.all_gather(own, PLANE + ("c",)).reshape(16, 2, *own.shape)
     grad_query, grad_key, grad_value, grad_output, grad_up, grad_down = place_gradients(gathered, width)
 

time: 574 us -> 566 us (0.986)
  waiting for transfers between devices: 294 us -> 251 us
  starting transfers between devices: 44.4 us -> 62.5 us
  local copies, waits for them, and re-layouts: 35.7 us -> 46.3 us
    reduce_scatter x1, waiting for transfers between devices: 80.3 us -> 0.02 us  [local(): rest = lax.psum_scatter(rest, PLANE, tiled=True)]
    ppermute x0 -> x12, waiting for transfers between devices: none -> 43.3 us  [ring_parts(): received.append(lax.ppermute(sent, axis, pairs))]
    ppermute x0 -> x12, starting transfers between devices: none -> 16.2 us  [ring_parts(): received.append(lax.ppermute(sent, axis, pairs))]
    ppermute x22 -> x23, waiting for transfers between devices: 171 us -> 156 us  [swap(): return lax.ppermute(values, axis, SWAP)]
    all_gather x1, waiting for transfers between devices: 0.01 us -> 11.6 us  [local(): gathered2 = lax.all_gather(pieces2, PLANE + ('c',))]
    unnamed x212 -> x262, local copies, waits for them, and re-layouts: 27.2 us -> 32.8 us
    ppermute x22 -> x23, starting transfers between devices: 37.3 us -> 41 us  [swap(): return lax.ppermute(values, axis, SWAP)]
  transfers between devices with their start and end apart: 33 -> 46, of which waited for: 24 -> 30; matrix products, arithmetic and copies ran while one was open for 11% -> 11% of each run, Pallas kernels for 15% -> 16%
where the time goes in v3:
time: 566 us; the launch traced here: 557 us
  waiting for transfers between devices  251 us (44%)
  Pallas kernels  121 us (21%)
  starting transfers between devices  62.5 us (11%)
  local copies, waits for them, and re-layouts  46.3 us (8%)
  other arithmetic  29.7 us (5%)
  matrix products  29.3 us (5%)
  between operations  17.1 us (3%)
    ppermute x23, waiting for transfers between devices, swap(): return lax.ppermute(values, axis, SWAP)  156 us
    ppermute x12, waiting for transfers between devices, ring_parts(): received.append(lax.ppermute(sent, axis, pairs))  43.3 us
    ppermute x23, starting transfers between devices, swap(): return lax.ppermute(values, axis, SWAP)  41 us
    unnamed x262, local copies, waits for them, and re-layouts  32.8 us
    pallas_call x4, Pallas kernels, feed_sums(): pl.pallas_call(lambda *refs: feed_sums_kernel(bool(more), *refs), grid=(4...  26.4 us
    ppermute x4, waiting for transfers between devices, local(): small = small + lax.ppermute(small, axis, pairs)  25.3 us
    pallas_call x2, Pallas kernels, attend_back(): pl.pallas_call(attend_back_kernel, grid=(steps,), in_specs=[SCALAR, part,...  24.7 us
    pallas_call x2, Pallas kernels, attend(): pl.pallas_call(attend_kernel, grid=(steps,), in_specs=[SCALAR, whole, wei...  19.5 us
  transfers between devices with their start and end apart: 46, of which 30 were waited for; matrix products, arithmetic and copies ran while one was open for 11% of the time, Pallas kernels for 16%

profile of v3, /device:TPU:0, one launch (start us, length us, event | category | flops | bytes accessed | tf_op | source)
XLA Modules:
  0.0 556.9 jit_solution(14461016995759586480)
XLA Ops:
  7.3 2.3 copy-done.1
  12.1 4.0 collective-permute-start.1
  16.0 7.0 %collective-permute-done.1 = f32[96,768]{1,0:T(8,128)S(1)} collective-permute-done((f32[96,768]{1,0:T(8,128)S(1)}, f32[96,768]{1,0:T(8,128)S(1)}, u32[]{:S(2)}, u32[]{:S(2)}) %collective-permute-start.1) | collective-permute-done | bytes 294944 | tf_op jit(solution)/shard_map/ppermute | solution.py:65
  27.1 9.8 %attend.2 = (bf16[512,384]{1,0:T(8,128)(2,1)S(1)}, bf16[512,384]{1,0:T(8,128)(2,1)S(1)}, bf16[512,384]{1,0:T(8,128)(2,1)S(1)}, bf16[512,384]{1,0:T(8,128)(2,1)S(...) custom-call(s32[1]{0:T(128)} %copy.62.length_ref, bf16[512,768]{1,0:T(8,128)(2,1)S(1)} %copy-done, ...), custom_call_target="tpu_custom_call" | custom-call | flops 1610612736 | bytes 5505024 | tf_op jit(solution)/shard_map/attend/pallas_call | solution.py:172
  40.0 2.1 constant_dynamic-slice_fusion.2
  42.1 3.2 collective-permute-start
  45.8 3.2 collective-permute-start.3
  50.4 14.2 %collective-permute-done.2 = f32[2,1536]{1,0:T(2,128)S(1)} collective-permute-done((f32[2,1536]{1,0:T(2,128)S(1)}, f32[2,1536]{1,0:T(2,128)S(1)}, u32[]{:S(2)}, u32[]{:S(2)}) %collective-permute-start.2) | collective-permute-done | bytes 12320 | tf_op jit(solution)/shard_map/ppermute | solution.py:65
  67.1 4.1 multiply_convert_fusion.3
  73.0 8.0 %all-gather.7.cloned.1.call-done = f32[3072,768]{1,0:T(8,128)} async-done(((f32[96,768]{1,0:T(8,128)}), f32[3072,768]{1,0:T(8,128)}) %all-gather.7.cloned.1.call-update) | async-done | bytes 9437200 | tf_op jit(solution)/shard_map/all_gather | solution.py:505
  81.0 4.4 sort_weights.2
  91.2 3.2 collective-permute-start.4
  94.4 18.4 %collective-permute-done.4 = f32[256,768]{1,0:T(8,128)} collective-permute-done((f32[256,768]{1,0:T(8,128)}, f32[256,768]{1,0:T(8,128)}, u32[]{:S(2)}, u32[]{:S(2)}) %collective-permute-start.4) | collective-permute-done | bytes 786464 | tf_op jit(solution)/shard_map/ppermute | solution.py:65
  116.0 9.8 %attend.3 = (bf16[512,384]{1,0:T(8,128)(2,1)S(1)}, bf16[512,384]{1,0:T(8,128)(2,1)S(1)}, bf16[512,384]{1,0:T(8,128)(2,1)S(1)}, bf16[512,384]{1,0:T(8,128)(2,1)S(...) custom-call(s32[1]{0:T(128)} %copy.62.length_ref, bf16[512,768]{1,0:T(8,128)(2,1)S(1)} %fusion.40.slot_ref.refs_5_, ...), custom_call_target="tpu_custom_call" | custom-call | flops 1610612736 | bytes 5505024 | tf_op jit(solution)/shard_map/attend/pallas_call | solution.py:172
  128.0 2.2 constant_dynamic-slice_fusion.1
  130.3 3.6 collective-permute-start.5
  134.5 11.6 %all-gather.9.cloned.1.call-done = f32[3072,768]{1,0:T(8,128)} async-done(((f32[96,768]{1,0:T(8,128)}), f32[3072,768]{1,0:T(8,128)}) %all-gather.9.cloned.1.call-update) | async-done | bytes 9437200 | tf_op jit(solution)/shard_map/all_gather | solution.py:576
  146.2 4.5 sort_weights.3
  153.8 2.5 multiply_convert_fusion.1
  165.4 4.8 feed_sums.4
  171.8 3.4 multiply_reduce_fusion.2
  176.6 3.1 collective-permute-start.7
  179.8 5.5 collective-permute-done.6.refs_7_
  185.3 8.4 %feed_sums.5 = f32[1536,1536]{1,0:T(8,128)} custom-call(s32[1]{0:T(128)} %bitcast.1.refs_0_, bf16[256,1536]{1,0:T(8,128)(2,1)S(1)} %get-tuple-element.263.refs_1_, bf16[256,1536]{1,0:T(8,128)(2,1)S(1)} %get-tuple-element.265.refs_2_, bf16[256,1536]{1,0:T(8,128)(2,1)S(1)} %get-tuple-element.274.refs_3_, bf16[256,1536]{1,0:T(8,128)(2,1)S(1)} %get-tuple-element.278.refs_4_, ...), custom_call_target="tpu_custom_call" | custom-call | flops 1207959552 | bytes 18874368 | tf_op jit(solution)/shard_map/feed_sums/pallas_call | solution.py:329
  193.6 4.1 collective-permute-done.7
  201.0 12.4 %attend_back.2 = (bf16[512,384]{1,0:T(8,128)(2,1)S(1)}, bf16[512,384]{1,0:T(8,128)(2,1)S(1)}, bf16[512,384]{1,0:T(8,128)(2,1)S(1)}, f32[512,768]{1,0:T(8,128)}, ...) custom-call(s32[1]{0:T(128)} %copy.62.length_ref, bf16[512,384]{1,0:T(8,128)(2,1)S(1)} %copy-done.48, ...), custom_call_target="tpu_custom_call" | custom-call | flops 2214592512 | bytes 5505024 | tf_op jit(solution)/shard_map/attend_back/pallas_call | solution.py:250
  215.2 3.2 collective-permute-start.8
  218.4 16.8 %collective-permute-done.8 = f32[256,768]{1,0:T(8,128)S(1)} collective-permute-done((f32[256,768]{1,0:T(8,128)S(1)}, f32[256,768]{1,0:T(8,128)S(1)}, u32[]{:S(2)}, u32[]{:S(2)}) %collective-permute-start.8) | collective-permute-done | bytes 786464 | tf_op jit(solution)/shard_map/ppermute | solution.py:65
  235.2 2.3 multiply_reduce_fusion.3
  242.7 4.8 feed_sums.6
  247.6 2.8 fusion.44
  253.2 3.3 collective-permute-start.11
  256.5 6.0 %collective-permute-done.10.refs_7_ = f32[1536,1536]{1,0:T(8,128)} collective-permute-done((f32[1536,1536]{1,0:T(8,128)}, f32[1536,1536]{1,0:T(8,128)}, u32[]{:S(2)}, u32[]{:S(2)}) %collective-permute-start.10) | collective-permute-done | bytes 9437216 | tf_op jit(solution)/shard_map/ppermute | solution.py:65
  262.5 8.4 %feed_sums.7 = f32[1536,1536]{1,0:T(8,128)} custom-call(s32[1]{0:T(128)} %bitcast.1.refs_0_, bf16[256,1536]{1,0:T(8,128)(2,1)S(1)} %copy-done.3, bf16[256,1536]{1,0:T(8,128)(2,1)S(1)} %get-tuple-element.259.refs_2_, bf16[256,1536]{1,0:T(8,128)(2,1)S(1)} %get-tuple-element.272.refs_3_, bf16[256,1536]{1,0:T(8,128)(2,1)S(1)} %get-tuple-element.276.refs_4_, ...), custom_call_target="tpu_custom_call" | custom-call | flops 1207959552 | bytes 18874368 | tf_op jit(solution)/shard_map/feed_sums/pallas_call | solution.py:329
  270.9 4.1 collective-permute-done.11
  278.9 12.3 %attend_back.3 = (bf16[512,384]{1,0:T(8,128)(2,1)S(1)}, bf16[512,384]{1,0:T(8,128)(2,1)S(1)}, bf16[512,384]{1,0:T(8,128)(2,1)S(1)}, f32[512,768]{1,0:T(8,128)}, ...) custom-call(s32[1]{0:T(128)} %copy.62.length_ref, bf16[512,384]{1,0:T(8,128)(2,1)S(1)} %copy-done.42, ...), custom_call_target="tpu_custom_call" | custom-call | flops 2214592512 | bytes 5505024 | tf_op jit(solution)/shard_map/attend_back/pallas_call | solution.py:250
  297.5 3.1 attention_sums.5
  300.7 3.1 attention_sums.4
  308.5 4.9 attention_sums.6.refs_8_
  313.4 4.8 attention_sums.7
  318.2 3.0 fusion.72
  322.5 2.9 collective-permute-start.24
  330.5 16.0 %collective-permute-done.24 = f32[4,48,768]{2,1,0:T(8,128)} collective-permute-done((f32[4,48,768]{2,1,0:T(8,128)}, f32[4,48,768]{2,1,0:T(8,128)}, u32[]{:S(2)}, u32[]{:S(2)}) %collective-permute-start.24) | collective-permute-done | bytes 589856 | tf_op jit(solution)/shard_map/ppermute | solution.py:83
  347.5 19.2 %collective-permute-done.23 = f32[4,48,768]{2,1,0:T(8,128)S(1)} collective-permute-done((f32[4,48,768]{2,1,0:T(8,128)}, f32[4,48,768]{2,1,0:T(8,128)S(1)}, u32[]{:S(2)}, u32[]{:S(2)}) %collective-permute-start.23) | collective-permute-done | bytes 589856 | tf_op jit(solution)/shard_map/ppermute | solution.py:83
  366.8 2.1 collective-permute-done.20
  368.9 5.5 collective-permute-done.19
  374.6 3.0 collective-permute-start.27
  383.7 2.6 collective-permute-start.16
  391.0 11.5 %collective-permute-done.14 = f32[96,768]{1,0:T(8,128)S(1)} collective-permute-done((f32[96,768]{1,0:T(8,128)S(1)}, f32[96,768]{1,0:T(8,128)S(1)}, u32[]{:S(2)}, u32[]{:S(2)}) %collective-permute-start.14) | collective-permute-done | bytes 294944 | tf_op jit(solution)/shard_map/ppermute | solution.py:65
  402.5 3.9 collective-permute-done.31
  407.6 2.6 collective-permute-start.32
  412.3 5.8 %collective-permute-done.32 = f32[96,768]{1,0:T(8,128)S(1)} collective-permute-done((f32[96,768]{1,0:T(8,128)S(1)}, f32[96,768]{1,0:T(8,128)S(1)}, u32[]{:S(2)}, u32[]{:S(2)}) %collective-permute-start.32) | collective-permute-done | bytes 294944 | tf_op jit(solution)/shard_map/ppermute | solution.py:65
  418.1 6.4 %collective-permute-done.34 = f32[96,768]{1,0:T(8,128)S(1)} collective-permute-done((f32[96,768]{1,0:T(8,128)S(1)}, f32[96,768]{1,0:T(8,128)S(1)}, u32[]{:S(2)}, u32[]{:S(2)}) %collective-permute-start.34) | collective-permute-done | bytes 294944 | tf_op jit(solution)/shard_map/ppermute | solution.py:617
  427.4 35.8 %collective-permute-done.12 = f32[512,768]{1,0:T(8,128)S(1)} collective-permute-done((f32[512,768]{1,0:T(8,128)}, f32[512,768]{1,0:T(8,128)S(1)}, u32[]{:S(2)}, u32[]{:S(2)}) %collective-permute-start.12) | collective-permute-done | bytes 1572896 | tf_op jit(solution)/shard_map/ppermute | solution.py:65
  463.2 2.9 add_add_fusion
  467.2 2.9 collective-permute-start.9
  470.2 15.8 %collective-permute-done.9 = f32[14,768]{1,0:T(8,128)S(1)} collective-permute-done((f32[14,768]{1,0:T(8,128)S(1)}, f32[14,768]{1,0:T(8,128)S(1)}, u32[]{:S(2)}, u32[]{:S(2)}) %collective-permute-start.9) | collective-permute-done | bytes 43040 | tf_op jit(solution)/shard_map/ppermute | solution.py:65
  489.2 6.4 %collective-permute-done.36 = f32[18,768]{1,0:T(8,128)S(1)} collective-permute-done((f32[18,768]{1,0:T(8,128)S(1)}, f32[18,768]{1,0:T(8,128)S(1)}, u32[]{:S(2)}, u32[]{:S(2)}) %collective-permute-start.36) | collective-permute-done | bytes 55328 | tf_op jit(solution)/shard_map/ppermute | solution.py:638
  495.7 7.4 %collective-permute-done.37 = f32[18,768]{1,0:T(8,128)S(1)} collective-permute-done((f32[18,768]{1,0:T(8,128)S(1)}, f32[18,768]{1,0:T(8,128)S(1)}, u32[]{:S(2)}, u32[]{:S(2)}) %collective-permute-start.37) | collective-permute-done | bytes 55328 | tf_op jit(solution)/shard_map/ppermute | solution.py:638
  503.2 5.9 %collective-permute-done.38 = f32[18,768]{1,0:T(8,128)S(1)} collective-permute-done((f32[18,768]{1,0:T(8,128)S(1)}, f32[18,768]{1,0:T(8,128)S(1)}, u32[]{:S(2)}, u32[]{:S(2)}) %collective-permute-start.38) | collective-permute-done | bytes 55328 | tf_op jit(solution)/shard_map/ppermute | solution.py:638
  510.7 5.6 %collective-permute-done.39 = f32[18,768]{1,0:T(8,128)S(1)} collective-permute-done((f32[18,768]{1,0:T(8,128)S(1)}, f32[18,768]{1,0:T(8,128)S(1)}, u32[]{:S(2)}, u32[]{:S(2)}) %collective-permute-start.39) | collective-permute-done | bytes 55328 | tf_op jit(solution)/shard_map/ppermute | solution.py:638
  516.4 4.3 collective-permute-done.40
  526.2 8.0 %place_attention.1 = (f32[2,768,384]{2,1,0:T(8,128)}, f32[2,768,384]{2,1,0:T(8,128)}, f32[2,768,384]{2,1,0:T(8,128)}, f32[2,384,768]{2,1,0:T(8,128)}) custom-call(f32[16,2,96,2304]{3,2,1,0:T(8,128)} %bitcast.137, f32[16,2,96,2304]{3,2,1,0:T(8,128)} %bitcast.138, f32[16,2,96,2304]{3,2,1,0:T(8,128)} %bitcast.139, f32[16,2,96,2304]{3,2,1,0:T(8,128)} %bitcast.140), custom_call_target="tpu_custom_call" | custom-call | tf_op jit(solution)/shard_map/place_attention/pallas_call | solution.py:460
  534.3 15.6 %place_feed.1 = (f32[2,1536,768]{2,1,0:T(8,128)}, f32[2,768,1536]{2,1,0:T(8,128)}) custom-call(f32[16,2,96,2304]{3,2,1,0:T(8,128)} %bitcast.141, f32[16,2,96,2304]{3,2,1,0:T(8,128)} %bitcast.142), custom_call_target="tpu_custom_call" | custom-call | tf_op jit(solution)/shard_map/place_feed/pallas_call | solution.py:443
  (443 shorter events, 104.7 us)
Async XLA Ops:
  7.2 73.8 %all-gather.7.cloned.1.call-start = ((), (), s32[]{:S(2)}) async-start(), calls=%async_computation.4 | async-start | bytes 9732096 | tf_op jit(solution)/shard_map/all_gather | solution.py:505
  12.1 11.0 %collective-permute-start.1 = (f32[96,768]{1,0:T(8,128)S(1)}, f32[96,768]{1,0:T(8,128)S(1)}, u32[]{:S(2)}, u32[]{:S(2)}) collective-permute-start(f32[96,768]{1,0:T(8,128)S(1)} %get-tuple-element.242), channel_id=1, source_target_pairs={{0,1},{1,0},{2,3},{3,2},{4,5},{5,4},{6,7},{7,6},{8,9},{9,8},{10,11... | collective-permute-start | bytes 884744 | tf_op jit(solution)/shard_map/ppermute | solution.py:65
  23.8 122.4 %all-gather.9.cloned.1.call-start = ((), (), s32[]{:S(2)}) async-start(), calls=%async_computation.5 | async-start | bytes 9732096 | tf_op jit(solution)/shard_map/all_gather | solution.py:576
  42.1 22.5 %collective-permute-start = (f32[256,768]{1,0:T(8,128)}, f32[256,768]{1,0:T(8,128)}, u32[]{:S(2)}, u32[]{:S(2)}) collective-permute-start(f32[256,768]{1,0:T(8,128)} %constant_dynamic-slice_fusion.2), channel_id=1, source_target_pairs={{0,1},{1,0},{2,3},{3,2},{4,5},{5,4},{6,7},{7,6},{8,9},{9,8},{10,11... | collective-permute-start | bytes 2359304 | tf_op jit(solution)/shard_map/ppermute | solution.py:65
  45.4 19.2 %collective-permute-start.2 = (f32[2,1536]{1,0:T(2,128)S(1)}, f32[2,1536]{1,0:T(2,128)S(1)}, u32[]{:S(2)}, u32[]{:S(2)}) collective-permute-start(f32[2,1536]{1,0:T(2,128)S(1)} %convert_element_type.141), channel_id=1, source_target_pairs={{0,1},{1,0},{2,3},{3,2},{4,5},{5,4},{6,7},{7,6},{8,9},{9,8},{10,11... | collective-permute-start | bytes 36872 | tf_op jit(solution)/shard_map/ppermute | solution.py:65
  45.8 44.6 %collective-permute-start.3 = (f32[96,768]{1,0:T(8,128)}, f32[96,768]{1,0:T(8,128)S(1)}, u32[]{:S(2)}, u32[]{:S(2)}) collective-permute-start(f32[96,768]{1,0:T(8,128)} %get-tuple-element.94), channel_id=1, source_target_pairs={{0,1},{1,0},{2,3},{3,2},{4,5},{5,4},{6,7},{7,6},{8,9},{9,8},{10,11... | collective-permute-start | bytes 884744 | tf_op jit(solution)/shard_map/ppermute | solution.py:65
  50.3 120.8 %copy-start.79 = (f32[768]{0:T(1024)}, f32[768]{0:T(1024)S(1)}, u32[]{:S(2)}) copy-start(f32[768]{0:T(1024)S(1)} %get-tuple-element.284) | copy-start | bytes 9220
  89.0 62.4 %copy-start.82 = (f32[256]{0:T(256)}, f32[256]{0:T(256)S(1)}, u32[]{:S(2)}) copy-start(f32[256]{0:T(256)S(1)} %broadcast_multiply_fusion.11) | copy-start | bytes 3076
  89.3 62.2 %copy-start.84 = (f32[256]{0:T(256)}, f32[256]{0:T(256)S(1)}, u32[]{:S(2)}) copy-start(f32[256]{0:T(256)S(1)} %add_rsqrt_fusion.2) | copy-start | bytes 3076
  91.1 202.4 %reduce-scatter.3.cloned.1.call-start = ((), (), s32[]{:S(2)}) async-start(), calls=%async_computation.2 | async-start | bytes 10027008 | tf_op jit(solution)/shard_map/reduce_scatter | solution.py:595
  91.2 21.6 %collective-permute-start.4 = (f32[256,768]{1,0:T(8,128)}, f32[256,768]{1,0:T(8,128)}, u32[]{:S(2)}, u32[]{:S(2)}) collective-permute-start(f32[256,768]{1,0:T(8,128)} %fusion.62), channel_id=1, source_target_pairs={{0,1},{1,0},{2,3},{3,2},{4,5},{5,4},{6,7},{7,6},{8,9},{9,8},{10,11... | collective-permute-start | bytes 2359304 | tf_op jit(solution)/shard_map/ppermute | solution.py:65
  130.3 21.2 %collective-permute-start.5 = (f32[256,768]{1,0:T(8,128)}, f32[256,768]{1,0:T(8,128)}, u32[]{:S(2)}, u32[]{:S(2)}) collective-permute-start(f32[256,768]{1,0:T(8,128)} %constant_dynamic-slice_fusion.1), channel_id=1, source_target_pairs={{0,1},{1,0},{2,3},{3,2},{4,5},{5,4},{6,7},{7,6},{8,9},{9,8},{10,11... | collective-permute-start | bytes 2359304 | tf_op jit(solution)/shard_map/ppermute | solution.py:65
  170.2 15.1 %collective-permute-start.6 = (f32[1536,1536]{1,0:T(8,128)}, f32[1536,1536]{1,0:T(8,128)}, u32[]{:S(2)}, u32[]{:S(2)}) collective-permute-start(f32[1536,1536]{1,0:T(8,128)} %feed_sums.4), channel_id=1, source_target_pairs={{0,2},{2,0},{1,3},{3,1},{4,6},{6,4},{5,7},{7,5},{8,10},{10,8},{9,1... | collective-permute-start | bytes 28311560 | tf_op jit(solution)/shard_map/ppermute | solution.py:65
  176.6 21.1 %collective-permute-start.7 = (f32[256,768]{1,0:T(8,128)}, f32[256,768]{1,0:T(8,128)}, u32[]{:S(2)}, u32[]{:S(2)}) collective-permute-start(f32[256,768]{1,0:T(8,128)} %get-tuple-element.205), channel_id=1, source_target_pairs={{0,1},{1,0},{2,3},{3,2},{4,5},{5,4},{6,7},{7,6},{8,9},{9,8},{10,11... | collective-permute-start | bytes 2359304 | tf_op jit(solution)/shard_map/ppermute | solution.py:65
  197.8 208.7 %reduce-scatter.5.cloned.1.call-start = ((), (), s32[]{:S(2)}) async-start(), calls=%async_computation.3 | async-start | bytes 10027008 | tf_op jit(solution)/shard_map/reduce_scatter | solution.py:610
  215.2 20.0 %collective-permute-start.8 = (f32[256,768]{1,0:T(8,128)S(1)}, f32[256,768]{1,0:T(8,128)S(1)}, u32[]{:S(2)}, u32[]{:S(2)}) collective-permute-start(f32[256,768]{1,0:T(8,128)S(1)} %constant_dynamic-slice_fusion), channel_id=1, source_target_pairs={{0,1},{1,0},{2,3},{3,2},{4,5},{5,4},{6,7},{7,6},{8,9},{9,8},{10,11... | collective-permute-start | bytes 2359304 | tf_op jit(solution)/shard_map/ppermute | solution.py:65
  247.5 15.0 %collective-permute-start.10 = (f32[1536,1536]{1,0:T(8,128)}, f32[1536,1536]{1,0:T(8,128)}, u32[]{:S(2)}, u32[]{:S(2)}) collective-permute-start(f32[1536,1536]{1,0:T(8,128)} %feed_sums.6), channel_id=1, source_target_pairs={{0,2},{2,0},{1,3},{3,1},{4,6},{6,4},{5,7},{7,5},{8,10},{10,8},{9,1... | collective-permute-start | bytes 28311560 | tf_op jit(solution)/shard_map/ppermute | solution.py:65
  253.2 21.8 %collective-permute-start.11 = (f32[256,768]{1,0:T(8,128)}, f32[256,768]{1,0:T(8,128)}, u32[]{:S(2)}, u32[]{:S(2)}) collective-permute-start(f32[256,768]{1,0:T(8,128)} %multiply_multiply_fusion.4), channel_id=1, source_target_pairs={{0,1},{1,0},{2,3},{3,2},{4,5},{5,4},{6,7},{7,6},{8,9},{9,8},{10,11... | collective-permute-start | bytes 2359304 | tf_op jit(solution)/shard_map/ppermute | solution.py:65
  293.5 232.7 %all-gather.11.cloned.1.call-start = ((), (), s32[]{:S(2)}) async-start(), calls=%async_computation.6 | async-start | bytes 29196288 | tf_op jit(solution)/shard_map/all_gather | solution.py:624
  300.6 4.9 collective-permute-start.18
  303.8 9.6 %collective-permute-start.17 = (f32[1536,384]{1,0:T(8,128)}, f32[1536,384]{1,0:T(8,128)}, u32[]{:S(2)}, u32[]{:S(2)}) collective-permute-start(f32[1536,384]{1,0:T(8,128)} %attention_sums.4), channel_id=1, source_target_pairs={{0,2},{2,0},{1,3},{3,1},{4,6},{6,4},{5,7},{7,5},{8,10},{10,8},{9,1... | collective-permute-start | bytes 7077896 | tf_op jit(solution)/shard_map/ppermute | solution.py:65
  322.5 24.0 %collective-permute-start.24 = (f32[4,48,768]{2,1,0:T(8,128)}, f32[4,48,768]{2,1,0:T(8,128)}, u32[]{:S(2)}, u32[]{:S(2)}) collective-permute-start(f32[4,48,768]{2,1,0:T(8,128)} %get-tuple-element.214), channel_id=1, source_target_pairs={{0,64},{32,96},{64,0},{96,32},{1,65},{33,97},{65,1},{97,33},{2,66}... | collective-permute-start | bytes 1769480 | tf_op jit(solution)/shard_map/ppermute | solution.py:83
  325.3 41.4 %collective-permute-start.23 = (f32[4,48,768]{2,1,0:T(8,128)}, f32[4,48,768]{2,1,0:T(8,128)S(1)}, u32[]{:S(2)}, u32[]{:S(2)}) collective-permute-start(f32[4,48,768]{2,1,0:T(8,128)} %get-tuple-element.215), channel_id=1, source_target_pairs={{0,96},{32,0},{64,32},{96,64},{1,97},{33,1},{65,33},{97,65},{2,98}... | collective-permute-start | bytes 1769480 | tf_op jit(solution)/shard_map/ppermute | solution.py:83
  326.5 40.3 %collective-permute-start.22 = (f32[4,48,768]{2,1,0:T(8,128)}, f32[4,48,768]{2,1,0:T(8,128)S(1)}, u32[]{:S(2)}, u32[]{:S(2)}) collective-permute-start(f32[4,48,768]{2,1,0:T(8,128)} %get-tuple-element.216), channel_id=1, source_target_pairs={{0,32},{32,64},{64,96},{96,0},{1,33},{33,65},{65,97},{97,1},{2,34}... | collective-permute-start | bytes 1769480 | tf_op jit(solution)/shard_map/ppermute | solution.py:83
  327.5 39.3 %collective-permute-start.21 = (f32[4,48,768]{2,1,0:T(8,128)S(1)}, f32[4,48,768]{2,1,0:T(8,128)S(1)}, u32[]{:S(2)}, u32[]{:S(2)}) collective-permute-start(f32[4,48,768]{2,1,0:T(8,128)S(1)} %get-tuple-element.218), channel_id=1, source_target_pairs={{0,8},{4,12},{8,0},{12,4},{1,9},{5,13},{9,1},{13,5},{2,10},{6,14},... | collective-permute-start | bytes 1769480 | tf_op jit(solution)/shard_map/ppermute | solution.py:83
  329.1 39.8 %collective-permute-start.20 = (f32[4,48,768]{2,1,0:T(8,128)S(1)}, f32[4,48,768]{2,1,0:T(8,128)S(1)}, u32[]{:S(2)}, u32[]{:S(2)}) collective-permute-start(f32[4,48,768]{2,1,0:T(8,128)S(1)} %get-tuple-element.219), channel_id=1, source_target_pairs={{0,12},{4,0},{8,4},{12,8},{1,13},{5,1},{9,5},{13,9},{2,14},{6,2},{... | collective-permute-start | bytes 1769480 | tf_op jit(solution)/shard_map/ppermute | solution.py:83
  346.5 27.9 %collective-permute-start.19 = (f32[4,48,768]{2,1,0:T(8,128)S(1)}, f32[4,48,768]{2,1,0:T(8,128)S(1)}, u32[]{:S(2)}, u32[]{:S(2)}) collective-permute-start(f32[4,48,768]{2,1,0:T(8,128)S(1)} %get-tuple-element.220), channel_id=1, source_target_pairs={{0,4},{4,8},{8,12},{12,0},{1,5},{5,9},{9,13},{13,1},{2,6},{6,10},{... | collective-permute-start | bytes 1769480 | tf_op jit(solution)/shard_map/ppermute | solution.py:83
  374.6 7.5 %collective-permute-start.27 = (f32[48,768]{1,0:T(8,128)S(1)}, f32[48,768]{1,0:T(8,128)S(1)}, u32[]{:S(2)}, u32[]{:S(2)}) collective-permute-start(f32[48,768]{1,0:T(8,128)S(1)} %get-tuple-element.236), channel_id=1, source_target_pairs={{0,64},{32,96},{64,0},{96,32},{1,65},{33,97},{65,1},{97,33},{2,66}... | collective-permute-start | bytes 442376 | tf_op jit(solution)/shard_map/ppermute | solution.py:83
  377.7 6.0 %collective-permute-start.26 = (f32[48,768]{1,0:T(8,128)S(1)}, f32[48,768]{1,0:T(8,128)S(1)}, u32[]{:S(2)}, u32[]{:S(2)}) collective-permute-start(f32[48,768]{1,0:T(8,128)S(1)} %get-tuple-element.237), channel_id=1, source_target_pairs={{0,96},{32,0},{64,32},{96,64},{1,97},{33,1},{65,33},{97,65},{2,98}... | collective-permute-start | bytes 442376 | tf_op jit(solution)/shard_map/ppermute | solution.py:83
  378.3 8.0 %collective-permute-start.25 = (f32[48,768]{1,0:T(8,128)S(1)}, f32[48,768]{1,0:T(8,128)S(1)}, u32[]{:S(2)}, u32[]{:S(2)}) collective-permute-start(f32[48,768]{1,0:T(8,128)S(1)} %get-tuple-element.238), channel_id=1, source_target_pairs={{0,32},{32,64},{64,96},{96,0},{1,33},{33,65},{65,97},{97,1},{2,34}... | collective-permute-start | bytes 442376 | tf_op jit(solution)/shard_map/ppermute | solution.py:83
  381.0 7.2 %collective-permute-start.30 = (f32[48,768]{1,0:T(8,128)S(1)}, f32[48,768]{1,0:T(8,128)S(1)}, u32[]{:S(2)}, u32[]{:S(2)}) collective-permute-start(f32[48,768]{1,0:T(8,128)S(1)} %get-tuple-element.232), channel_id=1, source_target_pairs={{0,8},{4,12},{8,0},{12,4},{1,9},{5,13},{9,1},{13,5},{2,10},{6,14},... | collective-permute-start | bytes 442376 | tf_op jit(solution)/shard_map/ppermute | solution.py:83
  381.6 7.7 %collective-permute-start.29 = (f32[48,768]{1,0:T(8,128)S(1)}, f32[48,768]{1,0:T(8,128)S(1)}, u32[]{:S(2)}, u32[]{:S(2)}) collective-permute-start(f32[48,768]{1,0:T(8,128)S(1)} %get-tuple-element.233), channel_id=1, source_target_pairs={{0,12},{4,0},{8,4},{12,8},{1,13},{5,1},{9,5},{13,9},{2,14},{6,2},{... | collective-permute-start | bytes 442376 | tf_op jit(solution)/shard_map/ppermute | solution.py:83
  382.2 7.1 %collective-permute-start.28 = (f32[48,768]{1,0:T(8,128)S(1)}, f32[48,768]{1,0:T(8,128)S(1)}, u32[]{:S(2)}, u32[]{:S(2)}) collective-permute-start(f32[48,768]{1,0:T(8,128)S(1)} %get-tuple-element.234), channel_id=1, source_target_pairs={{0,4},{4,8},{8,12},{12,0},{1,5},{5,9},{9,13},{13,1},{2,6},{6,10},{... | collective-permute-start | bytes 442376 | tf_op jit(solution)/shard_map/ppermute | solution.py:83
  383.7 18.8 %collective-permute-start.16 = (f32[96,768]{1,0:T(8,128)S(1)}, f32[96,768]{1,0:T(8,128)S(1)}, u32[]{:S(2)}, u32[]{:S(2)}) collective-permute-start(f32[96,768]{1,0:T(8,128)S(1)} %get-tuple-element.241), channel_id=1, source_target_pairs={{0,17},{17,0},{1,16},{16,1},{2,19},{19,2},{3,18},{18,3},{4,21},{21... | collective-permute-start | bytes 884744 | tf_op jit(solution)/shard_map/ppermute | solution.py:617
  386.3 16.2 %collective-permute-start.15 = (f32[96,768]{1,0:T(8,128)S(1)}, f32[96,768]{1,0:T(8,128)S(1)}, u32[]{:S(2)}, u32[]{:S(2)}) collective-permute-start(f32[96,768]{1,0:T(8,128)S(1)} %get-tuple-element.241), channel_id=1, source_target_pairs={{0,1},{1,0},{2,3},{3,2},{4,5},{5,4},{6,7},{7,6},{8,9},{9,8},{10,11... | collective-permute-start | bytes 884744 | tf_op jit(solution)/shard_map/ppermute | solution.py:65
  388.2 14.2 %collective-permute-start.14 = (f32[96,768]{1,0:T(8,128)S(1)}, f32[96,768]{1,0:T(8,128)S(1)}, u32[]{:S(2)}, u32[]{:S(2)}) collective-permute-start(f32[96,768]{1,0:T(8,128)S(1)} %get-tuple-element.240), channel_id=1, source_target_pairs={{0,16},{16,0},{1,17},{17,1},{2,18},{18,2},{3,19},{19,3},{4,20},{20... | collective-permute-start | bytes 884744 | tf_op jit(solution)/shard_map/ppermute | solution.py:65
  389.4 17.0 %collective-permute-start.31 = (f32[96,768]{1,0:T(8,128)S(1)}, f32[96,768]{1,0:T(8,128)S(1)}, u32[]{:S(2)}, u32[]{:S(2)}) collective-permute-start(f32[96,768]{1,0:T(8,128)S(1)} %pad_maximum_fusion.1), channel_id=1, source_target_pairs={{0,16},{16,0},{1,17},{17,1},{2,18},{18,2},{3,19},{19,3},{4,20},{20... | collective-permute-start | bytes 884744 | tf_op jit(solution)/shard_map/ppermute | solution.py:65
  407.6 10.5 %collective-permute-start.32 = (f32[96,768]{1,0:T(8,128)S(1)}, f32[96,768]{1,0:T(8,128)S(1)}, u32[]{:S(2)}, u32[]{:S(2)}) collective-permute-start(f32[96,768]{1,0:T(8,128)S(1)} %get-tuple-element.230), channel_id=1, source_target_pairs={{0,16},{16,0},{1,17},{17,1},{2,18},{18,2},{3,19},{19,3},{4,20},{20... | collective-permute-start | bytes 884744 | tf_op jit(solution)/shard_map/ppermute | solution.py:65
  410.1 14.4 %collective-permute-start.34 = (f32[96,768]{1,0:T(8,128)S(1)}, f32[96,768]{1,0:T(8,128)S(1)}, u32[]{:S(2)}, u32[]{:S(2)}) collective-permute-start(f32[96,768]{1,0:T(8,128)S(1)} %get-tuple-element.231), channel_id=1, source_target_pairs={{0,17},{17,0},{1,16},{16,1},{2,19},{19,2},{3,18},{18,3},{4,21},{21... | collective-permute-start | bytes 884744 | tf_op jit(solution)/shard_map/ppermute | solution.py:617
  410.7 13.8 %collective-permute-start.33 = (f32[96,768]{1,0:T(8,128)S(1)}, f32[96,768]{1,0:T(8,128)S(1)}, u32[]{:S(2)}, u32[]{:S(2)}) collective-permute-start(f32[96,768]{1,0:T(8,128)S(1)} %get-tuple-element.231), channel_id=1, source_target_pairs={{0,1},{1,0},{2,3},{3,2},{4,5},{5,4},{6,7},{7,6},{8,9},{9,8},{10,11... | collective-permute-start | bytes 884744 | tf_op jit(solution)/shard_map/ppermute | solution.py:65
  426.6 40.3 %copy-start.90 = (f32[768]{0:T(1024)S(1)}, f32[768]{0:T(1024)}, u32[]{:S(2)}) copy-start(f32[768]{0:T(1024)} %get-tuple-element.169) | copy-start | bytes 9220
  426.6 40.3 %copy-start.91 = (f32[768]{0:T(1024)S(1)}, f32[768]{0:T(1024)}, u32[]{:S(2)}) copy-start(f32[768]{0:T(1024)} %get-tuple-element.199) | copy-start | bytes 9220
  426.6 40.3 %copy-start.108 = (f32[1536]{0:T(1024)S(1)}, f32[1536]{0:T(1024)}, u32[]{:S(2)}) copy-start(f32[1536]{0:T(1024)} %get-tuple-element.273) | copy-start | bytes 18436
  426.6 40.3 %copy-start.107 = (f32[1536]{0:T(1024)S(1)}, f32[1536]{0:T(1024)}, u32[]{:S(2)}) copy-start(f32[1536]{0:T(1024)} %get-tuple-element.277) | copy-start | bytes 18436
  426.6 40.3 %copy-start.115 = (f32[768]{0:T(1024)S(1)}, f32[768]{0:T(1024)}, u32[]{:S(2)}) copy-start(f32[768]{0:T(1024)} %get-tuple-element.165) | copy-start | bytes 9220
  426.6 40.3 %copy-start.114 = (f32[768]{0:T(1024)S(1)}, f32[768]{0:T(1024)}, u32[]{:S(2)}) copy-start(f32[768]{0:T(1024)} %get-tuple-element.177) | copy-start | bytes 9220
  426.6 40.4 %copy-start.96 = (f32[768]{0:T(1024)S(1)}, f32[768]{0:T(1024)}, u32[]{:S(2)}) copy-start(f32[768]{0:T(1024)} %get-tuple-element.167) | copy-start | bytes 9220
  426.6 40.4 %copy-start.110 = (f32[1536]{0:T(1024)S(1)}, f32[1536]{0:T(1024)}, u32[]{:S(2)}) copy-start(f32[1536]{0:T(1024)} %get-tuple-element.275) | copy-start | bytes 18436
  426.7 40.4 %copy-start.93 = (f32[768]{0:T(1024)S(1)}, f32[768]{0:T(1024)}, u32[]{:S(2)}) copy-start(f32[768]{0:T(1024)} %get-tuple-element.201) | copy-start | bytes 9220
  426.7 40.4 %copy-start.95 = (f32[768]{0:T(1024)S(1)}, f32[768]{0:T(1024)}, u32[]{:S(2)}) copy-start(f32[768]{0:T(1024)} %get-tuple-element.178) | copy-start | bytes 9220
  426.7 40.4 %copy-start.117 = (f32[768]{0:T(1024)S(1)}, f32[768]{0:T(1024)}, u32[]{:S(2)}) copy-start(f32[768]{0:T(1024)} %get-tuple-element.164) | copy-start | bytes 9220
  426.7 40.4 %copy-start.116 = (f32[768]{0:T(1024)S(1)}, f32[768]{0:T(1024)}, u32[]{:S(2)}) copy-start(f32[768]{0:T(1024)} %get-tuple-element.176) | copy-start | bytes 9220
  426.7 43.4 %copy-start.92 = (f32[768]{0:T(1024)S(1)}, f32[768]{0:T(1024)}, u32[]{:S(2)}) copy-start(f32[768]{0:T(1024)} %get-tuple-element.195) | copy-start | bytes 9220
  426.7 43.4 %copy-start.109 = (f32[1536]{0:T(1024)S(1)}, f32[1536]{0:T(1024)}, u32[]{:S(2)}) copy-start(f32[1536]{0:T(1024)} %get-tuple-element.271) | copy-start | bytes 18436
  426.7 59.3 %copy-start.94 = (f32[768]{0:T(1024)S(1)}, f32[768]{0:T(1024)}, u32[]{:S(2)}) copy-start(f32[768]{0:T(1024)} %get-tuple-element.197) | copy-start | bytes 9220
  426.7 36.5 %collective-permute-start.12 = (f32[512,768]{1,0:T(8,128)}, f32[512,768]{1,0:T(8,128)S(1)}, u32[]{:S(2)}, u32[]{:S(2)}) collective-permute-start(f32[512,768]{1,0:T(8,128)} %get-tuple-element.118), channel_id=1, source_target_pairs={{0,1},{1,0},{2,3},{3,2},{4,5},{5,4},{6,7},{7,6},{8,9},{9,8},{10,11... | collective-permute-start | bytes 4718600 | tf_op jit(solution)/shard_map/ppermute | solution.py:65
  466.0 20.1 %collective-permute-start.13 = (f32[256,768]{1,0:T(8,128)S(1)}, f32[256,768]{1,0:T(8,128)S(1)}, u32[]{:S(2)}, u32[]{:S(2)}) collective-permute-start(f32[256,768]{1,0:T(8,128)S(1)} %copy-done.71), channel_id=1, source_target_pairs={{0,1},{1,0},{2,3},{3,2},{4,5},{5,4},{6,7},{7,6},{8,9},{9,8},{10,11... | collective-permute-start | bytes 2359304 | tf_op jit(solution)/shard_map/ppermute | solution.py:65
  467.2 18.8 %collective-permute-start.9 = (f32[14,768]{1,0:T(8,128)S(1)}, f32[14,768]{1,0:T(8,128)S(1)}, u32[]{:S(2)}, u32[]{:S(2)}) collective-permute-start(f32[14,768]{1,0:T(8,128)S(1)} %concatenate.38), channel_id=1, source_target_pairs={{0,1},{1,0},{2,3},{3,2},{4,5},{5,4},{6,7},{7,6},{8,9},{9,8},{10,11... | collective-permute-start | bytes 129032 | tf_op jit(solution)/shard_map/ppermute | solution.py:65
  487.9 1.3 collective-permute-start.35
  489.1 6.5 %collective-permute-start.36 = (f32[18,768]{1,0:T(8,128)S(1)}, f32[18,768]{1,0:T(8,128)S(1)}, u32[]{:S(2)}, u32[]{:S(2)}) collective-permute-start(f32[18,768]{1,0:T(8,128)S(1)} %add.537), channel_id=1, source_target_pairs={{0,4},{4,0},{8,12},{12,8},{1,5},{5,1},{9,13},{13,9},{2,6},{6,2},{1... | collective-permute-start | bytes 165896 | tf_op jit(solution)/shard_map/ppermute | solution.py:638
  495.6 7.5 %collective-permute-start.37 = (f32[18,768]{1,0:T(8,128)S(1)}, f32[18,768]{1,0:T(8,128)S(1)}, u32[]{:S(2)}, u32[]{:S(2)}) collective-permute-start(f32[18,768]{1,0:T(8,128)S(1)} %add.538), channel_id=1, source_target_pairs={{4,8},{8,4},{12,0},{0,12},{5,9},{9,5},{13,1},{1,13},{6,10},{10,6},... | collective-permute-start | bytes 165896 | tf_op jit(solution)/shard_map/ppermute | solution.py:638
  503.1 6.0 %collective-permute-start.38 = (f32[18,768]{1,0:T(8,128)S(1)}, f32[18,768]{1,0:T(8,128)S(1)}, u32[]{:S(2)}, u32[]{:S(2)}) collective-permute-start(f32[18,768]{1,0:T(8,128)S(1)} %add.539), channel_id=1, source_target_pairs={{0,32},{32,0},{64,96},{96,64},{1,33},{33,1},{65,97},{97,65},{2,34}... | collective-permute-start | bytes 165896 | tf_op jit(solution)/shard_map/ppermute | solution.py:638
  509.1 7.2 %collective-permute-start.39 = (f32[18,768]{1,0:T(8,128)S(1)}, f32[18,768]{1,0:T(8,128)S(1)}, u32[]{:S(2)}, u32[]{:S(2)}) collective-permute-start(f32[18,768]{1,0:T(8,128)S(1)} %add.540), channel_id=1, source_target_pairs={{32,64},{64,32},{96,0},{0,96},{33,65},{65,33},{97,1},{1,97},{34,66... | collective-permute-start | bytes 165896 | tf_op jit(solution)/shard_map/ppermute | solution.py:638
  516.3 4.4 collective-permute-start.40
  (109 other events, 899.4 us)
Sparse Core Ops, SparseCore 0:
  23.9 57.0 all-gather.6
  91.2 54.9 all-gather.8
  197.9 86.9 reduce-scatter.2
  293.7 109.6 reduce-scatter.4
  426.7 97.5 all-gather.10

commit v4 on v3

--- a/solution.py
+++ b/solution.py
@@ -299,45 +299,44 @@
     )(jnp.stack([chip, core]), down_weight, up_weight)
 
 
-def feed_sums_kernel(received, part_ref, act_own, act_peer, pre_own, pre_peer, ffn_low, hidden_low, *refs):
+def feed_sums_kernel(received, part_ref, active, pre_low, ffn_low, hidden_low, *refs):
     out_ref = refs[-1]
-    width = ffn_low.shape[1]
-
-    def write(own, peer, right):
-        for k, left in enumerate((own, peer)):
-            total = t_dot_in_kernel(left[...], right[...])
-            cut = slice(k * width, (k + 1) * width)
-            out_ref[:, cut] = total + refs[0][:, cut] if received else total
+
+    def write(left, right):
+        total = t_dot_in_kernel(left[...], right[...])
+        out_ref[...] = total + refs[0][...] if received else total
 
     @pl.when(part_ref[0] == 0)
     def _():
-        write(act_own, act_peer, ffn_low)
+        write(active, ffn_low)
 
     @pl.when(part_ref[0] != 0)
     def _():
-        write(pre_own, pre_peer, hidden_low)
-
-
-def feed_sums(part, actives, pre_lows, ffn_low, hidden_low, columns, received=None):
-    slots, units = actives[0].shape
+        write(pre_low, hidden_low)
+
+
+def feed_sums(part, active, pre_low, ffn_low, hidden_low, received=None, columns=None, into=None):
+    slots, units = active.shape
     width = ffn_low.shape[1]
     block = units // 4
     left = pl.BlockSpec((slots, block), lambda i: (0, i))
     right = pl.BlockSpec((slots, width), lambda i: (0, 0))
-    rows = pl.BlockSpec((block, 2 * width), lambda i: (i, 0))
-    more = [] if received is None else [received]
+    rows = pl.BlockSpec((block, width), lambda i: (i, 0))
+    more = [item for item in (received, into) if item is not None]
+    place = 0 if into is None else 1
     return pl.pallas_call(
-        lambda *refs: feed_sums_kernel(bool(more), *refs),
+        lambda *refs: feed_sums_kernel(received is not None, *refs),
         grid=(4,),
-        in_specs=[SCALAR] + [left] * 4 + [right] * 2 + [rows] * len(more),
-        out_specs=rows,
-        out_shape=jax.ShapeDtypeStruct((units, columns), F32),
+        in_specs=[SCALAR] + [left] * 2 + [right] * 2 + [rows, pl.BlockSpec(memory_space=pl.ANY)][: len(more)],
+        out_specs=pl.BlockSpec((block, width), lambda i: (i, place)),
+        out_shape=jax.ShapeDtypeStruct((units, width if columns is None else columns), F32),
+        input_output_aliases={6: 0} if place else {},
         compiler_params=LIMIT,
         cost_estimate=pl.CostEstimate(
-            flops=4 * slots * units * width, bytes_accessed=(8 + 8 * len(more)) * units * width, transcendentals=0
+            flops=2 * slots * units * width, bytes_accessed=(8 if more else 4) * units * width, transcendentals=0
         ),
         name="feed_sums",
-    )(part.reshape(1), *actives, *pre_lows, ffn_low, hidden_low, *more)
+    )(part.reshape(1), active, pre_low, ffn_low, hidden_low, *more)
 
 
 def attention_sums_kernel(received, part_ref, query_ref, key_ref, value_ref, mixture_ref, slot_ref, grad_ref, *refs):
@@ -356,22 +355,21 @@
     write(3, mixture_ref, grad_ref)
 
 
-def attention_sums(part, lows, mixture, rounded, attended_low, received=None, columns=None, into=None):
+def attention_sums(part, lows, mixture, rounded, attended_low, received=None, into=None, place=0):
     slots, heads = mixture.shape
     half = rounded.shape[1] // 2
     left = pl.BlockSpec((slots, heads), lambda i: (0, 0))
     right = pl.BlockSpec((slots, half), lambda i: (0, i // 2))
     rows = pl.BlockSpec((heads, half), lambda i: (i, 0))
     more = [item for item in (received, into) if item is not None]
-    place = 0 if into is None else 1
-    shape = (4 * heads, half if columns is None else columns)
+    shape = (4 * heads, half) if into is None else into.shape
     return pl.pallas_call(
         lambda *refs: attention_sums_kernel(received is not None, *refs),
         grid=(4,),
         in_specs=[SCALAR] + [left] * 4 + [right] * 2 + [rows, pl.BlockSpec(memory_space=pl.ANY)][: len(more)],
         out_specs=pl.BlockSpec((heads, half), lambda i: (i, place)),
         out_shape=jax.ShapeDtypeStruct(shape, F32),
-        input_output_aliases={8: 0} if place else {},
+        input_output_aliases={} if into is None else {8: 0},
         compiler_params=LIMIT,
         cost_estimate=pl.CostEstimate(flops=8 * slots * heads * half, bytes_accessed=16 * heads * half, transcendentals=0),
         name="attention_sums",
@@ -508,6 +506,15 @@
     def own_slots(values):
         return piece(values, side, half_slots)
 
+    def feed_weights_back(saved, pre_lows, ffn_low, columns):
+        actives, hidden_low = saved[3], saved[4]
+        received = [
+            swap(feed_sums(1 - core, active, pre_low, ffn_low, hidden_low), "c")
+            for active, pre_low in zip(actives, pre_lows, strict=True)
+        ]
+        total = feed_sums(core, actives[0], pre_lows[0], ffn_low, hidden_low, received[0], columns)
+        return feed_sums(core, actives[1], pre_lows[1], ffn_low, hidden_low, received[1], columns, total)
+
     def attention_forward(layer, rounded):
         *attention, share = attend(
             layer,
@@ -589,8 +596,7 @@
     grad_one_own, ffn_low, pre_lows, shared2, biases2 = feed_back(1, gradient2, saved2)
     sent = 0.5 * grad_one_own
     received = swap(sent, "h")
-    feed2_received = swap(feed_sums(1 - core, saved2[3], pre_lows, ffn_low, saved2[4], 2 * width), "c")
-    feed2 = feed_sums(core, saved2[3], pre_lows, ffn_low, saved2[4], 2 * width, feed2_received)
+    feed2 = feed_weights_back(saved2, pre_lows, ffn_low, 2 * width)
     feed2, received = together(feed2, received)
     feed2 = lax.psum_scatter(feed2, PLANE, tiled=True)
     _, lows2, attended_low2, share, small_att2 = attention_back(1, att2, sent, received)
@@ -601,26 +607,25 @@
     grad_one_own1, ffn_low, pre_lows, shared1, biases1 = feed_back(0, gradient1, saved1)
     sent = 0.5 * grad_one_own1
     received = swap(sent, "h")
-    feed1_received = swap(feed_sums(1 - core, saved1[3], pre_lows, ffn_low, saved1[4], 2 * width), "c")
-    rest = feed_sums(core, saved1[3], pre_lows, ffn_low, saved1[4], 2 * width, feed1_received)
-    rest, received = together(rest, received)
+    rest = feed_weights_back(saved1, pre_lows, ffn_low, 2 * width + columns)
+    rest = attention_sums(core, lows2, mixture, x2_low, attended_low2, attn2_received, rest, 2 * width // columns)
+    rest, received, feed2 = together(rest, received, feed2)
+    rest = lax.psum_scatter(rest, PLANE, tiled=True)
     grad_one1, lows1, attended_low1, share, small_att1 = attention_back(0, att1, sent, received)
-    attn = attention_sums(core, lows2, mixture, x2_low, attended_low2, attn2_received, width)
-    rest, feed2, *lows1 = together(rest, feed2, *lows1)
-    rest = lax.psum_scatter(rest, PLANE, tiled=True)
     attn1_received = swap(attention_sums(1 - core, lows1, att1[3], tokens, attended_low1), "c")
-    attn = attention_sums(core, lows1, att1[3], tokens, attended_low1, attn1_received, width, attn)
-    attn = plane_sum(attn)
-
-    def across(values):
-        own, peer = values[:, :width], values[:, width:]
+    attn1 = plane_sum(attention_sums(core, lows1, att1[3], tokens, attended_low1, attn1_received))
+
+    def across(own, peer):
         diagonal = lax.ppermute(peer, ("zl", "h"), ((0, 3), (3, 0), (1, 2), (2, 1)))
-        return own + swap(own, "zl") + (swap(peer, "h") + diagonal)
-
-    feed2 = across(feed2)
-    attn = attn + swap(attn, "zl")
-    feed2, attn, rest = together(feed2, attn, rest)
-    own = jnp.concatenate([feed2, across(rest), attn], axis=1)
+        own = own + swap(own, "zl")
+        peer = swap(peer, "h") + diagonal
+        return jnp.concatenate([own[:, :width] + peer, own[:, width:]], axis=1)
+
+    feed2 = across(feed2[:, :width], feed2[:, width:])
+    attn1 = attn1 + swap(attn1, "zl")
+    feed2, attn1, rest = together(feed2, attn1, rest)
+    rest = across(jnp.concatenate([rest[:, :width], rest[:, 2 * width :]], axis=1), rest[:, width : 2 * width])
+    own = jnp.concatenate([feed2, rest, attn1], axis=1)
     gathered = lax.all_gather(own, PLANE + ("c",)).reshape(16, 2, *own.shape)
     grad_query, grad_key, grad_value, grad_output, grad_up, grad_down = place_gradients(gathered, width)
 

time: 566 us -> 563 us (level)
  local copies, waits for them, and re-layouts: 46.3 us -> 35.7 us
  Pallas kernels: 121 us -> 127 us
    reduce_scatter x1, waiting for transfers between devices: 0.02 us -> 22 us  [local(): rest = lax.psum_scatter(rest, PLANE, tiled=True)]
    ppermute x12, waiting for transfers between devices: 43.3 us -> 26.6 us  [ring_parts(): received.append(lax.ppermute(sent, axis, pairs))]
    pallas_call x4 -> x8, Pallas kernels: 26.4 us -> 36 us  [feed_sums(): pl.pallas_call(lambda *refs: feed_sums_kernel(received is not None, *refs...]
    unnamed x262 -> x242, local copies, waits for them, and re-layouts: 32.8 us -> 26.1 us
    ppermute x2, waiting for transfers between devices: 6.44 us -> 0.01 us  [across(): diagonal = lax.ppermute(peer, ('zl', 'h'), ((0, 3), (3, 0), (1, 2), (2, 1)))]
    ppermute x23 -> x25, waiting for transfers between devices: 156 us -> 154 us  [swap(): return lax.ppermute(values, axis, SWAP)]
    ppermute x23 -> x25, starting transfers between devices: 41 us -> 40.1 us  [swap(): return lax.ppermute(values, axis, SWAP)]
  transfers between devices with their start and end apart: 46 -> 48, of which waited for: 30 -> 30; matrix products, arithmetic and copies ran while one was open for 11% -> 10% of each run, Pallas kernels for 16% -> 18%
where the time goes in v4:
time: 563 us; the launch traced here: 553 us
  waiting for transfers between devices  253 us (45%)
  Pallas kernels  127 us (23%)
  starting transfers between devices  61.5 us (11%)
  local copies, waits for them, and re-layouts  35.7 us (6%)
  matrix products  30.5 us (5%)
  other arithmetic  28.6 us (5%)
  between operations  17.1 us (3%)
    ppermute x25, waiting for transfers between devices, swap(): return lax.ppermute(values, axis, SWAP)  154 us
    ppermute x25, starting transfers between devices, swap(): return lax.ppermute(values, axis, SWAP)  40.1 us
    pallas_call x8, Pallas kernels, feed_sums(): pl.pallas_call(lambda *refs: feed_sums_kernel(received is not None, *refs...  36 us
    ppermute x4, waiting for transfers between devices, local(): small = small + lax.ppermute(small, axis, pairs)  26.8 us
    ppermute x12, waiting for transfers between devices, ring_parts(): received.append(lax.ppermute(sent, axis, pairs))  26.6 us
    unnamed x242, local copies, waits for them, and re-layouts  26.1 us
    pallas_call x2, Pallas kernels, attend_back(): pl.pallas_call(attend_back_kernel, grid=(steps,), in_specs=[SCALAR, part,...  24.6 us
    reduce_scatter x1, waiting for transfers between devices, local(): rest = lax.psum_scatter(rest, PLANE, tiled=True)  22 us
  transfers between devices with their start and end apart: 48, of which 30 were waited for; matrix products, arithmetic and copies ran while one was open for 10% of the time, Pallas kernels for 18%

profile of v4, /device:TPU:0, one launch (start us, length us, event | category | flops | bytes accessed | tf_op | source)
XLA Modules:
  0.0 553.2 jit_solution(16517609225522704682)
XLA Ops:
  7.3 2.3 copy-done.1
  12.3 4.0 collective-permute-start.1
  16.3 7.0 %collective-permute-done.1 = f32[96,768]{1,0:T(8,128)S(1)} collective-permute-done((f32[96,768]{1,0:T(8,128)S(1)}, f32[96,768]{1,0:T(8,128)S(1)}, u32[]{:S(2)}, u32[]{:S(2)}) %collective-permute-start.1) | collective-permute-done | bytes 294944 | tf_op jit(solution)/shard_map/ppermute | solution.py:65
  26.1 9.8 %attend.2 = (bf16[512,384]{1,0:T(8,128)(2,1)S(1)}, bf16[512,384]{1,0:T(8,128)(2,1)S(1)}, bf16[512,384]{1,0:T(8,128)(2,1)S(1)}, bf16[512,384]{1,0:T(8,128)(2,1)S(...) custom-call(s32[1]{0:T(128)} %copy.66.length_ref, bf16[512,768]{1,0:T(8,128)(2,1)S(1)} %copy-done, ...), custom_call_target="tpu_custom_call" | custom-call | flops 1610612736 | bytes 5505024 | tf_op jit(solution)/shard_map/attend/pallas_call | solution.py:172
  40.2 3.3 collective-permute-start
  43.9 3.2 collective-permute-start.3
  50.2 12.3 %collective-permute-done.2 = f32[2,1536]{1,0:T(2,128)S(1)} collective-permute-done((f32[2,1536]{1,0:T(2,128)S(1)}, f32[2,1536]{1,0:T(2,128)S(1)}, u32[]{:S(2)}, u32[]{:S(2)}) %collective-permute-start.2) | collective-permute-done | bytes 12320 | tf_op jit(solution)/shard_map/ppermute | solution.py:65
  66.3 3.7 multiply_convert_fusion.3
  70.0 3.5 fusion.11
  73.4 7.8 %all-gather.7.cloned.1.call-done = f32[3072,768]{1,0:T(8,128)} async-done(((f32[96,768]{1,0:T(8,128)}), f32[3072,768]{1,0:T(8,128)}) %all-gather.7.cloned.1.call-update) | async-done | bytes 9437200 | tf_op jit(solution)/shard_map/all_gather | solution.py:503
  81.2 4.4 sort_weights.2
  90.8 3.2 collective-permute-start.4
  94.1 18.4 %collective-permute-done.4 = f32[256,768]{1,0:T(8,128)} collective-permute-done((f32[256,768]{1,0:T(8,128)}, f32[256,768]{1,0:T(8,128)}, u32[]{:S(2)}, u32[]{:S(2)}) %collective-permute-start.4) | collective-permute-done | bytes 786464 | tf_op jit(solution)/shard_map/ppermute | solution.py:65
  115.7 9.8 %attend.3 = (bf16[512,384]{1,0:T(8,128)(2,1)S(1)}, bf16[512,384]{1,0:T(8,128)(2,1)S(1)}, bf16[512,384]{1,0:T(8,128)(2,1)S(1)}, bf16[512,384]{1,0:T(8,128)(2,1)S(...) custom-call(s32[1]{0:T(128)} %copy.66.length_ref, bf16[512,768]{1,0:T(8,128)(2,1)S(1)} %fusion.40.slot_ref.refs_5_, ...), custom_call_target="tpu_custom_call" | custom-call | flops 1610612736 | bytes 5505024 | tf_op jit(solution)/shard_map/attend/pallas_call | solution.py:172
  131.2 3.6 collective-permute-start.5
  136.1 9.8 %all-gather.9.cloned.1.call-done = f32[3072,768]{1,0:T(8,128)} async-done(((f32[96,768]{1,0:T(8,128)}), f32[3072,768]{1,0:T(8,128)}) %all-gather.9.cloned.1.call-update) | async-done | bytes 9437200 | tf_op jit(solution)/shard_map/all_gather | solution.py:583
  145.9 4.8 sort_weights.3
  154.8 2.5 multiply_convert_fusion.1
  166.4 3.3 feed_sums.9
  169.7 3.3 feed_sums.8
  174.3 3.4 multiply_reduce_fusion.2
  179.2 3.1 collective-permute-start.8
  184.5 5.6 %feed_sums.10.refs_6_ = f32[1536,1536]{1,0:T(8,128)} custom-call(s32[1]{0:T(128)} %bitcast.1.refs_0_, bf16[256,1536]{1,0:T(8,128)(2,1)S(1)} %get-tuple-element.257.refs_1_, bf16[256,1536]{1,0:T(8,128)(2,1)S(1)} %get-tuple-element.266.refs_2_, bf16[256,768]{1,0:T(8,128)(2,1)S(1)} %get-tuple-element.192.refs_3_, bf16[256,768]{1,0:T(8,128)(2,1)S(1)} %fusion.63.refs_4_, ...), custom_call_target="tpu_custom_call" | custom-call | flops 603979776 | bytes 9437184 | tf_op jit(solution)/shard_map/feed_sums/pallas_call | solution.py:327
  190.1 5.6 %feed_sums.11 = f32[1536,1536]{1,0:T(8,128)} custom-call(s32[1]{0:T(128)} %bitcast.1.refs_0_, bf16[256,1536]{1,0:T(8,128)(2,1)S(1)} %get-tuple-element.255.refs_1_, bf16[256,1536]{1,0:T(8,128)(2,1)S(1)} %get-tuple-element.270.refs_2_, bf16[256,768]{1,0:T(8,128)(2,1)S(1)} %get-tuple-element.192.refs_3_, ...), custom_call_target="tpu_custom_call", output_to_operand_aliasing={{}: (6, {})} | custom-call | flops 603979776 | bytes 9437184 | tf_op jit(solution)/shard_map/feed_sums/pallas_call | solution.py:327
  195.7 5.0 collective-permute-done.8
  204.3 12.3 %attend_back.2 = (bf16[512,384]{1,0:T(8,128)(2,1)S(1)}, bf16[512,384]{1,0:T(8,128)(2,1)S(1)}, bf16[512,384]{1,0:T(8,128)(2,1)S(1)}, f32[512,768]{1,0:T(8,128)}, ...) custom-call(s32[1]{0:T(128)} %copy.66.length_ref, bf16[512,384]{1,0:T(8,128)(2,1)S(1)} %copy-done.29, ...), custom_call_target="tpu_custom_call" | custom-call | flops 2214592512 | bytes 5505024 | tf_op jit(solution)/shard_map/attend_back/pallas_call | solution.py:250
  218.0 3.2 collective-permute-start.9
  221.2 17.3 %collective-permute-done.9 = f32[256,768]{1,0:T(8,128)S(1)} collective-permute-done((f32[256,768]{1,0:T(8,128)S(1)}, f32[256,768]{1,0:T(8,128)S(1)}, u32[]{:S(2)}, u32[]{:S(2)}) %collective-permute-start.9) | collective-permute-done | bytes 786464 | tf_op jit(solution)/shard_map/ppermute | solution.py:65
  238.5 2.2 multiply_reduce_fusion.3
  244.0 3.4 feed_sums.13
  249.0 3.3 feed_sums.12
  254.9 2.7 fusion.44
  260.4 3.3 collective-permute-start.14
  263.7 5.8 %feed_sums.14.refs_6_ = f32[1536,1920]{1,0:T(8,128)} custom-call(s32[1]{0:T(128)} %bitcast.1.refs_0_, bf16[256,1536]{1,0:T(8,128)(2,1)S(1)} %get-tuple-element.249.refs_1_, bf16[256,1536]{1,0:T(8,128)(2,1)S(1)} %get-tuple-element.264.refs_2_, bf16[256,768]{1,0:T(8,128)(2,1)S(1)} %get-tuple-element.194.refs_3_, bf16[256,768]{1,0:T(8,128)(2,1)S(1)} %fusion.61.refs_4_, ...), custom_call_target="tpu_custom_call" | custom-call | flops 603979776 | bytes 9437184 | tf_op jit(solution)/shard_map/feed_sums/pallas_call | solution.py:327
  269.5 5.7 %feed_sums.15.refs_8_ = f32[1536,1920]{1,0:T(8,128)} custom-call(s32[1]{0:T(128)} %bitcast.1.refs_0_, bf16[256,1536]{1,0:T(8,128)(2,1)S(1)} %get-tuple-element.251.refs_1_, bf16[256,1536]{1,0:T(8,128)(2,1)S(1)} %get-tuple-element.268.refs_2_, bf16[256,768]{1,0:T(8,128)(2,1)S(1)} %get-tuple-element.194.refs_3_, ...), custom_call_target="tpu_custom_call", output_to_operand_aliasing={{}: (6, {})} | custom-call | flops 603979776 | bytes 9437184 | tf_op jit(solution)/shard_map/feed_sums/pallas_call | solution.py:327
  275.2 3.3 attention_sums.5
  278.5 3.8 collective-permute-done.14
  282.3 5.6 %reduce-scatter.3.cloned.1.call-done = f32[96,1536]{1,0:T(8,128)} async-done(((f32[1536,1536]{1,0:T(8,128)}), f32[96,1536]{1,0:T(8,128)}) %reduce-scatter.3.cloned.1.call-update) | async-done | bytes 589840 | tf_op jit(solution)/shard_map/reduce_scatter | solution.py:601
  291.9 12.3 %attend_back.3 = (bf16[512,384]{1,0:T(8,128)(2,1)S(1)}, bf16[512,384]{1,0:T(8,128)(2,1)S(1)}, bf16[512,384]{1,0:T(8,128)(2,1)S(1)}, f32[512,768]{1,0:T(8,128)}, ...) custom-call(s32[1]{0:T(128)} %copy.66.length_ref, bf16[512,384]{1,0:T(8,128)(2,1)S(1)} %copy-done.23, ...), custom_call_target="tpu_custom_call" | custom-call | flops 2214592512 | bytes 5505024 | tf_op jit(solution)/shard_map/attend_back/pallas_call | solution.py:250
  304.1 3.1 attention_sums.6
  307.2 4.9 collective-permute-done.20.refs_7_
  312.1 3.7 attention_sums.7
  316.1 2.7 collective-permute-start.26
  324.0 9.4 %collective-permute-done.26 = f32[4,48,384]{2,1,0:T(8,128)S(1)} collective-permute-done((f32[4,48,384]{2,1,0:T(8,128)S(1)}, f32[4,48,384]{2,1,0:T(8,128)S(1)}, u32[]{:S(2)}, u32[]{:S(2)}) %collective-permute-start.26) | collective-permute-done | bytes 294944 | tf_op jit(solution)/shard_map/ppermute | solution.py:83
  335.3 7.3 %collective-permute-done.25 = f32[4,48,384]{2,1,0:T(8,128)S(1)} collective-permute-done((f32[4,48,384]{2,1,0:T(8,128)S(1)}, f32[4,48,384]{2,1,0:T(8,128)S(1)}, u32[]{:S(2)}, u32[]{:S(2)}) %collective-permute-start.25) | collective-permute-done | bytes 294944 | tf_op jit(solution)/shard_map/ppermute | solution.py:83
  344.0 5.2 collective-permute-done.21
  349.3 2.4 collective-permute-start.29
  358.9 2.8 collective-permute-start.19
  361.7 2.3 collective-permute-start.18
  366.1 8.9 %collective-permute-done.17 = f32[96,768]{1,0:T(8,128)S(1)} collective-permute-done((f32[96,768]{1,0:T(8,128)S(1)}, f32[96,768]{1,0:T(8,128)S(1)}, u32[]{:S(2)}, u32[]{:S(2)}) %collective-permute-start.17) | collective-permute-done | bytes 294944 | tf_op jit(solution)/shard_map/ppermute | solution.py:65
  376.7 22.0 %reduce-scatter.5.cloned.1.call-done = f32[96,1920]{1,0:T(8,128)} async-done(((f32[1536,1920]{1,0:T(8,128)}), f32[96,1920]{1,0:T(8,128)}) %reduce-scatter.5.cloned.1.call-update) | async-done | bytes 737296 | tf_op jit(solution)/shard_map/reduce_scatter | solution.py:613
  405.3 8.7 %collective-permute-done.34 = f32[96,1152]{1,0:T(8,128)S(1)} collective-permute-done((f32[96,1152]{1,0:T(8,128)S(1)}, f32[96,1152]{1,0:T(8,128)S(1)}, u32[]{:S(2)}, u32[]{:S(2)}) %collective-permute-start.34) | collective-permute-done | bytes 442400 | tf_op jit(solution)/shard_map/ppermute | solution.py:65
  414.0 7.2 %collective-permute-done.35 = f32[96,768]{1,0:T(8,128)S(1)} collective-permute-done((f32[96,768]{1,0:T(8,128)S(1)}, f32[96,768]{1,0:T(8,128)S(1)}, u32[]{:S(2)}, u32[]{:S(2)}) %collective-permute-start.35) | collective-permute-done | bytes 294944 | tf_op jit(solution)/shard_map/ppermute | solution.py:65
  423.2 36.0 %collective-permute-done.15 = f32[512,768]{1,0:T(8,128)S(1)} collective-permute-done((f32[512,768]{1,0:T(8,128)}, f32[512,768]{1,0:T(8,128)S(1)}, u32[]{:S(2)}, u32[]{:S(2)}) %collective-permute-start.15) | collective-permute-done | bytes 1572896 | tf_op jit(solution)/shard_map/ppermute | solution.py:65
  459.3 2.9 add_add_fusion
  463.6 2.5 collective-permute-start.10
  466.3 16.0 %collective-permute-done.10 = f32[14,768]{1,0:T(8,128)S(1)} collective-permute-done((f32[14,768]{1,0:T(8,128)S(1)}, f32[14,768]{1,0:T(8,128)S(1)}, u32[]{:S(2)}, u32[]{:S(2)}) %collective-permute-start.10) | collective-permute-done | bytes 43040 | tf_op jit(solution)/shard_map/ppermute | solution.py:65
  485.6 6.4 %collective-permute-done.38 = f32[18,768]{1,0:T(8,128)S(1)} collective-permute-done((f32[18,768]{1,0:T(8,128)S(1)}, f32[18,768]{1,0:T(8,128)S(1)}, u32[]{:S(2)}, u32[]{:S(2)}) %collective-permute-start.38) | collective-permute-done | bytes 55328 | tf_op jit(solution)/shard_map/ppermute | solution.py:643
  492.1 7.4 %collective-permute-done.39 = f32[18,768]{1,0:T(8,128)S(1)} collective-permute-done((f32[18,768]{1,0:T(8,128)S(1)}, f32[18,768]{1,0:T(8,128)S(1)}, u32[]{:S(2)}, u32[]{:S(2)}) %collective-permute-start.39) | collective-permute-done | bytes 55328 | tf_op jit(solution)/shard_map/ppermute | solution.py:643
  499.5 5.9 %collective-permute-done.40 = f32[18,768]{1,0:T(8,128)S(1)} collective-permute-done((f32[18,768]{1,0:T(8,128)S(1)}, f32[18,768]{1,0:T(8,128)S(1)}, u32[]{:S(2)}, u32[]{:S(2)}) %collective-permute-start.40) | collective-permute-done | bytes 55328 | tf_op jit(solution)/shard_map/ppermute | solution.py:643
  505.6 7.1 %collective-permute-done.41 = f32[18,768]{1,0:T(8,128)S(1)} collective-permute-done((f32[18,768]{1,0:T(8,128)S(1)}, f32[18,768]{1,0:T(8,128)S(1)}, u32[]{:S(2)}, u32[]{:S(2)}) %collective-permute-start.41) | collective-permute-done | bytes 55328 | tf_op jit(solution)/shard_map/ppermute | solution.py:643
  513.1 4.0 collective-permute-done.42
  522.6 8.0 %place_attention.1 = (f32[2,768,384]{2,1,0:T(8,128)}, f32[2,768,384]{2,1,0:T(8,128)}, f32[2,768,384]{2,1,0:T(8,128)}, f32[2,384,768]{2,1,0:T(8,128)}) custom-call(f32[16,2,96,2304]{3,2,1,0:T(8,128)} %bitcast.136, f32[16,2,96,2304]{3,2,1,0:T(8,128)} %bitcast.137, f32[16,2,96,2304]{3,2,1,0:T(8,128)} %bitcast.138, f32[16,2,96,2304]{3,2,1,0:T(8,128)} %bitcast.139), custom_call_target="tpu_custom_call" | custom-call | tf_op jit(solution)/shard_map/place_attention/pallas_call | solution.py:458
  530.6 15.6 %place_feed.1 = (f32[2,1536,768]{2,1,0:T(8,128)}, f32[2,768,1536]{2,1,0:T(8,128)}) custom-call(f32[16,2,96,2304]{3,2,1,0:T(8,128)} %bitcast.140, f32[16,2,96,2304]{3,2,1,0:T(8,128)} %bitcast.141), custom_call_target="tpu_custom_call" | custom-call | tf_op jit(solution)/shard_map/place_feed/pallas_call | solution.py:441
  (434 shorter events, 106.5 us)
Async XLA Ops:
  7.2 74.0 %all-gather.7.cloned.1.call-start = ((), (), s32[]{:S(2)}) async-start(), calls=%async_computation.4 | async-start | bytes 9732096 | tf_op jit(solution)/shard_map/all_gather | solution.py:503
  12.3 11.0 %collective-permute-start.1 = (f32[96,768]{1,0:T(8,128)S(1)}, f32[96,768]{1,0:T(8,128)S(1)}, u32[]{:S(2)}, u32[]{:S(2)}) collective-permute-start(f32[96,768]{1,0:T(8,128)S(1)} %get-tuple-element.226), channel_id=1, source_target_pairs={{0,1},{1,0},{2,3},{3,2},{4,5},{5,4},{6,7},{7,6},{8,9},{9,8},{10,11... | collective-permute-start | bytes 884744 | tf_op jit(solution)/shard_map/ppermute | solution.py:65
  24.0 121.8 %all-gather.9.cloned.1.call-start = ((), (), s32[]{:S(2)}) async-start(), calls=%async_computation.5 | async-start | bytes 9732096 | tf_op jit(solution)/shard_map/all_gather | solution.py:583
  40.2 22.9 %collective-permute-start = (f32[256,768]{1,0:T(8,128)S(1)}, f32[256,768]{1,0:T(8,128)S(1)}, u32[]{:S(2)}, u32[]{:S(2)}) collective-permute-start(f32[256,768]{1,0:T(8,128)S(1)} %constant_dynamic-slice_fusion.2), channel_id=1, source_target_pairs={{0,1},{1,0},{2,3},{3,2},{4,5},{5,4},{6,7},{7,6},{8,9},{9,8},{10,11... | collective-permute-start | bytes 2359304 | tf_op jit(solution)/shard_map/ppermute | solution.py:65
  43.5 19.0 %collective-permute-start.2 = (f32[2,1536]{1,0:T(2,128)S(1)}, f32[2,1536]{1,0:T(2,128)S(1)}, u32[]{:S(2)}, u32[]{:S(2)}) collective-permute-start(f32[2,1536]{1,0:T(2,128)S(1)} %convert_element_type.141), channel_id=1, source_target_pairs={{0,1},{1,0},{2,3},{3,2},{4,5},{5,4},{6,7},{7,6},{8,9},{9,8},{10,11... | collective-permute-start | bytes 36872 | tf_op jit(solution)/shard_map/ppermute | solution.py:65
  43.9 46.9 %collective-permute-start.3 = (f32[96,768]{1,0:T(8,128)}, f32[96,768]{1,0:T(8,128)}, u32[]{:S(2)}, u32[]{:S(2)}) collective-permute-start(f32[96,768]{1,0:T(8,128)} %get-tuple-element.90), channel_id=1, source_target_pairs={{0,1},{1,0},{2,3},{3,2},{4,5},{5,4},{6,7},{7,6},{8,9},{9,8},{10,11... | collective-permute-start | bytes 884744 | tf_op jit(solution)/shard_map/ppermute | solution.py:65
  90.8 197.2 %reduce-scatter.3.cloned.1.call-start = ((), (), s32[]{:S(2)}) async-start(), calls=%async_computation.2 | async-start | bytes 10027008 | tf_op jit(solution)/shard_map/reduce_scatter | solution.py:601
  90.8 21.6 %collective-permute-start.4 = (f32[256,768]{1,0:T(8,128)}, f32[256,768]{1,0:T(8,128)}, u32[]{:S(2)}, u32[]{:S(2)}) collective-permute-start(f32[256,768]{1,0:T(8,128)} %fusion.62), channel_id=1, source_target_pairs={{0,1},{1,0},{2,3},{3,2},{4,5},{5,4},{6,7},{7,6},{8,9},{9,8},{10,11... | collective-permute-start | bytes 2359304 | tf_op jit(solution)/shard_map/ppermute | solution.py:65
  131.2 21.2 %collective-permute-start.5 = (f32[256,768]{1,0:T(8,128)}, f32[256,768]{1,0:T(8,128)}, u32[]{:S(2)}, u32[]{:S(2)}) collective-permute-start(f32[256,768]{1,0:T(8,128)} %constant_dynamic-slice_fusion.1), channel_id=1, source_target_pairs={{0,1},{1,0},{2,3},{3,2},{4,5},{5,4},{6,7},{7,6},{8,9},{9,8},{10,11... | collective-permute-start | bytes 2359304 | tf_op jit(solution)/shard_map/ppermute | solution.py:65
  169.7 12.6 %collective-permute-start.7 = (f32[1536,768]{1,0:T(8,128)}, f32[1536,768]{1,0:T(8,128)S(1)}, u32[]{:S(2)}, u32[]{:S(2)}) collective-permute-start(f32[1536,768]{1,0:T(8,128)} %feed_sums.9), channel_id=1, source_target_pairs={{0,2},{2,0},{1,3},{3,1},{4,6},{6,4},{5,7},{7,5},{8,10},{10,8},{9,1... | collective-permute-start | bytes 14155784 | tf_op jit(solution)/shard_map/ppermute | solution.py:65
  173.0 17.1 %collective-permute-start.6 = (f32[1536,768]{1,0:T(8,128)}, f32[1536,768]{1,0:T(8,128)}, u32[]{:S(2)}, u32[]{:S(2)}) collective-permute-start(f32[1536,768]{1,0:T(8,128)} %feed_sums.8), channel_id=1, source_target_pairs={{0,2},{2,0},{1,3},{3,1},{4,6},{6,4},{5,7},{7,5},{8,10},{10,8},{9,1... | collective-permute-start | bytes 14155784 | tf_op jit(solution)/shard_map/ppermute | solution.py:65
  179.2 21.6 %collective-permute-start.8 = (f32[256,768]{1,0:T(8,128)}, f32[256,768]{1,0:T(8,128)}, u32[]{:S(2)}, u32[]{:S(2)}) collective-permute-start(f32[256,768]{1,0:T(8,128)} %get-tuple-element.197), channel_id=1, source_target_pairs={{0,1},{1,0},{2,3},{3,2},{4,5},{5,4},{6,7},{7,6},{8,9},{9,8},{10,11... | collective-permute-start | bytes 2359304 | tf_op jit(solution)/shard_map/ppermute | solution.py:65
  200.8 197.9 %reduce-scatter.5.cloned.1.call-start = ((), (), s32[]{:S(2)}) async-start(), calls=%async_computation.3 | async-start | bytes 12533760 | tf_op jit(solution)/shard_map/reduce_scatter | solution.py:613
  218.0 20.5 %collective-permute-start.9 = (f32[256,768]{1,0:T(8,128)S(1)}, f32[256,768]{1,0:T(8,128)S(1)}, u32[]{:S(2)}, u32[]{:S(2)}) collective-permute-start(f32[256,768]{1,0:T(8,128)S(1)} %constant_dynamic-slice_fusion), channel_id=1, source_target_pairs={{0,1},{1,0},{2,3},{3,2},{4,5},{5,4},{6,7},{7,6},{8,9},{9,8},{10,11... | collective-permute-start | bytes 2359304 | tf_op jit(solution)/shard_map/ppermute | solution.py:65
  247.4 16.3 %collective-permute-start.13 = (f32[1536,768]{1,0:T(8,128)}, f32[1536,768]{1,0:T(8,128)}, u32[]{:S(2)}, u32[]{:S(2)}) collective-permute-start(f32[1536,768]{1,0:T(8,128)} %feed_sums.13), channel_id=1, source_target_pairs={{0,2},{2,0},{1,3},{3,1},{4,6},{6,4},{5,7},{7,5},{8,10},{10,8},{9,1... | collective-permute-start | bytes 14155784 | tf_op jit(solution)/shard_map/ppermute | solution.py:65
  252.4 17.1 %collective-permute-start.12 = (f32[1536,768]{1,0:T(8,128)}, f32[1536,768]{1,0:T(8,128)}, u32[]{:S(2)}, u32[]{:S(2)}) collective-permute-start(f32[1536,768]{1,0:T(8,128)} %feed_sums.12), channel_id=1, source_target_pairs={{0,2},{2,0},{1,3},{3,1},{4,6},{6,4},{5,7},{7,5},{8,10},{10,8},{9,1... | collective-permute-start | bytes 14155784 | tf_op jit(solution)/shard_map/ppermute | solution.py:65
  254.8 20.4 %collective-permute-start.11 = (f32[1536,384]{1,0:T(8,128)S(1)}, f32[1536,384]{1,0:T(8,128)S(1)}, u32[]{:S(2)}, u32[]{:S(2)}) collective-permute-start(f32[1536,384]{1,0:T(8,128)S(1)} %attention_sums.4), channel_id=1, source_target_pairs={{0,2},{2,0},{1,3},{3,1},{4,6},{6,4},{5,7},{7,5},{8,10},{10,8},{9,1... | collective-permute-start | bytes 7077896 | tf_op jit(solution)/shard_map/ppermute | solution.py:65
  260.4 21.9 %collective-permute-start.14 = (f32[256,768]{1,0:T(8,128)}, f32[256,768]{1,0:T(8,128)}, u32[]{:S(2)}, u32[]{:S(2)}) collective-permute-start(f32[256,768]{1,0:T(8,128)} %multiply_multiply_fusion.4), channel_id=1, source_target_pairs={{0,1},{1,0},{2,3},{3,2},{4,5},{5,4},{6,7},{7,6},{8,9},{9,8},{10,11... | collective-permute-start | bytes 2359304 | tf_op jit(solution)/shard_map/ppermute | solution.py:65
  288.0 234.6 %all-gather.11.cloned.1.call-start = ((), (), s32[]{:S(2)}) async-start(), calls=%async_computation.6 | async-start | bytes 29196288 | tf_op jit(solution)/shard_map/all_gather | solution.py:629
  307.2 4.9 collective-permute-start.20
  316.1 17.3 %collective-permute-start.26 = (f32[4,48,384]{2,1,0:T(8,128)S(1)}, f32[4,48,384]{2,1,0:T(8,128)S(1)}, u32[]{:S(2)}, u32[]{:S(2)}) collective-permute-start(f32[4,48,384]{2,1,0:T(8,128)S(1)} %get-tuple-element.214), channel_id=1, source_target_pairs={{0,64},{32,96},{64,0},{96,32},{1,65},{33,97},{65,1},{97,33},{2,66}... | collective-permute-start | bytes 884744 | tf_op jit(solution)/shard_map/ppermute | solution.py:83
  318.8 23.8 %collective-permute-start.25 = (f32[4,48,384]{2,1,0:T(8,128)S(1)}, f32[4,48,384]{2,1,0:T(8,128)S(1)}, u32[]{:S(2)}, u32[]{:S(2)}) collective-permute-start(f32[4,48,384]{2,1,0:T(8,128)S(1)} %get-tuple-element.215), channel_id=1, source_target_pairs={{0,96},{32,0},{64,32},{96,64},{1,97},{33,1},{65,33},{97,65},{2,98}... | collective-permute-start | bytes 884744 | tf_op jit(solution)/shard_map/ppermute | solution.py:83
  320.5 22.1 %collective-permute-start.24 = (f32[4,48,384]{2,1,0:T(8,128)S(1)}, f32[4,48,384]{2,1,0:T(8,128)S(1)}, u32[]{:S(2)}, u32[]{:S(2)}) collective-permute-start(f32[4,48,384]{2,1,0:T(8,128)S(1)} %get-tuple-element.216), channel_id=1, source_target_pairs={{0,32},{32,64},{64,96},{96,0},{1,33},{33,65},{65,97},{97,1},{2,34}... | collective-permute-start | bytes 884744 | tf_op jit(solution)/shard_map/ppermute | solution.py:83
  320.9 21.7 %collective-permute-start.23 = (f32[4,48,384]{2,1,0:T(8,128)S(1)}, f32[4,48,384]{2,1,0:T(8,128)S(1)}, u32[]{:S(2)}, u32[]{:S(2)}) collective-permute-start(f32[4,48,384]{2,1,0:T(8,128)S(1)} %get-tuple-element.218), channel_id=1, source_target_pairs={{0,8},{4,12},{8,0},{12,4},{1,9},{5,13},{9,1},{13,5},{2,10},{6,14},... | collective-permute-start | bytes 884744 | tf_op jit(solution)/shard_map/ppermute | solution.py:83
  322.5 21.5 %collective-permute-start.22 = (f32[4,48,384]{2,1,0:T(8,128)S(1)}, f32[4,48,384]{2,1,0:T(8,128)S(1)}, u32[]{:S(2)}, u32[]{:S(2)}) collective-permute-start(f32[4,48,384]{2,1,0:T(8,128)S(1)} %get-tuple-element.219), channel_id=1, source_target_pairs={{0,12},{4,0},{8,4},{12,8},{1,13},{5,1},{9,5},{13,9},{2,14},{6,2},{... | collective-permute-start | bytes 884744 | tf_op jit(solution)/shard_map/ppermute | solution.py:83
  333.4 15.7 %collective-permute-start.21 = (f32[4,48,384]{2,1,0:T(8,128)S(1)}, f32[4,48,384]{2,1,0:T(8,128)S(1)}, u32[]{:S(2)}, u32[]{:S(2)}) collective-permute-start(f32[4,48,384]{2,1,0:T(8,128)S(1)} %get-tuple-element.220), channel_id=1, source_target_pairs={{0,4},{4,8},{8,12},{12,0},{1,5},{5,9},{9,13},{13,1},{2,6},{6,10},{... | collective-permute-start | bytes 884744 | tf_op jit(solution)/shard_map/ppermute | solution.py:83
  349.3 7.9 %collective-permute-start.29 = (f32[48,384]{1,0:T(8,128)S(1)}, f32[48,384]{1,0:T(8,128)S(1)}, u32[]{:S(2)}, u32[]{:S(2)}) collective-permute-start(f32[48,384]{1,0:T(8,128)S(1)} %get-tuple-element.232), channel_id=1, source_target_pairs={{0,64},{32,96},{64,0},{96,32},{1,65},{33,97},{65,1},{97,33},{2,66}... | collective-permute-start | bytes 221192 | tf_op jit(solution)/shard_map/ppermute | solution.py:83
  351.7 7.2 %collective-permute-start.28 = (f32[48,384]{1,0:T(8,128)S(1)}, f32[48,384]{1,0:T(8,128)S(1)}, u32[]{:S(2)}, u32[]{:S(2)}) collective-permute-start(f32[48,384]{1,0:T(8,128)S(1)} %get-tuple-element.233), channel_id=1, source_target_pairs={{0,96},{32,0},{64,32},{96,64},{1,97},{33,1},{65,33},{97,65},{2,98}... | collective-permute-start | bytes 221192 | tf_op jit(solution)/shard_map/ppermute | solution.py:83
  353.8 7.9 %collective-permute-start.27 = (f32[48,384]{1,0:T(8,128)S(1)}, f32[48,384]{1,0:T(8,128)S(1)}, u32[]{:S(2)}, u32[]{:S(2)}) collective-permute-start(f32[48,384]{1,0:T(8,128)S(1)} %get-tuple-element.234), channel_id=1, source_target_pairs={{0,32},{32,64},{64,96},{96,0},{1,33},{33,65},{65,97},{97,1},{2,34}... | collective-permute-start | bytes 221192 | tf_op jit(solution)/shard_map/ppermute | solution.py:83
  354.1 9.8 %collective-permute-start.32 = (f32[48,384]{1,0:T(8,128)S(1)}, f32[48,384]{1,0:T(8,128)S(1)}, u32[]{:S(2)}, u32[]{:S(2)}) collective-permute-start(f32[48,384]{1,0:T(8,128)S(1)} %get-tuple-element.228), channel_id=1, source_target_pairs={{0,8},{4,12},{8,0},{12,4},{1,9},{5,13},{9,1},{13,5},{2,10},{6,14},... | collective-permute-start | bytes 221192 | tf_op jit(solution)/shard_map/ppermute | solution.py:83
  354.7 9.9 %collective-permute-start.31 = (f32[48,384]{1,0:T(8,128)S(1)}, f32[48,384]{1,0:T(8,128)S(1)}, u32[]{:S(2)}, u32[]{:S(2)}) collective-permute-start(f32[48,384]{1,0:T(8,128)S(1)} %get-tuple-element.229), channel_id=1, source_target_pairs={{0,12},{4,0},{8,4},{12,8},{1,13},{5,1},{9,5},{13,9},{2,14},{6,2},{... | collective-permute-start | bytes 221192 | tf_op jit(solution)/shard_map/ppermute | solution.py:83
  357.2 7.4 %collective-permute-start.30 = (f32[48,384]{1,0:T(8,128)S(1)}, f32[48,384]{1,0:T(8,128)S(1)}, u32[]{:S(2)}, u32[]{:S(2)}) collective-permute-start(f32[48,384]{1,0:T(8,128)S(1)} %get-tuple-element.230), channel_id=1, source_target_pairs={{0,4},{4,8},{8,12},{12,0},{1,5},{5,9},{9,13},{13,1},{2,6},{6,10},{... | collective-permute-start | bytes 221192 | tf_op jit(solution)/shard_map/ppermute | solution.py:83
  358.9 16.2 %collective-permute-start.19 = (f32[96,768]{1,0:T(8,128)S(1)}, f32[96,768]{1,0:T(8,128)S(1)}, u32[]{:S(2)}, u32[]{:S(2)}) collective-permute-start(f32[96,768]{1,0:T(8,128)S(1)} %get-tuple-element.225), channel_id=1, source_target_pairs={{0,17},{17,0},{1,16},{16,1},{2,19},{19,2},{3,18},{18,3},{4,21},{21... | collective-permute-start | bytes 884744 | tf_op jit(solution)/shard_map/ppermute | solution.py:619
  361.7 13.4 %collective-permute-start.18 = (f32[96,768]{1,0:T(8,128)S(1)}, f32[96,768]{1,0:T(8,128)S(1)}, u32[]{:S(2)}, u32[]{:S(2)}) collective-permute-start(f32[96,768]{1,0:T(8,128)S(1)} %get-tuple-element.225), channel_id=1, source_target_pairs={{0,1},{1,0},{2,3},{3,2},{4,5},{5,4},{6,7},{7,6},{8,9},{9,8},{10,11... | collective-permute-start | bytes 884744 | tf_op jit(solution)/shard_map/ppermute | solution.py:65
  363.9 11.1 %collective-permute-start.17 = (f32[96,768]{1,0:T(8,128)S(1)}, f32[96,768]{1,0:T(8,128)S(1)}, u32[]{:S(2)}, u32[]{:S(2)}) collective-permute-start(f32[96,768]{1,0:T(8,128)S(1)} %get-tuple-element.224), channel_id=1, source_target_pairs={{0,16},{16,0},{1,17},{17,1},{2,18},{18,2},{3,19},{19,3},{4,20},{20... | collective-permute-start | bytes 884744 | tf_op jit(solution)/shard_map/ppermute | solution.py:65
  364.6 12.0 %collective-permute-start.33 = (f32[96,384]{1,0:T(8,128)S(1)}, f32[96,384]{1,0:T(8,128)S(1)}, u32[]{:S(2)}, u32[]{:S(2)}) collective-permute-start(f32[96,384]{1,0:T(8,128)S(1)} %pad_maximum_fusion.2), channel_id=1, source_target_pairs={{0,16},{16,0},{1,17},{17,1},{2,18},{18,2},{3,19},{19,3},{4,20},{20... | collective-permute-start | bytes 442376 | tf_op jit(solution)/shard_map/ppermute | solution.py:65
  400.8 13.2 %collective-permute-start.34 = (f32[96,1152]{1,0:T(8,128)S(1)}, f32[96,1152]{1,0:T(8,128)S(1)}, u32[]{:S(2)}, u32[]{:S(2)}) collective-permute-start(f32[96,1152]{1,0:T(8,128)S(1)} %pad_maximum_fusion.1), channel_id=1, source_target_pairs={{0,16},{16,0},{1,17},{17,1},{2,18},{18,2},{3,19},{19,3},{4,20},{20... | collective-permute-start | bytes 1327112 | tf_op jit(solution)/shard_map/ppermute | solution.py:65
  402.4 11.6 %collective-permute-start.36 = (f32[96,768]{1,0:T(8,128)S(1)}, f32[96,768]{1,0:T(8,128)S(1)}, u32[]{:S(2)}, u32[]{:S(2)}) collective-permute-start(f32[96,768]{1,0:T(8,128)S(1)} %get-tuple-element.222), channel_id=1, source_target_pairs={{0,17},{17,0},{1,16},{16,1},{2,19},{19,2},{3,18},{18,3},{4,21},{21... | collective-permute-start | bytes 884744 | tf_op jit(solution)/shard_map/ppermute | solution.py:619
  404.6 16.7 %collective-permute-start.35 = (f32[96,768]{1,0:T(8,128)S(1)}, f32[96,768]{1,0:T(8,128)S(1)}, u32[]{:S(2)}, u32[]{:S(2)}) collective-permute-start(f32[96,768]{1,0:T(8,128)S(1)} %get-tuple-element.222), channel_id=1, source_target_pairs={{0,1},{1,0},{2,3},{3,2},{4,5},{5,4},{6,7},{7,6},{8,9},{9,8},{10,11... | collective-permute-start | bytes 884744 | tf_op jit(solution)/shard_map/ppermute | solution.py:65
  422.3 39.8 %copy-start.49 = (f32[256,768]{1,0:T(8,128)S(1)}, f32[256,768]{1,0:T(8,128)}, u32[]{:S(2)}) copy-start(f32[256,768]{1,0:T(8,128)} %copy-done.48) | copy-start | bytes 2359300
  422.3 40.9 %copy-start.80 = (f32[768]{0:T(1024)S(1)}, f32[768]{0:T(1024)}, u32[]{:S(2)}) copy-start(f32[768]{0:T(1024)} %get-tuple-element.161) | copy-start | bytes 9220
  422.3 40.9 %copy-start.79 = (f32[768]{0:T(1024)S(1)}, f32[768]{0:T(1024)}, u32[]{:S(2)}) copy-start(f32[768]{0:T(1024)} %get-tuple-element.167) | copy-start | bytes 9220
  422.4 40.9 %copy-start.81 = (f32[768]{0:T(1024)S(1)}, f32[768]{0:T(1024)}, u32[]{:S(2)}) copy-start(f32[768]{0:T(1024)} %get-tuple-element.191) | copy-start | bytes 9220
  422.4 40.9 %copy-start.99 = (f32[1536]{0:T(1024)S(1)}, f32[1536]{0:T(1024)}, u32[]{:S(2)}) copy-start(f32[1536]{0:T(1024)} %get-tuple-element.265) | copy-start | bytes 18436
  422.4 40.9 %copy-start.98 = (f32[1536]{0:T(1024)S(1)}, f32[1536]{0:T(1024)}, u32[]{:S(2)}) copy-start(f32[1536]{0:T(1024)} %get-tuple-element.269) | copy-start | bytes 18436
  422.4 41.0 %copy-start.107 = (f32[768]{0:T(1024)S(1)}, f32[768]{0:T(1024)}, u32[]{:S(2)}) copy-start(f32[768]{0:T(1024)} %get-tuple-element.157) | copy-start | bytes 9220
  422.4 41.0 %copy-start.106 = (f32[768]{0:T(1024)S(1)}, f32[768]{0:T(1024)}, u32[]{:S(2)}) copy-start(f32[768]{0:T(1024)} %get-tuple-element.169) | copy-start | bytes 9220
  422.4 41.0 %copy-start.85 = (f32[768]{0:T(1024)S(1)}, f32[768]{0:T(1024)}, u32[]{:S(2)}) copy-start(f32[768]{0:T(1024)} %get-tuple-element.159) | copy-start | bytes 9220
  422.4 41.0 %copy-start.101 = (f32[1536]{0:T(1024)S(1)}, f32[1536]{0:T(1024)}, u32[]{:S(2)}) copy-start(f32[1536]{0:T(1024)} %get-tuple-element.267) | copy-start | bytes 18436
  422.4 41.0 %copy-start.83 = (f32[768]{0:T(1024)S(1)}, f32[768]{0:T(1024)}, u32[]{:S(2)}) copy-start(f32[768]{0:T(1024)} %get-tuple-element.193) | copy-start | bytes 9220
  422.4 41.0 %copy-start.84 = (f32[768]{0:T(1024)S(1)}, f32[768]{0:T(1024)}, u32[]{:S(2)}) copy-start(f32[768]{0:T(1024)} %get-tuple-element.170) | copy-start | bytes 9220
  422.5 41.1 %copy-start.109 = (f32[768]{0:T(1024)S(1)}, f32[768]{0:T(1024)}, u32[]{:S(2)}) copy-start(f32[768]{0:T(1024)} %get-tuple-element.156) | copy-start | bytes 9220
  422.5 41.1 %copy-start.108 = (f32[768]{0:T(1024)S(1)}, f32[768]{0:T(1024)}, u32[]{:S(2)}) copy-start(f32[768]{0:T(1024)} %get-tuple-element.168) | copy-start | bytes 9220
  422.5 43.7 %copy-start.82 = (f32[768]{0:T(1024)S(1)}, f32[768]{0:T(1024)}, u32[]{:S(2)}) copy-start(f32[768]{0:T(1024)} %get-tuple-element.187) | copy-start | bytes 9220
  422.5 43.7 %copy-start.100 = (f32[1536]{0:T(1024)S(1)}, f32[1536]{0:T(1024)}, u32[]{:S(2)}) copy-start(f32[1536]{0:T(1024)} %get-tuple-element.263) | copy-start | bytes 18436
  422.5 36.8 %collective-permute-start.15 = (f32[512,768]{1,0:T(8,128)}, f32[512,768]{1,0:T(8,128)S(1)}, u32[]{:S(2)}, u32[]{:S(2)}) collective-permute-start(f32[512,768]{1,0:T(8,128)} %get-tuple-element.119), channel_id=1, source_target_pairs={{0,1},{1,0},{2,3},{3,2},{4,5},{5,4},{6,7},{7,6},{8,9},{9,8},{10,11... | collective-permute-start | bytes 4718600 | tf_op jit(solution)/shard_map/ppermute | solution.py:65
  462.1 20.3 %collective-permute-start.16 = (f32[256,768]{1,0:T(8,128)S(1)}, f32[256,768]{1,0:T(8,128)S(1)}, u32[]{:S(2)}, u32[]{:S(2)}) collective-permute-start(f32[256,768]{1,0:T(8,128)S(1)} %copy-done.49), channel_id=1, source_target_pairs={{0,1},{1,0},{2,3},{3,2},{4,5},{5,4},{6,7},{7,6},{8,9},{9,8},{10,11... | collective-permute-start | bytes 2359304 | tf_op jit(solution)/shard_map/ppermute | solution.py:65
  463.6 18.7 %collective-permute-start.10 = (f32[14,768]{1,0:T(8,128)S(1)}, f32[14,768]{1,0:T(8,128)S(1)}, u32[]{:S(2)}, u32[]{:S(2)}) collective-permute-start(f32[14,768]{1,0:T(8,128)S(1)} %concatenate.41), channel_id=1, source_target_pairs={{0,1},{1,0},{2,3},{3,2},{4,5},{5,4},{6,7},{7,6},{8,9},{9,8},{10,11... | collective-permute-start | bytes 129032 | tf_op jit(solution)/shard_map/ppermute | solution.py:65
  484.2 1.3 collective-permute-start.37
  485.5 6.5 %collective-permute-start.38 = (f32[18,768]{1,0:T(8,128)S(1)}, f32[18,768]{1,0:T(8,128)S(1)}, u32[]{:S(2)}, u32[]{:S(2)}) collective-permute-start(f32[18,768]{1,0:T(8,128)S(1)} %add.537), channel_id=1, source_target_pairs={{0,4},{4,0},{8,12},{12,8},{1,5},{5,1},{9,13},{13,9},{2,6},{6,2},{1... | collective-permute-start | bytes 165896 | tf_op jit(solution)/shard_map/ppermute | solution.py:643
  492.0 7.5 %collective-permute-start.39 = (f32[18,768]{1,0:T(8,128)S(1)}, f32[18,768]{1,0:T(8,128)S(1)}, u32[]{:S(2)}, u32[]{:S(2)}) collective-permute-start(f32[18,768]{1,0:T(8,128)S(1)} %add.538), channel_id=1, source_target_pairs={{4,8},{8,4},{12,0},{0,12},{5,9},{9,5},{13,1},{1,13},{6,10},{10,6},... | collective-permute-start | bytes 165896 | tf_op jit(solution)/shard_map/ppermute | solution.py:643
  499.4 6.0 %collective-permute-start.40 = (f32[18,768]{1,0:T(8,128)S(1)}, f32[18,768]{1,0:T(8,128)S(1)}, u32[]{:S(2)}, u32[]{:S(2)}) collective-permute-start(f32[18,768]{1,0:T(8,128)S(1)} %add.539), channel_id=1, source_target_pairs={{0,32},{32,0},{64,96},{96,64},{1,33},{33,1},{65,97},{97,65},{2,34}... | collective-permute-start | bytes 165896 | tf_op jit(solution)/shard_map/ppermute | solution.py:643
  505.5 7.2 %collective-permute-start.41 = (f32[18,768]{1,0:T(8,128)S(1)}, f32[18,768]{1,0:T(8,128)S(1)}, u32[]{:S(2)}, u32[]{:S(2)}) collective-permute-start(f32[18,768]{1,0:T(8,128)S(1)} %add.540), channel_id=1, source_target_pairs={{32,64},{64,32},{96,0},{0,96},{33,65},{65,33},{97,1},{1,97},{34,66... | collective-permute-start | bytes 165896 | tf_op jit(solution)/shard_map/ppermute | solution.py:643
  512.7 4.4 collective-permute-start.42
  (101 other events, 678.3 us)
Sparse Core Ops, SparseCore 0:
  24.1 57.0 all-gather.6
  90.9 54.9 all-gather.8
  200.9 86.9 reduce-scatter.2
  291.7 106.9 reduce-scatter.4
  422.4 97.6 all-gather.10

commit v5 on v4

--- a/solution.py
+++ b/solution.py
@@ -117,7 +117,7 @@
 
 
 def attend_kernel(
-    length_ref,
+    place_ref,
     slot_ref,
     query_weight,
     query_bias,
@@ -130,17 +130,18 @@
     value_ref,
     mixture_ref,
     logsum_ref,
-    share_ref,
+    own_ref,
+    sent_ref,
 ):
     slots = slot_ref[...]
     query_ref[...] = (dot(slots, query_weight[0]) + query_bias[...]).astype(BF16)
     key_ref[...] = dot(slots, key_weight[0]).astype(BF16)
     value_ref[...] = (dot(slots, value_weight[0]) + value_bias[...]).astype(BF16)
     count = slots.shape[0]
-    valid = lax.broadcasted_iota(jnp.int32, (count, count), 0) < length_ref[0]
+    valid = lax.broadcasted_iota(jnp.int32, (count, count), 0) < place_ref[0]
     for head in range(2):
         cut = slice(head * HEAD_DIM, (head + 1) * HEAD_DIM)
-        scores = across_lanes(key_ref[:, cut], query_ref[:, cut]) * HEAD_DIM**-0.5
+        scores = across_lanes(key_ref[:, cut], query_ref[:, cut] * HEAD_DIM**-0.5)
         scores = jnp.where(valid, scores, -1e30)
         highest = jnp.max(scores, axis=0, keepdims=True)
         raised = jnp.exp(scores - highest)
@@ -148,18 +149,21 @@
         probs = (raised * (1.0 / totals)).astype(BF16)
         mixture_ref[:, cut] = t_dot_in_kernel(probs, value_ref[:, cut]).astype(BF16)
         logsum_ref[0, head : head + 1, :] = highest + jnp.log(totals)
-    share = dot(mixture_ref[...], output_weight[0])
-
-    @pl.when(pl.program_id(0) == 0)
-    def _():
-        share_ref[...] = share
-
-    @pl.when(pl.program_id(0) != 0)
-    def _():
-        share_ref[...] += share
-
-
-def attend(layer, length, slots, query_weight, query_bias, key_weight, value_weight, value_bias, output_weight):
+    half = count // 2
+    for side, share_ref in ((place_ref[1], own_ref), (1 - place_ref[1], sent_ref)):
+        rows = mixture_ref[pl.ds(pl.multiple_of(side * half, half), half), :]
+        share = dot(rows, output_weight[0])
+
+        @pl.when(pl.program_id(0) == 0)
+        def _():
+            share_ref[...] = share
+
+        @pl.when(pl.program_id(0) != 0)
+        def _():
+            share_ref[...] += share
+
+
+def attend(layer, length, side, slots, query_weight, query_bias, key_weight, value_weight, value_bias, output_weight):
     count, width = slots.shape
     heads = query_weight.shape[2]
     pair = 2 * HEAD_DIM
@@ -174,9 +178,12 @@
         grid=(steps,),
         in_specs=[SCALAR, whole, weight, bias, weight, weight, bias]
         + [pl.BlockSpec((1, pair, width), lambda i: (layer, i, 0))],
-        out_specs=[part] * 4 + [pl.BlockSpec((1, 2, count), lambda i: (i, 0, 0)), whole],
+        out_specs=[part] * 4
+        + [pl.BlockSpec((1, 2, count), lambda i: (i, 0, 0))]
+        + [pl.BlockSpec((count // 2, width), lambda i: (0, 0))] * 2,
         out_shape=[part_shape] * 4
-        + [jax.ShapeDtypeStruct((steps, 2, count), F32), jax.ShapeDtypeStruct((count, width), F32)],
+        + [jax.ShapeDtypeStruct((steps, 2, count), F32)]
+        + [jax.ShapeDtypeStruct((count // 2, width), F32)] * 2,
         compiler_params=LIMIT,
         cost_estimate=pl.CostEstimate(
             flops=8 * count * width * heads + 4 * count * count * heads,
@@ -184,7 +191,7 @@
             transcendentals=count * count * heads // HEAD_DIM,
         ),
         name="attend",
-    )(length.reshape(1), slots, query_weight, query_bias, key_weight, value_weight, value_bias, output_weight)
+    )(jnp.stack([length, side]), slots, query_weight, query_bias, key_weight, value_weight, value_bias, output_weight)
 
 
 def attend_back_kernel(
@@ -212,7 +219,7 @@
     for head in range(2):
         cut = slice(head * HEAD_DIM, (head + 1) * HEAD_DIM)
         queries, keys, grad = query_ref[:, cut], key_ref[:, cut], grads[:, cut]
-        scores = jnp.where(valid, across_lanes(keys, queries) * scale, -1e30)
+        scores = jnp.where(valid, across_lanes(keys, queries * scale), -1e30)
         probs = jnp.exp(scores - logsum_ref[0, head : head + 1, :])
         grad_probs = across_lanes(value_ref[:, cut], grad)
         inner = jnp.sum(probs * grad_probs, axis=0, keepdims=True)
@@ -235,7 +242,7 @@
         share_ref[...] += share
 
 
-def attend_back(layer, length, saved, attended_low, query_weight, key_weight, value_weight, output_weight):
+def attend_back(layer, length, saved, attended_low, query_weight, key_weight, value_weight, output_weight, *earlier):
     queries, keys, values, _, logsum = saved
     count, width = attended_low.shape
     heads = queries.shape[1]
@@ -248,11 +255,12 @@
     sums = pl.BlockSpec((1, pair), lambda i: (0, i))
     sums_shape = jax.ShapeDtypeStruct((1, heads), F32)
     return pl.pallas_call(
-        attend_back_kernel,
+        lambda *refs: attend_back_kernel(*refs[:10], *refs[10 + len(earlier) :]),
         grid=(steps,),
         in_specs=[SCALAR, part, part, part, pl.BlockSpec((1, 2, count), lambda i: (i, 0, 0)), whole]
         + [weight] * 3
-        + [pl.BlockSpec((1, pair, width), lambda i: (layer, i, 0))],
+        + [pl.BlockSpec((1, pair, width), lambda i: (layer, i, 0))]
+        + [pl.BlockSpec(memory_space=pl.ANY)] * len(earlier),
         out_specs=[part] * 3 + [whole, sums, sums],
         out_shape=[part_shape] * 3 + [jax.ShapeDtypeStruct((count, width), F32), sums_shape, sums_shape],
         compiler_params=LIMIT,
@@ -262,7 +270,7 @@
             transcendentals=count * count * heads // HEAD_DIM,
         ),
         name="attend_back",
-    )(length.reshape(1), queries, keys, values, logsum, attended_low, query_weight, key_weight, value_weight, output_weight)
+    )(length.reshape(1), queries, keys, values, logsum, attended_low, query_weight, key_weight, value_weight, output_weight, *earlier)
 
 
 def pieces_kernel(place_ref, down_in, up_in, piece_ref):
@@ -413,58 +421,53 @@
     return ref[...].reshape(chips * rows, columns)
 
 
-def place_feed_kernel(down_in, up_in, down_ref, up_ref):
+def place_kernel(down_in, up_in, query_in, key_in, value_in, output_in, *refs):
+    down_ref, up_ref, query_ref, key_ref, value_ref, output_ref = refs[-6:]
     down_ref[0] = rows_of(down_in)
     up_ref[0] = rows_of(up_in).T
-
-
-def place_attention_kernel(query_in, key_in, value_in, output_in, query_ref, key_ref, value_ref, output_ref):
     query_ref[0] = rows_of(query_in).T
     key_ref[0] = rows_of(key_in).T
     value_ref[0] = rows_of(value_in).T
     output_ref[0] = rows_of(output_in)
 
 
-def place_gradients(gathered, width):
+def place_gradients(gathered, width, layer_feed, layer_attention, into=()):
     chips, _, rows, _ = gathered.shape
     step = 4
     units, block = chips * rows, step * rows
     half = width // 2
 
     def feed_in(core):
-        return pl.BlockSpec((step, 1, rows, width), lambda l, i: (i, core, 0, 1 - l))
+        return pl.BlockSpec((step, 1, rows, width), lambda i: (i, core, 0, 0))
 
     def attention_in(core, which):
-        return pl.BlockSpec((step, 1, rows, half), lambda l, i: (2 * i + which, core, 0, 5 - l))
-
-    limit = pltpu.CompilerParams(vmem_limit_bytes=40 * 2**20)
-    down, up = pl.pallas_call(
-        place_feed_kernel,
-        grid=(2, chips // step),
-        in_specs=[feed_in(0), feed_in(1)],
+        return pl.BlockSpec((step, 1, rows, half), lambda i: (2 * (i // 2) + which, core, 0, 2))
+
+    tall = pl.BlockSpec((1, half, block), lambda i: (layer_attention, i // 2, 0))
+    tall_shape = jax.ShapeDtypeStruct((2, width, block), F32)
+    return pl.pallas_call(
+        place_kernel,
+        grid=(chips // step,),
+        in_specs=[feed_in(0), feed_in(1)]
+        + [attention_in(0, 0), attention_in(0, 1), attention_in(1, 0), attention_in(1, 1)]
+        + [pl.BlockSpec(memory_space=pl.ANY)] * len(into),
         out_specs=[
-            pl.BlockSpec((1, block, width), lambda l, i: (l, i, 0)),
-            pl.BlockSpec((1, width, block), lambda l, i: (l, 0, i)),
-        ],
+            pl.BlockSpec((1, block, width), lambda i: (layer_feed, i, 0)),
+            pl.BlockSpec((1, width, block), lambda i: (layer_feed, 0, i)),
+        ]
+        + [tall] * 3
+        + [pl.BlockSpec((1, block, half), lambda i: (layer_attention, 0, i // 2))],
         out_shape=[
             jax.ShapeDtypeStruct((2, units, width), F32),
             jax.ShapeDtypeStruct((2, width, units), F32),
-        ],
-        compiler_params=limit,
-        name="place_feed",
-    )(gathered, gathered)
-    tall = pl.BlockSpec((1, half, block), lambda l, i: (l, i, 0))
-    tall_shape = jax.ShapeDtypeStruct((2, width, block), F32)
-    query, key, value, output = pl.pallas_call(
-        place_attention_kernel,
-        grid=(2, 2),
-        in_specs=[attention_in(0, 0), attention_in(0, 1), attention_in(1, 0), attention_in(1, 1)],
-        out_specs=[tall, tall, tall, pl.BlockSpec((1, block, half), lambda l, i: (l, 0, i))],
-        out_shape=[tall_shape, tall_shape, tall_shape, jax.ShapeDtypeStruct((2, block, width), F32)],
-        compiler_params=limit,
-        name="place_attention",
-    )(gathered, gathered, gathered, gathered)
-    return query, key, value, output, up, down
+        ]
+        + [tall_shape] * 3
+        + [jax.ShapeDtypeStruct((2, block, width), F32)],
+        input_output_aliases={6 + k: k for k in range(len(into))},
+        compiler_params=LIMIT,
+        cost_estimate=pl.CostEstimate(flops=0, bytes_accessed=24 * units * width, transcendentals=0),
+        name="place_gradients",
+    )(*[gathered] * 6, *into)
 
 
 def local(
@@ -516,9 +519,10 @@
         return feed_sums(core, actives[1], pre_lows[1], ffn_low, hidden_low, received[1], columns, total)
 
     def attention_forward(layer, rounded):
-        *attention, share = attend(
+        *attention, share, sent = attend(
             layer,
             length,
+            side,
             rounded,
             query_weight,
             query_bias[layer].astype(F32)[None],
@@ -527,13 +531,13 @@
             value_bias[layer].astype(F32)[None],
             output_weight,
         )
-        return attention, own_slots(share), piece(share, 1 - side, half_slots)
-
-    def attention_back(layer, saved, grad_one_sent, received):
+        return attention, share, sent
+
+    def attention_back(layer, saved, grad_one_sent, received, *earlier):
         grad_one = 2.0 * in_order(side, grad_one_sent, received)
         attended_low = grad_one.astype(BF16)
         *lows, share, query_sum, value_sum = attend_back(
-            layer, length, saved, attended_low, query_weight, key_weight, value_weight, output_weight
+            layer, length, saved, attended_low, query_weight, key_weight, value_weight, output_weight, *earlier
         )
         small = [jnp.concatenate([query_sum[0], value_sum[0]]), column_sum(attended_low)]
         return grad_one, lows, attended_low, share, small
@@ -597,9 +601,9 @@
     sent = 0.5 * grad_one_own
     received = swap(sent, "h")
     feed2 = feed_weights_back(saved2, pre_lows, ffn_low, 2 * width)
-    feed2, received = together(feed2, received)
+    earlier = feed2
     feed2 = lax.psum_scatter(feed2, PLANE, tiled=True)
-    _, lows2, attended_low2, share, small_att2 = attention_back(1, att2, sent, received)
+    _, lows2, attended_low2, share, small_att2 = attention_back(1, att2, sent, received, earlier)
     received = swap(piece(share, 1 - side, half_slots), "h")
     attn2_received = swap(attention_sums(1 - core, lows2, mixture, x2_low, attended_low2), "c")
     gradient1 = grad_one_own + own_slots(share) + received
@@ -621,13 +625,18 @@
         peer = swap(peer, "h") + diagonal
         return jnp.concatenate([own[:, :width] + peer, own[:, width:]], axis=1)
 
+    def gather(*parts):
+        own = jnp.concatenate(parts, axis=1)
+        return lax.all_gather(own, PLANE + ("c",)).reshape(16, 2, *own.shape)
+
     feed2 = across(feed2[:, :width], feed2[:, width:])
     attn1 = attn1 + swap(attn1, "zl")
     feed2, attn1, rest = together(feed2, attn1, rest)
+    gathered = gather(feed2, attn1)
     rest = across(jnp.concatenate([rest[:, :width], rest[:, 2 * width :]], axis=1), rest[:, width : 2 * width])
-    own = jnp.concatenate([feed2, rest, attn1], axis=1)
-    gathered = lax.all_gather(own, PLANE + ("c",)).reshape(16, 2, *own.shape)
-    grad_query, grad_key, grad_value, grad_output, grad_up, grad_down = place_gradients(gathered, width)
+    placed = place_gradients(gathered, width, 1, 0)
+    placed = place_gradients(gather(rest), width, 0, 1, placed)
+    grad_down, grad_up, grad_query, grad_key, grad_value, grad_output = placed
 
     token_grad = grad_one1 + pair_sum(share)
     scaled_last, token_grad = together(scaled_last, token_grad)

time: 563 us -> 578 us (1.027)
  waiting for transfers between devices: 253 us -> 270 us
    ppermute x25, waiting for transfers between devices: 154 us -> 171 us  [swap(): return lax.ppermute(values, axis, SWAP)]
    all_gather x1 -> x2, waiting for transfers between devices: 0.01 us -> 7.46 us  [gather(): return lax.all_gather(own, PLANE + ('c',)).reshape(16, 2, *own.shape)]
    unnamed x242 -> x272, local copies, waits for them, and re-layouts: 26.1 us -> 29.6 us
  transfers between devices with their start and end apart: 48 -> 49, of which waited for: 30 -> 30; matrix products, arithmetic and copies ran while one was open for 10% -> 9% of each run, Pallas kernels for 18% -> 18%
where the time goes in v5:
time: 578 us; the launch traced here: 568 us
  waiting for transfers between devices  270 us (47%)
  Pallas kernels  127 us (22%)
  starting transfers between devices  60.9 us (11%)
  local copies, waits for them, and re-layouts  34.8 us (6%)
  matrix products  32.1 us (6%)
  other arithmetic  25.7 us (4%)
  between operations  17.7 us (3%)
    ppermute x25, waiting for transfers between devices, swap(): return lax.ppermute(values, axis, SWAP)  171 us
    ppermute x25, starting transfers between devices, swap(): return lax.ppermute(values, axis, SWAP)  39.8 us
    pallas_call x8, Pallas kernels, feed_sums(): pl.pallas_call(lambda *refs: feed_sums_kernel(received is not None, *refs...  35.8 us
    unnamed x272, local copies, waits for them, and re-layouts  29.6 us
    ppermute x12, waiting for transfers between devices, ring_parts(): received.append(lax.ppermute(sent, axis, pairs))  26.7 us
    pallas_call x2, Pallas kernels, attend_back(): pl.pallas_call(lambda *refs: attend_back_kernel(*refs[:10], *refs[10 + le...  24.7 us
    pallas_call x2, Pallas kernels, place_gradients(): pl.pallas_call(place_kernel, grid=(chips // step,), in_specs=[feed_in(0),...  23.8 us
    ppermute x4, waiting for transfers between devices, local(): small = small + lax.ppermute(small, axis, pairs)  22.7 us
  transfers between devices with their start and end apart: 49, of which 30 were waited for; matrix products, arithmetic and copies ran while one was open for 9% of the time, Pallas kernels for 18%

profile of v5, /device:TPU:0, one launch (start us, length us, event | category | flops | bytes accessed | tf_op | source)
XLA Modules:
  0.0 568.1 jit_solution(13600992205874239339)
XLA Ops:
  8.0 2.3 copy-done.1
  12.7 4.0 collective-permute-start.1
  16.7 7.0 %collective-permute-done.1 = f32[96,768]{1,0:T(8,128)S(1)} collective-permute-done((f32[96,768]{1,0:T(8,128)S(1)}, f32[96,768]{1,0:T(8,128)S(1)}, u32[]{:S(2)}, u32[]{:S(2)}) %collective-permute-start.1) | collective-permute-done | bytes 294944 | tf_op jit(solution)/shard_map/ppermute | solution.py:65
  25.1 9.6 %attend.2 = (bf16[512,384]{1,0:T(8,128)(2,1)S(1)}, bf16[512,384]{1,0:T(8,128)(2,1)S(1)}, bf16[512,384]{1,0:T(8,128)(2,1)S(1)}, bf16[512,384]{1,0:T(8,128)(2,1)S(...) custom-call(s32[2]{0:T(128)S(1)} %get-tuple-element.283.place_ref, ...), custom_call_target="tpu_custom_call" | custom-call | flops 1610612736 | bytes 5505024 | tf_op jit(solution)/shard_map/attend/pallas_call | solution.py:176
  38.5 3.2 collective-permute-start
  42.1 3.2 collective-permute-start.3
  48.5 12.3 %collective-permute-done.2 = f32[2,1536]{1,0:T(2,128)S(1)} collective-permute-done((f32[2,1536]{1,0:T(2,128)S(1)}, f32[2,1536]{1,0:T(2,128)S(1)}, u32[]{:S(2)}, u32[]{:S(2)}) %collective-permute-start.2) | collective-permute-done | bytes 12320 | tf_op jit(solution)/shard_map/ppermute | solution.py:65
  64.4 3.8 multiply_convert_fusion.3
  68.3 3.4 fusion.11
  71.6 10.0 %all-gather.9.cloned.1.call-done = f32[3072,768]{1,0:T(8,128)} async-done(((f32[96,768]{1,0:T(8,128)}), f32[3072,768]{1,0:T(8,128)}) %all-gather.9.cloned.1.call-update) | async-done | bytes 9437200 | tf_op jit(solution)/shard_map/all_gather | solution.py:506
  81.6 4.4 sort_weights.2
  90.9 3.2 collective-permute-start.4
  94.2 18.1 %collective-permute-done.4 = f32[256,768]{1,0:T(8,128)S(1)} collective-permute-done((f32[256,768]{1,0:T(8,128)S(1)}, f32[256,768]{1,0:T(8,128)S(1)}, u32[]{:S(2)}, u32[]{:S(2)}) %collective-permute-start.4) | collective-permute-done | bytes 786464 | tf_op jit(solution)/shard_map/ppermute | solution.py:65
  113.6 10.4 %attend.3 = (bf16[512,384]{1,0:T(8,128)(2,1)S(1)}, bf16[512,384]{1,0:T(8,128)(2,1)S(1)}, bf16[512,384]{1,0:T(8,128)(2,1)S(1)}, bf16[512,384]{1,0:T(8,128)(2,1)S(...) custom-call(s32[2]{0:T(128)S(1)} %copy-done.25, ...), custom_call_target="tpu_custom_call" | custom-call | flops 1610612736 | bytes 5505024 | tf_op jit(solution)/shard_map/attend/pallas_call | solution.py:176
  127.1 3.6 collective-permute-start.5
  131.9 14.0 %all-gather.11.cloned.1.call-done = f32[3072,768]{1,0:T(8,128)} async-done(((f32[96,768]{1,0:T(8,128)}), f32[3072,768]{1,0:T(8,128)}) %all-gather.11.cloned.1.call-update) | async-done | bytes 9437200 | tf_op jit(solution)/shard_map/all_gather | solution.py:587
  146.0 4.5 sort_weights.3
  153.8 2.5 multiply_convert_fusion.1
  164.7 3.3 feed_sums.9
  168.3 3.3 feed_sums.8
  171.8 4.3 collective-permute-done.8.refs_5_
  178.3 5.6 feed_sums.10.refs_6_
  184.0 5.6 feed_sums.11.refs_10_
  189.7 2.8 fusion.81
  192.7 3.5 multiply_reduce_fusion.2
  197.4 3.3 collective-permute-start.6
  200.7 18.4 %collective-permute-done.6 = f32[256,768]{1,0:T(8,128)} collective-permute-done((f32[256,768]{1,0:T(8,128)}, f32[256,768]{1,0:T(8,128)}, u32[]{:S(2)}, u32[]{:S(2)}) %collective-permute-start.6) | collective-permute-done | bytes 786464 | tf_op jit(solution)/shard_map/ppermute | solution.py:65
  226.3 12.4 %attend_back.2 = (bf16[512,384]{1,0:T(8,128)(2,1)S(1)}, bf16[512,384]{1,0:T(8,128)(2,1)S(1)}, bf16[512,384]{1,0:T(8,128)(2,1)S(1)}, f32[512,768]{1,0:T(8,128)}, ...) custom-call(s32[1]{0:T(128)} %copy.78.refs_0_, bf16[512,384]{1,0:T(8,128)(2,1)S(1)} %copy-done.16, ...), custom_call_target="tpu_custom_call" | custom-call | flops 2214592512 | bytes 5505024 | tf_op jit(solution)/shard_map/attend_back/pallas_call | solution.py:257
  240.0 3.2 collective-permute-start.9
  243.2 17.3 %collective-permute-done.9 = f32[256,768]{1,0:T(8,128)S(1)} collective-permute-done((f32[256,768]{1,0:T(8,128)S(1)}, f32[256,768]{1,0:T(8,128)S(1)}, u32[]{:S(2)}, u32[]{:S(2)}) %collective-permute-start.9) | collective-permute-done | bytes 786464 | tf_op jit(solution)/shard_map/ppermute | solution.py:65
  260.5 2.3 multiply_reduce_fusion.3
  265.5 3.4 feed_sums.13
  270.5 3.3 feed_sums.12
  276.5 2.6 fusion.44
  281.0 3.4 collective-permute-start.14
  284.4 5.7 %feed_sums.14.refs_6_ = f32[1536,1920]{1,0:T(8,128)} custom-call(s32[1]{0:T(128)} %bitcast.2.refs_0_, bf16[256,1536]{1,0:T(8,128)(2,1)S(1)} %get-tuple-element.261.refs_1_, bf16[256,1536]{1,0:T(8,128)(2,1)S(1)} %get-tuple-element.276.refs_2_, bf16[256,768]{1,0:T(8,128)(2,1)S(1)} %get-tuple-element.206.refs_3_, bf16[256,768]{1,0:T(8,128)(2,1)S(1)} %fusion.61.refs_4_, ...), custom_call_target="tpu_custom_call" | custom-call | flops 603979776 | bytes 9437184 | tf_op jit(solution)/shard_map/feed_sums/pallas_call | solution.py:335
  290.1 5.6 feed_sums.15.refs_8_
  295.8 3.2 attention_sums.5
  299.0 3.9 collective-permute-done.14
  306.5 12.3 %attend_back.3 = (bf16[512,384]{1,0:T(8,128)(2,1)S(1)}, bf16[512,384]{1,0:T(8,128)(2,1)S(1)}, bf16[512,384]{1,0:T(8,128)(2,1)S(1)}, f32[512,768]{1,0:T(8,128)}, ...) custom-call(s32[1]{0:T(128)} %copy.78.refs_0_, bf16[512,384]{1,0:T(8,128)(2,1)S(1)} %copy-done.32, ...), custom_call_target="tpu_custom_call" | custom-call | flops 2214592512 | bytes 5505024 | tf_op jit(solution)/shard_map/attend_back/pallas_call | solution.py:257
  318.8 3.2 attention_sums.6
  322.0 4.9 collective-permute-done.20.refs_7_
  326.8 3.8 attention_sums.7
  330.9 2.9 collective-permute-start.26
  338.6 9.9 %collective-permute-done.26 = f32[4,48,384]{2,1,0:T(8,128)S(1)} collective-permute-done((f32[4,48,384]{2,1,0:T(8,128)S(1)}, f32[4,48,384]{2,1,0:T(8,128)S(1)}, u32[]{:S(2)}, u32[]{:S(2)}) %collective-permute-start.26) | collective-permute-done | bytes 294944 | tf_op jit(solution)/shard_map/ppermute | solution.py:83
  349.5 8.0 %collective-permute-done.25 = f32[4,48,384]{2,1,0:T(8,128)S(1)} collective-permute-done((f32[4,48,384]{2,1,0:T(8,128)S(1)}, f32[4,48,384]{2,1,0:T(8,128)S(1)}, u32[]{:S(2)}, u32[]{:S(2)}) %collective-permute-start.25) | collective-permute-done | bytes 294944 | tf_op jit(solution)/shard_map/ppermute | solution.py:83
  358.4 5.3 collective-permute-done.21
  373.8 2.5 collective-permute-start.19
  380.8 10.3 %collective-permute-done.17 = f32[96,768]{1,0:T(8,128)S(1)} collective-permute-done((f32[96,768]{1,0:T(8,128)S(1)}, f32[96,768]{1,0:T(8,128)S(1)}, u32[]{:S(2)}, u32[]{:S(2)}) %collective-permute-start.17) | collective-permute-done | bytes 294944 | tf_op jit(solution)/shard_map/ppermute | solution.py:65
  392.7 17.9 %reduce-scatter.5.cloned.1.call-done = f32[96,1920]{1,0:T(8,128)} async-done(((f32[1536,1920]{1,0:T(8,128)}), f32[96,1920]{1,0:T(8,128)}) %reduce-scatter.5.cloned.1.call-update) | async-done | bytes 737296 | tf_op jit(solution)/shard_map/reduce_scatter | solution.py:617
  416.9 8.7 %collective-permute-done.34 = f32[96,1152]{1,0:T(8,128)S(1)} collective-permute-done((f32[96,1152]{1,0:T(8,128)S(1)}, f32[96,1152]{1,0:T(8,128)S(1)}, u32[]{:S(2)}, u32[]{:S(2)}) %collective-permute-start.34) | collective-permute-done | bytes 442400 | tf_op jit(solution)/shard_map/ppermute | solution.py:65
  425.7 7.2 %collective-permute-done.35 = f32[96,768]{1,0:T(8,128)S(1)} collective-permute-done((f32[96,768]{1,0:T(8,128)S(1)}, f32[96,768]{1,0:T(8,128)S(1)}, u32[]{:S(2)}, u32[]{:S(2)}) %collective-permute-start.35) | collective-permute-done | bytes 294944 | tf_op jit(solution)/shard_map/ppermute | solution.py:65
  434.7 36.0 %collective-permute-done.15 = f32[512,768]{1,0:T(8,128)S(1)} collective-permute-done((f32[512,768]{1,0:T(8,128)}, f32[512,768]{1,0:T(8,128)S(1)}, u32[]{:S(2)}, u32[]{:S(2)}) %collective-permute-start.15) | collective-permute-done | bytes 1572896 | tf_op jit(solution)/shard_map/ppermute | solution.py:65
  470.7 2.9 add_add_fusion
  474.8 2.8 collective-permute-start.10
  477.7 15.7 %collective-permute-done.10 = f32[14,768]{1,0:T(8,128)S(1)} collective-permute-done((f32[14,768]{1,0:T(8,128)S(1)}, f32[14,768]{1,0:T(8,128)S(1)}, u32[]{:S(2)}, u32[]{:S(2)}) %collective-permute-start.10) | collective-permute-done | bytes 43040 | tf_op jit(solution)/shard_map/ppermute | solution.py:65
  496.6 6.1 %collective-permute-done.38 = f32[18,768]{1,0:T(8,128)S(1)} collective-permute-done((f32[18,768]{1,0:T(8,128)S(1)}, f32[18,768]{1,0:T(8,128)S(1)}, u32[]{:S(2)}, u32[]{:S(2)}) %collective-permute-start.38) | collective-permute-done | bytes 55328 | tf_op jit(solution)/shard_map/ppermute | solution.py:652
  502.9 5.5 collective-permute-done.39
  508.5 4.3 collective-permute-done.40
  513.0 6.7 %collective-permute-done.41 = f32[18,768]{1,0:T(8,128)S(1)} collective-permute-done((f32[18,768]{1,0:T(8,128)S(1)}, f32[18,768]{1,0:T(8,128)S(1)}, u32[]{:S(2)}, u32[]{:S(2)}) %collective-permute-start.41) | collective-permute-done | bytes 55328 | tf_op jit(solution)/shard_map/ppermute | solution.py:652
  519.7 4.3 collective-permute-done.42
  529.6 12.0 %place_gradients.2 = (f32[2,1536,768]{2,1,0:T(8,128)}, f32[2,768,1536]{2,1,0:T(8,128)}, f32[2,768,384]{2,1,0:T(8,128)}, f32[2,768,384]{2,1,0:T(8,128)}, f32[2,768,384]{2,1,0:T(8,128)}, /*index=5*/f32[2,384,768]{2,1,0:T(8,128)}) custom-call(f32[16,2,96,1152]{3,2,1,0:T(8,128)} %bitcast.144, f32[16,2,96,1152]{3,2,1,0:T(8,128)} %bitcast.145, ...), custom_call_target="tpu_custom_call" | custom-call | bytes 28311552 | tf_op jit(solution)/shard_map/place_gradients/pallas_call | solution.py:448
  541.6 7.5 %all-gather.13.cloned.1.call-done = f32[3072,1152]{1,0:T(8,128)} async-done(((f32[96,1152]{1,0:T(8,128)}), f32[3072,1152]{1,0:T(8,128)}) %all-gather.13.cloned.1.call-update) | async-done | bytes 14155792 | tf_op jit(solution)/shard_map/all_gather | solution.py:630
  549.1 11.7 %place_gradients.3 = (f32[2,1536,768]{2,1,0:T(8,128)}, f32[2,768,1536]{2,1,0:T(8,128)}, f32[2,768,384]{2,1,0:T(8,128)}, f32[2,768,384]{2,1,0:T(8,128)}, f32[2,768,384]{2,1,0:T(8,128)}, /*index=5*/f32[2,384,768]{2,1,0:T(8,128)}) custom-call(f32[16,2,96,1152]{3,2,1,0:T(8,128)} %bitcast.138, ...), custom_call_target="tpu_custom_call", output_to_operand_aliasing={{0}: (6, {}), {1}: (7, {}), {2}: (8, {}), {3}: (9, {}), {4}... | custom-call | bytes 28311552 | tf_op jit(solution)/shard_map/place_gradients/pallas_call | solution.py:448
  (466 shorter events, 101.8 us)
Async XLA Ops:
  7.2 74.4 %all-gather.9.cloned.1.call-start = ((), (), s32[]{:S(2)}) async-start(), calls=%async_computation.4 | async-start | bytes 9732096 | tf_op jit(solution)/shard_map/all_gather | solution.py:506
  12.7 11.0 %collective-permute-start.1 = (f32[96,768]{1,0:T(8,128)S(1)}, f32[96,768]{1,0:T(8,128)S(1)}, u32[]{:S(2)}, u32[]{:S(2)}) collective-permute-start(f32[96,768]{1,0:T(8,128)S(1)} %get-tuple-element.238), channel_id=1, source_target_pairs={{0,1},{1,0},{2,3},{3,2},{4,5},{5,4},{6,7},{7,6},{8,9},{9,8},{10,11... | collective-permute-start | bytes 884744 | tf_op jit(solution)/shard_map/ppermute | solution.py:65
  24.4 121.5 %all-gather.11.cloned.1.call-start = ((), (), s32[]{:S(2)}) async-start(), calls=%async_computation.5 | async-start | bytes 9732096 | tf_op jit(solution)/shard_map/all_gather | solution.py:587
  38.5 22.9 %collective-permute-start = (f32[256,768]{1,0:T(8,128)S(1)}, f32[256,768]{1,0:T(8,128)S(1)}, u32[]{:S(2)}, u32[]{:S(2)}) collective-permute-start(f32[256,768]{1,0:T(8,128)S(1)} %get-tuple-element.94), channel_id=1, source_target_pairs={{0,1},{1,0},{2,3},{3,2},{4,5},{5,4},{6,7},{7,6},{8,9},{9,8},{10,11... | collective-permute-start | bytes 2359304 | tf_op jit(solution)/shard_map/ppermute | solution.py:65
  41.8 19.0 %collective-permute-start.2 = (f32[2,1536]{1,0:T(2,128)S(1)}, f32[2,1536]{1,0:T(2,128)S(1)}, u32[]{:S(2)}, u32[]{:S(2)}) collective-permute-start(f32[2,1536]{1,0:T(2,128)S(1)} %convert_element_type.141), channel_id=1, source_target_pairs={{0,1},{1,0},{2,3},{3,2},{4,5},{5,4},{6,7},{7,6},{8,9},{9,8},{10,11... | collective-permute-start | bytes 36872 | tf_op jit(solution)/shard_map/ppermute | solution.py:65
  42.1 48.7 %collective-permute-start.3 = (f32[96,768]{1,0:T(8,128)}, f32[96,768]{1,0:T(8,128)}, u32[]{:S(2)}, u32[]{:S(2)}) collective-permute-start(f32[96,768]{1,0:T(8,128)} %get-tuple-element.97), channel_id=1, source_target_pairs={{0,1},{1,0},{2,3},{3,2},{4,5},{5,4},{6,7},{7,6},{8,9},{9,8},{10,11... | collective-permute-start | bytes 884744 | tf_op jit(solution)/shard_map/ppermute | solution.py:65
  47.9 42.1 %copy-start.60 = (f32[768]{0:T(1024)}, f32[768]{0:T(1024)S(1)}, u32[]{:S(2)}) copy-start(f32[768]{0:T(1024)S(1)} %get-tuple-element.289) | copy-start | bytes 9220
  47.9 42.1 %copy-start.70 = (f32[768]{0:T(1024)}, f32[768]{0:T(1024)S(1)}, u32[]{:S(2)}) copy-start(f32[768]{0:T(1024)S(1)} %get-tuple-element.188) | copy-start | bytes 9220
  90.9 211.9 %reduce-scatter.3.cloned.1.call-start = ((), (), s32[]{:S(2)}) async-start(), calls=%async_computation.2 | async-start | bytes 10027008 | tf_op jit(solution)/shard_map/reduce_scatter | solution.py:605
  90.9 21.3 %collective-permute-start.4 = (f32[256,768]{1,0:T(8,128)S(1)}, f32[256,768]{1,0:T(8,128)S(1)}, u32[]{:S(2)}, u32[]{:S(2)}) collective-permute-start(f32[256,768]{1,0:T(8,128)S(1)} %fusion.62), channel_id=1, source_target_pairs={{0,1},{1,0},{2,3},{3,2},{4,5},{5,4},{6,7},{7,6},{8,9},{9,8},{10,11... | collective-permute-start | bytes 2359304 | tf_op jit(solution)/shard_map/ppermute | solution.py:65
  127.1 23.5 %collective-permute-start.5 = (f32[256,768]{1,0:T(8,128)}, f32[256,768]{1,0:T(8,128)}, u32[]{:S(2)}, u32[]{:S(2)}) collective-permute-start(f32[256,768]{1,0:T(8,128)} %get-tuple-element.100), channel_id=1, source_target_pairs={{0,1},{1,0},{2,3},{3,2},{4,5},{5,4},{6,7},{7,6},{8,9},{9,8},{10,11... | collective-permute-start | bytes 2359304 | tf_op jit(solution)/shard_map/ppermute | solution.py:65
  168.0 8.1 %collective-permute-start.8 = (f32[1536,768]{1,0:T(8,128)}, f32[1536,768]{1,0:T(8,128)S(1)}, u32[]{:S(2)}, u32[]{:S(2)}) collective-permute-start(f32[1536,768]{1,0:T(8,128)} %feed_sums.9), channel_id=1, source_target_pairs={{0,2},{2,0},{1,3},{3,1},{4,6},{6,4},{5,7},{7,5},{8,10},{10,8},{9,1... | collective-permute-start | bytes 14155784 | tf_op jit(solution)/shard_map/ppermute | solution.py:65
  171.6 12.4 %collective-permute-start.7 = (f32[1536,768]{1,0:T(8,128)}, f32[1536,768]{1,0:T(8,128)}, u32[]{:S(2)}, u32[]{:S(2)}) collective-permute-start(f32[1536,768]{1,0:T(8,128)} %feed_sums.8), channel_id=1, source_target_pairs={{0,2},{2,0},{1,3},{3,1},{4,6},{6,4},{5,7},{7,5},{8,10},{10,8},{9,1... | collective-permute-start | bytes 14155784 | tf_op jit(solution)/shard_map/ppermute | solution.py:65
  189.6 221.0 %reduce-scatter.5.cloned.1.call-start = ((), (), s32[]{:S(2)}) async-start(), calls=%async_computation.3 | async-start | bytes 12533760 | tf_op jit(solution)/shard_map/reduce_scatter | solution.py:617
  197.4 21.7 %collective-permute-start.6 = (f32[256,768]{1,0:T(8,128)}, f32[256,768]{1,0:T(8,128)}, u32[]{:S(2)}, u32[]{:S(2)}) collective-permute-start(f32[256,768]{1,0:T(8,128)} %get-tuple-element.209), channel_id=1, source_target_pairs={{0,1},{1,0},{2,3},{3,2},{4,5},{5,4},{6,7},{7,6},{8,9},{9,8},{10,11... | collective-permute-start | bytes 2359304 | tf_op jit(solution)/shard_map/ppermute | solution.py:65
  219.1 44.1 %slice-start.2 = ((s8[4718592]{0:T(1024)(128)(4,1)}), s8[4194304]{0:T(1024)(128)(4,1)S(1)}, s32[]{:S(2)}) async-start(s8[4718592]{0:T(1024)(128)(4,1)} %bitcast.136), calls=%async_computation.10 | async-start | bytes 8388608
  240.0 20.5 %collective-permute-start.9 = (f32[256,768]{1,0:T(8,128)S(1)}, f32[256,768]{1,0:T(8,128)S(1)}, u32[]{:S(2)}, u32[]{:S(2)}) collective-permute-start(f32[256,768]{1,0:T(8,128)S(1)} %constant_dynamic-slice_fusion), channel_id=1, source_target_pairs={{0,1},{1,0},{2,3},{3,2},{4,5},{5,4},{6,7},{7,6},{8,9},{9,8},{10,11... | collective-permute-start | bytes 2359304 | tf_op jit(solution)/shard_map/ppermute | solution.py:65
  268.9 15.5 %collective-permute-start.13 = (f32[1536,768]{1,0:T(8,128)}, f32[1536,768]{1,0:T(8,128)}, u32[]{:S(2)}, u32[]{:S(2)}) collective-permute-start(f32[1536,768]{1,0:T(8,128)} %feed_sums.13), channel_id=1, source_target_pairs={{0,2},{2,0},{1,3},{3,1},{4,6},{6,4},{5,7},{7,5},{8,10},{10,8},{9,1... | collective-permute-start | bytes 14155784 | tf_op jit(solution)/shard_map/ppermute | solution.py:65
  273.9 16.3 %collective-permute-start.12 = (f32[1536,768]{1,0:T(8,128)}, f32[1536,768]{1,0:T(8,128)}, u32[]{:S(2)}, u32[]{:S(2)}) collective-permute-start(f32[1536,768]{1,0:T(8,128)} %feed_sums.12), channel_id=1, source_target_pairs={{0,2},{2,0},{1,3},{3,1},{4,6},{6,4},{5,7},{7,5},{8,10},{10,8},{9,1... | collective-permute-start | bytes 14155784 | tf_op jit(solution)/shard_map/ppermute | solution.py:65
  276.3 19.5 %collective-permute-start.11 = (f32[1536,384]{1,0:T(8,128)S(1)}, f32[1536,384]{1,0:T(8,128)S(1)}, u32[]{:S(2)}, u32[]{:S(2)}) collective-permute-start(f32[1536,384]{1,0:T(8,128)S(1)} %attention_sums.4), channel_id=1, source_target_pairs={{0,2},{2,0},{1,3},{3,1},{4,6},{6,4},{5,7},{7,5},{8,10},{10,8},{9,1... | collective-permute-start | bytes 7077896 | tf_op jit(solution)/shard_map/ppermute | solution.py:65
  281.0 21.8 %collective-permute-start.14 = (f32[256,768]{1,0:T(8,128)S(1)}, f32[256,768]{1,0:T(8,128)}, u32[]{:S(2)}, u32[]{:S(2)}) collective-permute-start(f32[256,768]{1,0:T(8,128)S(1)} %multiply_multiply_fusion.4), channel_id=1, source_target_pairs={{0,1},{1,0},{2,3},{3,2},{4,5},{5,4},{6,7},{7,6},{8,9},{9,8},{10,11... | collective-permute-start | bytes 2359304 | tf_op jit(solution)/shard_map/ppermute | solution.py:65
  302.9 226.7 %all-gather.15.cloned.1.call-start = ((), (), s32[]{:S(2)}) async-start(), calls=%async_computation.7 | async-start | bytes 14598144 | tf_op jit(solution)/shard_map/all_gather | solution.py:630
  322.0 4.9 collective-permute-start.20
  330.9 17.6 %collective-permute-start.26 = (f32[4,48,384]{2,1,0:T(8,128)S(1)}, f32[4,48,384]{2,1,0:T(8,128)S(1)}, u32[]{:S(2)}, u32[]{:S(2)}) collective-permute-start(f32[4,48,384]{2,1,0:T(8,128)S(1)} %get-tuple-element.226), channel_id=1, source_target_pairs={{0,64},{32,96},{64,0},{96,32},{1,65},{33,97},{65,1},{97,33},{2,66}... | collective-permute-start | bytes 884744 | tf_op jit(solution)/shard_map/ppermute | solution.py:83
  333.8 23.8 %collective-permute-start.25 = (f32[4,48,384]{2,1,0:T(8,128)S(1)}, f32[4,48,384]{2,1,0:T(8,128)S(1)}, u32[]{:S(2)}, u32[]{:S(2)}) collective-permute-start(f32[4,48,384]{2,1,0:T(8,128)S(1)} %get-tuple-element.227), channel_id=1, source_target_pairs={{0,96},{32,0},{64,32},{96,64},{1,97},{33,1},{65,33},{97,65},{2,98}... | collective-permute-start | bytes 884744 | tf_op jit(solution)/shard_map/ppermute | solution.py:83
  334.9 22.6 %collective-permute-start.24 = (f32[4,48,384]{2,1,0:T(8,128)S(1)}, f32[4,48,384]{2,1,0:T(8,128)S(1)}, u32[]{:S(2)}, u32[]{:S(2)}) collective-permute-start(f32[4,48,384]{2,1,0:T(8,128)S(1)} %get-tuple-element.228), channel_id=1, source_target_pairs={{0,32},{32,64},{64,96},{96,0},{1,33},{33,65},{65,97},{97,1},{2,34}... | collective-permute-start | bytes 884744 | tf_op jit(solution)/shard_map/ppermute | solution.py:83
  335.9 21.7 %collective-permute-start.23 = (f32[4,48,384]{2,1,0:T(8,128)S(1)}, f32[4,48,384]{2,1,0:T(8,128)S(1)}, u32[]{:S(2)}, u32[]{:S(2)}) collective-permute-start(f32[4,48,384]{2,1,0:T(8,128)S(1)} %get-tuple-element.230), channel_id=1, source_target_pairs={{0,8},{4,12},{8,0},{12,4},{1,9},{5,13},{9,1},{13,5},{2,10},{6,14},... | collective-permute-start | bytes 884744 | tf_op jit(solution)/shard_map/ppermute | solution.py:83
  337.4 21.0 %collective-permute-start.22 = (f32[4,48,384]{2,1,0:T(8,128)S(1)}, f32[4,48,384]{2,1,0:T(8,128)S(1)}, u32[]{:S(2)}, u32[]{:S(2)}) collective-permute-start(f32[4,48,384]{2,1,0:T(8,128)S(1)} %get-tuple-element.231), channel_id=1, source_target_pairs={{0,12},{4,0},{8,4},{12,8},{1,13},{5,1},{9,5},{13,9},{2,14},{6,2},{... | collective-permute-start | bytes 884744 | tf_op jit(solution)/shard_map/ppermute | solution.py:83
  348.5 15.3 %collective-permute-start.21 = (f32[4,48,384]{2,1,0:T(8,128)S(1)}, f32[4,48,384]{2,1,0:T(8,128)S(1)}, u32[]{:S(2)}, u32[]{:S(2)}) collective-permute-start(f32[4,48,384]{2,1,0:T(8,128)S(1)} %get-tuple-element.232), channel_id=1, source_target_pairs={{0,4},{4,8},{8,12},{12,0},{1,5},{5,9},{9,13},{13,1},{2,6},{6,10},{... | collective-permute-start | bytes 884744 | tf_op jit(solution)/shard_map/ppermute | solution.py:83
  363.9 7.6 %collective-permute-start.29 = (f32[48,384]{1,0:T(8,128)S(1)}, f32[48,384]{1,0:T(8,128)S(1)}, u32[]{:S(2)}, u32[]{:S(2)}) collective-permute-start(f32[48,384]{1,0:T(8,128)S(1)} %get-tuple-element.244), channel_id=1, source_target_pairs={{0,64},{32,96},{64,0},{96,32},{1,65},{33,97},{65,1},{97,33},{2,66}... | collective-permute-start | bytes 221192 | tf_op jit(solution)/shard_map/ppermute | solution.py:83
  366.2 7.7 %collective-permute-start.28 = (f32[48,384]{1,0:T(8,128)S(1)}, f32[48,384]{1,0:T(8,128)S(1)}, u32[]{:S(2)}, u32[]{:S(2)}) collective-permute-start(f32[48,384]{1,0:T(8,128)S(1)} %get-tuple-element.245), channel_id=1, source_target_pairs={{0,96},{32,0},{64,32},{96,64},{1,97},{33,1},{65,33},{97,65},{2,98}... | collective-permute-start | bytes 221192 | tf_op jit(solution)/shard_map/ppermute | solution.py:83
  368.1 8.2 %collective-permute-start.27 = (f32[48,384]{1,0:T(8,128)S(1)}, f32[48,384]{1,0:T(8,128)S(1)}, u32[]{:S(2)}, u32[]{:S(2)}) collective-permute-start(f32[48,384]{1,0:T(8,128)S(1)} %get-tuple-element.246), channel_id=1, source_target_pairs={{0,32},{32,64},{64,96},{96,0},{1,33},{33,65},{65,97},{97,1},{2,34}... | collective-permute-start | bytes 221192 | tf_op jit(solution)/shard_map/ppermute | solution.py:83
  368.5 10.0 %collective-permute-start.32 = (f32[48,384]{1,0:T(8,128)S(1)}, f32[48,384]{1,0:T(8,128)S(1)}, u32[]{:S(2)}, u32[]{:S(2)}) collective-permute-start(f32[48,384]{1,0:T(8,128)S(1)} %get-tuple-element.240), channel_id=1, source_target_pairs={{0,8},{4,12},{8,0},{12,4},{1,9},{5,13},{9,1},{13,5},{2,10},{6,14},... | collective-permute-start | bytes 221192 | tf_op jit(solution)/shard_map/ppermute | solution.py:83
  369.9 9.2 %collective-permute-start.31 = (f32[48,384]{1,0:T(8,128)S(1)}, f32[48,384]{1,0:T(8,128)S(1)}, u32[]{:S(2)}, u32[]{:S(2)}) collective-permute-start(f32[48,384]{1,0:T(8,128)S(1)} %get-tuple-element.241), channel_id=1, source_target_pairs={{0,12},{4,0},{8,4},{12,8},{1,13},{5,1},{9,5},{13,9},{2,14},{6,2},{... | collective-permute-start | bytes 221192 | tf_op jit(solution)/shard_map/ppermute | solution.py:83
  371.4 7.7 %collective-permute-start.30 = (f32[48,384]{1,0:T(8,128)S(1)}, f32[48,384]{1,0:T(8,128)S(1)}, u32[]{:S(2)}, u32[]{:S(2)}) collective-permute-start(f32[48,384]{1,0:T(8,128)S(1)} %get-tuple-element.242), channel_id=1, source_target_pairs={{0,4},{4,8},{8,12},{12,0},{1,5},{5,9},{9,13},{13,1},{2,6},{6,10},{... | collective-permute-start | bytes 221192 | tf_op jit(solution)/shard_map/ppermute | solution.py:83
  373.8 17.2 %collective-permute-start.19 = (f32[96,768]{1,0:T(8,128)S(1)}, f32[96,768]{1,0:T(8,128)S(1)}, u32[]{:S(2)}, u32[]{:S(2)}) collective-permute-start(f32[96,768]{1,0:T(8,128)S(1)} %get-tuple-element.237), channel_id=1, source_target_pairs={{0,17},{17,0},{1,16},{16,1},{2,19},{19,2},{3,18},{18,3},{4,21},{21... | collective-permute-start | bytes 884744 | tf_op jit(solution)/shard_map/ppermute | solution.py:623
  376.3 14.7 %collective-permute-start.18 = (f32[96,768]{1,0:T(8,128)S(1)}, f32[96,768]{1,0:T(8,128)S(1)}, u32[]{:S(2)}, u32[]{:S(2)}) collective-permute-start(f32[96,768]{1,0:T(8,128)S(1)} %get-tuple-element.237), channel_id=1, source_target_pairs={{0,1},{1,0},{2,3},{3,2},{4,5},{5,4},{6,7},{7,6},{8,9},{9,8},{10,11... | collective-permute-start | bytes 884744 | tf_op jit(solution)/shard_map/ppermute | solution.py:65
  378.6 12.5 %collective-permute-start.17 = (f32[96,768]{1,0:T(8,128)S(1)}, f32[96,768]{1,0:T(8,128)S(1)}, u32[]{:S(2)}, u32[]{:S(2)}) collective-permute-start(f32[96,768]{1,0:T(8,128)S(1)} %get-tuple-element.236), channel_id=1, source_target_pairs={{0,16},{16,0},{1,17},{17,1},{2,18},{18,2},{3,19},{19,3},{4,20},{20... | collective-permute-start | bytes 884744 | tf_op jit(solution)/shard_map/ppermute | solution.py:65
  379.2 13.4 %collective-permute-start.33 = (f32[96,384]{1,0:T(8,128)S(1)}, f32[96,384]{1,0:T(8,128)S(1)}, u32[]{:S(2)}, u32[]{:S(2)}) collective-permute-start(f32[96,384]{1,0:T(8,128)S(1)} %pad_maximum_fusion.3), channel_id=1, source_target_pairs={{0,16},{16,0},{1,17},{17,1},{2,18},{18,2},{3,19},{19,3},{4,20},{20... | collective-permute-start | bytes 442376 | tf_op jit(solution)/shard_map/ppermute | solution.py:65
  411.4 137.7 %all-gather.13.cloned.1.call-start = ((), (), s32[]{:S(2)}) async-start(), calls=%async_computation.6 | async-start | bytes 14598144 | tf_op jit(solution)/shard_map/all_gather | solution.py:630
  412.4 13.2 %collective-permute-start.34 = (f32[96,1152]{1,0:T(8,128)S(1)}, f32[96,1152]{1,0:T(8,128)S(1)}, u32[]{:S(2)}, u32[]{:S(2)}) collective-permute-start(f32[96,1152]{1,0:T(8,128)S(1)} %pad_maximum_fusion), channel_id=1, source_target_pairs={{0,16},{16,0},{1,17},{17,1},{2,18},{18,2},{3,19},{19,3},{4,20},{20... | collective-permute-start | bytes 1327112 | tf_op jit(solution)/shard_map/ppermute | solution.py:65
  414.1 11.6 %collective-permute-start.36 = (f32[96,768]{1,0:T(8,128)S(1)}, f32[96,768]{1,0:T(8,128)S(1)}, u32[]{:S(2)}, u32[]{:S(2)}) collective-permute-start(f32[96,768]{1,0:T(8,128)S(1)} %get-tuple-element.234), channel_id=1, source_target_pairs={{0,17},{17,0},{1,16},{16,1},{2,19},{19,2},{3,18},{18,3},{4,21},{21... | collective-permute-start | bytes 884744 | tf_op jit(solution)/shard_map/ppermute | solution.py:623
  416.2 16.7 %collective-permute-start.35 = (f32[96,768]{1,0:T(8,128)S(1)}, f32[96,768]{1,0:T(8,128)S(1)}, u32[]{:S(2)}, u32[]{:S(2)}) collective-permute-start(f32[96,768]{1,0:T(8,128)S(1)} %get-tuple-element.234), channel_id=1, source_target_pairs={{0,1},{1,0},{2,3},{3,2},{4,5},{5,4},{6,7},{7,6},{8,9},{9,8},{10,11... | collective-permute-start | bytes 884744 | tf_op jit(solution)/shard_map/ppermute | solution.py:65
  425.7 45.1 %copy-start.47 = (f32[256,768]{1,0:T(8,128)S(1)}, f32[256,768]{1,0:T(8,128)}, u32[]{:S(2)}) copy-start(f32[256,768]{1,0:T(8,128)} %copy-done.46) | copy-start | bytes 2359300
  425.7 45.1 %copy-start.49 = (f32[256,768]{1,0:T(8,128)S(1)}, f32[256,768]{1,0:T(8,128)}, u32[]{:S(2)}) copy-start(f32[256,768]{1,0:T(8,128)} %copy-done.48) | copy-start | bytes 2359300
  433.8 40.7 %copy-start.110 = (f32[1536]{0:T(1024)S(1)}, f32[1536]{0:T(1024)}, u32[]{:S(2)}) copy-start(f32[1536]{0:T(1024)} %get-tuple-element.281) | copy-start | bytes 18436
  433.8 40.7 %copy-start.118 = (f32[768]{0:T(1024)S(1)}, f32[768]{0:T(1024)}, u32[]{:S(2)}) copy-start(f32[768]{0:T(1024)} %get-tuple-element.169) | copy-start | bytes 9220
  433.9 40.7 %copy-start.117 = (f32[768]{0:T(1024)S(1)}, f32[768]{0:T(1024)}, u32[]{:S(2)}) copy-start(f32[768]{0:T(1024)} %get-tuple-element.181) | copy-start | bytes 9220
  433.9 40.7 %copy-start.89 = (f32[768]{0:T(1024)S(1)}, f32[768]{0:T(1024)}, u32[]{:S(2)}) copy-start(f32[768]{0:T(1024)} %get-tuple-element.199) | copy-start | bytes 9220
  433.9 40.7 %copy-start.23 = (f32[1,384]{1,0:T(1,128)S(1)}, f32[1,384]{1,0:T(1,128)}, u32[]{:S(2)}) copy-start(f32[1,384]{1,0:T(1,128)} %copy-done.22) | copy-start | bytes 4612
  433.9 40.8 %copy-start.91 = (f32[768]{0:T(1024)S(1)}, f32[768]{0:T(1024)}, u32[]{:S(2)}) copy-start(f32[768]{0:T(1024)} %get-tuple-element.171) | copy-start | bytes 9220
  433.9 40.8 %copy-start.112 = (f32[1536]{0:T(1024)S(1)}, f32[1536]{0:T(1024)}, u32[]{:S(2)}) copy-start(f32[1536]{0:T(1024)} %get-tuple-element.279) | copy-start | bytes 18436
  433.9 40.8 %copy-start.90 = (f32[768]{0:T(1024)S(1)}, f32[768]{0:T(1024)}, u32[]{:S(2)}) copy-start(f32[768]{0:T(1024)} %get-tuple-element.182) | copy-start | bytes 9220
  433.9 40.8 %copy-start.120 = (f32[768]{0:T(1024)S(1)}, f32[768]{0:T(1024)}, u32[]{:S(2)}) copy-start(f32[768]{0:T(1024)} %get-tuple-element.168) | copy-start | bytes 9220
  433.9 40.8 %copy-start.119 = (f32[768]{0:T(1024)S(1)}, f32[768]{0:T(1024)}, u32[]{:S(2)}) copy-start(f32[768]{0:T(1024)} %get-tuple-element.180) | copy-start | bytes 9220
  433.9 36.8 %collective-permute-start.15 = (f32[512,768]{1,0:T(8,128)}, f32[512,768]{1,0:T(8,128)S(1)}, u32[]{:S(2)}, u32[]{:S(2)}) collective-permute-start(f32[512,768]{1,0:T(8,128)} %get-tuple-element.125), channel_id=1, source_target_pairs={{0,1},{1,0},{2,3},{3,2},{4,5},{5,4},{6,7},{7,6},{8,9},{9,8},{10,11... | collective-permute-start | bytes 4718600 | tf_op jit(solution)/shard_map/ppermute | solution.py:65
  473.6 20.0 %collective-permute-start.16 = (f32[256,768]{1,0:T(8,128)S(1)}, f32[256,768]{1,0:T(8,128)S(1)}, u32[]{:S(2)}, u32[]{:S(2)}) collective-permute-start(f32[256,768]{1,0:T(8,128)S(1)} %copy-done.52), channel_id=1, source_target_pairs={{0,1},{1,0},{2,3},{3,2},{4,5},{5,4},{6,7},{7,6},{8,9},{9,8},{10,11... | collective-permute-start | bytes 2359304 | tf_op jit(solution)/shard_map/ppermute | solution.py:65
  474.8 18.6 %collective-permute-start.10 = (f32[14,768]{1,0:T(8,128)S(1)}, f32[14,768]{1,0:T(8,128)S(1)}, u32[]{:S(2)}, u32[]{:S(2)}) collective-permute-start(f32[14,768]{1,0:T(8,128)S(1)} %concatenate.44), channel_id=1, source_target_pairs={{0,1},{1,0},{2,3},{3,2},{4,5},{5,4},{6,7},{7,6},{8,9},{9,8},{10,11... | collective-permute-start | bytes 129032 | tf_op jit(solution)/shard_map/ppermute | solution.py:65
  495.3 1.3 collective-permute-start.37
  496.6 6.2 %collective-permute-start.38 = (f32[18,768]{1,0:T(8,128)S(1)}, f32[18,768]{1,0:T(8,128)S(1)}, u32[]{:S(2)}, u32[]{:S(2)}) collective-permute-start(f32[18,768]{1,0:T(8,128)S(1)} %add.533), channel_id=1, source_target_pairs={{0,4},{4,0},{8,12},{12,8},{1,5},{5,1},{9,13},{13,9},{2,6},{6,2},{1... | collective-permute-start | bytes 165896 | tf_op jit(solution)/shard_map/ppermute | solution.py:652
  502.8 5.6 collective-permute-start.39
  508.4 4.4 collective-permute-start.40
  512.9 6.8 %collective-permute-start.41 = (f32[18,768]{1,0:T(8,128)S(1)}, f32[18,768]{1,0:T(8,128)S(1)}, u32[]{:S(2)}, u32[]{:S(2)}) collective-permute-start(f32[18,768]{1,0:T(8,128)S(1)} %add.536), channel_id=1, source_target_pairs={{32,64},{64,32},{96,0},{0,96},{33,65},{65,33},{97,1},{1,97},{34,66... | collective-permute-start | bytes 165896 | tf_op jit(solution)/shard_map/ppermute | solution.py:652
  519.7 4.4 collective-permute-start.42
  (117 other events, 965.6 us)
Sparse Core Ops, SparseCore 0:
  24.5 57.0 all-gather.8
  91.0 54.9 all-gather.10
  189.7 87.1 reduce-scatter.2
  303.0 107.5 reduce-scatter.4
  413.2 65.6 all-gather.14
  481.0 68.0 all-gather.12

commit v6 on v3

--- a/solution.py
+++ b/solution.py
@@ -117,7 +117,7 @@
 
 
 def attend_kernel(
-    length_ref,
+    place_ref,
     slot_ref,
     query_weight,
     query_bias,
@@ -130,17 +130,18 @@
     value_ref,
     mixture_ref,
     logsum_ref,
-    share_ref,
+    own_ref,
+    sent_ref,
 ):
     slots = slot_ref[...]
     query_ref[...] = (dot(slots, query_weight[0]) + query_bias[...]).astype(BF16)
     key_ref[...] = dot(slots, key_weight[0]).astype(BF16)
     value_ref[...] = (dot(slots, value_weight[0]) + value_bias[...]).astype(BF16)
     count = slots.shape[0]
-    valid = lax.broadcasted_iota(jnp.int32, (count, count), 0) < length_ref[0]
+    valid = lax.broadcasted_iota(jnp.int32, (count, count), 0) < place_ref[0]
     for head in range(2):
         cut = slice(head * HEAD_DIM, (head + 1) * HEAD_DIM)
-        scores = across_lanes(key_ref[:, cut], query_ref[:, cut]) * HEAD_DIM**-0.5
+        scores = across_lanes(key_ref[:, cut], query_ref[:, cut] * HEAD_DIM**-0.5)
         scores = jnp.where(valid, scores, -1e30)
         highest = jnp.max(scores, axis=0, keepdims=True)
         raised = jnp.exp(scores - highest)
@@ -148,18 +149,21 @@
         probs = (raised * (1.0 / totals)).astype(BF16)
         mixture_ref[:, cut] = t_dot_in_kernel(probs, value_ref[:, cut]).astype(BF16)
         logsum_ref[0, head : head + 1, :] = highest + jnp.log(totals)
-    share = dot(mixture_ref[...], output_weight[0])
-
-    @pl.when(pl.program_id(0) == 0)
-    def _():
-        share_ref[...] = share
-
-    @pl.when(pl.program_id(0) != 0)
-    def _():
-        share_ref[...] += share
-
-
-def attend(layer, length, slots, query_weight, query_bias, key_weight, value_weight, value_bias, output_weight):
+    half = count // 2
+    for side, share_ref in ((place_ref[1], own_ref), (1 - place_ref[1], sent_ref)):
+        rows = mixture_ref[pl.ds(pl.multiple_of(side * half, half), half), :]
+        share = dot(rows, output_weight[0])
+
+        @pl.when(pl.program_id(0) == 0)
+        def _():
+            share_ref[...] = share
+
+        @pl.when(pl.program_id(0) != 0)
+        def _():
+            share_ref[...] += share
+
+
+def attend(layer, length, side, slots, query_weight, query_bias, key_weight, value_weight, value_bias, output_weight):
     count, width = slots.shape
     heads = query_weight.shape[2]
     pair = 2 * HEAD_DIM
@@ -174,9 +178,12 @@
         grid=(steps,),
         in_specs=[SCALAR, whole, weight, bias, weight, weight, bias]
         + [pl.BlockSpec((1, pair, width), lambda i: (layer, i, 0))],
-        out_specs=[part] * 4 + [pl.BlockSpec((1, 2, count), lambda i: (i, 0, 0)), whole],
+        out_specs=[part] * 4
+        + [pl.BlockSpec((1, 2, count), lambda i: (i, 0, 0))]
+        + [pl.BlockSpec((count // 2, width), lambda i: (0, 0))] * 2,
         out_shape=[part_shape] * 4
-        + [jax.ShapeDtypeStruct((steps, 2, count), F32), jax.ShapeDtypeStruct((count, width), F32)],
+        + [jax.ShapeDtypeStruct((steps, 2, count), F32)]
+        + [jax.ShapeDtypeStruct((count // 2, width), F32)] * 2,
         compiler_params=LIMIT,
         cost_estimate=pl.CostEstimate(
             flops=8 * count * width * heads + 4 * count * count * heads,
@@ -184,7 +191,7 @@
             transcendentals=count * count * heads // HEAD_DIM,
         ),
         name="attend",
-    )(length.reshape(1), slots, query_weight, query_bias, key_weight, value_weight, value_bias, output_weight)
+    )(jnp.stack([length, side]), slots, query_weight, query_bias, key_weight, value_weight, value_bias, output_weight)
 
 
 def attend_back_kernel(
@@ -212,7 +219,7 @@
     for head in range(2):
         cut = slice(head * HEAD_DIM, (head + 1) * HEAD_DIM)
         queries, keys, grad = query_ref[:, cut], key_ref[:, cut], grads[:, cut]
-        scores = jnp.where(valid, across_lanes(keys, queries) * scale, -1e30)
+        scores = jnp.where(valid, across_lanes(keys, queries * scale), -1e30)
         probs = jnp.exp(scores - logsum_ref[0, head : head + 1, :])
         grad_probs = across_lanes(value_ref[:, cut], grad)
         inner = jnp.sum(probs * grad_probs, axis=0, keepdims=True)
@@ -356,54 +363,59 @@
     write(3, mixture_ref, grad_ref)
 
 
-def attention_sums(part, lows, mixture, rounded, attended_low, received=None, columns=None, into=None):
+def attention_sums(part, lows, mixture, rounded, attended_low, received=None, into=None, place=0):
     slots, heads = mixture.shape
     half = rounded.shape[1] // 2
     left = pl.BlockSpec((slots, heads), lambda i: (0, 0))
     right = pl.BlockSpec((slots, half), lambda i: (0, i // 2))
     rows = pl.BlockSpec((heads, half), lambda i: (i, 0))
     more = [item for item in (received, into) if item is not None]
-    place = 0 if into is None else 1
-    shape = (4 * heads, half if columns is None else columns)
+    shape = (4 * heads, half) if into is None else into.shape
     return pl.pallas_call(
         lambda *refs: attention_sums_kernel(received is not None, *refs),
         grid=(4,),
         in_specs=[SCALAR] + [left] * 4 + [right] * 2 + [rows, pl.BlockSpec(memory_space=pl.ANY)][: len(more)],
         out_specs=pl.BlockSpec((heads, half), lambda i: (i, place)),
         out_shape=jax.ShapeDtypeStruct(shape, F32),
-        input_output_aliases={8: 0} if place else {},
+        input_output_aliases={} if into is None else {8: 0},
         compiler_params=LIMIT,
         cost_estimate=pl.CostEstimate(flops=8 * slots * heads * half, bytes_accessed=16 * heads * half, transcendentals=0),
         name="attention_sums",
     )(part.reshape(1), *lows, mixture, rounded, attended_low, *more)
 
 
-def sort_kernel(piece_ref, down_ref, up_ref):
-    chips, _, rows, width = piece_ref.shape
+def sort_kernel(units_rows, piece_ref, down_ref, up_ref, *output_refs):
+    chips, _, _, width = piece_ref.shape
+    rows = units_rows
     for i in range(chips):
-        down_ref[i * rows : (i + 1) * rows, :] = piece_ref[i, 0].astype(BF16)
-        up = piece_ref[i, 1].astype(BF16)
+        down_ref[i * rows : (i + 1) * rows, :] = piece_ref[i, 0, :rows].astype(BF16)
+        up = piece_ref[i, 1, :rows].astype(BF16)
         half = rows // 2
         up_ref[i * half : (i + 1) * half, :width] = up[:half]
         up_ref[i * half : (i + 1) * half, width:] = up[half:]
-
-
-def sort_weights(gathered):
+    for output_ref in output_refs:
+        output_ref[...] = piece_ref[:, 0, rows:].reshape(output_ref.shape).astype(BF16)
+
+
+def sort_weights(gathered, units):
     chips, _, rows, width = gathered.shape
     step = 4
-    units = chips * rows
+    heads = chips * rows - units
+    more = 1 if heads else 0
     return pl.pallas_call(
-        sort_kernel,
+        lambda *refs: sort_kernel(units // chips, *refs),
         grid=(chips // step,),
         in_specs=[pl.BlockSpec((step, 2, rows, width), lambda i: (i, 0, 0, 0))],
         out_specs=[
-            pl.BlockSpec((step * rows, width), lambda i: (i, 0)),
-            pl.BlockSpec((step * rows // 2, units), lambda i: (i, 0)),
-        ],
+            pl.BlockSpec((units * step // chips, width), lambda i: (i, 0)),
+            pl.BlockSpec((width * step // chips, units), lambda i: (i, 0)),
+        ]
+        + [pl.BlockSpec((heads * step // chips, width), lambda i: (i, 0))] * more,
         out_shape=[
             jax.ShapeDtypeStruct((units, width), BF16),
             jax.ShapeDtypeStruct((width, units), BF16),
-        ],
+        ]
+        + [jax.ShapeDtypeStruct((heads, width), BF16)] * more,
         compiler_params=LIMIT,
         cost_estimate=pl.CostEstimate(flops=0, bytes_accessed=12 * units * width, transcendentals=0),
         name="sort_weights",
@@ -502,16 +514,25 @@
 
     rows_down = units // 16
     pieces = weight_pieces(chip, core, down_weight, up_weight)
-    gathered1, pieces2 = lax.all_gather(swap(pieces[0], "h"), PLANE + ("c",)), pieces[1]
+    pieces2 = jnp.concatenate([pieces[1], piece(output_weight[1], chip, columns // 16).astype(F32)])
+    pieces1, pieces2 = together(swap(pieces[0], "h"), pieces2)
+    gathered1 = lax.all_gather(pieces1, PLANE + ("c",))
+    pieces2 = swap(pieces2, "h")
     peer_up_bias = swap(up_bias.astype(F32), "h")
 
     def own_slots(values):
         return piece(values, side, half_slots)
 
+    def feed_weights_back(saved, pre_lows, ffn_low, columns):
+        actives, hidden_low = saved[3], saved[4]
+        received = swap(feed_sums(1 - core, actives, pre_lows, ffn_low, hidden_low, 2 * width), "c")
+        return feed_sums(core, actives, pre_lows, ffn_low, hidden_low, columns, received)
+
     def attention_forward(layer, rounded):
-        *attention, share = attend(
+        *attention, share, sent = attend(
             layer,
             length,
+            side,
             rounded,
             query_weight,
             query_bias[layer].astype(F32)[None],
@@ -520,7 +541,7 @@
             value_bias[layer].astype(F32)[None],
             output_weight,
         )
-        return attention, own_slots(share), piece(share, 1 - side, half_slots)
+        return attention, share, sent
 
     def attention_back(layer, saved, grad_one_sent, received):
         grad_one = 2.0 * in_order(side, grad_one_sent, received)
@@ -551,8 +572,8 @@
         biases = [column_sum(item).reshape(-1, width) for item in pre_lows]
         return grad_one, ffn_low, pre_lows, shared, biases
 
-    def layer_forward(layer, x_own, share, received, peers):
-        attended = share + received + output_bias[layer]
+    def layer_forward(layer, x_own, attended, peers):
+        attended = attended + output_bias[layer]
         hidden, scaled, inverse = normalize(x_own + attended, attn_gain[layer], attn_shift[layer])
         hidden_low = hidden.astype(BF16)
         pre = dot(hidden_low, up_weight[layer]) + up_bias[layer]
@@ -568,17 +589,18 @@
 
     att1, share, sent = attention_forward(0, tokens)
     pieces2, sent = together(pieces2, sent)
-    pieces2 = swap(pieces2, "h")
-    peers1 = sort_weights(gathered1.reshape(16, 2, rows_down, width))
-    x2_own, saved1 = layer_forward(0, own_slots(tokens).astype(F32), share, swap(sent, "h"), peers1)
+    peers1 = sort_weights(gathered1.reshape(16, 2, rows_down, width), units)
+    gathered2 = lax.all_gather(pieces2, PLANE + ("c",))
+    x2_own, saved1 = layer_forward(0, own_slots(tokens).astype(F32), share + swap(sent, "h"), peers1)
     sent = 0.5 * x2_own
-    pieces2, sent = together(pieces2, sent)
-    gathered2 = lax.all_gather(pieces2, PLANE + ("c",))
     x2_low = (2.0 * in_order(side, sent, swap(sent, "h"))).astype(BF16)
-    att2, share, sent = attention_forward(1, x2_low)
-    peers2 = sort_weights(gathered2.reshape(16, 2, rows_down, width))
-    sent, peer_down, peer_up = together(swap(sent, "h"), *peers2)
-    _, saved2 = layer_forward(1, x2_own, share, sent, (peer_down, peer_up))
+    att2, share, _ = attention_forward(1, x2_low)
+    received = swap(0.5 * piece(att2[3], 1 - side, half_slots).astype(F32), "h")
+    received, *peers2 = together(
+        received, *sort_weights(gathered2.reshape(16, 2, rows_down + columns // 16, width), units)
+    )
+    attended = share + dot((2.0 * received).astype(BF16), peers2[2])
+    _, saved2 = layer_forward(1, x2_own, attended, peers2[:2])
     scaled_last = saved2[0]
     mixture = att2[3]
     peer_down, peer_up = (peers1[0], peers2[0]), (peers1[1], peers2[1])
@@ -589,8 +611,7 @@
     grad_one_own, ffn_low, pre_lows, shared2, biases2 = feed_back(1, gradient2, saved2)
     sent = 0.5 * grad_one_own
     received = swap(sent, "h")
-    feed2_received = swap(feed_sums(1 - core, saved2[3], pre_lows, ffn_low, saved2[4], 2 * width), "c")
-    feed2 = feed_sums(core, saved2[3], pre_lows, ffn_low, saved2[4], 2 * width, feed2_received)
+    feed2 = feed_weights_back(saved2, pre_lows, ffn_low, 2 * width)
     feed2, received = together(feed2, received)
     feed2 = lax.psum_scatter(feed2, PLANE, tiled=True)
     _, lows2, attended_low2, share, small_att2 = attention_back(1, att2, sent, received)
@@ -601,26 +622,25 @@
     grad_one_own1, ffn_low, pre_lows, shared1, biases1 = feed_back(0, gradient1, saved1)
     sent = 0.5 * grad_one_own1
     received = swap(sent, "h")
-    feed1_received = swap(feed_sums(1 - core, saved1[3], pre_lows, ffn_low, saved1[4], 2 * width), "c")
-    rest = feed_sums(core, saved1[3], pre_lows, ffn_low, saved1[4], 2 * width, feed1_received)
-    rest, received = together(rest, received)
+    rest = feed_weights_back(saved1, pre_lows, ffn_low, 2 * width + columns)
+    rest = attention_sums(core, lows2, mixture, x2_low, attended_low2, attn2_received, rest, 2 * width // columns)
+    rest, received, feed2 = together(rest, received, feed2)
+    rest = lax.psum_scatter(rest, PLANE, tiled=True)
     grad_one1, lows1, attended_low1, share, small_att1 = attention_back(0, att1, sent, received)
-    attn = attention_sums(core, lows2, mixture, x2_low, attended_low2, attn2_received, width)
-    rest, feed2, *lows1 = together(rest, feed2, *lows1)
-    rest = lax.psum_scatter(rest, PLANE, tiled=True)
     attn1_received = swap(attention_sums(1 - core, lows1, att1[3], tokens, attended_low1), "c")
-    attn = attention_sums(core, lows1, att1[3], tokens, attended_low1, attn1_received, width, attn)
-    attn = plane_sum(attn)
-
-    def across(values):
-        own, peer = values[:, :width], values[:, width:]
+    attn1 = plane_sum(attention_sums(core, lows1, att1[3], tokens, attended_low1, attn1_received))
+
+    def across(own, peer):
         diagonal = lax.ppermute(peer, ("zl", "h"), ((0, 3), (3, 0), (1, 2), (2, 1)))
-        return own + swap(own, "zl") + (swap(peer, "h") + diagonal)
-
-    feed2 = across(feed2)
-    attn = attn + swap(attn, "zl")
-    feed2, attn, rest = together(feed2, attn, rest)
-    own = jnp.concatenate([feed2, across(rest), attn], axis=1)
+        own = own + swap(own, "zl")
+        peer = swap(peer, "h") + diagonal
+        return jnp.concatenate([own[:, :width] + peer, own[:, width:]], axis=1)
+
+    feed2 = across(feed2[:, :width], feed2[:, width:])
+    attn1 = attn1 + swap(attn1, "zl")
+    feed2, attn1, rest = together(feed2, attn1, rest)
+    rest = across(jnp.concatenate([rest[:, :width], rest[:, 2 * width :]], axis=1), rest[:, width : 2 * width])
+    own = jnp.concatenate([feed2, rest, attn1], axis=1)
     gathered = lax.all_gather(own, PLANE + ("c",)).reshape(16, 2, *own.shape)
     grad_query, grad_key, grad_value, grad_output, grad_up, grad_down = place_gradients(gathered, width)
 

time: 566 us -> 557 us (0.984)
  local copies, waits for them, and re-layouts: 46.3 us -> 29.9 us
  waiting for transfers between devices: 251 us -> 263 us
    reduce_scatter x1, waiting for transfers between devices: 0.02 us -> 19.9 us  [local(): rest = lax.psum_scatter(rest, PLANE, tiled=True)]
    ppermute x12, waiting for transfers between devices: 43.3 us -> 27.8 us  [ring_parts(): received.append(lax.ppermute(sent, axis, pairs))]
    unnamed x262 -> x252, local copies, waits for them, and re-layouts: 32.8 us -> 22.6 us
    ppermute x23, waiting for transfers between devices: 156 us -> 163 us  [swap(): return lax.ppermute(values, axis, SWAP)]
    ppermute x2, waiting for transfers between devices: 6.44 us -> 0.01 us  [across(): diagonal = lax.ppermute(peer, ('zl', 'h'), ((0, 3), (3, 0), (1, 2), (2, 1)))]
    dot_general x8 -> x9, matrix products: 13.8 us -> 14.9 us  [dot(): return jnp.dot(left, right, preferred_element_type=F32)]
  transfers between devices with their start and end apart: 46 -> 46, of which waited for: 30 -> 31; matrix products, arithmetic and copies ran while one was open for 11% -> 10% of each run, Pallas kernels for 16% -> 16%
where the time goes in v6:
time: 557 us; the launch traced here: 548 us
  waiting for transfers between devices  263 us (47%)
  Pallas kernels  118 us (21%)
  starting transfers between devices  59.9 us (11%)
  matrix products  30.3 us (5%)
  local copies, waits for them, and re-layouts  29.9 us (5%)
  other arithmetic  29.7 us (5%)
  between operations  17.3 us (3%)
    ppermute x23, waiting for transfers between devices, swap(): return lax.ppermute(values, axis, SWAP)  163 us
    ppermute x23, starting transfers between devices, swap(): return lax.ppermute(values, axis, SWAP)  39.6 us
    ppermute x12, waiting for transfers between devices, ring_parts(): received.append(lax.ppermute(sent, axis, pairs))  27.8 us
    ppermute x4, waiting for transfers between devices, local(): small = small + lax.ppermute(small, axis, pairs)  26.8 us
    pallas_call x4, Pallas kernels, feed_sums(): pl.pallas_call(lambda *refs: feed_sums_kernel(bool(more), *refs), grid=(4...  26.5 us
    pallas_call x2, Pallas kernels, attend_back(): pl.pallas_call(attend_back_kernel, grid=(steps,), in_specs=[SCALAR, part,...  24.6 us
    unnamed x252, local copies, waits for them, and re-layouts  22.6 us
    pallas_call x2, Pallas kernels, attend(): pl.pallas_call(attend_kernel, grid=(steps,), in_specs=[SCALAR, whole, wei...  20.3 us
  transfers between devices with their start and end apart: 46, of which 31 were waited for; matrix products, arithmetic and copies ran while one was open for 10% of the time, Pallas kernels for 16%

profile of v6, /device:TPU:0, one launch (start us, length us, event | category | flops | bytes accessed | tf_op | source)
XLA Modules:
  0.0 547.9 jit_solution(2120275022916443075)
XLA Ops:
  8.0 2.3 copy-done.1
  12.7 4.0 collective-permute-start
  17.4 6.4 %collective-permute-done = f32[96,768]{1,0:T(8,128)S(1)} collective-permute-done((f32[96,768]{1,0:T(8,128)}, f32[96,768]{1,0:T(8,128)S(1)}, u32[]{:S(2)}, u32[]{:S(2)}) %collective-permute-start) | collective-permute-done | bytes 294944 | tf_op jit(solution)/shard_map/ppermute | solution.py:65
  24.7 3.3 collective-permute-start.1
  28.1 9.6 %attend.2 = (bf16[512,384]{1,0:T(8,128)(2,1)S(1)}, bf16[512,384]{1,0:T(8,128)(2,1)S(1)}, bf16[512,384]{1,0:T(8,128)(2,1)S(1)}, bf16[512,384]{1,0:T(8,128)(2,1)S(...) custom-call(s32[2]{0:T(128)S(1)} %get-tuple-element.277.place_ref, ...), custom_call_target="tpu_custom_call" | custom-call | flops 1610612736 | bytes 5505024 | tf_op jit(solution)/shard_map/attend/pallas_call | solution.py:176
  42.1 3.3 collective-permute-start.3
  48.6 13.4 %collective-permute-done.3 = f32[2,1536]{1,0:T(2,128)S(1)} collective-permute-done((f32[2,1536]{1,0:T(2,128)S(1)}, f32[2,1536]{1,0:T(2,128)S(1)}, u32[]{:S(2)}, u32[]{:S(2)}) %collective-permute-start.3) | collective-permute-done | bytes 12320 | tf_op jit(solution)/shard_map/ppermute | solution.py:65
  65.9 3.8 multiply_convert_fusion.3
  71.4 10.4 %all-gather.7.cloned.1.call-done = f32[3072,768]{1,0:T(8,128)} async-done(((f32[96,768]{1,0:T(8,128)}), f32[3072,768]{1,0:T(8,128)}) %all-gather.7.cloned.1.call-update) | async-done | bytes 9437200 | tf_op jit(solution)/shard_map/all_gather | solution.py:519
  81.8 4.4 sort_weights.2
  91.3 3.1 collective-permute-start.4
  94.5 18.4 %collective-permute-done.4 = f32[256,768]{1,0:T(8,128)} collective-permute-done((f32[256,768]{1,0:T(8,128)}, f32[256,768]{1,0:T(8,128)}, u32[]{:S(2)}, u32[]{:S(2)}) %collective-permute-start.4) | collective-permute-done | bytes 786464 | tf_op jit(solution)/shard_map/ppermute | solution.py:65
  115.6 10.7 %attend.3 = (bf16[512,384]{1,0:T(8,128)(2,1)S(1)}, bf16[512,384]{1,0:T(8,128)(2,1)S(1)}, bf16[512,384]{1,0:T(8,128)(2,1)S(1)}, bf16[512,384]{1,0:T(8,128)(2,1)S(...) custom-call(s32[2]{0:T(128)S(1)} %get-tuple-element.277.place_ref, ...), custom_call_target="tpu_custom_call" | custom-call | flops 1610612736 | bytes 5505024 | tf_op jit(solution)/shard_map/attend/pallas_call | solution.py:176
  130.3 3.6 collective-permute-start.5
  135.1 9.4 %all-gather.9.cloned.1.call-done = f32[3840,768]{1,0:T(8,128)} async-done(((f32[120,768]{1,0:T(8,128)}), f32[3840,768]{1,0:T(8,128)}) %all-gather.9.cloned.1.call-update) | async-done | bytes 11796496 | tf_op jit(solution)/shard_map/all_gather | solution.py:593
  144.6 5.0 sort_weights.3
  152.3 2.5 multiply_convert_fusion.1
  163.2 4.8 feed_sums.4
  168.3 2.5 fusion.50
  173.8 3.2 collective-permute-start.7
  177.0 6.1 %collective-permute-done.6.refs_7_ = f32[1536,1536]{1,0:T(8,128)} collective-permute-done((f32[1536,1536]{1,0:T(8,128)}, f32[1536,1536]{1,0:T(8,128)}, u32[]{:S(2)}, u32[]{:S(2)}) %collective-permute-start.6) | collective-permute-done | bytes 9437216 | tf_op jit(solution)/shard_map/ppermute | solution.py:65
  183.0 8.4 %feed_sums.5 = f32[1536,1536]{1,0:T(8,128)} custom-call(s32[1]{0:T(128)} %bitcast.2.refs_0_, bf16[256,1536]{1,0:T(8,128)(2,1)S(1)} %get-tuple-element.261.refs_1_, bf16[256,1536]{1,0:T(8,128)(2,1)S(1)} %get-tuple-element.263.refs_2_, bf16[256,1536]{1,0:T(8,128)(2,1)S(1)} %get-tuple-element.272.refs_3_, bf16[256,1536]{1,0:T(8,128)(2,1)S(1)} %get-tuple-element.276.refs_4_, ...), custom_call_target="tpu_custom_call" | custom-call | flops 1207959552 | bytes 18874368 | tf_op jit(solution)/shard_map/feed_sums/pallas_call | solution.py:336
  191.4 3.9 collective-permute-done.7
  198.9 12.3 %attend_back.2 = (bf16[512,384]{1,0:T(8,128)(2,1)S(1)}, bf16[512,384]{1,0:T(8,128)(2,1)S(1)}, bf16[512,384]{1,0:T(8,128)(2,1)S(1)}, f32[512,768]{1,0:T(8,128)}, ...) custom-call(s32[1]{0:T(128)} %copy.62.length_ref, bf16[512,384]{1,0:T(8,128)(2,1)S(1)} %copy-done.32, ...), custom_call_target="tpu_custom_call" | custom-call | flops 2214592512 | bytes 5505024 | tf_op jit(solution)/shard_map/attend_back/pallas_call | solution.py:257
  212.9 3.2 collective-permute-start.8
  216.1 17.2 %collective-permute-done.8 = f32[256,768]{1,0:T(8,128)S(1)} collective-permute-done((f32[256,768]{1,0:T(8,128)S(1)}, f32[256,768]{1,0:T(8,128)S(1)}, u32[]{:S(2)}, u32[]{:S(2)}) %collective-permute-start.8) | collective-permute-done | bytes 786464 | tf_op jit(solution)/shard_map/ppermute | solution.py:65
  233.4 2.4 multiply_reduce_fusion.3
  241.8 4.8 feed_sums.6
  246.7 2.0 attention_sums.4
  250.2 3.4 multiply_reduce_fusion
  254.8 3.3 collective-permute-start.12
  258.1 3.5 collective-permute-done.11.refs_7_
  261.7 8.4 %feed_sums.7.refs_8_ = f32[1536,1920]{1,0:T(8,128)} custom-call(s32[1]{0:T(128)} %bitcast.2.refs_0_, bf16[256,1536]{1,0:T(8,128)(2,1)S(1)} %get-tuple-element.255.refs_1_, bf16[256,1536]{1,0:T(8,128)(2,1)S(1)} %get-tuple-element.257.refs_2_, bf16[256,1536]{1,0:T(8,128)(2,1)S(1)} %get-tuple-element.270.refs_3_, ...), custom_call_target="tpu_custom_call" | custom-call | flops 1207959552 | bytes 18874368 | tf_op jit(solution)/shard_map/feed_sums/pallas_call | solution.py:336
  270.1 3.3 attention_sums.5
  273.3 3.4 collective-permute-done.12
  276.7 5.5 %reduce-scatter.3.cloned.1.call-done = f32[96,1536]{1,0:T(8,128)} async-done(((f32[1536,1536]{1,0:T(8,128)}), f32[96,1536]{1,0:T(8,128)}) %reduce-scatter.3.cloned.1.call-update) | async-done | bytes 589840 | tf_op jit(solution)/shard_map/reduce_scatter | solution.py:616
  286.2 12.3 %attend_back.3 = (bf16[512,384]{1,0:T(8,128)(2,1)S(1)}, bf16[512,384]{1,0:T(8,128)(2,1)S(1)}, bf16[512,384]{1,0:T(8,128)(2,1)S(1)}, f32[512,768]{1,0:T(8,128)}, ...) custom-call(s32[1]{0:T(128)} %copy.62.length_ref, bf16[512,384]{1,0:T(8,128)(2,1)S(1)} %copy-done.26, ...), custom_call_target="tpu_custom_call" | custom-call | flops 2214592512 | bytes 5505024 | tf_op jit(solution)/shard_map/attend_back/pallas_call | solution.py:257
  298.4 3.1 attention_sums.6
  301.5 4.9 collective-permute-done.18.refs_7_
  306.4 3.7 attention_sums.7
  311.2 2.6 collective-permute-start.24
  318.8 9.9 %collective-permute-done.24 = f32[4,48,384]{2,1,0:T(8,128)S(1)} collective-permute-done((f32[4,48,384]{2,1,0:T(8,128)}, f32[4,48,384]{2,1,0:T(8,128)S(1)}, u32[]{:S(2)}, u32[]{:S(2)}) %collective-permute-start.24) | collective-permute-done | bytes 294944 | tf_op jit(solution)/shard_map/ppermute | solution.py:83
  330.0 7.8 %collective-permute-done.23 = f32[4,48,384]{2,1,0:T(8,128)S(1)} collective-permute-done((f32[4,48,384]{2,1,0:T(8,128)}, f32[4,48,384]{2,1,0:T(8,128)S(1)}, u32[]{:S(2)}, u32[]{:S(2)}) %collective-permute-start.23) | collective-permute-done | bytes 294944 | tf_op jit(solution)/shard_map/ppermute | solution.py:83
  338.6 5.9 %collective-permute-done.19 = f32[4,48,384]{2,1,0:T(8,128)S(1)} collective-permute-done((f32[4,48,384]{2,1,0:T(8,128)S(1)}, f32[4,48,384]{2,1,0:T(8,128)S(1)}, u32[]{:S(2)}, u32[]{:S(2)}) %collective-permute-start.19) | collective-permute-done | bytes 294944 | tf_op jit(solution)/shard_map/ppermute | solution.py:83
  344.7 2.4 collective-permute-start.27
  352.0 2.6 collective-permute-done.26
  354.6 2.2 collective-permute-start.17
  356.8 2.2 collective-permute-start.16
  361.2 10.8 %collective-permute-done.15 = f32[96,768]{1,0:T(8,128)S(1)} collective-permute-done((f32[96,768]{1,0:T(8,128)S(1)}, f32[96,768]{1,0:T(8,128)S(1)}, u32[]{:S(2)}, u32[]{:S(2)}) %collective-permute-start.15) | collective-permute-done | bytes 294944 | tf_op jit(solution)/shard_map/ppermute | solution.py:65
  373.6 19.9 %reduce-scatter.5.cloned.1.call-done = f32[96,1920]{1,0:T(8,128)} async-done(((f32[1536,1920]{1,0:T(8,128)}), f32[96,1920]{1,0:T(8,128)}) %reduce-scatter.5.cloned.1.call-update) | async-done | bytes 737296 | tf_op jit(solution)/shard_map/reduce_scatter | solution.py:628
  397.2 2.2 collective-permute-start.34
  400.1 8.6 %collective-permute-done.32 = f32[96,1152]{1,0:T(8,128)S(1)} collective-permute-done((f32[96,1152]{1,0:T(8,128)S(1)}, f32[96,1152]{1,0:T(8,128)S(1)}, u32[]{:S(2)}, u32[]{:S(2)}) %collective-permute-start.32) | collective-permute-done | bytes 442400 | tf_op jit(solution)/shard_map/ppermute | solution.py:65
  408.8 7.2 %collective-permute-done.33 = f32[96,768]{1,0:T(8,128)S(1)} collective-permute-done((f32[96,768]{1,0:T(8,128)S(1)}, f32[96,768]{1,0:T(8,128)S(1)}, u32[]{:S(2)}, u32[]{:S(2)}) %collective-permute-start.33) | collective-permute-done | bytes 294944 | tf_op jit(solution)/shard_map/ppermute | solution.py:65
  418.0 36.0 %collective-permute-done.13 = f32[512,768]{1,0:T(8,128)S(1)} collective-permute-done((f32[512,768]{1,0:T(8,128)}, f32[512,768]{1,0:T(8,128)S(1)}, u32[]{:S(2)}, u32[]{:S(2)}) %collective-permute-start.13) | collective-permute-done | bytes 1572896 | tf_op jit(solution)/shard_map/ppermute | solution.py:65
  454.0 2.9 add_add_fusion
  458.3 2.5 collective-permute-start.9
  461.0 16.1 %collective-permute-done.9 = f32[14,768]{1,0:T(8,128)S(1)} collective-permute-done((f32[14,768]{1,0:T(8,128)S(1)}, f32[14,768]{1,0:T(8,128)S(1)}, u32[]{:S(2)}, u32[]{:S(2)}) %collective-permute-start.9) | collective-permute-done | bytes 43040 | tf_op jit(solution)/shard_map/ppermute | solution.py:65
  480.3 6.4 %collective-permute-done.36 = f32[18,768]{1,0:T(8,128)S(1)} collective-permute-done((f32[18,768]{1,0:T(8,128)S(1)}, f32[18,768]{1,0:T(8,128)S(1)}, u32[]{:S(2)}, u32[]{:S(2)}) %collective-permute-start.36) | collective-permute-done | bytes 55328 | tf_op jit(solution)/shard_map/ppermute | solution.py:658
  486.8 7.4 %collective-permute-done.37 = f32[18,768]{1,0:T(8,128)S(1)} collective-permute-done((f32[18,768]{1,0:T(8,128)S(1)}, f32[18,768]{1,0:T(8,128)S(1)}, u32[]{:S(2)}, u32[]{:S(2)}) %collective-permute-start.37) | collective-permute-done | bytes 55328 | tf_op jit(solution)/shard_map/ppermute | solution.py:658
  494.2 5.9 %collective-permute-done.38 = f32[18,768]{1,0:T(8,128)S(1)} collective-permute-done((f32[18,768]{1,0:T(8,128)S(1)}, f32[18,768]{1,0:T(8,128)S(1)}, u32[]{:S(2)}, u32[]{:S(2)}) %collective-permute-start.38) | collective-permute-done | bytes 55328 | tf_op jit(solution)/shard_map/ppermute | solution.py:658
  500.3 7.1 %collective-permute-done.39 = f32[18,768]{1,0:T(8,128)S(1)} collective-permute-done((f32[18,768]{1,0:T(8,128)S(1)}, f32[18,768]{1,0:T(8,128)S(1)}, u32[]{:S(2)}, u32[]{:S(2)}) %collective-permute-start.39) | collective-permute-done | bytes 55328 | tf_op jit(solution)/shard_map/ppermute | solution.py:658
  507.7 4.1 collective-permute-done.40
  517.3 8.0 %place_attention.1 = (f32[2,768,384]{2,1,0:T(8,128)}, f32[2,768,384]{2,1,0:T(8,128)}, f32[2,768,384]{2,1,0:T(8,128)}, f32[2,384,768]{2,1,0:T(8,128)}) custom-call(f32[16,2,96,2304]{3,2,1,0:T(8,128)} %bitcast.143, f32[16,2,96,2304]{3,2,1,0:T(8,128)} %bitcast.144, f32[16,2,96,2304]{3,2,1,0:T(8,128)} %bitcast.145, f32[16,2,96,2304]{3,2,1,0:T(8,128)} %bitcast.146), custom_call_target="tpu_custom_call" | custom-call | tf_op jit(solution)/shard_map/place_attention/pallas_call | solution.py:472
  525.3 15.6 %place_feed.1 = (f32[2,1536,768]{2,1,0:T(8,128)}, f32[2,768,1536]{2,1,0:T(8,128)}) custom-call(f32[16,2,96,2304]{3,2,1,0:T(8,128)} %bitcast.147, f32[16,2,96,2304]{3,2,1,0:T(8,128)} %bitcast.148), custom_call_target="tpu_custom_call" | custom-call | tf_op jit(solution)/shard_map/place_feed/pallas_call | solution.py:455
  (441 shorter events, 94.8 us)
Async XLA Ops:
  7.2 74.6 %all-gather.7.cloned.1.call-start = ((), (), s32[]{:S(2)}) async-start(), calls=%async_computation.4 | async-start | bytes 9732096 | tf_op jit(solution)/shard_map/all_gather | solution.py:519
  12.7 11.2 %collective-permute-start = (f32[96,768]{1,0:T(8,128)}, f32[96,768]{1,0:T(8,128)S(1)}, u32[]{:S(2)}, u32[]{:S(2)}) collective-permute-start(f32[96,768]{1,0:T(8,128)} %get-tuple-element.233), channel_id=1, source_target_pairs={{0,1},{1,0},{2,3},{3,2},{4,5},{5,4},{6,7},{7,6},{8,9},{9,8},{10,11... | collective-permute-start | bytes 884744 | tf_op jit(solution)/shard_map/ppermute | solution.py:65
  24.6 119.9 %all-gather.9.cloned.1.call-start = ((), (), s32[]{:S(2)}) async-start(), calls=%async_computation.5 | async-start | bytes 12165120 | tf_op jit(solution)/shard_map/all_gather | solution.py:593
  24.7 17.0 %collective-permute-start.1 = (f32[120,768]{1,0:T(8,128)}, f32[120,768]{1,0:T(8,128)}, u32[]{:S(2)}, u32[]{:S(2)}) collective-permute-start(f32[120,768]{1,0:T(8,128)} %pad_maximum_fusion.2), channel_id=1, source_target_pairs={{0,1},{1,0},{2,3},{3,2},{4,5},{5,4},{6,7},{7,6},{8,9},{9,8},{10,11... | collective-permute-start | bytes 1105928 | tf_op jit(solution)/shard_map/ppermute | solution.py:65
  28.1 41.6 %slice-start = ((s8[4718592]{0:T(1024)(128)(4,1)}), s8[524288]{0:T(1024)(128)(4,1)S(1)}, s32[]{:S(2)}) async-start(s8[4718592]{0:T(1024)(128)(4,1)} %bitcast.137), calls=%async_computation.7 | async-start | bytes 1048576
  41.7 240.5 %reduce-scatter.3.cloned.1.call-start = ((), (), s32[]{:S(2)}) async-start(), calls=%async_computation.2 | async-start | bytes 10027008 | tf_op jit(solution)/shard_map/reduce_scatter | solution.py:616
  41.8 20.8 %collective-permute-start.2 = (f32[256,768]{1,0:T(8,128)}, f32[256,768]{1,0:T(8,128)S(1)}, u32[]{:S(2)}, u32[]{:S(2)}) collective-permute-start(f32[256,768]{1,0:T(8,128)} %copy-done.24), channel_id=1, source_target_pairs={{0,1},{1,0},{2,3},{3,2},{4,5},{5,4},{6,7},{7,6},{8,9},{9,8},{10,11... | collective-permute-start | bytes 2359304 | tf_op jit(solution)/shard_map/ppermute | solution.py:65
  42.1 19.8 %collective-permute-start.3 = (f32[2,1536]{1,0:T(2,128)S(1)}, f32[2,1536]{1,0:T(2,128)S(1)}, u32[]{:S(2)}, u32[]{:S(2)}) collective-permute-start(f32[2,1536]{1,0:T(2,128)S(1)} %convert_element_type.155), channel_id=1, source_target_pairs={{0,1},{1,0},{2,3},{3,2},{4,5},{5,4},{6,7},{7,6},{8,9},{9,8},{10,11... | collective-permute-start | bytes 36872 | tf_op jit(solution)/shard_map/ppermute | solution.py:65
  91.3 21.5 %collective-permute-start.4 = (f32[256,768]{1,0:T(8,128)}, f32[256,768]{1,0:T(8,128)}, u32[]{:S(2)}, u32[]{:S(2)}) collective-permute-start(f32[256,768]{1,0:T(8,128)} %fusion.62), channel_id=1, source_target_pairs={{0,1},{1,0},{2,3},{3,2},{4,5},{5,4},{6,7},{7,6},{8,9},{9,8},{10,11... | collective-permute-start | bytes 2359304 | tf_op jit(solution)/shard_map/ppermute | solution.py:65
  130.3 19.3 %collective-permute-start.5 = (f32[256,384]{1,0:T(8,128)}, f32[256,384]{1,0:T(8,128)}, u32[]{:S(2)}, u32[]{:S(2)}) collective-permute-start(f32[256,384]{1,0:T(8,128)} %convert_multiply_fusion.1), channel_id=1, source_target_pairs={{0,1},{1,0},{2,3},{3,2},{4,5},{5,4},{6,7},{7,6},{8,9},{9,8},{10,11... | collective-permute-start | bytes 1179656 | tf_op jit(solution)/shard_map/ppermute | solution.py:65
  168.0 15.0 %collective-permute-start.6 = (f32[1536,1536]{1,0:T(8,128)}, f32[1536,1536]{1,0:T(8,128)}, u32[]{:S(2)}, u32[]{:S(2)}) collective-permute-start(f32[1536,1536]{1,0:T(8,128)} %feed_sums.4), channel_id=1, source_target_pairs={{0,2},{2,0},{1,3},{3,1},{4,6},{6,4},{5,7},{7,5},{8,10},{10,8},{9,1... | collective-permute-start | bytes 28311560 | tf_op jit(solution)/shard_map/ppermute | solution.py:65
  173.8 21.5 %collective-permute-start.7 = (f32[256,768]{1,0:T(8,128)}, f32[256,768]{1,0:T(8,128)}, u32[]{:S(2)}, u32[]{:S(2)}) collective-permute-start(f32[256,768]{1,0:T(8,128)} %get-tuple-element.203), channel_id=1, source_target_pairs={{0,1},{1,0},{2,3},{3,2},{4,5},{5,4},{6,7},{7,6},{8,9},{9,8},{10,11... | collective-permute-start | bytes 2359304 | tf_op jit(solution)/shard_map/ppermute | solution.py:65
  195.4 198.1 %reduce-scatter.5.cloned.1.call-start = ((), (), s32[]{:S(2)}) async-start(), calls=%async_computation.3 | async-start | bytes 12533760 | tf_op jit(solution)/shard_map/reduce_scatter | solution.py:628
  212.9 20.5 %collective-permute-start.8 = (f32[256,768]{1,0:T(8,128)S(1)}, f32[256,768]{1,0:T(8,128)S(1)}, u32[]{:S(2)}, u32[]{:S(2)}) collective-permute-start(f32[256,768]{1,0:T(8,128)S(1)} %constant_dynamic-slice_fusion), channel_id=1, source_target_pairs={{0,1},{1,0},{2,3},{3,2},{4,5},{5,4},{6,7},{7,6},{8,9},{9,8},{10,11... | collective-permute-start | bytes 2359304 | tf_op jit(solution)/shard_map/ppermute | solution.py:65
  246.7 15.0 %collective-permute-start.11 = (f32[1536,1536]{1,0:T(8,128)}, f32[1536,1536]{1,0:T(8,128)}, u32[]{:S(2)}, u32[]{:S(2)}) collective-permute-start(f32[1536,1536]{1,0:T(8,128)} %feed_sums.6), channel_id=1, source_target_pairs={{0,2},{2,0},{1,3},{3,1},{4,6},{6,4},{5,7},{7,5},{8,10},{10,8},{9,1... | collective-permute-start | bytes 28311560 | tf_op jit(solution)/shard_map/ppermute | solution.py:65
  248.8 21.3 %collective-permute-start.10 = (f32[1536,384]{1,0:T(8,128)S(1)}, f32[1536,384]{1,0:T(8,128)S(1)}, u32[]{:S(2)}, u32[]{:S(2)}) collective-permute-start(f32[1536,384]{1,0:T(8,128)S(1)} %attention_sums.4), channel_id=1, source_target_pairs={{0,2},{2,0},{1,3},{3,1},{4,6},{6,4},{5,7},{7,5},{8,10},{10,8},{9,1... | collective-permute-start | bytes 7077896 | tf_op jit(solution)/shard_map/ppermute | solution.py:65
  254.8 21.9 %collective-permute-start.12 = (f32[256,768]{1,0:T(8,128)}, f32[256,768]{1,0:T(8,128)}, u32[]{:S(2)}, u32[]{:S(2)}) collective-permute-start(f32[256,768]{1,0:T(8,128)} %multiply_multiply_fusion.4), channel_id=1, source_target_pairs={{0,1},{1,0},{2,3},{3,2},{4,5},{5,4},{6,7},{7,6},{8,9},{9,8},{10,11... | collective-permute-start | bytes 2359304 | tf_op jit(solution)/shard_map/ppermute | solution.py:65
  282.3 235.0 %all-gather.11.cloned.1.call-start = ((), (), s32[]{:S(2)}) async-start(), calls=%async_computation.6 | async-start | bytes 29196288 | tf_op jit(solution)/shard_map/all_gather | solution.py:644
  301.5 4.9 collective-permute-start.18
  311.2 17.5 %collective-permute-start.24 = (f32[4,48,384]{2,1,0:T(8,128)}, f32[4,48,384]{2,1,0:T(8,128)S(1)}, u32[]{:S(2)}, u32[]{:S(2)}) collective-permute-start(f32[4,48,384]{2,1,0:T(8,128)} %get-tuple-element.220), channel_id=1, source_target_pairs={{0,64},{32,96},{64,0},{96,32},{1,65},{33,97},{65,1},{97,33},{2,66}... | collective-permute-start | bytes 884744 | tf_op jit(solution)/shard_map/ppermute | solution.py:83
  313.9 24.0 %collective-permute-start.23 = (f32[4,48,384]{2,1,0:T(8,128)}, f32[4,48,384]{2,1,0:T(8,128)S(1)}, u32[]{:S(2)}, u32[]{:S(2)}) collective-permute-start(f32[4,48,384]{2,1,0:T(8,128)} %get-tuple-element.221), channel_id=1, source_target_pairs={{0,96},{32,0},{64,32},{96,64},{1,97},{33,1},{65,33},{97,65},{2,98}... | collective-permute-start | bytes 884744 | tf_op jit(solution)/shard_map/ppermute | solution.py:83
  315.2 22.6 %collective-permute-start.22 = (f32[4,48,384]{2,1,0:T(8,128)S(1)}, f32[4,48,384]{2,1,0:T(8,128)S(1)}, u32[]{:S(2)}, u32[]{:S(2)}) collective-permute-start(f32[4,48,384]{2,1,0:T(8,128)S(1)} %get-tuple-element.222), channel_id=1, source_target_pairs={{0,32},{32,64},{64,96},{96,0},{1,33},{33,65},{65,97},{97,1},{2,34}... | collective-permute-start | bytes 884744 | tf_op jit(solution)/shard_map/ppermute | solution.py:83
  316.0 21.9 %collective-permute-start.21 = (f32[4,48,384]{2,1,0:T(8,128)S(1)}, f32[4,48,384]{2,1,0:T(8,128)S(1)}, u32[]{:S(2)}, u32[]{:S(2)}) collective-permute-start(f32[4,48,384]{2,1,0:T(8,128)S(1)} %get-tuple-element.224), channel_id=1, source_target_pairs={{0,8},{4,12},{8,0},{12,4},{1,9},{5,13},{9,1},{13,5},{2,10},{6,14},... | collective-permute-start | bytes 884744 | tf_op jit(solution)/shard_map/ppermute | solution.py:83
  317.6 21.0 %collective-permute-start.20 = (f32[4,48,384]{2,1,0:T(8,128)S(1)}, f32[4,48,384]{2,1,0:T(8,128)S(1)}, u32[]{:S(2)}, u32[]{:S(2)}) collective-permute-start(f32[4,48,384]{2,1,0:T(8,128)S(1)} %get-tuple-element.225), channel_id=1, source_target_pairs={{0,12},{4,0},{8,4},{12,8},{1,13},{5,1},{9,5},{13,9},{2,14},{6,2},{... | collective-permute-start | bytes 884744 | tf_op jit(solution)/shard_map/ppermute | solution.py:83
  328.7 15.8 %collective-permute-start.19 = (f32[4,48,384]{2,1,0:T(8,128)S(1)}, f32[4,48,384]{2,1,0:T(8,128)S(1)}, u32[]{:S(2)}, u32[]{:S(2)}) collective-permute-start(f32[4,48,384]{2,1,0:T(8,128)S(1)} %get-tuple-element.226), channel_id=1, source_target_pairs={{0,4},{4,8},{8,12},{12,0},{1,5},{5,9},{9,13},{13,1},{2,6},{6,10},{... | collective-permute-start | bytes 884744 | tf_op jit(solution)/shard_map/ppermute | solution.py:83
  344.7 7.3 %collective-permute-start.27 = (f32[48,384]{1,0:T(8,128)S(1)}, f32[48,384]{1,0:T(8,128)S(1)}, u32[]{:S(2)}, u32[]{:S(2)}) collective-permute-start(f32[48,384]{1,0:T(8,128)S(1)} %get-tuple-element.238), channel_id=1, source_target_pairs={{0,64},{32,96},{64,0},{96,32},{1,65},{33,97},{65,1},{97,33},{2,66}... | collective-permute-start | bytes 221192 | tf_op jit(solution)/shard_map/ppermute | solution.py:83
  347.1 7.5 %collective-permute-start.26 = (f32[48,384]{1,0:T(8,128)S(1)}, f32[48,384]{1,0:T(8,128)S(1)}, u32[]{:S(2)}, u32[]{:S(2)}) collective-permute-start(f32[48,384]{1,0:T(8,128)S(1)} %get-tuple-element.239), channel_id=1, source_target_pairs={{0,96},{32,0},{64,32},{96,64},{1,97},{33,1},{65,33},{97,65},{2,98}... | collective-permute-start | bytes 221192 | tf_op jit(solution)/shard_map/ppermute | solution.py:83
  348.7 8.1 %collective-permute-start.25 = (f32[48,384]{1,0:T(8,128)S(1)}, f32[48,384]{1,0:T(8,128)S(1)}, u32[]{:S(2)}, u32[]{:S(2)}) collective-permute-start(f32[48,384]{1,0:T(8,128)S(1)} %get-tuple-element.240), channel_id=1, source_target_pairs={{0,32},{32,64},{64,96},{96,0},{1,33},{33,65},{65,97},{97,1},{2,34}... | collective-permute-start | bytes 221192 | tf_op jit(solution)/shard_map/ppermute | solution.py:83
  349.2 9.8 %collective-permute-start.30 = (f32[48,384]{1,0:T(8,128)S(1)}, f32[48,384]{1,0:T(8,128)S(1)}, u32[]{:S(2)}, u32[]{:S(2)}) collective-permute-start(f32[48,384]{1,0:T(8,128)S(1)} %get-tuple-element.234), channel_id=1, source_target_pairs={{0,8},{4,12},{8,0},{12,4},{1,9},{5,13},{9,1},{13,5},{2,10},{6,14},... | collective-permute-start | bytes 221192 | tf_op jit(solution)/shard_map/ppermute | solution.py:83
  349.6 10.3 %collective-permute-start.29 = (f32[48,384]{1,0:T(8,128)S(1)}, f32[48,384]{1,0:T(8,128)S(1)}, u32[]{:S(2)}, u32[]{:S(2)}) collective-permute-start(f32[48,384]{1,0:T(8,128)S(1)} %get-tuple-element.235), channel_id=1, source_target_pairs={{0,12},{4,0},{8,4},{12,8},{1,13},{5,1},{9,5},{13,9},{2,14},{6,2},{... | collective-permute-start | bytes 221192 | tf_op jit(solution)/shard_map/ppermute | solution.py:83
  351.9 7.9 %collective-permute-start.28 = (f32[48,384]{1,0:T(8,128)S(1)}, f32[48,384]{1,0:T(8,128)S(1)}, u32[]{:S(2)}, u32[]{:S(2)}) collective-permute-start(f32[48,384]{1,0:T(8,128)S(1)} %get-tuple-element.236), channel_id=1, source_target_pairs={{0,4},{4,8},{8,12},{12,0},{1,5},{5,9},{9,13},{13,1},{2,6},{6,10},{... | collective-permute-start | bytes 221192 | tf_op jit(solution)/shard_map/ppermute | solution.py:83
  354.6 17.4 %collective-permute-start.17 = (f32[96,768]{1,0:T(8,128)S(1)}, f32[96,768]{1,0:T(8,128)S(1)}, u32[]{:S(2)}, u32[]{:S(2)}) collective-permute-start(f32[96,768]{1,0:T(8,128)S(1)} %get-tuple-element.231), channel_id=1, source_target_pairs={{0,17},{17,0},{1,16},{16,1},{2,19},{19,2},{3,18},{18,3},{4,21},{21... | collective-permute-start | bytes 884744 | tf_op jit(solution)/shard_map/ppermute | solution.py:634
  356.8 15.2 %collective-permute-start.16 = (f32[96,768]{1,0:T(8,128)S(1)}, f32[96,768]{1,0:T(8,128)S(1)}, u32[]{:S(2)}, u32[]{:S(2)}) collective-permute-start(f32[96,768]{1,0:T(8,128)S(1)} %get-tuple-element.231), channel_id=1, source_target_pairs={{0,1},{1,0},{2,3},{3,2},{4,5},{5,4},{6,7},{7,6},{8,9},{9,8},{10,11... | collective-permute-start | bytes 884744 | tf_op jit(solution)/shard_map/ppermute | solution.py:65
  359.0 13.0 %collective-permute-start.15 = (f32[96,768]{1,0:T(8,128)S(1)}, f32[96,768]{1,0:T(8,128)S(1)}, u32[]{:S(2)}, u32[]{:S(2)}) collective-permute-start(f32[96,768]{1,0:T(8,128)S(1)} %get-tuple-element.230), channel_id=1, source_target_pairs={{0,16},{16,0},{1,17},{17,1},{2,18},{18,2},{3,19},{19,3},{4,20},{20... | collective-permute-start | bytes 884744 | tf_op jit(solution)/shard_map/ppermute | solution.py:65
  359.9 13.6 %collective-permute-start.31 = (f32[96,384]{1,0:T(8,128)S(1)}, f32[96,384]{1,0:T(8,128)S(1)}, u32[]{:S(2)}, u32[]{:S(2)}) collective-permute-start(f32[96,384]{1,0:T(8,128)S(1)} %pad_maximum_fusion.3), channel_id=1, source_target_pairs={{0,16},{16,0},{1,17},{17,1},{2,18},{18,2},{3,19},{19,3},{4,20},{20... | collective-permute-start | bytes 442376 | tf_op jit(solution)/shard_map/ppermute | solution.py:65
  395.5 13.2 %collective-permute-start.32 = (f32[96,1152]{1,0:T(8,128)S(1)}, f32[96,1152]{1,0:T(8,128)S(1)}, u32[]{:S(2)}, u32[]{:S(2)}) collective-permute-start(f32[96,1152]{1,0:T(8,128)S(1)} %pad_maximum_fusion.1), channel_id=1, source_target_pairs={{0,16},{16,0},{1,17},{17,1},{2,18},{18,2},{3,19},{19,3},{4,20},{20... | collective-permute-start | bytes 1327112 | tf_op jit(solution)/shard_map/ppermute | solution.py:65
  397.2 11.6 %collective-permute-start.34 = (f32[96,768]{1,0:T(8,128)S(1)}, f32[96,768]{1,0:T(8,128)S(1)}, u32[]{:S(2)}, u32[]{:S(2)}) collective-permute-start(f32[96,768]{1,0:T(8,128)S(1)} %get-tuple-element.228), channel_id=1, source_target_pairs={{0,17},{17,0},{1,16},{16,1},{2,19},{19,2},{3,18},{18,3},{4,21},{21... | collective-permute-start | bytes 884744 | tf_op jit(solution)/shard_map/ppermute | solution.py:634
  399.4 16.6 %collective-permute-start.33 = (f32[96,768]{1,0:T(8,128)S(1)}, f32[96,768]{1,0:T(8,128)S(1)}, u32[]{:S(2)}, u32[]{:S(2)}) collective-permute-start(f32[96,768]{1,0:T(8,128)S(1)} %get-tuple-element.228), channel_id=1, source_target_pairs={{0,1},{1,0},{2,3},{3,2},{4,5},{5,4},{6,7},{7,6},{8,9},{9,8},{10,11... | collective-permute-start | bytes 884744 | tf_op jit(solution)/shard_map/ppermute | solution.py:65
  416.0 37.9 %copy-start.48 = (f32[256,768]{1,0:T(8,128)S(1)}, f32[256,768]{1,0:T(8,128)}, u32[]{:S(2)}) copy-start(f32[256,768]{1,0:T(8,128)} %copy-done.47) | copy-start | bytes 2359300
  416.1 37.9 %copy-start.50 = (f32[256,768]{1,0:T(8,128)S(1)}, f32[256,768]{1,0:T(8,128)}, u32[]{:S(2)}) copy-start(f32[256,768]{1,0:T(8,128)} %copy-done.49) | copy-start | bytes 2359300
  417.1 39.8 %copy-start.52 = (f32[256,768]{1,0:T(8,128)S(1)}, f32[256,768]{1,0:T(8,128)}, u32[]{:S(2)}) copy-start(f32[256,768]{1,0:T(8,128)} %copy-done.51) | copy-start | bytes 2359300
  417.1 40.9 %copy-start.82 = (f32[768]{0:T(1024)S(1)}, f32[768]{0:T(1024)}, u32[]{:S(2)}) copy-start(f32[768]{0:T(1024)} %get-tuple-element.167) | copy-start | bytes 9220
  417.1 40.9 %copy-start.81 = (f32[768]{0:T(1024)S(1)}, f32[768]{0:T(1024)}, u32[]{:S(2)}) copy-start(f32[768]{0:T(1024)} %get-tuple-element.173) | copy-start | bytes 9220
  417.1 40.9 %copy-start.83 = (f32[768]{0:T(1024)S(1)}, f32[768]{0:T(1024)}, u32[]{:S(2)}) copy-start(f32[768]{0:T(1024)} %get-tuple-element.197) | copy-start | bytes 9220
  417.1 40.9 %copy-start.103 = (f32[1536]{0:T(1024)S(1)}, f32[1536]{0:T(1024)}, u32[]{:S(2)}) copy-start(f32[1536]{0:T(1024)} %get-tuple-element.271) | copy-start | bytes 18436
  417.1 40.9 %copy-start.102 = (f32[1536]{0:T(1024)S(1)}, f32[1536]{0:T(1024)}, u32[]{:S(2)}) copy-start(f32[1536]{0:T(1024)} %get-tuple-element.275) | copy-start | bytes 18436
  417.1 40.9 %copy-start.111 = (f32[768]{0:T(1024)S(1)}, f32[768]{0:T(1024)}, u32[]{:S(2)}) copy-start(f32[768]{0:T(1024)} %get-tuple-element.163) | copy-start | bytes 9220
  417.1 40.9 %copy-start.110 = (f32[768]{0:T(1024)S(1)}, f32[768]{0:T(1024)}, u32[]{:S(2)}) copy-start(f32[768]{0:T(1024)} %get-tuple-element.175) | copy-start | bytes 9220
  417.2 41.0 %copy-start.87 = (f32[768]{0:T(1024)S(1)}, f32[768]{0:T(1024)}, u32[]{:S(2)}) copy-start(f32[768]{0:T(1024)} %get-tuple-element.165) | copy-start | bytes 9220
  417.2 41.0 %copy-start.105 = (f32[1536]{0:T(1024)S(1)}, f32[1536]{0:T(1024)}, u32[]{:S(2)}) copy-start(f32[1536]{0:T(1024)} %get-tuple-element.273) | copy-start | bytes 18436
  417.2 41.0 %copy-start.85 = (f32[768]{0:T(1024)S(1)}, f32[768]{0:T(1024)}, u32[]{:S(2)}) copy-start(f32[768]{0:T(1024)} %get-tuple-element.199) | copy-start | bytes 9220
  417.2 41.0 %copy-start.86 = (f32[768]{0:T(1024)S(1)}, f32[768]{0:T(1024)}, u32[]{:S(2)}) copy-start(f32[768]{0:T(1024)} %get-tuple-element.176) | copy-start | bytes 9220
  417.2 41.0 %copy-start.112 = (f32[768]{0:T(1024)S(1)}, f32[768]{0:T(1024)}, u32[]{:S(2)}) copy-start(f32[768]{0:T(1024)} %get-tuple-element.162) | copy-start | bytes 9220
  417.2 43.6 %copy-start.84 = (f32[768]{0:T(1024)S(1)}, f32[768]{0:T(1024)}, u32[]{:S(2)}) copy-start(f32[768]{0:T(1024)} %get-tuple-element.193) | copy-start | bytes 9220
  417.2 43.6 %copy-start.104 = (f32[1536]{0:T(1024)S(1)}, f32[1536]{0:T(1024)}, u32[]{:S(2)}) copy-start(f32[1536]{0:T(1024)} %get-tuple-element.269) | copy-start | bytes 18436
  417.2 36.7 %collective-permute-start.13 = (f32[512,768]{1,0:T(8,128)}, f32[512,768]{1,0:T(8,128)S(1)}, u32[]{:S(2)}, u32[]{:S(2)}) collective-permute-start(f32[512,768]{1,0:T(8,128)} %get-tuple-element.125), channel_id=1, source_target_pairs={{0,1},{1,0},{2,3},{3,2},{4,5},{5,4},{6,7},{7,6},{8,9},{9,8},{10,11... | collective-permute-start | bytes 4718600 | tf_op jit(solution)/shard_map/ppermute | solution.py:65
  456.8 20.4 %collective-permute-start.14 = (f32[256,768]{1,0:T(8,128)S(1)}, f32[256,768]{1,0:T(8,128)S(1)}, u32[]{:S(2)}, u32[]{:S(2)}) collective-permute-start(f32[256,768]{1,0:T(8,128)S(1)} %copy-done.52), channel_id=1, source_target_pairs={{0,1},{1,0},{2,3},{3,2},{4,5},{5,4},{6,7},{7,6},{8,9},{9,8},{10,11... | collective-permute-start | bytes 2359304 | tf_op jit(solution)/shard_map/ppermute | solution.py:65
  458.3 18.7 %collective-permute-start.9 = (f32[14,768]{1,0:T(8,128)S(1)}, f32[14,768]{1,0:T(8,128)S(1)}, u32[]{:S(2)}, u32[]{:S(2)}) collective-permute-start(f32[14,768]{1,0:T(8,128)S(1)} %concatenate.45), channel_id=1, source_target_pairs={{0,1},{1,0},{2,3},{3,2},{4,5},{5,4},{6,7},{7,6},{8,9},{9,8},{10,11... | collective-permute-start | bytes 129032 | tf_op jit(solution)/shard_map/ppermute | solution.py:65
  478.9 1.3 collective-permute-start.35
  480.2 6.5 %collective-permute-start.36 = (f32[18,768]{1,0:T(8,128)S(1)}, f32[18,768]{1,0:T(8,128)S(1)}, u32[]{:S(2)}, u32[]{:S(2)}) collective-permute-start(f32[18,768]{1,0:T(8,128)S(1)} %add.538), channel_id=1, source_target_pairs={{0,4},{4,0},{8,12},{12,8},{1,5},{5,1},{9,13},{13,9},{2,6},{6,2},{1... | collective-permute-start | bytes 165896 | tf_op jit(solution)/shard_map/ppermute | solution.py:658
  486.7 7.5 %collective-permute-start.37 = (f32[18,768]{1,0:T(8,128)S(1)}, f32[18,768]{1,0:T(8,128)S(1)}, u32[]{:S(2)}, u32[]{:S(2)}) collective-permute-start(f32[18,768]{1,0:T(8,128)S(1)} %add.539), channel_id=1, source_target_pairs={{4,8},{8,4},{12,0},{0,12},{5,9},{9,5},{13,1},{1,13},{6,10},{10,6},... | collective-permute-start | bytes 165896 | tf_op jit(solution)/shard_map/ppermute | solution.py:658
  494.1 6.0 %collective-permute-start.38 = (f32[18,768]{1,0:T(8,128)S(1)}, f32[18,768]{1,0:T(8,128)S(1)}, u32[]{:S(2)}, u32[]{:S(2)}) collective-permute-start(f32[18,768]{1,0:T(8,128)S(1)} %add.540), channel_id=1, source_target_pairs={{0,32},{32,0},{64,96},{96,64},{1,33},{33,1},{65,97},{97,65},{2,34}... | collective-permute-start | bytes 165896 | tf_op jit(solution)/shard_map/ppermute | solution.py:658
  500.2 7.2 %collective-permute-start.39 = (f32[18,768]{1,0:T(8,128)S(1)}, f32[18,768]{1,0:T(8,128)S(1)}, u32[]{:S(2)}, u32[]{:S(2)}) collective-permute-start(f32[18,768]{1,0:T(8,128)S(1)} %add.541), channel_id=1, source_target_pairs={{32,64},{64,32},{96,0},{0,96},{33,65},{65,33},{97,1},{1,97},{34,66... | collective-permute-start | bytes 165896 | tf_op jit(solution)/shard_map/ppermute | solution.py:658
  507.4 4.4 collective-permute-start.40
  (105 other events, 666.9 us)
Sparse Core Ops, SparseCore 0:
  24.7 57.0 all-gather.6
  84.1 60.4 all-gather.8
  195.5 86.6 reduce-scatter.2
  286.0 107.4 reduce-scatter.4
  417.2 97.6 all-gather.10

commit v7 on v6

--- a/solution.py
+++ b/solution.py
@@ -117,6 +117,7 @@
 
 
 def attend_kernel(
+    sends_mixture,
     place_ref,
     slot_ref,
     query_weight,
@@ -150,9 +151,17 @@
         mixture_ref[:, cut] = t_dot_in_kernel(probs, value_ref[:, cut]).astype(BF16)
         logsum_ref[0, head : head + 1, :] = highest + jnp.log(totals)
     half = count // 2
-    for side, share_ref in ((place_ref[1], own_ref), (1 - place_ref[1], sent_ref)):
-        rows = mixture_ref[pl.ds(pl.multiple_of(side * half, half), half), :]
-        share = dot(rows, output_weight[0])
+
+    def rows_at(side):
+        return mixture_ref[pl.ds(pl.multiple_of(side * half, half), half), :]
+
+    parts = [(place_ref[1], own_ref)]
+    if sends_mixture:
+        sent_ref[...] = 0.5 * rows_at(1 - place_ref[1]).astype(F32)
+    else:
+        parts.append((1 - place_ref[1], sent_ref))
+    for side, share_ref in parts:
+        share = dot(rows_at(side), output_weight[0])
 
         @pl.when(pl.program_id(0) == 0)
         def _():
@@ -163,7 +172,9 @@
             share_ref[...] += share
 
 
-def attend(layer, length, side, slots, query_weight, query_bias, key_weight, value_weight, value_bias, output_weight):
+def attend(
+    layer, length, side, slots, query_weight, query_bias, key_weight, value_weight, value_bias, output_weight, sends_mixture
+):
     count, width = slots.shape
     heads = query_weight.shape[2]
     pair = 2 * HEAD_DIM
@@ -173,17 +184,21 @@
     bias = pl.BlockSpec((1, pair), lambda i: (0, i))
     part = pl.BlockSpec((count, pair), lambda i: (0, i))
     part_shape = jax.ShapeDtypeStruct((count, heads), BF16)
+    shared = pl.BlockSpec((count // 2, width), lambda i: (0, 0))
+    sent, sent_width = shared, width
+    if sends_mixture:
+        sent, sent_width = pl.BlockSpec((count // 2, pair), lambda i: (0, i)), heads
     return pl.pallas_call(
-        attend_kernel,
+        lambda *refs: attend_kernel(sends_mixture, *refs),
         grid=(steps,),
         in_specs=[SCALAR, whole, weight, bias, weight, weight, bias]
         + [pl.BlockSpec((1, pair, width), lambda i: (layer, i, 0))],
         out_specs=[part] * 4
         + [pl.BlockSpec((1, 2, count), lambda i: (i, 0, 0))]
-        + [pl.BlockSpec((count // 2, width), lambda i: (0, 0))] * 2,
+        + [shared, sent],
         out_shape=[part_shape] * 4
         + [jax.ShapeDtypeStruct((steps, 2, count), F32)]
-        + [jax.ShapeDtypeStruct((count // 2, width), F32)] * 2,
+        + [jax.ShapeDtypeStruct((count // 2, width), F32), jax.ShapeDtypeStruct((count // 2, sent_width), F32)],
         compiler_params=LIMIT,
         cost_estimate=pl.CostEstimate(
             flops=8 * count * width * heads + 4 * count * count * heads,
@@ -384,38 +399,32 @@
     )(part.reshape(1), *lows, mixture, rounded, attended_low, *more)
 
 
-def sort_kernel(units_rows, piece_ref, down_ref, up_ref, *output_refs):
-    chips, _, _, width = piece_ref.shape
-    rows = units_rows
+def sort_kernel(piece_ref, down_ref, up_ref):
+    chips, _, rows, width = piece_ref.shape
     for i in range(chips):
-        down_ref[i * rows : (i + 1) * rows, :] = piece_ref[i, 0, :rows].astype(BF16)
-        up = piece_ref[i, 1, :rows].astype(BF16)
+        down_ref[i * rows : (i + 1) * rows, :] = piece_ref[i, 0].astype(BF16)
+        up = piece_ref[i, 1].astype(BF16)
         half = rows // 2
         up_ref[i * half : (i + 1) * half, :width] = up[:half]
         up_ref[i * half : (i + 1) * half, width:] = up[half:]
-    for output_ref in output_refs:
-        output_ref[...] = piece_ref[:, 0, rows:].reshape(output_ref.shape).astype(BF16)
-
-
-def sort_weights(gathered, units):
+
+
+def sort_weights(gathered):
     chips, _, rows, width = gathered.shape
-    step = 4
-    heads = chips * rows - units
-    more = 1 if heads else 0
+    step = 2
+    units = chips * rows
     return pl.pallas_call(
-        lambda *refs: sort_kernel(units // chips, *refs),
+        sort_kernel,
         grid=(chips // step,),
         in_specs=[pl.BlockSpec((step, 2, rows, width), lambda i: (i, 0, 0, 0))],
         out_specs=[
-            pl.BlockSpec((units * step // chips, width), lambda i: (i, 0)),
-            pl.BlockSpec((width * step // chips, units), lambda i: (i, 0)),
-        ]
-        + [pl.BlockSpec((heads * step // chips, width), lambda i: (i, 0))] * more,
+            pl.BlockSpec((step * rows, width), lambda i: (i, 0)),
+            pl.BlockSpec((step * rows // 2, units), lambda i: (i, 0)),
+        ],
         out_shape=[
             jax.ShapeDtypeStruct((units, width), BF16),
             jax.ShapeDtypeStruct((width, units), BF16),
-        ]
-        + [jax.ShapeDtypeStruct((heads, width), BF16)] * more,
+        ],
         compiler_params=LIMIT,
         cost_estimate=pl.CostEstimate(flops=0, bytes_accessed=12 * units * width, transcendentals=0),
         name="sort_weights",
@@ -514,8 +523,7 @@
 
     rows_down = units // 16
     pieces = weight_pieces(chip, core, down_weight, up_weight)
-    pieces2 = jnp.concatenate([pieces[1], piece(output_weight[1], chip, columns // 16).astype(F32)])
-    pieces1, pieces2 = together(swap(pieces[0], "h"), pieces2)
+    pieces1, pieces2 = together(swap(pieces[0], "h"), pieces[1])
     gathered1 = lax.all_gather(pieces1, PLANE + ("c",))
     pieces2 = swap(pieces2, "h")
     peer_up_bias = swap(up_bias.astype(F32), "h")
@@ -540,6 +548,7 @@
             value_weight,
             value_bias[layer].astype(F32)[None],
             output_weight,
+            layer == 1,
         )
         return attention, share, sent
 
@@ -589,18 +598,18 @@
 
     att1, share, sent = attention_forward(0, tokens)
     pieces2, sent = together(pieces2, sent)
-    peers1 = sort_weights(gathered1.reshape(16, 2, rows_down, width), units)
+    peers1 = sort_weights(gathered1.reshape(16, 2, rows_down, width))
     gathered2 = lax.all_gather(pieces2, PLANE + ("c",))
-    x2_own, saved1 = layer_forward(0, own_slots(tokens).astype(F32), share + swap(sent, "h"), peers1)
-    sent = 0.5 * x2_own
+    received, peer_output = together(swap(sent, "h"), 0.5 * output_weight[1].astype(F32))
+    peer_output = swap(peer_output, "h")
+    x2_own, saved1 = layer_forward(0, own_slots(tokens).astype(F32), share + received, peers1)
+    sent, peer_output = together(0.5 * x2_own, peer_output)
+    peer_output = (2.0 * peer_output).astype(BF16)
     x2_low = (2.0 * in_order(side, sent, swap(sent, "h"))).astype(BF16)
-    att2, share, _ = attention_forward(1, x2_low)
-    received = swap(0.5 * piece(att2[3], 1 - side, half_slots).astype(F32), "h")
-    received, *peers2 = together(
-        received, *sort_weights(gathered2.reshape(16, 2, rows_down + columns // 16, width), units)
-    )
-    attended = share + dot((2.0 * received).astype(BF16), peers2[2])
-    _, saved2 = layer_forward(1, x2_own, attended, peers2[:2])
+    att2, share, sent = attention_forward(1, x2_low)
+    received, *peers2 = together(swap(sent, "h"), *sort_weights(gathered2.reshape(16, 2, rows_down, width)))
+    attended = share + dot((2.0 * received).astype(BF16), peer_output)
+    _, saved2 = layer_forward(1, x2_own, attended, peers2)
     scaled_last = saved2[0]
     mixture = att2[3]
     peer_down, peer_up = (peers1[0], peers2[0]), (peers1[1], peers2[1])

time: 557 us -> 553 us (level)
  waiting for transfers between devices: 263 us -> 252 us
    all_gather x1, waiting for transfers between devices: 9.41 us -> 3.67 us  [local(): gathered2 = lax.all_gather(pieces2, PLANE + ('c',))]
    ppermute x23 -> x24, waiting for transfers between devices: 163 us -> 159 us  [swap(): return lax.ppermute(values, axis, SWAP)]
    ppermute x23 -> x24, starting transfers between devices: 39.6 us -> 42 us  [swap(): return lax.ppermute(values, axis, SWAP)]
    unnamed x252 -> x242, local copies, waits for them, and re-layouts: 22.6 us -> 24.9 us
  transfers between devices with their start and end apart: 46 -> 47, of which waited for: 31 -> 31; matrix products, arithmetic and copies ran while one was open for 10% -> 10% of each run, Pallas kernels for 16% -> 17%
where the time goes in v7:
time: 553 us; the launch traced here: 544 us
  waiting for transfers between devices  252 us (46%)
  Pallas kernels  120 us (22%)
  starting transfers between devices  63.1 us (11%)
  local copies, waits for them, and re-layouts  31.6 us (6%)
  matrix products  31.1 us (6%)
  other arithmetic  29.1 us (5%)
  between operations  17.2 us (3%)
    ppermute x24, waiting for transfers between devices, swap(): return lax.ppermute(values, axis, SWAP)  159 us
    ppermute x24, starting transfers between devices, swap(): return lax.ppermute(values, axis, SWAP)  42 us
    ppermute x12, waiting for transfers between devices, ring_parts(): received.append(lax.ppermute(sent, axis, pairs))  27.7 us
    ppermute x4, waiting for transfers between devices, local(): small = small + lax.ppermute(small, axis, pairs)  26.8 us
    pallas_call x4, Pallas kernels, feed_sums(): pl.pallas_call(lambda *refs: feed_sums_kernel(bool(more), *refs), grid=(4...  26.5 us
    unnamed x242, local copies, waits for them, and re-layouts  24.9 us
    pallas_call x2, Pallas kernels, attend_back(): pl.pallas_call(attend_back_kernel, grid=(steps,), in_specs=[SCALAR, part,...  24.6 us
    reduce_scatter x1, waiting for transfers between devices, local(): rest = lax.psum_scatter(rest, PLANE, tiled=True)  21.6 us
  transfers between devices with their start and end apart: 47, of which 31 were waited for; matrix products, arithmetic and copies ran while one was open for 10% of the time, Pallas kernels for 17%

profile of v7, /device:TPU:0, one launch (start us, length us, event | category | flops | bytes accessed | tf_op | source)
XLA Modules:
  0.0 543.6 jit_solution(1361539846099765535)
XLA Ops:
  8.0 2.3 copy-done.1
  12.0 4.0 collective-permute-start
  16.1 7.0 %collective-permute-done = f32[96,768]{1,0:T(8,128)S(1)} collective-permute-done((f32[96,768]{1,0:T(8,128)S(1)}, f32[96,768]{1,0:T(8,128)S(1)}, u32[]{:S(2)}, u32[]{:S(2)}) %collective-permute-start) | collective-permute-done | bytes 294944 | tf_op jit(solution)/shard_map/ppermute | solution.py:65
  23.8 3.3 collective-permute-start.1
  27.3 10.4 %attend.2 = (bf16[512,384]{1,0:T(8,128)(2,1)S(1)}, bf16[512,384]{1,0:T(8,128)(2,1)S(1)}, bf16[512,384]{1,0:T(8,128)(2,1)S(1)}, bf16[512,384]{1,0:T(8,128)(2,1)S(...) custom-call(s32[2]{0:T(128)S(1)} %get-tuple-element.283.refs_0_, ...), custom_call_target="tpu_custom_call" | custom-call | flops 1610612736 | bytes 5505024 | tf_op jit(solution)/shard_map/attend/pallas_call | solution.py:191
  43.2 3.2 collective-permute-start.2
  48.3 2.2 multiply_bitcast_fusion
  51.7 11.4 %collective-permute-done.2 = f32[256,768]{1,0:T(8,128)S(1)} collective-permute-done((f32[256,768]{1,0:T(8,128)}, f32[256,768]{1,0:T(8,128)S(1)}, u32[]{:S(2)}, u32[]{:S(2)}) %collective-permute-start.2) | collective-permute-done | bytes 786464 | tf_op jit(solution)/shard_map/ppermute | solution.py:65
  63.2 2.8 collective-permute-start.4
  68.2 4.2 multiply_convert_fusion.3
  74.1 6.9 %all-gather.7.cloned.1.call-done = f32[3072,768]{1,0:T(8,128)} async-done(((f32[96,768]{1,0:T(8,128)}), f32[3072,768]{1,0:T(8,128)}) %all-gather.7.cloned.1.call-update) | async-done | bytes 9437200 | tf_op jit(solution)/shard_map/all_gather | solution.py:527
  81.0 5.9 %sort_weights.2 = (bf16[1536,768]{1,0:T(8,128)(2,1)S(1)}, bf16[768,1536]{1,0:T(8,128)(2,1)S(1)}) custom-call(f32[16,2,96,768]{3,2,1,0:T(8,128)} %bitcast.148), custom_call_target="tpu_custom_call" | custom-call | bytes 14155776 | tf_op jit(solution)/shard_map/sort_weights/pallas_call | solution.py:416
  91.7 3.2 collective-permute-start.5
  94.9 18.2 %collective-permute-done.5 = f32[256,768]{1,0:T(8,128)} collective-permute-done((f32[256,768]{1,0:T(8,128)S(1)}, f32[256,768]{1,0:T(8,128)}, u32[]{:S(2)}, u32[]{:S(2)}) %collective-permute-start.5) | collective-permute-done | bytes 786464 | tf_op jit(solution)/shard_map/ppermute | solution.py:65
  116.4 9.2 %attend.3 = (bf16[512,384]{1,0:T(8,128)(2,1)S(1)}, bf16[512,384]{1,0:T(8,128)(2,1)S(1)}, bf16[512,384]{1,0:T(8,128)(2,1)S(1)}, bf16[512,384]{1,0:T(8,128)(2,1)S(...) custom-call(s32[2]{0:T(128)S(1)} %get-tuple-element.283.refs_0_, ...), custom_call_target="tpu_custom_call" | custom-call | flops 1610612736 | bytes 5505024 | tf_op jit(solution)/shard_map/attend/pallas_call | solution.py:191
  130.2 3.7 collective-permute-start.6
  135.1 3.7 all-gather.9.cloned.1.call-done
  138.8 5.9 %sort_weights.3 = (bf16[1536,768]{1,0:T(8,128)(2,1)S(1)}, bf16[768,1536]{1,0:T(8,128)(2,1)S(1)}) custom-call(f32[16,2,96,768]{3,2,1,0:T(8,128)} %bitcast.147), custom_call_target="tpu_custom_call" | custom-call | bytes 14155776 | tf_op jit(solution)/shard_map/sort_weights/pallas_call | solution.py:416
  147.9 2.5 multiply_convert_fusion.1
  158.8 4.8 feed_sums.4
  163.8 2.5 fusion.50
  169.4 3.1 collective-permute-start.8
  172.5 6.0 %collective-permute-done.7.refs_7_ = f32[1536,1536]{1,0:T(8,128)} collective-permute-done((f32[1536,1536]{1,0:T(8,128)}, f32[1536,1536]{1,0:T(8,128)}, u32[]{:S(2)}, u32[]{:S(2)}) %collective-permute-start.7) | collective-permute-done | bytes 9437216 | tf_op jit(solution)/shard_map/ppermute | solution.py:65
  178.6 8.4 %feed_sums.5 = f32[1536,1536]{1,0:T(8,128)} custom-call(s32[1]{0:T(128)} %bitcast.2.refs_0_, bf16[256,1536]{1,0:T(8,128)(2,1)S(1)} %get-tuple-element.267.refs_1_, bf16[256,1536]{1,0:T(8,128)(2,1)S(1)} %get-tuple-element.269.refs_2_, bf16[256,1536]{1,0:T(8,128)(2,1)S(1)} %get-tuple-element.278.refs_3_, bf16[256,1536]{1,0:T(8,128)(2,1)S(1)} %get-tuple-element.282.refs_4_, ...), custom_call_target="tpu_custom_call" | custom-call | flops 1207959552 | bytes 18874368 | tf_op jit(solution)/shard_map/feed_sums/pallas_call | solution.py:351
  187.0 3.9 collective-permute-done.8
  194.4 12.3 %attend_back.2 = (bf16[512,384]{1,0:T(8,128)(2,1)S(1)}, bf16[512,384]{1,0:T(8,128)(2,1)S(1)}, bf16[512,384]{1,0:T(8,128)(2,1)S(1)}, f32[512,768]{1,0:T(8,128)}, ...) custom-call(s32[1]{0:T(128)} %copy.62.length_ref, bf16[512,384]{1,0:T(8,128)(2,1)S(1)} %copy-done.32, ...), custom_call_target="tpu_custom_call" | custom-call | flops 2214592512 | bytes 5505024 | tf_op jit(solution)/shard_map/attend_back/pallas_call | solution.py:272
  208.4 3.2 collective-permute-start.9
  211.6 17.2 %collective-permute-done.9 = f32[256,768]{1,0:T(8,128)S(1)} collective-permute-done((f32[256,768]{1,0:T(8,128)S(1)}, f32[256,768]{1,0:T(8,128)S(1)}, u32[]{:S(2)}, u32[]{:S(2)}) %collective-permute-start.9) | collective-permute-done | bytes 786464 | tf_op jit(solution)/shard_map/ppermute | solution.py:65
  228.9 2.4 multiply_reduce_fusion.3
  237.3 4.8 feed_sums.6
  245.7 3.4 multiply_reduce_fusion
  250.3 3.4 collective-permute-start.13
  253.7 3.5 collective-permute-done.12.refs_7_
  257.2 8.5 %feed_sums.7.refs_8_ = f32[1536,1920]{1,0:T(8,128)} custom-call(s32[1]{0:T(128)} %bitcast.2.refs_0_, bf16[256,1536]{1,0:T(8,128)(2,1)S(1)} %get-tuple-element.261.refs_1_, bf16[256,1536]{1,0:T(8,128)(2,1)S(1)} %get-tuple-element.263.refs_2_, bf16[256,1536]{1,0:T(8,128)(2,1)S(1)} %get-tuple-element.276.refs_3_, ...), custom_call_target="tpu_custom_call" | custom-call | flops 1207959552 | bytes 18874368 | tf_op jit(solution)/shard_map/feed_sums/pallas_call | solution.py:351
  265.6 3.2 attention_sums.5
  268.9 3.4 collective-permute-done.13
  272.2 5.8 %reduce-scatter.3.cloned.1.call-done = f32[96,1536]{1,0:T(8,128)} async-done(((f32[1536,1536]{1,0:T(8,128)}), f32[96,1536]{1,0:T(8,128)}) %reduce-scatter.3.cloned.1.call-update) | async-done | bytes 589840 | tf_op jit(solution)/shard_map/reduce_scatter | solution.py:625
  281.9 12.3 %attend_back.3 = (bf16[512,384]{1,0:T(8,128)(2,1)S(1)}, bf16[512,384]{1,0:T(8,128)(2,1)S(1)}, bf16[512,384]{1,0:T(8,128)(2,1)S(1)}, f32[512,768]{1,0:T(8,128)}, ...) custom-call(s32[1]{0:T(128)} %copy.62.length_ref, bf16[512,384]{1,0:T(8,128)(2,1)S(1)} %copy-done.26, ...), custom_call_target="tpu_custom_call" | custom-call | flops 2214592512 | bytes 5505024 | tf_op jit(solution)/shard_map/attend_back/pallas_call | solution.py:272
  294.2 3.1 attention_sums.6
  297.3 4.9 collective-permute-done.19.refs_7_
  302.2 3.7 attention_sums.7
  307.0 2.6 collective-permute-start.25
  314.6 9.9 %collective-permute-done.25 = f32[4,48,384]{2,1,0:T(8,128)S(1)} collective-permute-done((f32[4,48,384]{2,1,0:T(8,128)}, f32[4,48,384]{2,1,0:T(8,128)S(1)}, u32[]{:S(2)}, u32[]{:S(2)}) %collective-permute-start.25) | collective-permute-done | bytes 294944 | tf_op jit(solution)/shard_map/ppermute | solution.py:83
  325.8 7.7 %collective-permute-done.24 = f32[4,48,384]{2,1,0:T(8,128)S(1)} collective-permute-done((f32[4,48,384]{2,1,0:T(8,128)}, f32[4,48,384]{2,1,0:T(8,128)S(1)}, u32[]{:S(2)}, u32[]{:S(2)}) %collective-permute-start.24) | collective-permute-done | bytes 294944 | tf_op jit(solution)/shard_map/ppermute | solution.py:83
  334.4 6.0 %collective-permute-done.20 = f32[4,48,384]{2,1,0:T(8,128)S(1)} collective-permute-done((f32[4,48,384]{2,1,0:T(8,128)S(1)}, f32[4,48,384]{2,1,0:T(8,128)S(1)}, u32[]{:S(2)}, u32[]{:S(2)}) %collective-permute-start.20) | collective-permute-done | bytes 294944 | tf_op jit(solution)/shard_map/ppermute | solution.py:83
  340.6 2.3 collective-permute-start.28
  347.9 2.4 collective-permute-done.27
  350.3 3.0 collective-permute-start.18
  357.0 8.9 %collective-permute-done.16 = f32[96,768]{1,0:T(8,128)S(1)} collective-permute-done((f32[96,768]{1,0:T(8,128)S(1)}, f32[96,768]{1,0:T(8,128)S(1)}, u32[]{:S(2)}, u32[]{:S(2)}) %collective-permute-start.16) | collective-permute-done | bytes 294944 | tf_op jit(solution)/shard_map/ppermute | solution.py:65
  367.5 21.6 %reduce-scatter.5.cloned.1.call-done = f32[96,1920]{1,0:T(8,128)} async-done(((f32[1536,1920]{1,0:T(8,128)}), f32[96,1920]{1,0:T(8,128)}) %reduce-scatter.5.cloned.1.call-update) | async-done | bytes 737296 | tf_op jit(solution)/shard_map/reduce_scatter | solution.py:637
  392.8 2.1 collective-permute-start.35
  395.7 8.7 %collective-permute-done.33 = f32[96,1152]{1,0:T(8,128)S(1)} collective-permute-done((f32[96,1152]{1,0:T(8,128)S(1)}, f32[96,1152]{1,0:T(8,128)S(1)}, u32[]{:S(2)}, u32[]{:S(2)}) %collective-permute-start.33) | collective-permute-done | bytes 442400 | tf_op jit(solution)/shard_map/ppermute | solution.py:65
  404.4 7.2 %collective-permute-done.34 = f32[96,768]{1,0:T(8,128)S(1)} collective-permute-done((f32[96,768]{1,0:T(8,128)S(1)}, f32[96,768]{1,0:T(8,128)S(1)}, u32[]{:S(2)}, u32[]{:S(2)}) %collective-permute-start.34) | collective-permute-done | bytes 294944 | tf_op jit(solution)/shard_map/ppermute | solution.py:65
  413.7 35.9 %collective-permute-done.14 = f32[512,768]{1,0:T(8,128)S(1)} collective-permute-done((f32[512,768]{1,0:T(8,128)}, f32[512,768]{1,0:T(8,128)S(1)}, u32[]{:S(2)}, u32[]{:S(2)}) %collective-permute-start.14) | collective-permute-done | bytes 1572896 | tf_op jit(solution)/shard_map/ppermute | solution.py:65
  449.6 2.9 add_add_fusion
  454.1 2.3 collective-permute-start.10
  456.6 16.1 %collective-permute-done.10 = f32[14,768]{1,0:T(8,128)S(1)} collective-permute-done((f32[14,768]{1,0:T(8,128)S(1)}, f32[14,768]{1,0:T(8,128)S(1)}, u32[]{:S(2)}, u32[]{:S(2)}) %collective-permute-start.10) | collective-permute-done | bytes 43040 | tf_op jit(solution)/shard_map/ppermute | solution.py:65
  475.9 6.4 %collective-permute-done.37 = f32[18,768]{1,0:T(8,128)S(1)} collective-permute-done((f32[18,768]{1,0:T(8,128)S(1)}, f32[18,768]{1,0:T(8,128)S(1)}, u32[]{:S(2)}, u32[]{:S(2)}) %collective-permute-start.37) | collective-permute-done | bytes 55328 | tf_op jit(solution)/shard_map/ppermute | solution.py:667
  482.4 7.4 %collective-permute-done.38 = f32[18,768]{1,0:T(8,128)S(1)} collective-permute-done((f32[18,768]{1,0:T(8,128)S(1)}, f32[18,768]{1,0:T(8,128)S(1)}, u32[]{:S(2)}, u32[]{:S(2)}) %collective-permute-start.38) | collective-permute-done | bytes 55328 | tf_op jit(solution)/shard_map/ppermute | solution.py:667
  489.9 5.9 %collective-permute-done.39 = f32[18,768]{1,0:T(8,128)S(1)} collective-permute-done((f32[18,768]{1,0:T(8,128)S(1)}, f32[18,768]{1,0:T(8,128)S(1)}, u32[]{:S(2)}, u32[]{:S(2)}) %collective-permute-start.39) | collective-permute-done | bytes 55328 | tf_op jit(solution)/shard_map/ppermute | solution.py:667
  495.9 7.1 %collective-permute-done.40 = f32[18,768]{1,0:T(8,128)S(1)} collective-permute-done((f32[18,768]{1,0:T(8,128)S(1)}, f32[18,768]{1,0:T(8,128)S(1)}, u32[]{:S(2)}, u32[]{:S(2)}) %collective-permute-start.40) | collective-permute-done | bytes 55328 | tf_op jit(solution)/shard_map/ppermute | solution.py:667
  503.4 4.1 collective-permute-done.41
  512.9 8.0 %place_attention.1 = (f32[2,768,384]{2,1,0:T(8,128)}, f32[2,768,384]{2,1,0:T(8,128)}, f32[2,768,384]{2,1,0:T(8,128)}, f32[2,384,768]{2,1,0:T(8,128)}) custom-call(f32[16,2,96,2304]{3,2,1,0:T(8,128)} %bitcast.141, f32[16,2,96,2304]{3,2,1,0:T(8,128)} %bitcast.142, f32[16,2,96,2304]{3,2,1,0:T(8,128)} %bitcast.143, f32[16,2,96,2304]{3,2,1,0:T(8,128)} %bitcast.144), custom_call_target="tpu_custom_call" | custom-call | tf_op jit(solution)/shard_map/place_attention/pallas_call | solution.py:481
  521.0 15.6 %place_feed.1 = (f32[2,1536,768]{2,1,0:T(8,128)}, f32[2,768,1536]{2,1,0:T(8,128)}) custom-call(f32[16,2,96,2304]{3,2,1,0:T(8,128)} %bitcast.145, f32[16,2,96,2304]{3,2,1,0:T(8,128)} %bitcast.146), custom_call_target="tpu_custom_call" | custom-call | tf_op jit(solution)/shard_map/place_feed/pallas_call | solution.py:464
  (429 shorter events, 98.1 us)
Async XLA Ops:
  7.2 73.8 %all-gather.7.cloned.1.call-start = ((), (), s32[]{:S(2)}) async-start(), calls=%async_computation.4 | async-start | bytes 9732096 | tf_op jit(solution)/shard_map/all_gather | solution.py:527
  12.0 11.0 %collective-permute-start = (f32[96,768]{1,0:T(8,128)S(1)}, f32[96,768]{1,0:T(8,128)S(1)}, u32[]{:S(2)}, u32[]{:S(2)}) collective-permute-start(f32[96,768]{1,0:T(8,128)S(1)} %get-tuple-element.239), channel_id=1, source_target_pairs={{0,1},{1,0},{2,3},{3,2},{4,5},{5,4},{6,7},{7,6},{8,9},{9,8},{10,11... | collective-permute-start | bytes 884744 | tf_op jit(solution)/shard_map/ppermute | solution.py:65
  23.8 115.0 %all-gather.9.cloned.1.call-start = ((), (), s32[]{:S(2)}) async-start(), calls=%async_computation.5 | async-start | bytes 9732096 | tf_op jit(solution)/shard_map/all_gather | solution.py:602
  23.8 17.5 %collective-permute-start.1 = (f32[96,768]{1,0:T(8,128)S(1)}, f32[96,768]{1,0:T(8,128)S(1)}, u32[]{:S(2)}, u32[]{:S(2)}) collective-permute-start(f32[96,768]{1,0:T(8,128)S(1)} %get-tuple-element.93), channel_id=1, source_target_pairs={{0,1},{1,0},{2,3},{3,2},{4,5},{5,4},{6,7},{7,6},{8,9},{9,8},{10,11... | collective-permute-start | bytes 884744 | tf_op jit(solution)/shard_map/ppermute | solution.py:65
  42.1 235.9 %reduce-scatter.3.cloned.1.call-start = ((), (), s32[]{:S(2)}) async-start(), calls=%async_computation.2 | async-start | bytes 10027008 | tf_op jit(solution)/shard_map/reduce_scatter | solution.py:625
  42.2 8.9 %collective-permute-start.3 = (f32[2,1536]{1,0:T(2,128)S(1)}, f32[2,1536]{1,0:T(2,128)S(1)}, u32[]{:S(2)}, u32[]{:S(2)}) collective-permute-start(f32[2,1536]{1,0:T(2,128)S(1)} %convert_element_type.152), channel_id=1, source_target_pairs={{0,1},{1,0},{2,3},{3,2},{4,5},{5,4},{6,7},{7,6},{8,9},{9,8},{10,11... | collective-permute-start | bytes 36872 | tf_op jit(solution)/shard_map/ppermute | solution.py:65
  43.2 20.0 %collective-permute-start.2 = (f32[256,768]{1,0:T(8,128)}, f32[256,768]{1,0:T(8,128)S(1)}, u32[]{:S(2)}, u32[]{:S(2)}) collective-permute-start(f32[256,768]{1,0:T(8,128)} %get-tuple-element.95), channel_id=1, source_target_pairs={{0,1},{1,0},{2,3},{3,2},{4,5},{5,4},{6,7},{7,6},{8,9},{9,8},{10,11... | collective-permute-start | bytes 2359304 | tf_op jit(solution)/shard_map/ppermute | solution.py:65
  47.6 41.3 %copy-start.62 = (f32[768]{0:T(1024)}, f32[768]{0:T(1024)S(1)}, u32[]{:S(2)}) copy-start(f32[768]{0:T(1024)S(1)} %get-tuple-element.287) | copy-start | bytes 9220
  63.2 28.5 %collective-permute-start.4 = (f32[384,768]{1,0:T(8,128)}, f32[384,768]{1,0:T(8,128)}, u32[]{:S(2)}, u32[]{:S(2)}) collective-permute-start(f32[384,768]{1,0:T(8,128)} %multiply_bitcast_fusion), channel_id=1, source_target_pairs={{0,1},{1,0},{2,3},{3,2},{4,5},{5,4},{6,7},{7,6},{8,9},{9,8},{10,11... | collective-permute-start | bytes 3538952 | tf_op jit(solution)/shard_map/ppermute | solution.py:65
  91.7 21.4 %collective-permute-start.5 = (f32[256,768]{1,0:T(8,128)S(1)}, f32[256,768]{1,0:T(8,128)}, u32[]{:S(2)}, u32[]{:S(2)}) collective-permute-start(f32[256,768]{1,0:T(8,128)S(1)} %fusion.62), channel_id=1, source_target_pairs={{0,1},{1,0},{2,3},{3,2},{4,5},{5,4},{6,7},{7,6},{8,9},{9,8},{10,11... | collective-permute-start | bytes 2359304 | tf_op jit(solution)/shard_map/ppermute | solution.py:65
  130.2 14.6 %collective-permute-start.6 = (f32[256,384]{1,0:T(8,128)}, f32[256,384]{1,0:T(8,128)}, u32[]{:S(2)}, u32[]{:S(2)}) collective-permute-start(f32[256,384]{1,0:T(8,128)} %get-tuple-element.103), channel_id=1, source_target_pairs={{0,1},{1,0},{2,3},{3,2},{4,5},{5,4},{6,7},{7,6},{8,9},{9,8},{10,11... | collective-permute-start | bytes 1179656 | tf_op jit(solution)/shard_map/ppermute | solution.py:65
  163.6 15.0 %collective-permute-start.7 = (f32[1536,1536]{1,0:T(8,128)}, f32[1536,1536]{1,0:T(8,128)}, u32[]{:S(2)}, u32[]{:S(2)}) collective-permute-start(f32[1536,1536]{1,0:T(8,128)} %feed_sums.4), channel_id=1, source_target_pairs={{0,2},{2,0},{1,3},{3,1},{4,6},{6,4},{5,7},{7,5},{8,10},{10,8},{9,1... | collective-permute-start | bytes 28311560 | tf_op jit(solution)/shard_map/ppermute | solution.py:65
  169.4 21.5 %collective-permute-start.8 = (f32[256,768]{1,0:T(8,128)}, f32[256,768]{1,0:T(8,128)}, u32[]{:S(2)}, u32[]{:S(2)}) collective-permute-start(f32[256,768]{1,0:T(8,128)} %get-tuple-element.209), channel_id=1, source_target_pairs={{0,1},{1,0},{2,3},{3,2},{4,5},{5,4},{6,7},{7,6},{8,9},{9,8},{10,11... | collective-permute-start | bytes 2359304 | tf_op jit(solution)/shard_map/ppermute | solution.py:65
  190.9 198.2 %reduce-scatter.5.cloned.1.call-start = ((), (), s32[]{:S(2)}) async-start(), calls=%async_computation.3 | async-start | bytes 12533760 | tf_op jit(solution)/shard_map/reduce_scatter | solution.py:637
  208.4 20.5 %collective-permute-start.9 = (f32[256,768]{1,0:T(8,128)S(1)}, f32[256,768]{1,0:T(8,128)S(1)}, u32[]{:S(2)}, u32[]{:S(2)}) collective-permute-start(f32[256,768]{1,0:T(8,128)S(1)} %constant_dynamic-slice_fusion), channel_id=1, source_target_pairs={{0,1},{1,0},{2,3},{3,2},{4,5},{5,4},{6,7},{7,6},{8,9},{9,8},{10,11... | collective-permute-start | bytes 2359304 | tf_op jit(solution)/shard_map/ppermute | solution.py:65
  242.2 15.0 %collective-permute-start.12 = (f32[1536,1536]{1,0:T(8,128)}, f32[1536,1536]{1,0:T(8,128)}, u32[]{:S(2)}, u32[]{:S(2)}) collective-permute-start(f32[1536,1536]{1,0:T(8,128)} %feed_sums.6), channel_id=1, source_target_pairs={{0,2},{2,0},{1,3},{3,1},{4,6},{6,4},{5,7},{7,5},{8,10},{10,8},{9,1... | collective-permute-start | bytes 28311560 | tf_op jit(solution)/shard_map/ppermute | solution.py:65
  244.3 21.3 %collective-permute-start.11 = (f32[1536,384]{1,0:T(8,128)S(1)}, f32[1536,384]{1,0:T(8,128)S(1)}, u32[]{:S(2)}, u32[]{:S(2)}) collective-permute-start(f32[1536,384]{1,0:T(8,128)S(1)} %attention_sums.4), channel_id=1, source_target_pairs={{0,2},{2,0},{1,3},{3,1},{4,6},{6,4},{5,7},{7,5},{8,10},{10,8},{9,1... | collective-permute-start | bytes 7077896 | tf_op jit(solution)/shard_map/ppermute | solution.py:65
  250.3 21.9 %collective-permute-start.13 = (f32[256,768]{1,0:T(8,128)}, f32[256,768]{1,0:T(8,128)}, u32[]{:S(2)}, u32[]{:S(2)}) collective-permute-start(f32[256,768]{1,0:T(8,128)} %multiply_multiply_fusion.4), channel_id=1, source_target_pairs={{0,1},{1,0},{2,3},{3,2},{4,5},{5,4},{6,7},{7,6},{8,9},{9,8},{10,11... | collective-permute-start | bytes 2359304 | tf_op jit(solution)/shard_map/ppermute | solution.py:65
  278.0 234.9 %all-gather.11.cloned.1.call-start = ((), (), s32[]{:S(2)}) async-start(), calls=%async_computation.6 | async-start | bytes 29196288 | tf_op jit(solution)/shard_map/all_gather | solution.py:653
  297.3 4.9 collective-permute-start.19
  307.0 17.5 %collective-permute-start.25 = (f32[4,48,384]{2,1,0:T(8,128)}, f32[4,48,384]{2,1,0:T(8,128)S(1)}, u32[]{:S(2)}, u32[]{:S(2)}) collective-permute-start(f32[4,48,384]{2,1,0:T(8,128)} %get-tuple-element.226), channel_id=1, source_target_pairs={{0,64},{32,96},{64,0},{96,32},{1,65},{33,97},{65,1},{97,33},{2,66}... | collective-permute-start | bytes 884744 | tf_op jit(solution)/shard_map/ppermute | solution.py:83
  309.6 23.9 %collective-permute-start.24 = (f32[4,48,384]{2,1,0:T(8,128)}, f32[4,48,384]{2,1,0:T(8,128)S(1)}, u32[]{:S(2)}, u32[]{:S(2)}) collective-permute-start(f32[4,48,384]{2,1,0:T(8,128)} %get-tuple-element.227), channel_id=1, source_target_pairs={{0,96},{32,0},{64,32},{96,64},{1,97},{33,1},{65,33},{97,65},{2,98}... | collective-permute-start | bytes 884744 | tf_op jit(solution)/shard_map/ppermute | solution.py:83
  311.0 22.5 %collective-permute-start.23 = (f32[4,48,384]{2,1,0:T(8,128)S(1)}, f32[4,48,384]{2,1,0:T(8,128)S(1)}, u32[]{:S(2)}, u32[]{:S(2)}) collective-permute-start(f32[4,48,384]{2,1,0:T(8,128)S(1)} %get-tuple-element.228), channel_id=1, source_target_pairs={{0,32},{32,64},{64,96},{96,0},{1,33},{33,65},{65,97},{97,1},{2,34}... | collective-permute-start | bytes 884744 | tf_op jit(solution)/shard_map/ppermute | solution.py:83
  311.7 21.8 %collective-permute-start.22 = (f32[4,48,384]{2,1,0:T(8,128)S(1)}, f32[4,48,384]{2,1,0:T(8,128)S(1)}, u32[]{:S(2)}, u32[]{:S(2)}) collective-permute-start(f32[4,48,384]{2,1,0:T(8,128)S(1)} %get-tuple-element.230), channel_id=1, source_target_pairs={{0,8},{4,12},{8,0},{12,4},{1,9},{5,13},{9,1},{13,5},{2,10},{6,14},... | collective-permute-start | bytes 884744 | tf_op jit(solution)/shard_map/ppermute | solution.py:83
  313.4 21.0 %collective-permute-start.21 = (f32[4,48,384]{2,1,0:T(8,128)S(1)}, f32[4,48,384]{2,1,0:T(8,128)S(1)}, u32[]{:S(2)}, u32[]{:S(2)}) collective-permute-start(f32[4,48,384]{2,1,0:T(8,128)S(1)} %get-tuple-element.231), channel_id=1, source_target_pairs={{0,12},{4,0},{8,4},{12,8},{1,13},{5,1},{9,5},{13,9},{2,14},{6,2},{... | collective-permute-start | bytes 884744 | tf_op jit(solution)/shard_map/ppermute | solution.py:83
  324.5 16.0 %collective-permute-start.20 = (f32[4,48,384]{2,1,0:T(8,128)S(1)}, f32[4,48,384]{2,1,0:T(8,128)S(1)}, u32[]{:S(2)}, u32[]{:S(2)}) collective-permute-start(f32[4,48,384]{2,1,0:T(8,128)S(1)} %get-tuple-element.232), channel_id=1, source_target_pairs={{0,4},{4,8},{8,12},{12,0},{1,5},{5,9},{9,13},{13,1},{2,6},{6,10},{... | collective-permute-start | bytes 884744 | tf_op jit(solution)/shard_map/ppermute | solution.py:83
  340.6 7.3 %collective-permute-start.28 = (f32[48,384]{1,0:T(8,128)S(1)}, f32[48,384]{1,0:T(8,128)S(1)}, u32[]{:S(2)}, u32[]{:S(2)}) collective-permute-start(f32[48,384]{1,0:T(8,128)S(1)} %get-tuple-element.244), channel_id=1, source_target_pairs={{0,64},{32,96},{64,0},{96,32},{1,65},{33,97},{65,1},{97,33},{2,66}... | collective-permute-start | bytes 221192 | tf_op jit(solution)/shard_map/ppermute | solution.py:83
  342.9 7.4 %collective-permute-start.27 = (f32[48,384]{1,0:T(8,128)S(1)}, f32[48,384]{1,0:T(8,128)S(1)}, u32[]{:S(2)}, u32[]{:S(2)}) collective-permute-start(f32[48,384]{1,0:T(8,128)S(1)} %get-tuple-element.245), channel_id=1, source_target_pairs={{0,96},{32,0},{64,32},{96,64},{1,97},{33,1},{65,33},{97,65},{2,98}... | collective-permute-start | bytes 221192 | tf_op jit(solution)/shard_map/ppermute | solution.py:83
  344.4 8.9 %collective-permute-start.26 = (f32[48,384]{1,0:T(8,128)S(1)}, f32[48,384]{1,0:T(8,128)S(1)}, u32[]{:S(2)}, u32[]{:S(2)}) collective-permute-start(f32[48,384]{1,0:T(8,128)S(1)} %get-tuple-element.246), channel_id=1, source_target_pairs={{0,32},{32,64},{64,96},{96,0},{1,33},{33,65},{65,97},{97,1},{2,34}... | collective-permute-start | bytes 221192 | tf_op jit(solution)/shard_map/ppermute | solution.py:83
  345.1 9.8 %collective-permute-start.31 = (f32[48,384]{1,0:T(8,128)S(1)}, f32[48,384]{1,0:T(8,128)S(1)}, u32[]{:S(2)}, u32[]{:S(2)}) collective-permute-start(f32[48,384]{1,0:T(8,128)S(1)} %get-tuple-element.240), channel_id=1, source_target_pairs={{0,8},{4,12},{8,0},{12,4},{1,9},{5,13},{9,1},{13,5},{2,10},{6,14},... | collective-permute-start | bytes 221192 | tf_op jit(solution)/shard_map/ppermute | solution.py:83
  345.4 10.2 %collective-permute-start.30 = (f32[48,384]{1,0:T(8,128)S(1)}, f32[48,384]{1,0:T(8,128)S(1)}, u32[]{:S(2)}, u32[]{:S(2)}) collective-permute-start(f32[48,384]{1,0:T(8,128)S(1)} %get-tuple-element.241), channel_id=1, source_target_pairs={{0,12},{4,0},{8,4},{12,8},{1,13},{5,1},{9,5},{13,9},{2,14},{6,2},{... | collective-permute-start | bytes 221192 | tf_op jit(solution)/shard_map/ppermute | solution.py:83
  347.9 7.7 %collective-permute-start.29 = (f32[48,384]{1,0:T(8,128)S(1)}, f32[48,384]{1,0:T(8,128)S(1)}, u32[]{:S(2)}, u32[]{:S(2)}) collective-permute-start(f32[48,384]{1,0:T(8,128)S(1)} %get-tuple-element.242), channel_id=1, source_target_pairs={{0,4},{4,8},{8,12},{12,0},{1,5},{5,9},{9,13},{13,1},{2,6},{6,10},{... | collective-permute-start | bytes 221192 | tf_op jit(solution)/shard_map/ppermute | solution.py:83
  350.3 15.6 %collective-permute-start.18 = (f32[96,768]{1,0:T(8,128)S(1)}, f32[96,768]{1,0:T(8,128)S(1)}, u32[]{:S(2)}, u32[]{:S(2)}) collective-permute-start(f32[96,768]{1,0:T(8,128)S(1)} %get-tuple-element.237), channel_id=1, source_target_pairs={{0,17},{17,0},{1,16},{16,1},{2,19},{19,2},{3,18},{18,3},{4,21},{21... | collective-permute-start | bytes 884744 | tf_op jit(solution)/shard_map/ppermute | solution.py:643
  353.4 12.5 %collective-permute-start.17 = (f32[96,768]{1,0:T(8,128)S(1)}, f32[96,768]{1,0:T(8,128)S(1)}, u32[]{:S(2)}, u32[]{:S(2)}) collective-permute-start(f32[96,768]{1,0:T(8,128)S(1)} %get-tuple-element.237), channel_id=1, source_target_pairs={{0,1},{1,0},{2,3},{3,2},{4,5},{5,4},{6,7},{7,6},{8,9},{9,8},{10,11... | collective-permute-start | bytes 884744 | tf_op jit(solution)/shard_map/ppermute | solution.py:65
  354.9 11.0 %collective-permute-start.16 = (f32[96,768]{1,0:T(8,128)S(1)}, f32[96,768]{1,0:T(8,128)S(1)}, u32[]{:S(2)}, u32[]{:S(2)}) collective-permute-start(f32[96,768]{1,0:T(8,128)S(1)} %get-tuple-element.236), channel_id=1, source_target_pairs={{0,16},{16,0},{1,17},{17,1},{2,18},{18,2},{3,19},{19,3},{4,20},{20... | collective-permute-start | bytes 884744 | tf_op jit(solution)/shard_map/ppermute | solution.py:65
  355.7 11.8 %collective-permute-start.32 = (f32[96,384]{1,0:T(8,128)S(1)}, f32[96,384]{1,0:T(8,128)S(1)}, u32[]{:S(2)}, u32[]{:S(2)}) collective-permute-start(f32[96,384]{1,0:T(8,128)S(1)} %pad_maximum_fusion.2), channel_id=1, source_target_pairs={{0,16},{16,0},{1,17},{17,1},{2,18},{18,2},{3,19},{19,3},{4,20},{20... | collective-permute-start | bytes 442376 | tf_op jit(solution)/shard_map/ppermute | solution.py:65
  391.2 13.2 %collective-permute-start.33 = (f32[96,1152]{1,0:T(8,128)S(1)}, f32[96,1152]{1,0:T(8,128)S(1)}, u32[]{:S(2)}, u32[]{:S(2)}) collective-permute-start(f32[96,1152]{1,0:T(8,128)S(1)} %pad_maximum_fusion.1), channel_id=1, source_target_pairs={{0,16},{16,0},{1,17},{17,1},{2,18},{18,2},{3,19},{19,3},{4,20},{20... | collective-permute-start | bytes 1327112 | tf_op jit(solution)/shard_map/ppermute | solution.py:65
  392.8 11.6 %collective-permute-start.35 = (f32[96,768]{1,0:T(8,128)S(1)}, f32[96,768]{1,0:T(8,128)S(1)}, u32[]{:S(2)}, u32[]{:S(2)}) collective-permute-start(f32[96,768]{1,0:T(8,128)S(1)} %get-tuple-element.234), channel_id=1, source_target_pairs={{0,17},{17,0},{1,16},{16,1},{2,19},{19,2},{3,18},{18,3},{4,21},{21... | collective-permute-start | bytes 884744 | tf_op jit(solution)/shard_map/ppermute | solution.py:643
  395.0 16.6 %collective-permute-start.34 = (f32[96,768]{1,0:T(8,128)S(1)}, f32[96,768]{1,0:T(8,128)S(1)}, u32[]{:S(2)}, u32[]{:S(2)}) collective-permute-start(f32[96,768]{1,0:T(8,128)S(1)} %get-tuple-element.234), channel_id=1, source_target_pairs={{0,1},{1,0},{2,3},{3,2},{4,5},{5,4},{6,7},{7,6},{8,9},{9,8},{10,11... | collective-permute-start | bytes 884744 | tf_op jit(solution)/shard_map/ppermute | solution.py:65
  411.7 37.9 %copy-start.48 = (f32[256,768]{1,0:T(8,128)S(1)}, f32[256,768]{1,0:T(8,128)}, u32[]{:S(2)}) copy-start(f32[256,768]{1,0:T(8,128)} %copy-done.47) | copy-start | bytes 2359300
  412.7 39.8 %copy-start.52 = (f32[256,768]{1,0:T(8,128)S(1)}, f32[256,768]{1,0:T(8,128)}, u32[]{:S(2)}) copy-start(f32[256,768]{1,0:T(8,128)} %copy-done.51) | copy-start | bytes 2359300
  412.7 41.1 %copy-start.79 = (f32[768]{0:T(1024)S(1)}, f32[768]{0:T(1024)}, u32[]{:S(2)}) copy-start(f32[768]{0:T(1024)} %get-tuple-element.173) | copy-start | bytes 9220
  412.7 41.1 %copy-start.78 = (f32[768]{0:T(1024)S(1)}, f32[768]{0:T(1024)}, u32[]{:S(2)}) copy-start(f32[768]{0:T(1024)} %get-tuple-element.179) | copy-start | bytes 9220
  412.7 41.1 %copy-start.80 = (f32[768]{0:T(1024)S(1)}, f32[768]{0:T(1024)}, u32[]{:S(2)}) copy-start(f32[768]{0:T(1024)} %get-tuple-element.203) | copy-start | bytes 9220
  412.7 41.1 %copy-start.99 = (f32[1536]{0:T(1024)S(1)}, f32[1536]{0:T(1024)}, u32[]{:S(2)}) copy-start(f32[1536]{0:T(1024)} %get-tuple-element.277) | copy-start | bytes 18436
  412.7 41.1 %copy-start.98 = (f32[1536]{0:T(1024)S(1)}, f32[1536]{0:T(1024)}, u32[]{:S(2)}) copy-start(f32[1536]{0:T(1024)} %get-tuple-element.281) | copy-start | bytes 18436
  412.7 41.1 %copy-start.106 = (f32[768]{0:T(1024)S(1)}, f32[768]{0:T(1024)}, u32[]{:S(2)}) copy-start(f32[768]{0:T(1024)} %get-tuple-element.169) | copy-start | bytes 9220
  412.8 41.1 %copy-start.105 = (f32[768]{0:T(1024)S(1)}, f32[768]{0:T(1024)}, u32[]{:S(2)}) copy-start(f32[768]{0:T(1024)} %get-tuple-element.181) | copy-start | bytes 9220
  412.8 41.2 %copy-start.84 = (f32[768]{0:T(1024)S(1)}, f32[768]{0:T(1024)}, u32[]{:S(2)}) copy-start(f32[768]{0:T(1024)} %get-tuple-element.171) | copy-start | bytes 9220
  412.8 41.2 %copy-start.101 = (f32[1536]{0:T(1024)S(1)}, f32[1536]{0:T(1024)}, u32[]{:S(2)}) copy-start(f32[1536]{0:T(1024)} %get-tuple-element.279) | copy-start | bytes 18436
  412.8 41.2 %copy-start.82 = (f32[768]{0:T(1024)S(1)}, f32[768]{0:T(1024)}, u32[]{:S(2)}) copy-start(f32[768]{0:T(1024)} %get-tuple-element.205) | copy-start | bytes 9220
  412.8 41.2 %copy-start.83 = (f32[768]{0:T(1024)S(1)}, f32[768]{0:T(1024)}, u32[]{:S(2)}) copy-start(f32[768]{0:T(1024)} %get-tuple-element.182) | copy-start | bytes 9220
  412.8 41.2 %copy-start.107 = (f32[768]{0:T(1024)S(1)}, f32[768]{0:T(1024)}, u32[]{:S(2)}) copy-start(f32[768]{0:T(1024)} %get-tuple-element.168) | copy-start | bytes 9220
  412.8 43.6 %copy-start.81 = (f32[768]{0:T(1024)S(1)}, f32[768]{0:T(1024)}, u32[]{:S(2)}) copy-start(f32[768]{0:T(1024)} %get-tuple-element.199) | copy-start | bytes 9220
  412.8 43.7 %copy-start.100 = (f32[1536]{0:T(1024)S(1)}, f32[1536]{0:T(1024)}, u32[]{:S(2)}) copy-start(f32[1536]{0:T(1024)} %get-tuple-element.275) | copy-start | bytes 18436
  412.8 36.8 %collective-permute-start.14 = (f32[512,768]{1,0:T(8,128)}, f32[512,768]{1,0:T(8,128)S(1)}, u32[]{:S(2)}, u32[]{:S(2)}) collective-permute-start(f32[512,768]{1,0:T(8,128)} %get-tuple-element.131), channel_id=1, source_target_pairs={{0,1},{1,0},{2,3},{3,2},{4,5},{5,4},{6,7},{7,6},{8,9},{9,8},{10,11... | collective-permute-start | bytes 4718600 | tf_op jit(solution)/shard_map/ppermute | solution.py:65
  452.5 20.4 %collective-permute-start.15 = (f32[256,768]{1,0:T(8,128)S(1)}, f32[256,768]{1,0:T(8,128)S(1)}, u32[]{:S(2)}, u32[]{:S(2)}) collective-permute-start(f32[256,768]{1,0:T(8,128)S(1)} %copy-done.52), channel_id=1, source_target_pairs={{0,1},{1,0},{2,3},{3,2},{4,5},{5,4},{6,7},{7,6},{8,9},{9,8},{10,11... | collective-permute-start | bytes 2359304 | tf_op jit(solution)/shard_map/ppermute | solution.py:65
  454.1 18.5 %collective-permute-start.10 = (f32[14,768]{1,0:T(8,128)S(1)}, f32[14,768]{1,0:T(8,128)S(1)}, u32[]{:S(2)}, u32[]{:S(2)}) collective-permute-start(f32[14,768]{1,0:T(8,128)S(1)} %concatenate.41), channel_id=1, source_target_pairs={{0,1},{1,0},{2,3},{3,2},{4,5},{5,4},{6,7},{7,6},{8,9},{9,8},{10,11... | collective-permute-start | bytes 129032 | tf_op jit(solution)/shard_map/ppermute | solution.py:65
  474.5 1.3 collective-permute-start.36
  475.8 6.5 %collective-permute-start.37 = (f32[18,768]{1,0:T(8,128)S(1)}, f32[18,768]{1,0:T(8,128)S(1)}, u32[]{:S(2)}, u32[]{:S(2)}) collective-permute-start(f32[18,768]{1,0:T(8,128)S(1)} %add.533), channel_id=1, source_target_pairs={{0,4},{4,0},{8,12},{12,8},{1,5},{5,1},{9,13},{13,9},{2,6},{6,2},{1... | collective-permute-start | bytes 165896 | tf_op jit(solution)/shard_map/ppermute | solution.py:667
  482.3 7.5 %collective-permute-start.38 = (f32[18,768]{1,0:T(8,128)S(1)}, f32[18,768]{1,0:T(8,128)S(1)}, u32[]{:S(2)}, u32[]{:S(2)}) collective-permute-start(f32[18,768]{1,0:T(8,128)S(1)} %add.534), channel_id=1, source_target_pairs={{4,8},{8,4},{12,0},{0,12},{5,9},{9,5},{13,1},{1,13},{6,10},{10,6},... | collective-permute-start | bytes 165896 | tf_op jit(solution)/shard_map/ppermute | solution.py:667
  489.8 6.0 %collective-permute-start.39 = (f32[18,768]{1,0:T(8,128)S(1)}, f32[18,768]{1,0:T(8,128)S(1)}, u32[]{:S(2)}, u32[]{:S(2)}) collective-permute-start(f32[18,768]{1,0:T(8,128)S(1)} %add.535), channel_id=1, source_target_pairs={{0,32},{32,0},{64,96},{96,64},{1,33},{33,1},{65,97},{97,65},{2,34}... | collective-permute-start | bytes 165896 | tf_op jit(solution)/shard_map/ppermute | solution.py:667
  495.8 7.2 %collective-permute-start.40 = (f32[18,768]{1,0:T(8,128)S(1)}, f32[18,768]{1,0:T(8,128)S(1)}, u32[]{:S(2)}, u32[]{:S(2)}) collective-permute-start(f32[18,768]{1,0:T(8,128)S(1)} %add.536), channel_id=1, source_target_pairs={{32,64},{64,32},{96,0},{0,96},{33,65},{65,33},{97,1},{1,97},{34,66... | collective-permute-start | bytes 165896 | tf_op jit(solution)/shard_map/ppermute | solution.py:667
  503.0 4.4 collective-permute-start.41
  (100 other events, 664.2 us)
Sparse Core Ops, SparseCore 0:
  23.9 57.0 all-gather.6
  83.8 54.9 all-gather.8
  191.1 86.9 reduce-scatter.2
  281.8 107.3 reduce-scatter.4
  412.8 97.7 all-gather.10

commit v8 on v7

--- a/solution.py
+++ b/solution.py
@@ -108,7 +108,7 @@
     return lax.dot_general(left, right, (((0,), (0,)), ((), ())), preferred_element_type=F32)
 
 
-LIMIT = pltpu.CompilerParams(vmem_limit_bytes=48 * 2**20)
+LIMIT = pltpu.CompilerParams(vmem_limit_bytes=24 * 2**20)
 SCALAR = pl.BlockSpec(memory_space=pltpu.SMEM)
 
 
@@ -411,7 +411,7 @@
 
 def sort_weights(gathered):
     chips, _, rows, width = gathered.shape
-    step = 2
+    step = 4
     units = chips * rows
     return pl.pallas_call(
         sort_kernel,

time: 553 us -> 551 us (level)
  Pallas kernels: 120 us -> 88 us
  local copies, waits for them, and re-layouts: 31.6 us -> 57.9 us
  waiting for transfers between devices: 252 us -> 258 us
    unnamed x242 -> x270, local copies, waits for them, and re-layouts: 24.9 us -> 52.8 us
    pallas_call x4, Pallas kernels: 26.5 us -> 10.5 us  [feed_sums(): pl.pallas_call(lambda *refs: feed_sums_kernel(bool(more), *refs), grid=(4...]
    pallas_call x2, Pallas kernels: 11.8 us -> 1.02 us  [sort_weights(): pl.pallas_call(sort_kernel, grid=(chips // step,), in_specs=[pl.BlockSpec...]
    reduce_scatter x1, waiting for transfers between devices: 5.77 us -> 12.2 us  [local(): feed2 = lax.psum_scatter(feed2, PLANE, tiled=True)]
  transfers between devices with their start and end apart: 47 -> 47, of which waited for: 31 -> 33; matrix products, arithmetic and copies ran while one was open for 10% -> 9% of each run, Pallas kernels for 17% -> 11%
where the time goes in v8:
time: 551 us; the launch traced here: 542 us
  waiting for transfers between devices  258 us (47%)
  Pallas kernels  88 us (16%)
  starting transfers between devices  61.4 us (11%)
  local copies, waits for them, and re-layouts  57.9 us (11%)
  matrix products  30.6 us (6%)
  other arithmetic  29.1 us (5%)
  between operations  17.2 us (3%)
    ppermute x24, waiting for transfers between devices, swap(): return lax.ppermute(values, axis, SWAP)  163 us
    unnamed x270, local copies, waits for them, and re-layouts  52.8 us
    ppermute x24, starting transfers between devices, swap(): return lax.ppermute(values, axis, SWAP)  39.5 us
    ppermute x12, waiting for transfers between devices, ring_parts(): received.append(lax.ppermute(sent, axis, pairs))  26.9 us
    ppermute x4, waiting for transfers between devices, local(): small = small + lax.ppermute(small, axis, pairs)  26.6 us
    pallas_call x2, Pallas kernels, attend_back(): pl.pallas_call(attend_back_kernel, grid=(steps,), in_specs=[SCALAR, part,...  20.7 us
    reduce_scatter x1, waiting for transfers between devices, local(): rest = lax.psum_scatter(rest, PLANE, tiled=True)  19.4 us
    pallas_call x2, Pallas kernels, attend(): pl.pallas_call(lambda *refs: attend_kernel(sends_mixture, *refs), grid=(s...  18.7 us
  transfers between devices with their start and end apart: 47, of which 33 were waited for; matrix products, arithmetic and copies ran while one was open for 9% of the time, Pallas kernels for 11%

profile of v8, /device:TPU:0, one launch (start us, length us, event | category | flops | bytes accessed | tf_op | source)
XLA Modules:
  0.0 541.8 jit_solution(11528940229360521618)
XLA Ops:
  8.0 2.3 copy-done.5
  10.3 2.3 copy-done.6
  13.4 4.0 collective-permute-start
  17.4 7.0 %collective-permute-done = f32[96,768]{1,0:T(8,128)S(1)} collective-permute-done((f32[96,768]{1,0:T(8,128)S(1)}, f32[96,768]{1,0:T(8,128)S(1)}, u32[]{:S(2)}, u32[]{:S(2)}) %collective-permute-start) | collective-permute-done | bytes 294944 | tf_op jit(solution)/shard_map/ppermute | solution.py:65
  25.2 3.3 collective-permute-start.1
  32.4 10.0 %attend.2 = (bf16[512,384]{1,0:T(8,128)(2,1)S(1)}, bf16[512,384]{1,0:T(8,128)(2,1)S(1)}, bf16[512,384]{1,0:T(8,128)(2,1)S(1)}, bf16[512,384]{1,0:T(8,128)(2,1)S(...) custom-call(s32[2]{0:T(128)S(1)} %get-tuple-element.283.refs_0_, ...), custom_call_target="tpu_custom_call" | custom-call | flops 1610612736 | bytes 5505024 | tf_op jit(solution)/shard_map/attend/pallas_call | solution.py:191
  47.8 3.2 collective-permute-start.2
  55.2 12.7 %collective-permute-done.2 = f32[256,768]{1,0:T(8,128)} collective-permute-done((f32[256,768]{1,0:T(8,128)}, f32[256,768]{1,0:T(8,128)}, u32[]{:S(2)}, u32[]{:S(2)}) %collective-permute-start.2) | collective-permute-done | bytes 786464 | tf_op jit(solution)/shard_map/ppermute | solution.py:65
  67.9 2.8 collective-permute-start.4
  72.9 4.2 multiply_convert_fusion.3
  78.8 3.6 all-gather.7.cloned.1.call-done
  82.4 3.7 copy-done.3
  91.3 4.2 collective-permute-done.4
  95.5 2.4 collective-permute-start.5
  97.9 15.7 %collective-permute-done.5 = f32[256,768]{1,0:T(8,128)} collective-permute-done((f32[256,768]{1,0:T(8,128)S(1)}, f32[256,768]{1,0:T(8,128)}, u32[]{:S(2)}, u32[]{:S(2)}) %collective-permute-start.5) | collective-permute-done | bytes 786464 | tf_op jit(solution)/shard_map/ppermute | solution.py:65
  117.0 8.8 %attend.3 = (bf16[512,384]{1,0:T(8,128)(2,1)S(1)}, bf16[512,384]{1,0:T(8,128)(2,1)S(1)}, bf16[512,384]{1,0:T(8,128)(2,1)S(1)}, bf16[512,384]{1,0:T(8,128)(2,1)S(...) custom-call(s32[2]{0:T(128)S(1)} %get-tuple-element.283.refs_0_, ...), custom_call_target="tpu_custom_call" | custom-call | flops 1610612736 | bytes 5505024 | tf_op jit(solution)/shard_map/attend/pallas_call | solution.py:191
  130.3 2.4 collective-permute-start.6
  133.9 6.3 %all-gather.9.cloned.1.call-done = f32[3072,768]{1,0:T(8,128)} async-done(((f32[96,768]{1,0:T(8,128)}), f32[3072,768]{1,0:T(8,128)}) %all-gather.9.cloned.1.call-update) | async-done | bytes 9437200 | tf_op jit(solution)/shard_map/all_gather | solution.py:602
  140.2 3.7 copy-done.2
  147.6 2.5 multiply_convert_fusion.1
  154.9 2.0 convert_reduce_fusion.6
  160.4 2.5 feed_sums.4
  168.2 3.1 collective-permute-start.8
  171.3 6.3 %collective-permute-done.7.refs_7_ = f32[1536,1536]{1,0:T(8,128)S(1)} collective-permute-done((f32[1536,1536]{1,0:T(8,128)S(1)}, f32[1536,1536]{1,0:T(8,128)S(1)}, u32[]{:S(2)}, u32[]{:S(2)}) %collective-permute-start.7) | collective-permute-done | bytes 9437216 | tf_op jit(solution)/shard_map/ppermute | solution.py:65
  177.6 2.5 feed_sums.5
  180.1 3.7 copy-done.1
  183.9 5.9 %collective-permute-done.8 = f32[256,768]{1,0:T(8,128)} collective-permute-done((f32[256,768]{1,0:T(8,128)}, f32[256,768]{1,0:T(8,128)}, u32[]{:S(2)}, u32[]{:S(2)}) %collective-permute-start.8) | collective-permute-done | bytes 786464 | tf_op jit(solution)/shard_map/ppermute | solution.py:65
  194.5 10.4 %attend_back.2 = (bf16[512,384]{1,0:T(8,128)(2,1)S(1)}, bf16[512,384]{1,0:T(8,128)(2,1)S(1)}, bf16[512,384]{1,0:T(8,128)(2,1)S(1)}, f32[512,768]{1,0:T(8,128)S(1...) custom-call(s32[1]{0:T(128)} %copy.62.length_ref, bf16[512,384]{1,0:T(8,128)(2,1)S(1)} %copy-done.46, ...), custom_call_target="tpu_custom_call" | custom-call | flops 2214592512 | bytes 5505024 | tf_op jit(solution)/shard_map/attend_back/pallas_call | solution.py:272
  205.0 3.2 collective-permute-start.9
  208.1 17.3 %collective-permute-done.9 = f32[256,768]{1,0:T(8,128)S(1)} collective-permute-done((f32[256,768]{1,0:T(8,128)S(1)}, f32[256,768]{1,0:T(8,128)S(1)}, u32[]{:S(2)}, u32[]{:S(2)}) %collective-permute-start.9) | collective-permute-done | bytes 786464 | tf_op jit(solution)/shard_map/ppermute | solution.py:65
  232.5 2.4 feed_sums.6
  235.1 2.0 attention_sums.4
  238.6 3.5 multiply_reduce_fusion
  243.2 3.3 collective-permute-start.13
  246.5 3.2 collective-permute-done.12.refs_7_
  249.7 3.1 feed_sums.7.refs_8_
  255.2 3.8 attention_sums.5
  259.1 4.3 copy-done
  264.8 12.2 %reduce-scatter.3.cloned.1.call-done = f32[96,1536]{1,0:T(8,128)} async-done(((f32[1536,1536]{1,0:T(8,128)}), f32[96,1536]{1,0:T(8,128)}) %reduce-scatter.3.cloned.1.call-update) | async-done | bytes 589840 | tf_op jit(solution)/shard_map/reduce_scatter | solution.py:625
  282.0 10.4 %attend_back.3 = (bf16[512,384]{1,0:T(8,128)(2,1)S(1)}, bf16[512,384]{1,0:T(8,128)(2,1)S(1)}, bf16[512,384]{1,0:T(8,128)(2,1)S(1)}, f32[512,768]{1,0:T(8,128)S(1...) custom-call(s32[1]{0:T(128)} %copy.62.length_ref, bf16[512,384]{1,0:T(8,128)(2,1)S(1)} %copy-done.40, ...), custom_call_target="tpu_custom_call" | custom-call | flops 2214592512 | bytes 5505024 | tf_op jit(solution)/shard_map/attend_back/pallas_call | solution.py:272
  293.6 3.1 attention_sums.6
  296.7 4.9 collective-permute-done.19.refs_7_
  301.6 3.8 attention_sums.7
  306.4 2.4 collective-permute-start.25
  313.9 10.4 %collective-permute-done.25 = f32[4,48,384]{2,1,0:T(8,128)S(1)} collective-permute-done((f32[4,48,384]{2,1,0:T(8,128)}, f32[4,48,384]{2,1,0:T(8,128)S(1)}, u32[]{:S(2)}, u32[]{:S(2)}) %collective-permute-start.25) | collective-permute-done | bytes 294944 | tf_op jit(solution)/shard_map/ppermute | solution.py:83
  324.9 7.7 %collective-permute-done.24 = f32[4,48,384]{2,1,0:T(8,128)S(1)} collective-permute-done((f32[4,48,384]{2,1,0:T(8,128)}, f32[4,48,384]{2,1,0:T(8,128)S(1)}, u32[]{:S(2)}, u32[]{:S(2)}) %collective-permute-start.24) | collective-permute-done | bytes 294944 | tf_op jit(solution)/shard_map/ppermute | solution.py:83
  333.8 5.8 %collective-permute-done.20 = f32[4,48,384]{2,1,0:T(8,128)S(1)} collective-permute-done((f32[4,48,384]{2,1,0:T(8,128)S(1)}, f32[4,48,384]{2,1,0:T(8,128)S(1)}, u32[]{:S(2)}, u32[]{:S(2)}) %collective-permute-start.20) | collective-permute-done | bytes 294944 | tf_op jit(solution)/shard_map/ppermute | solution.py:83
  339.7 2.2 collective-permute-start.28
  348.8 3.7 collective-permute-start.18
  356.1 10.1 %collective-permute-done.16 = f32[96,768]{1,0:T(8,128)S(1)} collective-permute-done((f32[96,768]{1,0:T(8,128)S(1)}, f32[96,768]{1,0:T(8,128)S(1)}, u32[]{:S(2)}, u32[]{:S(2)}) %collective-permute-start.16) | collective-permute-done | bytes 294944 | tf_op jit(solution)/shard_map/ppermute | solution.py:65
  368.5 19.4 %reduce-scatter.5.cloned.1.call-done = f32[96,1920]{1,0:T(8,128)} async-done(((f32[1536,1920]{1,0:T(8,128)}), f32[96,1920]{1,0:T(8,128)}) %reduce-scatter.5.cloned.1.call-update) | async-done | bytes 737296 | tf_op jit(solution)/shard_map/reduce_scatter | solution.py:637
  391.5 2.2 collective-permute-start.35
  394.4 8.7 %collective-permute-done.33 = f32[96,1152]{1,0:T(8,128)S(1)} collective-permute-done((f32[96,1152]{1,0:T(8,128)S(1)}, f32[96,1152]{1,0:T(8,128)S(1)}, u32[]{:S(2)}, u32[]{:S(2)}) %collective-permute-start.33) | collective-permute-done | bytes 442400 | tf_op jit(solution)/shard_map/ppermute | solution.py:65
  403.2 7.2 %collective-permute-done.34 = f32[96,768]{1,0:T(8,128)S(1)} collective-permute-done((f32[96,768]{1,0:T(8,128)S(1)}, f32[96,768]{1,0:T(8,128)S(1)}, u32[]{:S(2)}, u32[]{:S(2)}) %collective-permute-start.34) | collective-permute-done | bytes 294944 | tf_op jit(solution)/shard_map/ppermute | solution.py:65
  413.1 35.8 %collective-permute-done.14 = f32[512,768]{1,0:T(8,128)S(1)} collective-permute-done((f32[512,768]{1,0:T(8,128)S(1)}, f32[512,768]{1,0:T(8,128)S(1)}, u32[]{:S(2)}, u32[]{:S(2)}) %collective-permute-start.14) | collective-permute-done | bytes 1572896 | tf_op jit(solution)/shard_map/ppermute | solution.py:65
  451.5 2.9 collective-permute-start.10
  454.5 15.8 %collective-permute-done.10 = f32[14,768]{1,0:T(8,128)S(1)} collective-permute-done((f32[14,768]{1,0:T(8,128)S(1)}, f32[14,768]{1,0:T(8,128)S(1)}, u32[]{:S(2)}, u32[]{:S(2)}) %collective-permute-start.10) | collective-permute-done | bytes 43040 | tf_op jit(solution)/shard_map/ppermute | solution.py:65
  474.2 6.4 %collective-permute-done.37 = f32[18,768]{1,0:T(8,128)S(1)} collective-permute-done((f32[18,768]{1,0:T(8,128)S(1)}, f32[18,768]{1,0:T(8,128)S(1)}, u32[]{:S(2)}, u32[]{:S(2)}) %collective-permute-start.37) | collective-permute-done | bytes 55328 | tf_op jit(solution)/shard_map/ppermute | solution.py:667
  480.7 7.4 %collective-permute-done.38 = f32[18,768]{1,0:T(8,128)S(1)} collective-permute-done((f32[18,768]{1,0:T(8,128)S(1)}, f32[18,768]{1,0:T(8,128)S(1)}, u32[]{:S(2)}, u32[]{:S(2)}) %collective-permute-start.38) | collective-permute-done | bytes 55328 | tf_op jit(solution)/shard_map/ppermute | solution.py:667
  488.1 5.9 %collective-permute-done.39 = f32[18,768]{1,0:T(8,128)S(1)} collective-permute-done((f32[18,768]{1,0:T(8,128)S(1)}, f32[18,768]{1,0:T(8,128)S(1)}, u32[]{:S(2)}, u32[]{:S(2)}) %collective-permute-start.39) | collective-permute-done | bytes 55328 | tf_op jit(solution)/shard_map/ppermute | solution.py:667
  494.3 6.9 %collective-permute-done.40 = f32[18,768]{1,0:T(8,128)S(1)} collective-permute-done((f32[18,768]{1,0:T(8,128)S(1)}, f32[18,768]{1,0:T(8,128)S(1)}, u32[]{:S(2)}, u32[]{:S(2)}) %collective-permute-start.40) | collective-permute-done | bytes 55328 | tf_op jit(solution)/shard_map/ppermute | solution.py:667
  501.6 4.1 collective-permute-done.41
  511.2 8.0 %place_attention.1 = (f32[2,768,384]{2,1,0:T(8,128)}, f32[2,768,384]{2,1,0:T(8,128)}, f32[2,768,384]{2,1,0:T(8,128)}, f32[2,384,768]{2,1,0:T(8,128)}) custom-call(f32[16,2,96,2304]{3,2,1,0:T(8,128)} %bitcast.145, f32[16,2,96,2304]{3,2,1,0:T(8,128)} %bitcast.146, f32[16,2,96,2304]{3,2,1,0:T(8,128)} %bitcast.147, f32[16,2,96,2304]{3,2,1,0:T(8,128)} %bitcast.148), custom_call_target="tpu_custom_call" | custom-call | tf_op jit(solution)/shard_map/place_attention/pallas_call | solution.py:481
  519.2 15.6 %place_feed.1 = (f32[2,1536,768]{2,1,0:T(8,128)}, f32[2,768,1536]{2,1,0:T(8,128)}) custom-call(f32[16,2,96,2304]{3,2,1,0:T(8,128)} %bitcast.149, f32[16,2,96,2304]{3,2,1,0:T(8,128)} %bitcast.150), custom_call_target="tpu_custom_call" | custom-call | tf_op jit(solution)/shard_map/place_feed/pallas_call | solution.py:464
  (458 shorter events, 114.1 us)
Async XLA Ops:
  7.2 75.2 %all-gather.7.cloned.1.call-start = ((), (), s32[]{:S(2)}) async-start(), calls=%async_computation.4 | async-start | bytes 9732096 | tf_op jit(solution)/shard_map/all_gather | solution.py:527
  13.4 11.0 %collective-permute-start = (f32[96,768]{1,0:T(8,128)S(1)}, f32[96,768]{1,0:T(8,128)S(1)}, u32[]{:S(2)}, u32[]{:S(2)}) collective-permute-start(f32[96,768]{1,0:T(8,128)S(1)} %get-tuple-element.239), channel_id=1, source_target_pairs={{0,1},{1,0},{2,3},{3,2},{4,5},{5,4},{6,7},{7,6},{8,9},{9,8},{10,11... | collective-permute-start | bytes 884744 | tf_op jit(solution)/shard_map/ppermute | solution.py:65
  25.1 115.0 %all-gather.9.cloned.1.call-start = ((), (), s32[]{:S(2)}) async-start(), calls=%async_computation.5 | async-start | bytes 9732096 | tf_op jit(solution)/shard_map/all_gather | solution.py:602
  25.2 20.8 %collective-permute-start.1 = (f32[96,768]{1,0:T(8,128)S(1)}, f32[96,768]{1,0:T(8,128)S(1)}, u32[]{:S(2)}, u32[]{:S(2)}) collective-permute-start(f32[96,768]{1,0:T(8,128)S(1)} %get-tuple-element.93), channel_id=1, source_target_pairs={{0,1},{1,0},{2,3},{3,2},{4,5},{5,4},{6,7},{7,6},{8,9},{9,8},{10,11... | collective-permute-start | bytes 884744 | tf_op jit(solution)/shard_map/ppermute | solution.py:65
  46.7 230.2 %reduce-scatter.3.cloned.1.call-start = ((), (), s32[]{:S(2)}) async-start(), calls=%async_computation.2 | async-start | bytes 10027008 | tf_op jit(solution)/shard_map/reduce_scatter | solution.py:625
  46.8 7.8 %collective-permute-start.3 = (f32[2,1536]{1,0:T(2,128)S(1)}, f32[2,1536]{1,0:T(2,128)S(1)}, u32[]{:S(2)}, u32[]{:S(2)}) collective-permute-start(f32[2,1536]{1,0:T(2,128)S(1)} %convert_element_type.152), channel_id=1, source_target_pairs={{0,1},{1,0},{2,3},{3,2},{4,5},{5,4},{6,7},{7,6},{8,9},{9,8},{10,11... | collective-permute-start | bytes 36872 | tf_op jit(solution)/shard_map/ppermute | solution.py:65
  47.8 20.1 %collective-permute-start.2 = (f32[256,768]{1,0:T(8,128)}, f32[256,768]{1,0:T(8,128)}, u32[]{:S(2)}, u32[]{:S(2)}) collective-permute-start(f32[256,768]{1,0:T(8,128)} %get-tuple-element.95), channel_id=1, source_target_pairs={{0,1},{1,0},{2,3},{3,2},{4,5},{5,4},{6,7},{7,6},{8,9},{9,8},{10,11... | collective-permute-start | bytes 2359304 | tf_op jit(solution)/shard_map/ppermute | solution.py:65
  52.3 36.3 %copy-start.74 = (f32[768]{0:T(1024)}, f32[768]{0:T(1024)S(1)}, u32[]{:S(2)}) copy-start(f32[768]{0:T(1024)S(1)} %get-tuple-element.287) | copy-start | bytes 9220
  67.9 27.6 %collective-permute-start.4 = (f32[384,768]{1,0:T(8,128)}, f32[384,768]{1,0:T(8,128)}, u32[]{:S(2)}, u32[]{:S(2)}) collective-permute-start(f32[384,768]{1,0:T(8,128)} %multiply_bitcast_fusion), channel_id=1, source_target_pairs={{0,1},{1,0},{2,3},{3,2},{4,5},{5,4},{6,7},{7,6},{8,9},{9,8},{10,11... | collective-permute-start | bytes 3538952 | tf_op jit(solution)/shard_map/ppermute | solution.py:65
  95.5 18.1 %collective-permute-start.5 = (f32[256,768]{1,0:T(8,128)S(1)}, f32[256,768]{1,0:T(8,128)}, u32[]{:S(2)}, u32[]{:S(2)}) collective-permute-start(f32[256,768]{1,0:T(8,128)S(1)} %fusion.62), channel_id=1, source_target_pairs={{0,1},{1,0},{2,3},{3,2},{4,5},{5,4},{6,7},{7,6},{8,9},{9,8},{10,11... | collective-permute-start | bytes 2359304 | tf_op jit(solution)/shard_map/ppermute | solution.py:65
  130.3 14.2 %collective-permute-start.6 = (f32[256,384]{1,0:T(8,128)}, f32[256,384]{1,0:T(8,128)}, u32[]{:S(2)}, u32[]{:S(2)}) collective-permute-start(f32[256,384]{1,0:T(8,128)} %get-tuple-element.103), channel_id=1, source_target_pairs={{0,1},{1,0},{2,3},{3,2},{4,5},{5,4},{6,7},{7,6},{8,9},{9,8},{10,11... | collective-permute-start | bytes 1179656 | tf_op jit(solution)/shard_map/ppermute | solution.py:65
  162.9 14.7 %collective-permute-start.7 = (f32[1536,1536]{1,0:T(8,128)S(1)}, f32[1536,1536]{1,0:T(8,128)S(1)}, u32[]{:S(2)}, u32[]{:S(2)}) collective-permute-start(f32[1536,1536]{1,0:T(8,128)S(1)} %feed_sums.4), channel_id=1, source_target_pairs={{0,2},{2,0},{1,3},{3,1},{4,6},{6,4},{5,7},{7,5},{8,10},{10,8},{9,1... | collective-permute-start | bytes 28311560 | tf_op jit(solution)/shard_map/ppermute | solution.py:65
  168.2 21.5 %collective-permute-start.8 = (f32[256,768]{1,0:T(8,128)}, f32[256,768]{1,0:T(8,128)}, u32[]{:S(2)}, u32[]{:S(2)}) collective-permute-start(f32[256,768]{1,0:T(8,128)} %get-tuple-element.209), channel_id=1, source_target_pairs={{0,1},{1,0},{2,3},{3,2},{4,5},{5,4},{6,7},{7,6},{8,9},{9,8},{10,11... | collective-permute-start | bytes 2359304 | tf_op jit(solution)/shard_map/ppermute | solution.py:65
  189.8 198.1 %reduce-scatter.5.cloned.1.call-start = ((), (), s32[]{:S(2)}) async-start(), calls=%async_computation.3 | async-start | bytes 12533760 | tf_op jit(solution)/shard_map/reduce_scatter | solution.py:637
  205.0 20.5 %collective-permute-start.9 = (f32[256,768]{1,0:T(8,128)S(1)}, f32[256,768]{1,0:T(8,128)S(1)}, u32[]{:S(2)}, u32[]{:S(2)}) collective-permute-start(f32[256,768]{1,0:T(8,128)S(1)} %constant_dynamic-slice_fusion), channel_id=1, source_target_pairs={{0,1},{1,0},{2,3},{3,2},{4,5},{5,4},{6,7},{7,6},{8,9},{9,8},{10,11... | collective-permute-start | bytes 2359304 | tf_op jit(solution)/shard_map/ppermute | solution.py:65
  235.0 14.7 %collective-permute-start.12 = (f32[1536,1536]{1,0:T(8,128)S(1)}, f32[1536,1536]{1,0:T(8,128)S(1)}, u32[]{:S(2)}, u32[]{:S(2)}) collective-permute-start(f32[1536,1536]{1,0:T(8,128)S(1)} %feed_sums.6), channel_id=1, source_target_pairs={{0,2},{2,0},{1,3},{3,1},{4,6},{6,4},{5,7},{7,5},{8,10},{10,8},{9,1... | collective-permute-start | bytes 28311560 | tf_op jit(solution)/shard_map/ppermute | solution.py:65
  237.2 16.0 %collective-permute-start.11 = (f32[1536,384]{1,0:T(8,128)S(1)}, f32[1536,384]{1,0:T(8,128)}, u32[]{:S(2)}, u32[]{:S(2)}) collective-permute-start(f32[1536,384]{1,0:T(8,128)S(1)} %attention_sums.4), channel_id=1, source_target_pairs={{0,2},{2,0},{1,3},{3,1},{4,6},{6,4},{5,7},{7,5},{8,10},{10,8},{9,1... | collective-permute-start | bytes 7077896 | tf_op jit(solution)/shard_map/ppermute | solution.py:65
  243.2 21.5 %collective-permute-start.13 = (f32[256,768]{1,0:T(8,128)}, f32[256,768]{1,0:T(8,128)}, u32[]{:S(2)}, u32[]{:S(2)}) collective-permute-start(f32[256,768]{1,0:T(8,128)} %multiply_multiply_fusion.4), channel_id=1, source_target_pairs={{0,1},{1,0},{2,3},{3,2},{4,5},{5,4},{6,7},{7,6},{8,9},{9,8},{10,11... | collective-permute-start | bytes 2359304 | tf_op jit(solution)/shard_map/ppermute | solution.py:65
  276.9 234.2 %all-gather.11.cloned.1.call-start = ((), (), s32[]{:S(2)}) async-start(), calls=%async_computation.6 | async-start | bytes 29196288 | tf_op jit(solution)/shard_map/all_gather | solution.py:653
  296.7 4.9 collective-permute-start.19
  306.4 17.8 %collective-permute-start.25 = (f32[4,48,384]{2,1,0:T(8,128)}, f32[4,48,384]{2,1,0:T(8,128)S(1)}, u32[]{:S(2)}, u32[]{:S(2)}) collective-permute-start(f32[4,48,384]{2,1,0:T(8,128)} %get-tuple-element.226), channel_id=1, source_target_pairs={{0,64},{32,96},{64,0},{96,32},{1,65},{33,97},{65,1},{97,33},{2,66}... | collective-permute-start | bytes 884744 | tf_op jit(solution)/shard_map/ppermute | solution.py:83
  308.8 23.8 %collective-permute-start.24 = (f32[4,48,384]{2,1,0:T(8,128)}, f32[4,48,384]{2,1,0:T(8,128)S(1)}, u32[]{:S(2)}, u32[]{:S(2)}) collective-permute-start(f32[4,48,384]{2,1,0:T(8,128)} %get-tuple-element.227), channel_id=1, source_target_pairs={{0,96},{32,0},{64,32},{96,64},{1,97},{33,1},{65,33},{97,65},{2,98}... | collective-permute-start | bytes 884744 | tf_op jit(solution)/shard_map/ppermute | solution.py:83
  310.2 22.4 %collective-permute-start.23 = (f32[4,48,384]{2,1,0:T(8,128)S(1)}, f32[4,48,384]{2,1,0:T(8,128)S(1)}, u32[]{:S(2)}, u32[]{:S(2)}) collective-permute-start(f32[4,48,384]{2,1,0:T(8,128)S(1)} %get-tuple-element.228), channel_id=1, source_target_pairs={{0,32},{32,64},{64,96},{96,0},{1,33},{33,65},{65,97},{97,1},{2,34}... | collective-permute-start | bytes 884744 | tf_op jit(solution)/shard_map/ppermute | solution.py:83
  310.9 21.7 %collective-permute-start.22 = (f32[4,48,384]{2,1,0:T(8,128)S(1)}, f32[4,48,384]{2,1,0:T(8,128)S(1)}, u32[]{:S(2)}, u32[]{:S(2)}) collective-permute-start(f32[4,48,384]{2,1,0:T(8,128)S(1)} %get-tuple-element.230), channel_id=1, source_target_pairs={{0,8},{4,12},{8,0},{12,4},{1,9},{5,13},{9,1},{13,5},{2,10},{6,14},... | collective-permute-start | bytes 884744 | tf_op jit(solution)/shard_map/ppermute | solution.py:83
  312.5 21.3 %collective-permute-start.21 = (f32[4,48,384]{2,1,0:T(8,128)S(1)}, f32[4,48,384]{2,1,0:T(8,128)S(1)}, u32[]{:S(2)}, u32[]{:S(2)}) collective-permute-start(f32[4,48,384]{2,1,0:T(8,128)S(1)} %get-tuple-element.231), channel_id=1, source_target_pairs={{0,12},{4,0},{8,4},{12,8},{1,13},{5,1},{9,5},{13,9},{2,14},{6,2},{... | collective-permute-start | bytes 884744 | tf_op jit(solution)/shard_map/ppermute | solution.py:83
  324.3 15.3 %collective-permute-start.20 = (f32[4,48,384]{2,1,0:T(8,128)S(1)}, f32[4,48,384]{2,1,0:T(8,128)S(1)}, u32[]{:S(2)}, u32[]{:S(2)}) collective-permute-start(f32[4,48,384]{2,1,0:T(8,128)S(1)} %get-tuple-element.232), channel_id=1, source_target_pairs={{0,4},{4,8},{8,12},{12,0},{1,5},{5,9},{9,13},{13,1},{2,6},{6,10},{... | collective-permute-start | bytes 884744 | tf_op jit(solution)/shard_map/ppermute | solution.py:83
  339.7 7.4 %collective-permute-start.28 = (f32[48,384]{1,0:T(8,128)S(1)}, f32[48,384]{1,0:T(8,128)S(1)}, u32[]{:S(2)}, u32[]{:S(2)}) collective-permute-start(f32[48,384]{1,0:T(8,128)S(1)} %get-tuple-element.244), channel_id=1, source_target_pairs={{0,64},{32,96},{64,0},{96,32},{1,65},{33,97},{65,1},{97,33},{2,66}... | collective-permute-start | bytes 221192 | tf_op jit(solution)/shard_map/ppermute | solution.py:83
  342.0 6.8 %collective-permute-start.27 = (f32[48,384]{1,0:T(8,128)S(1)}, f32[48,384]{1,0:T(8,128)S(1)}, u32[]{:S(2)}, u32[]{:S(2)}) collective-permute-start(f32[48,384]{1,0:T(8,128)S(1)} %get-tuple-element.245), channel_id=1, source_target_pairs={{0,96},{32,0},{64,32},{96,64},{1,97},{33,1},{65,33},{97,65},{2,98}... | collective-permute-start | bytes 221192 | tf_op jit(solution)/shard_map/ppermute | solution.py:83
  343.4 9.1 %collective-permute-start.26 = (f32[48,384]{1,0:T(8,128)S(1)}, f32[48,384]{1,0:T(8,128)S(1)}, u32[]{:S(2)}, u32[]{:S(2)}) collective-permute-start(f32[48,384]{1,0:T(8,128)S(1)} %get-tuple-element.246), channel_id=1, source_target_pairs={{0,32},{32,64},{64,96},{96,0},{1,33},{33,65},{65,97},{97,1},{2,34}... | collective-permute-start | bytes 221192 | tf_op jit(solution)/shard_map/ppermute | solution.py:83
  344.3 9.5 %collective-permute-start.31 = (f32[48,384]{1,0:T(8,128)S(1)}, f32[48,384]{1,0:T(8,128)S(1)}, u32[]{:S(2)}, u32[]{:S(2)}) collective-permute-start(f32[48,384]{1,0:T(8,128)S(1)} %get-tuple-element.240), channel_id=1, source_target_pairs={{0,8},{4,12},{8,0},{12,4},{1,9},{5,13},{9,1},{13,5},{2,10},{6,14},... | collective-permute-start | bytes 221192 | tf_op jit(solution)/shard_map/ppermute | solution.py:83
  344.8 9.6 %collective-permute-start.30 = (f32[48,384]{1,0:T(8,128)S(1)}, f32[48,384]{1,0:T(8,128)S(1)}, u32[]{:S(2)}, u32[]{:S(2)}) collective-permute-start(f32[48,384]{1,0:T(8,128)S(1)} %get-tuple-element.241), channel_id=1, source_target_pairs={{0,12},{4,0},{8,4},{12,8},{1,13},{5,1},{9,5},{13,9},{2,14},{6,2},{... | collective-permute-start | bytes 221192 | tf_op jit(solution)/shard_map/ppermute | solution.py:83
  347.1 7.3 %collective-permute-start.29 = (f32[48,384]{1,0:T(8,128)S(1)}, f32[48,384]{1,0:T(8,128)S(1)}, u32[]{:S(2)}, u32[]{:S(2)}) collective-permute-start(f32[48,384]{1,0:T(8,128)S(1)} %get-tuple-element.242), channel_id=1, source_target_pairs={{0,4},{4,8},{8,12},{12,0},{1,5},{5,9},{9,13},{13,1},{2,6},{6,10},{... | collective-permute-start | bytes 221192 | tf_op jit(solution)/shard_map/ppermute | solution.py:83
  348.8 17.4 %collective-permute-start.18 = (f32[96,768]{1,0:T(8,128)S(1)}, f32[96,768]{1,0:T(8,128)S(1)}, u32[]{:S(2)}, u32[]{:S(2)}) collective-permute-start(f32[96,768]{1,0:T(8,128)S(1)} %get-tuple-element.237), channel_id=1, source_target_pairs={{0,17},{17,0},{1,16},{16,1},{2,19},{19,2},{3,18},{18,3},{4,21},{21... | collective-permute-start | bytes 884744 | tf_op jit(solution)/shard_map/ppermute | solution.py:643
  352.5 13.7 %collective-permute-start.17 = (f32[96,768]{1,0:T(8,128)S(1)}, f32[96,768]{1,0:T(8,128)S(1)}, u32[]{:S(2)}, u32[]{:S(2)}) collective-permute-start(f32[96,768]{1,0:T(8,128)S(1)} %get-tuple-element.237), channel_id=1, source_target_pairs={{0,1},{1,0},{2,3},{3,2},{4,5},{5,4},{6,7},{7,6},{8,9},{9,8},{10,11... | collective-permute-start | bytes 884744 | tf_op jit(solution)/shard_map/ppermute | solution.py:65
  353.9 12.3 %collective-permute-start.16 = (f32[96,768]{1,0:T(8,128)S(1)}, f32[96,768]{1,0:T(8,128)S(1)}, u32[]{:S(2)}, u32[]{:S(2)}) collective-permute-start(f32[96,768]{1,0:T(8,128)S(1)} %get-tuple-element.236), channel_id=1, source_target_pairs={{0,16},{16,0},{1,17},{17,1},{2,18},{18,2},{3,19},{19,3},{4,20},{20... | collective-permute-start | bytes 884744 | tf_op jit(solution)/shard_map/ppermute | solution.py:65
  354.5 13.3 %collective-permute-start.32 = (f32[96,384]{1,0:T(8,128)S(1)}, f32[96,384]{1,0:T(8,128)S(1)}, u32[]{:S(2)}, u32[]{:S(2)}) collective-permute-start(f32[96,384]{1,0:T(8,128)S(1)} %pad_maximum_fusion.2), channel_id=1, source_target_pairs={{0,16},{16,0},{1,17},{17,1},{2,18},{18,2},{3,19},{19,3},{4,20},{20... | collective-permute-start | bytes 442376 | tf_op jit(solution)/shard_map/ppermute | solution.py:65
  389.9 13.2 %collective-permute-start.33 = (f32[96,1152]{1,0:T(8,128)S(1)}, f32[96,1152]{1,0:T(8,128)S(1)}, u32[]{:S(2)}, u32[]{:S(2)}) collective-permute-start(f32[96,1152]{1,0:T(8,128)S(1)} %pad_maximum_fusion.1), channel_id=1, source_target_pairs={{0,16},{16,0},{1,17},{17,1},{2,18},{18,2},{3,19},{19,3},{4,20},{20... | collective-permute-start | bytes 1327112 | tf_op jit(solution)/shard_map/ppermute | solution.py:65
  391.5 11.6 %collective-permute-start.35 = (f32[96,768]{1,0:T(8,128)S(1)}, f32[96,768]{1,0:T(8,128)S(1)}, u32[]{:S(2)}, u32[]{:S(2)}) collective-permute-start(f32[96,768]{1,0:T(8,128)S(1)} %get-tuple-element.234), channel_id=1, source_target_pairs={{0,17},{17,0},{1,16},{16,1},{2,19},{19,2},{3,18},{18,3},{4,21},{21... | collective-permute-start | bytes 884744 | tf_op jit(solution)/shard_map/ppermute | solution.py:643
  393.7 16.7 %collective-permute-start.34 = (f32[96,768]{1,0:T(8,128)S(1)}, f32[96,768]{1,0:T(8,128)S(1)}, u32[]{:S(2)}, u32[]{:S(2)}) collective-permute-start(f32[96,768]{1,0:T(8,128)S(1)} %get-tuple-element.234), channel_id=1, source_target_pairs={{0,1},{1,0},{2,3},{3,2},{4,5},{5,4},{6,7},{7,6},{8,9},{9,8},{10,11... | collective-permute-start | bytes 884744 | tf_op jit(solution)/shard_map/ppermute | solution.py:65
  410.4 38.6 %copy-start.64 = (f32[256,768]{1,0:T(8,128)S(1)}, f32[256,768]{1,0:T(8,128)}, u32[]{:S(2)}) copy-start(f32[256,768]{1,0:T(8,128)} %copy-done.63) | copy-start | bytes 2359300
  410.4 38.5 %copy-start.62 = (f32[256,768]{1,0:T(8,128)S(1)}, f32[256,768]{1,0:T(8,128)}, u32[]{:S(2)}) copy-start(f32[256,768]{1,0:T(8,128)} %copy-done.61) | copy-start | bytes 2359300
  412.2 38.9 %copy-start.91 = (f32[768]{0:T(1024)S(1)}, f32[768]{0:T(1024)}, u32[]{:S(2)}) copy-start(f32[768]{0:T(1024)} %get-tuple-element.173) | copy-start | bytes 9220
  412.2 38.9 %copy-start.90 = (f32[768]{0:T(1024)S(1)}, f32[768]{0:T(1024)}, u32[]{:S(2)}) copy-start(f32[768]{0:T(1024)} %get-tuple-element.179) | copy-start | bytes 9220
  412.2 38.9 %copy-start.92 = (f32[768]{0:T(1024)S(1)}, f32[768]{0:T(1024)}, u32[]{:S(2)}) copy-start(f32[768]{0:T(1024)} %get-tuple-element.203) | copy-start | bytes 9220
  412.2 38.9 %copy-start.111 = (f32[1536]{0:T(1024)S(1)}, f32[1536]{0:T(1024)}, u32[]{:S(2)}) copy-start(f32[1536]{0:T(1024)} %get-tuple-element.277) | copy-start | bytes 18436
  412.2 39.0 %copy-start.110 = (f32[1536]{0:T(1024)S(1)}, f32[1536]{0:T(1024)}, u32[]{:S(2)}) copy-start(f32[1536]{0:T(1024)} %get-tuple-element.281) | copy-start | bytes 18436
  412.2 39.0 %copy-start.118 = (f32[768]{0:T(1024)S(1)}, f32[768]{0:T(1024)}, u32[]{:S(2)}) copy-start(f32[768]{0:T(1024)} %get-tuple-element.169) | copy-start | bytes 9220
  412.2 39.0 %copy-start.117 = (f32[768]{0:T(1024)S(1)}, f32[768]{0:T(1024)}, u32[]{:S(2)}) copy-start(f32[768]{0:T(1024)} %get-tuple-element.181) | copy-start | bytes 9220
  412.3 39.0 %copy-start.96 = (f32[768]{0:T(1024)S(1)}, f32[768]{0:T(1024)}, u32[]{:S(2)}) copy-start(f32[768]{0:T(1024)} %get-tuple-element.171) | copy-start | bytes 9220
  412.3 39.0 %copy-start.113 = (f32[1536]{0:T(1024)S(1)}, f32[1536]{0:T(1024)}, u32[]{:S(2)}) copy-start(f32[1536]{0:T(1024)} %get-tuple-element.279) | copy-start | bytes 18436
  412.3 39.1 %copy-start.94 = (f32[768]{0:T(1024)S(1)}, f32[768]{0:T(1024)}, u32[]{:S(2)}) copy-start(f32[768]{0:T(1024)} %get-tuple-element.205) | copy-start | bytes 9220
  412.3 39.1 %copy-start.95 = (f32[768]{0:T(1024)S(1)}, f32[768]{0:T(1024)}, u32[]{:S(2)}) copy-start(f32[768]{0:T(1024)} %get-tuple-element.182) | copy-start | bytes 9220
  412.3 39.1 %copy-start.119 = (f32[768]{0:T(1024)S(1)}, f32[768]{0:T(1024)}, u32[]{:S(2)}) copy-start(f32[768]{0:T(1024)} %get-tuple-element.168) | copy-start | bytes 9220
  412.3 42.1 %copy-start.93 = (f32[768]{0:T(1024)S(1)}, f32[768]{0:T(1024)}, u32[]{:S(2)}) copy-start(f32[768]{0:T(1024)} %get-tuple-element.199) | copy-start | bytes 9220
  412.3 42.1 %copy-start.112 = (f32[1536]{0:T(1024)S(1)}, f32[1536]{0:T(1024)}, u32[]{:S(2)}) copy-start(f32[1536]{0:T(1024)} %get-tuple-element.275) | copy-start | bytes 18436
  412.3 36.6 %collective-permute-start.14 = (f32[512,768]{1,0:T(8,128)S(1)}, f32[512,768]{1,0:T(8,128)S(1)}, u32[]{:S(2)}, u32[]{:S(2)}) collective-permute-start(f32[512,768]{1,0:T(8,128)S(1)} %copy-done.16), channel_id=1, source_target_pairs={{0,1},{1,0},{2,3},{3,2},{4,5},{5,4},{6,7},{7,6},{8,9},{9,8},{10,11... | collective-permute-start | bytes 4718600 | tf_op jit(solution)/shard_map/ppermute | solution.py:65
  450.4 20.1 %collective-permute-start.15 = (f32[256,768]{1,0:T(8,128)}, f32[256,768]{1,0:T(8,128)S(1)}, u32[]{:S(2)}, u32[]{:S(2)}) collective-permute-start(f32[256,768]{1,0:T(8,128)} %get-tuple-element.132), channel_id=1, source_target_pairs={{0,1},{1,0},{2,3},{3,2},{4,5},{5,4},{6,7},{7,6},{8,9},{9,8},{10,11... | collective-permute-start | bytes 2359304 | tf_op jit(solution)/shard_map/ppermute | solution.py:65
  451.5 18.9 %collective-permute-start.10 = (f32[14,768]{1,0:T(8,128)S(1)}, f32[14,768]{1,0:T(8,128)S(1)}, u32[]{:S(2)}, u32[]{:S(2)}) collective-permute-start(f32[14,768]{1,0:T(8,128)S(1)} %concatenate.41), channel_id=1, source_target_pairs={{0,1},{1,0},{2,3},{3,2},{4,5},{5,4},{6,7},{7,6},{8,9},{9,8},{10,11... | collective-permute-start | bytes 129032 | tf_op jit(solution)/shard_map/ppermute | solution.py:65
  472.8 1.3 collective-permute-start.36
  474.1 6.5 %collective-permute-start.37 = (f32[18,768]{1,0:T(8,128)S(1)}, f32[18,768]{1,0:T(8,128)S(1)}, u32[]{:S(2)}, u32[]{:S(2)}) collective-permute-start(f32[18,768]{1,0:T(8,128)S(1)} %add.533), channel_id=1, source_target_pairs={{0,4},{4,0},{8,12},{12,8},{1,5},{5,1},{9,13},{13,9},{2,6},{6,2},{1... | collective-permute-start | bytes 165896 | tf_op jit(solution)/shard_map/ppermute | solution.py:667
  480.6 7.5 %collective-permute-start.38 = (f32[18,768]{1,0:T(8,128)S(1)}, f32[18,768]{1,0:T(8,128)S(1)}, u32[]{:S(2)}, u32[]{:S(2)}) collective-permute-start(f32[18,768]{1,0:T(8,128)S(1)} %add.534), channel_id=1, source_target_pairs={{4,8},{8,4},{12,0},{0,12},{5,9},{9,5},{13,1},{1,13},{6,10},{10,6},... | collective-permute-start | bytes 165896 | tf_op jit(solution)/shard_map/ppermute | solution.py:667
  488.0 6.0 %collective-permute-start.39 = (f32[18,768]{1,0:T(8,128)S(1)}, f32[18,768]{1,0:T(8,128)S(1)}, u32[]{:S(2)}, u32[]{:S(2)}) collective-permute-start(f32[18,768]{1,0:T(8,128)S(1)} %add.535), channel_id=1, source_target_pairs={{0,32},{32,0},{64,96},{96,64},{1,33},{33,1},{65,97},{97,65},{2,34}... | collective-permute-start | bytes 165896 | tf_op jit(solution)/shard_map/ppermute | solution.py:667
  494.1 7.2 %collective-permute-start.40 = (f32[18,768]{1,0:T(8,128)S(1)}, f32[18,768]{1,0:T(8,128)S(1)}, u32[]{:S(2)}, u32[]{:S(2)}) collective-permute-start(f32[18,768]{1,0:T(8,128)S(1)} %add.536), channel_id=1, source_target_pairs={{32,64},{64,32},{96,0},{0,96},{33,65},{65,33},{97,1},{1,97},{34,66... | collective-permute-start | bytes 165896 | tf_op jit(solution)/shard_map/ppermute | solution.py:667
  501.3 4.4 collective-permute-start.41
  (114 other events, 642.3 us)
Sparse Core Ops, SparseCore 0:
  25.3 57.0 all-gather.6
  85.2 54.9 all-gather.8
  189.9 86.9 reduce-scatter.2
  280.7 107.1 reduce-scatter.4
  411.6 97.7 all-gather.10

commit v9 on v8

--- a/solution.py
+++ b/solution.py
@@ -287,18 +287,28 @@
     )(length.reshape(1), queries, keys, values, logsum, attended_low, query_weight, key_weight, value_weight, output_weight)
 
 
-def pieces_kernel(place_ref, down_in, up_in, piece_ref):
-    width = piece_ref.shape[2]
+def pieces_kernel(place_ref, down_ref, up_ref, piece_ref, down_rows, up_rows, done):
+    layers, rows, width = piece_ref.shape
+    chip = place_ref[0]
+    half = rows // 2
 
     @pl.when(place_ref[1] == 0)
     def _():
-        piece_ref[0] = down_in[0].astype(F32)
+        source = down_ref.at[:, pl.ds(pl.multiple_of(chip * rows, rows), rows), :]
+        copy = pltpu.make_async_copy(source, down_rows, done)
+        copy.start()
+        copy.wait()
+        piece_ref[...] = down_rows[...].astype(F32)
 
     @pl.when(place_ref[1] != 0)
     def _():
-        half = up_in.shape[1]
-        piece_ref[0, :half, :] = up_in[0, :, :width].astype(F32)
-        piece_ref[0, half:, :] = up_in[0, :, width:].astype(F32)
+        source = up_ref.at[:, pl.ds(pl.multiple_of(chip * half, half), half), :]
+        copy = pltpu.make_async_copy(source, up_rows, done)
+        copy.start()
+        copy.wait()
+        for layer in range(layers):
+            piece_ref[layer, :half, :] = up_rows[layer, :, :width].astype(F32)
+            piece_ref[layer, half:, :] = up_rows[layer, :, width:].astype(F32)
 
 
 def weight_pieces(chip, core, down_weight, up_weight):
@@ -306,16 +316,14 @@
     rows = units // 16
     return pl.pallas_call(
         pieces_kernel,
-        grid_spec=pltpu.PrefetchScalarGridSpec(
-            num_scalar_prefetch=1,
-            grid=(layers,),
-            in_specs=[
-                pl.BlockSpec((1, rows, width), lambda l, place: (l, place[0], 0)),
-                pl.BlockSpec((1, rows // 2, units), lambda l, place: (l, place[0], 0)),
-            ],
-            out_specs=pl.BlockSpec((1, rows, width), lambda l, place: (l, 0, 0)),
-        ),
+        in_specs=[SCALAR] + [pl.BlockSpec(memory_space=pltpu.HBM)] * 2,
+        out_specs=pl.BlockSpec(memory_space=pltpu.VMEM),
         out_shape=jax.ShapeDtypeStruct((layers, rows, width), F32),
+        scratch_shapes=[
+            pltpu.VMEM((layers, rows, width), BF16),
+            pltpu.VMEM((layers, rows // 2, units), BF16),
+            pltpu.SemaphoreType.DMA,
+        ],
         compiler_params=LIMIT,
         name="weight_pieces",
     )(jnp.stack([chip, core]), down_weight, up_weight)
@@ -531,10 +539,13 @@
     def own_slots(values):
         return piece(values, side, half_slots)
 
-    def feed_weights_back(saved, pre_lows, ffn_low, columns):
+    def feed_weights_back(saved, pre_lows, ffn_low, columns, *first):
         actives, hidden_low = saved[3], saved[4]
         received = swap(feed_sums(1 - core, actives, pre_lows, ffn_low, hidden_low, 2 * width), "c")
-        return feed_sums(core, actives, pre_lows, ffn_low, hidden_low, columns, received)
+        if first:
+            received, *first = together(received, *first)
+        total = feed_sums(core, actives, pre_lows, ffn_low, hidden_low, columns, received)
+        return total, *first
 
     def attention_forward(layer, rounded):
         *attention, share, sent = attend(
@@ -619,9 +630,10 @@
     gradient2 = own_slots(cotangent).astype(F32) * weighting
     grad_one_own, ffn_low, pre_lows, shared2, biases2 = feed_back(1, gradient2, saved2)
     sent = 0.5 * grad_one_own
-    received = swap(sent, "h")
-    feed2 = feed_weights_back(saved2, pre_lows, ffn_low, 2 * width)
-    feed2, received = together(feed2, received)
+    cut = half_slots * 5 // 8
+    received, late = swap(sent[:cut], "h"), swap(sent[cut:], "h")
+    feed2, received = feed_weights_back(saved2, pre_lows, ffn_low, 2 * width, received)
+    received = jnp.concatenate([received, late])
     feed2 = lax.psum_scatter(feed2, PLANE, tiled=True)
     _, lows2, attended_low2, share, small_att2 = attention_back(1, att2, sent, received)
     received = swap(piece(share, 1 - side, half_slots), "h")
@@ -631,7 +643,7 @@
     grad_one_own1, ffn_low, pre_lows, shared1, biases1 = feed_back(0, gradient1, saved1)
     sent = 0.5 * grad_one_own1
     received = swap(sent, "h")
-    rest = feed_weights_back(saved1, pre_lows, ffn_low, 2 * width + columns)
+    (rest,) = feed_weights_back(saved1, pre_lows, ffn_low, 2 * width + columns)
     rest = attention_sums(core, lows2, mixture, x2_low, attended_low2, attn2_received, rest, 2 * width // columns)
     rest, received, feed2 = together(rest, received, feed2)
     rest = lax.psum_scatter(rest, PLANE, tiled=True)

time: 551 us -> 552 us (level)
    ppermute x24 -> x25, waiting for transfers between devices: 163 us -> 171 us  [swap(): return lax.ppermute(values, axis, SWAP)]
    reduce_scatter x1, waiting for transfers between devices: 12.2 us -> 3.79 us  [local(): feed2 = lax.psum_scatter(feed2, PLANE, tiled=True)]
    ppermute x24 -> x25, starting transfers between devices: 39.5 us -> 43.7 us  [swap(): return lax.ppermute(values, axis, SWAP)]
    unnamed x270 -> x283, local copies, waits for them, and re-layouts: 52.8 us -> 53.3 us
  transfers between devices with their start and end apart: 47 -> 48, of which waited for: 33 -> 33; matrix products, arithmetic and copies ran while one was open for 9% -> 9% of each run, Pallas kernels for 11% -> 10%
where the time goes in v9:
time: 552 us; the launch traced here: 542 us
  waiting for transfers between devices  257 us (47%)
  Pallas kernels  85.4 us (15%)
  starting transfers between devices  65.6 us (12%)
  local copies, waits for them, and re-layouts  61.9 us (11%)
  matrix products  28.6 us (5%)
  other arithmetic  27.3 us (5%)
  between operations  17.2 us (3%)
    ppermute x25, waiting for transfers between devices, swap(): return lax.ppermute(values, axis, SWAP)  171 us
    unnamed x283, local copies, waits for them, and re-layouts  53.3 us
    ppermute x25, starting transfers between devices, swap(): return lax.ppermute(values, axis, SWAP)  43.7 us
    ppermute x4, waiting for transfers between devices, local(): small = small + lax.ppermute(small, axis, pairs)  26.5 us
    ppermute x12, waiting for transfers between devices, ring_parts(): received.append(lax.ppermute(sent, axis, pairs))  26.4 us
    pallas_call x2, Pallas kernels, attend_back(): pl.pallas_call(attend_back_kernel, grid=(steps,), in_specs=[SCALAR, part,...  20.7 us
    reduce_scatter x1, waiting for transfers between devices, local(): rest = lax.psum_scatter(rest, PLANE, tiled=True)  19 us
    pallas_call x2, Pallas kernels, attend(): pl.pallas_call(lambda *refs: attend_kernel(sends_mixture, *refs), grid=(s...  17.9 us
  transfers between devices with their start and end apart: 48, of which 33 were waited for; matrix products, arithmetic and copies ran while one was open for 9% of the time, Pallas kernels for 10%

profile of v9, /device:TPU:0, one launch (start us, length us, event | category | flops | bytes accessed | tf_op | source)
XLA Modules:
  0.0 542.5 jit_solution(10985151320605630479)
XLA Ops:
  8.0 2.3 copy-done.5
  10.3 2.3 copy-done.6
  14.1 4.0 collective-permute-start
  18.0 7.0 %collective-permute-done = f32[96,768]{1,0:T(8,128)S(1)} collective-permute-done((f32[96,768]{1,0:T(8,128)S(1)}, f32[96,768]{1,0:T(8,128)S(1)}, u32[]{:S(2)}, u32[]{:S(2)}) %collective-permute-start) | collective-permute-done | bytes 294944 | tf_op jit(solution)/shard_map/ppermute | solution.py:65
  25.8 3.3 collective-permute-start.1
  33.0 9.1 %attend.2 = (bf16[512,384]{1,0:T(8,128)(2,1)S(1)}, bf16[512,384]{1,0:T(8,128)(2,1)S(1)}, bf16[512,384]{1,0:T(8,128)(2,1)S(1)}, bf16[512,384]{1,0:T(8,128)(2,1)S(...) custom-call(s32[2]{0:T(128)S(1)} %get-tuple-element.283.refs_0_, ...), custom_call_target="tpu_custom_call" | custom-call | flops 1610612736 | bytes 5505024 | tf_op jit(solution)/shard_map/attend/pallas_call | solution.py:191
  48.4 3.2 collective-permute-start.2
  55.9 12.6 %collective-permute-done.2 = f32[256,768]{1,0:T(8,128)} collective-permute-done((f32[256,768]{1,0:T(8,128)}, f32[256,768]{1,0:T(8,128)}, u32[]{:S(2)}, u32[]{:S(2)}) %collective-permute-start.2) | collective-permute-done | bytes 786464 | tf_op jit(solution)/shard_map/ppermute | solution.py:65
  68.5 2.8 collective-permute-start.4
  73.5 4.2 multiply_convert_fusion.3
  79.4 3.6 all-gather.7.cloned.1.call-done
  83.0 3.7 copy-done.3
  92.0 4.1 collective-permute-done.4
  96.1 2.3 collective-permute-start.5
  98.5 15.7 %collective-permute-done.5 = f32[256,768]{1,0:T(8,128)} collective-permute-done((f32[256,768]{1,0:T(8,128)S(1)}, f32[256,768]{1,0:T(8,128)}, u32[]{:S(2)}, u32[]{:S(2)}) %collective-permute-start.5) | collective-permute-done | bytes 786464 | tf_op jit(solution)/shard_map/ppermute | solution.py:65
  117.7 8.8 %attend.3 = (bf16[512,384]{1,0:T(8,128)(2,1)S(1)}, bf16[512,384]{1,0:T(8,128)(2,1)S(1)}, bf16[512,384]{1,0:T(8,128)(2,1)S(1)}, bf16[512,384]{1,0:T(8,128)(2,1)S(...) custom-call(s32[2]{0:T(128)S(1)} %get-tuple-element.283.refs_0_, ...), custom_call_target="tpu_custom_call" | custom-call | flops 1610612736 | bytes 5505024 | tf_op jit(solution)/shard_map/attend/pallas_call | solution.py:191
  130.9 2.5 collective-permute-start.6
  134.7 6.1 %all-gather.9.cloned.1.call-done = f32[3072,768]{1,0:T(8,128)} async-done(((f32[96,768]{1,0:T(8,128)}), f32[3072,768]{1,0:T(8,128)}) %all-gather.9.cloned.1.call-update) | async-done | bytes 9437200 | tf_op jit(solution)/shard_map/all_gather | solution.py:613
  140.7 3.7 copy-done.2
  148.1 2.5 multiply_convert_fusion.1
  160.9 2.4 feed_sums.4
  168.4 3.2 collective-permute-start.8
  171.6 11.7 %collective-permute-done.8 = f32[160,768]{1,0:T(8,128)S(1)} collective-permute-done((f32[160,768]{1,0:T(8,128)S(1)}, f32[160,768]{1,0:T(8,128)S(1)}, u32[]{:S(2)}, u32[]{:S(2)}) %collective-permute-start.8) | collective-permute-done | bytes 491552 | tf_op jit(solution)/shard_map/ppermute | solution.py:65
  184.2 2.5 feed_sums.7
  186.6 3.7 copy-done.1
  192.2 3.3 collective-permute-start.9
  196.6 5.9 %collective-permute-done.9 = f32[96,768]{1,0:T(8,128)} collective-permute-done((f32[96,768]{1,0:T(8,128)}, f32[96,768]{1,0:T(8,128)}, u32[]{:S(2)}, u32[]{:S(2)}) %collective-permute-start.9) | collective-permute-done | bytes 294944 | tf_op jit(solution)/shard_map/ppermute | solution.py:65
  206.3 10.4 %attend_back.2 = (bf16[512,384]{1,0:T(8,128)(2,1)S(1)}, bf16[512,384]{1,0:T(8,128)(2,1)S(1)}, bf16[512,384]{1,0:T(8,128)(2,1)S(1)}, f32[512,768]{1,0:T(8,128)S(1...) custom-call(s32[1]{0:T(128)} %copy.63.length_ref, bf16[512,384]{1,0:T(8,128)(2,1)S(1)} %copy-done.43, ...), custom_call_target="tpu_custom_call" | custom-call | flops 2214592512 | bytes 5505024 | tf_op jit(solution)/shard_map/attend_back/pallas_call | solution.py:272
  216.7 3.2 collective-permute-start.10
  219.9 16.3 %collective-permute-done.10 = f32[256,768]{1,0:T(8,128)S(1)} collective-permute-done((f32[256,768]{1,0:T(8,128)S(1)}, f32[256,768]{1,0:T(8,128)S(1)}, u32[]{:S(2)}, u32[]{:S(2)}) %collective-permute-start.10) | collective-permute-done | bytes 786464 | tf_op jit(solution)/shard_map/ppermute | solution.py:65
  243.1 2.4 feed_sums.5
  252.0 3.3 collective-permute-start.14
  255.2 5.0 collective-permute-done.13.refs_7_
  260.3 3.1 feed_sums.6.refs_8_
  263.7 2.2 attention_sums.5
  265.9 4.3 copy-done
  270.2 3.4 collective-permute-done.14
  273.6 3.8 reduce-scatter.3.cloned.1.call-done
  282.5 10.4 %attend_back.3 = (bf16[512,384]{1,0:T(8,128)(2,1)S(1)}, bf16[512,384]{1,0:T(8,128)(2,1)S(1)}, bf16[512,384]{1,0:T(8,128)(2,1)S(1)}, f32[512,768]{1,0:T(8,128)S(1...) custom-call(s32[1]{0:T(128)} %copy.63.length_ref, bf16[512,384]{1,0:T(8,128)(2,1)S(1)} %copy-done.37, ...), custom_call_target="tpu_custom_call" | custom-call | flops 2214592512 | bytes 5505024 | tf_op jit(solution)/shard_map/attend_back/pallas_call | solution.py:272
  294.0 3.1 attention_sums.6
  297.1 4.9 collective-permute-done.20.refs_7_
  302.0 3.7 attention_sums.7
  306.8 2.7 collective-permute-start.26
  314.5 9.9 %collective-permute-done.26 = f32[4,48,384]{2,1,0:T(8,128)S(1)} collective-permute-done((f32[4,48,384]{2,1,0:T(8,128)}, f32[4,48,384]{2,1,0:T(8,128)S(1)}, u32[]{:S(2)}, u32[]{:S(2)}) %collective-permute-start.26) | collective-permute-done | bytes 294944 | tf_op jit(solution)/shard_map/ppermute | solution.py:83
  325.7 8.0 %collective-permute-done.25 = f32[4,48,384]{2,1,0:T(8,128)S(1)} collective-permute-done((f32[4,48,384]{2,1,0:T(8,128)S(1)}, f32[4,48,384]{2,1,0:T(8,128)S(1)}, u32[]{:S(2)}, u32[]{:S(2)}) %collective-permute-start.25) | collective-permute-done | bytes 294944 | tf_op jit(solution)/shard_map/ppermute | solution.py:83
  334.2 5.6 %collective-permute-done.21 = f32[4,48,384]{2,1,0:T(8,128)S(1)} collective-permute-done((f32[4,48,384]{2,1,0:T(8,128)S(1)}, f32[4,48,384]{2,1,0:T(8,128)S(1)}, u32[]{:S(2)}, u32[]{:S(2)}) %collective-permute-start.21) | collective-permute-done | bytes 294944 | tf_op jit(solution)/shard_map/ppermute | solution.py:83
  339.9 2.6 collective-permute-start.29
  349.7 2.9 collective-permute-start.19
  352.6 2.1 collective-permute-start.18
  356.9 10.3 %collective-permute-done.17 = f32[96,768]{1,0:T(8,128)S(1)} collective-permute-done((f32[96,768]{1,0:T(8,128)S(1)}, f32[96,768]{1,0:T(8,128)S(1)}, u32[]{:S(2)}, u32[]{:S(2)}) %collective-permute-start.17) | collective-permute-done | bytes 294944 | tf_op jit(solution)/shard_map/ppermute | solution.py:65
  369.5 19.0 %reduce-scatter.5.cloned.1.call-done = f32[96,1920]{1,0:T(8,128)} async-done(((f32[1536,1920]{1,0:T(8,128)}), f32[96,1920]{1,0:T(8,128)}) %reduce-scatter.5.cloned.1.call-update) | async-done | bytes 737296 | tf_op jit(solution)/shard_map/reduce_scatter | solution.py:649
  392.2 2.2 collective-permute-start.36
  395.1 8.7 %collective-permute-done.34 = f32[96,1152]{1,0:T(8,128)S(1)} collective-permute-done((f32[96,1152]{1,0:T(8,128)S(1)}, f32[96,1152]{1,0:T(8,128)S(1)}, u32[]{:S(2)}, u32[]{:S(2)}) %collective-permute-start.34) | collective-permute-done | bytes 442400 | tf_op jit(solution)/shard_map/ppermute | solution.py:65
  403.8 7.2 %collective-permute-done.35 = f32[96,768]{1,0:T(8,128)S(1)} collective-permute-done((f32[96,768]{1,0:T(8,128)S(1)}, f32[96,768]{1,0:T(8,128)S(1)}, u32[]{:S(2)}, u32[]{:S(2)}) %collective-permute-start.35) | collective-permute-done | bytes 294944 | tf_op jit(solution)/shard_map/ppermute | solution.py:65
  413.8 35.8 %collective-permute-done.15 = f32[512,768]{1,0:T(8,128)S(1)} collective-permute-done((f32[512,768]{1,0:T(8,128)S(1)}, f32[512,768]{1,0:T(8,128)S(1)}, u32[]{:S(2)}, u32[]{:S(2)}) %collective-permute-start.15) | collective-permute-done | bytes 1572896 | tf_op jit(solution)/shard_map/ppermute | solution.py:65
  452.1 2.9 collective-permute-start.11
  455.2 15.8 %collective-permute-done.11 = f32[14,768]{1,0:T(8,128)S(1)} collective-permute-done((f32[14,768]{1,0:T(8,128)S(1)}, f32[14,768]{1,0:T(8,128)S(1)}, u32[]{:S(2)}, u32[]{:S(2)}) %collective-permute-start.11) | collective-permute-done | bytes 43040 | tf_op jit(solution)/shard_map/ppermute | solution.py:65
  474.9 6.4 %collective-permute-done.38 = f32[18,768]{1,0:T(8,128)S(1)} collective-permute-done((f32[18,768]{1,0:T(8,128)S(1)}, f32[18,768]{1,0:T(8,128)S(1)}, u32[]{:S(2)}, u32[]{:S(2)}) %collective-permute-start.38) | collective-permute-done | bytes 55328 | tf_op jit(solution)/shard_map/ppermute | solution.py:679
  481.4 7.4 %collective-permute-done.39 = f32[18,768]{1,0:T(8,128)S(1)} collective-permute-done((f32[18,768]{1,0:T(8,128)S(1)}, f32[18,768]{1,0:T(8,128)S(1)}, u32[]{:S(2)}, u32[]{:S(2)}) %collective-permute-start.39) | collective-permute-done | bytes 55328 | tf_op jit(solution)/shard_map/ppermute | solution.py:679
  488.8 5.9 %collective-permute-done.40 = f32[18,768]{1,0:T(8,128)S(1)} collective-permute-done((f32[18,768]{1,0:T(8,128)S(1)}, f32[18,768]{1,0:T(8,128)S(1)}, u32[]{:S(2)}, u32[]{:S(2)}) %collective-permute-start.40) | collective-permute-done | bytes 55328 | tf_op jit(solution)/shard_map/ppermute | solution.py:679
  495.1 6.8 %collective-permute-done.41 = f32[18,768]{1,0:T(8,128)S(1)} collective-permute-done((f32[18,768]{1,0:T(8,128)S(1)}, f32[18,768]{1,0:T(8,128)S(1)}, u32[]{:S(2)}, u32[]{:S(2)}) %collective-permute-start.41) | collective-permute-done | bytes 55328 | tf_op jit(solution)/shard_map/ppermute | solution.py:679
  502.2 4.2 collective-permute-done.42
  511.9 8.0 %place_attention.1 = (f32[2,768,384]{2,1,0:T(8,128)}, f32[2,768,384]{2,1,0:T(8,128)}, f32[2,768,384]{2,1,0:T(8,128)}, f32[2,384,768]{2,1,0:T(8,128)}) custom-call(f32[16,2,96,2304]{3,2,1,0:T(8,128)} %bitcast.147, f32[16,2,96,2304]{3,2,1,0:T(8,128)} %bitcast.148, f32[16,2,96,2304]{3,2,1,0:T(8,128)} %bitcast.149, f32[16,2,96,2304]{3,2,1,0:T(8,128)} %bitcast.150), custom_call_target="tpu_custom_call" | custom-call | tf_op jit(solution)/shard_map/place_attention/pallas_call | solution.py:489
  519.9 15.6 %place_feed.1 = (f32[2,1536,768]{2,1,0:T(8,128)}, f32[2,768,1536]{2,1,0:T(8,128)}) custom-call(f32[16,2,96,2304]{3,2,1,0:T(8,128)} %bitcast.151, f32[16,2,96,2304]{3,2,1,0:T(8,128)} %bitcast.152), custom_call_target="tpu_custom_call" | custom-call | tf_op jit(solution)/shard_map/place_feed/pallas_call | solution.py:472
  (477 shorter events, 119.0 us)
Async XLA Ops:
  7.2 75.8 %all-gather.7.cloned.1.call-start = ((), (), s32[]{:S(2)}) async-start(), calls=%async_computation.4 | async-start | bytes 9732096 | tf_op jit(solution)/shard_map/all_gather | solution.py:535
  14.1 11.0 %collective-permute-start = (f32[96,768]{1,0:T(8,128)S(1)}, f32[96,768]{1,0:T(8,128)S(1)}, u32[]{:S(2)}, u32[]{:S(2)}) collective-permute-start(f32[96,768]{1,0:T(8,128)S(1)} %get-tuple-element.239), channel_id=1, source_target_pairs={{0,1},{1,0},{2,3},{3,2},{4,5},{5,4},{6,7},{7,6},{8,9},{9,8},{10,11... | collective-permute-start | bytes 884744 | tf_op jit(solution)/shard_map/ppermute | solution.py:65
  25.8 115.0 %all-gather.9.cloned.1.call-start = ((), (), s32[]{:S(2)}) async-start(), calls=%async_computation.5 | async-start | bytes 9732096 | tf_op jit(solution)/shard_map/all_gather | solution.py:613
  25.8 20.8 %collective-permute-start.1 = (f32[96,768]{1,0:T(8,128)}, f32[96,768]{1,0:T(8,128)S(1)}, u32[]{:S(2)}, u32[]{:S(2)}) collective-permute-start(f32[96,768]{1,0:T(8,128)} %get-tuple-element.93), channel_id=1, source_target_pairs={{0,1},{1,0},{2,3},{3,2},{4,5},{5,4},{6,7},{7,6},{8,9},{9,8},{10,11... | collective-permute-start | bytes 884744 | tf_op jit(solution)/shard_map/ppermute | solution.py:65
  47.3 230.0 %reduce-scatter.3.cloned.1.call-start = ((), (), s32[]{:S(2)}) async-start(), calls=%async_computation.2 | async-start | bytes 10027008 | tf_op jit(solution)/shard_map/reduce_scatter | solution.py:637
  47.4 7.8 %collective-permute-start.3 = (f32[2,1536]{1,0:T(2,128)S(1)}, f32[2,1536]{1,0:T(2,128)S(1)}, u32[]{:S(2)}, u32[]{:S(2)}) collective-permute-start(f32[2,1536]{1,0:T(2,128)S(1)} %convert_element_type.152), channel_id=1, source_target_pairs={{0,1},{1,0},{2,3},{3,2},{4,5},{5,4},{6,7},{7,6},{8,9},{9,8},{10,11... | collective-permute-start | bytes 36872 | tf_op jit(solution)/shard_map/ppermute | solution.py:65
  48.4 20.1 %collective-permute-start.2 = (f32[256,768]{1,0:T(8,128)}, f32[256,768]{1,0:T(8,128)}, u32[]{:S(2)}, u32[]{:S(2)}) collective-permute-start(f32[256,768]{1,0:T(8,128)} %copy-done.35), channel_id=1, source_target_pairs={{0,1},{1,0},{2,3},{3,2},{4,5},{5,4},{6,7},{7,6},{8,9},{9,8},{10,11... | collective-permute-start | bytes 2359304 | tf_op jit(solution)/shard_map/ppermute | solution.py:65
  68.5 27.6 %collective-permute-start.4 = (f32[384,768]{1,0:T(8,128)}, f32[384,768]{1,0:T(8,128)}, u32[]{:S(2)}, u32[]{:S(2)}) collective-permute-start(f32[384,768]{1,0:T(8,128)} %multiply_bitcast_fusion), channel_id=1, source_target_pairs={{0,1},{1,0},{2,3},{3,2},{4,5},{5,4},{6,7},{7,6},{8,9},{9,8},{10,11... | collective-permute-start | bytes 3538952 | tf_op jit(solution)/shard_map/ppermute | solution.py:65
  96.1 18.1 %collective-permute-start.5 = (f32[256,768]{1,0:T(8,128)S(1)}, f32[256,768]{1,0:T(8,128)}, u32[]{:S(2)}, u32[]{:S(2)}) collective-permute-start(f32[256,768]{1,0:T(8,128)S(1)} %fusion.62), channel_id=1, source_target_pairs={{0,1},{1,0},{2,3},{3,2},{4,5},{5,4},{6,7},{7,6},{8,9},{9,8},{10,11... | collective-permute-start | bytes 2359304 | tf_op jit(solution)/shard_map/ppermute | solution.py:65
  130.9 14.1 %collective-permute-start.6 = (f32[256,384]{1,0:T(8,128)}, f32[256,384]{1,0:T(8,128)}, u32[]{:S(2)}, u32[]{:S(2)}) collective-permute-start(f32[256,384]{1,0:T(8,128)} %get-tuple-element.103), channel_id=1, source_target_pairs={{0,1},{1,0},{2,3},{3,2},{4,5},{5,4},{6,7},{7,6},{8,9},{9,8},{10,11... | collective-permute-start | bytes 1179656 | tf_op jit(solution)/shard_map/ppermute | solution.py:65
  163.4 20.0 %collective-permute-start.7 = (f32[1536,1536]{1,0:T(8,128)S(1)}, f32[1536,1536]{1,0:T(8,128)S(1)}, u32[]{:S(2)}, u32[]{:S(2)}) collective-permute-start(f32[1536,1536]{1,0:T(8,128)S(1)} %feed_sums.4), channel_id=1, source_target_pairs={{0,2},{2,0},{1,3},{3,1},{4,6},{6,4},{5,7},{7,5},{8,10},{10,8},{9,1... | collective-permute-start | bytes 28311560 | tf_op jit(solution)/shard_map/ppermute | solution.py:65
  168.4 15.0 %collective-permute-start.8 = (f32[160,768]{1,0:T(8,128)S(1)}, f32[160,768]{1,0:T(8,128)S(1)}, u32[]{:S(2)}, u32[]{:S(2)}) collective-permute-start(f32[160,768]{1,0:T(8,128)S(1)} %slice.208), channel_id=1, source_target_pairs={{0,1},{1,0},{2,3},{3,2},{4,5},{5,4},{6,7},{7,6},{8,9},{9,8},{10,11... | collective-permute-start | bytes 1474568 | tf_op jit(solution)/shard_map/ppermute | solution.py:65
  190.4 198.1 %reduce-scatter.5.cloned.1.call-start = ((), (), s32[]{:S(2)}) async-start(), calls=%async_computation.3 | async-start | bytes 12533760 | tf_op jit(solution)/shard_map/reduce_scatter | solution.py:649
  192.2 10.3 %collective-permute-start.9 = (f32[96,768]{1,0:T(8,128)}, f32[96,768]{1,0:T(8,128)}, u32[]{:S(2)}, u32[]{:S(2)}) collective-permute-start(f32[96,768]{1,0:T(8,128)} %slice.209), channel_id=1, source_target_pairs={{0,1},{1,0},{2,3},{3,2},{4,5},{5,4},{6,7},{7,6},{8,9},{9,8},{10,11... | collective-permute-start | bytes 884744 | tf_op jit(solution)/shard_map/ppermute | solution.py:65
  216.7 19.5 %collective-permute-start.10 = (f32[256,768]{1,0:T(8,128)S(1)}, f32[256,768]{1,0:T(8,128)S(1)}, u32[]{:S(2)}, u32[]{:S(2)}) collective-permute-start(f32[256,768]{1,0:T(8,128)S(1)} %constant_dynamic-slice_fusion), channel_id=1, source_target_pairs={{0,1},{1,0},{2,3},{3,2},{4,5},{5,4},{6,7},{7,6},{8,9},{9,8},{10,11... | collective-permute-start | bytes 2359304 | tf_op jit(solution)/shard_map/ppermute | solution.py:65
  245.6 14.7 %collective-permute-start.13 = (f32[1536,1536]{1,0:T(8,128)S(1)}, f32[1536,1536]{1,0:T(8,128)S(1)}, u32[]{:S(2)}, u32[]{:S(2)}) collective-permute-start(f32[1536,1536]{1,0:T(8,128)S(1)} %feed_sums.5), channel_id=1, source_target_pairs={{0,2},{2,0},{1,3},{3,1},{4,6},{6,4},{5,7},{7,5},{8,10},{10,8},{9,1... | collective-permute-start | bytes 28311560 | tf_op jit(solution)/shard_map/ppermute | solution.py:65
  247.7 15.9 %collective-permute-start.12 = (f32[1536,384]{1,0:T(8,128)S(1)}, f32[1536,384]{1,0:T(8,128)S(1)}, u32[]{:S(2)}, u32[]{:S(2)}) collective-permute-start(f32[1536,384]{1,0:T(8,128)S(1)} %attention_sums.4), channel_id=1, source_target_pairs={{0,2},{2,0},{1,3},{3,1},{4,6},{6,4},{5,7},{7,5},{8,10},{10,8},{9,1... | collective-permute-start | bytes 7077896 | tf_op jit(solution)/shard_map/ppermute | solution.py:65
  252.0 21.6 %collective-permute-start.14 = (f32[256,768]{1,0:T(8,128)}, f32[256,768]{1,0:T(8,128)}, u32[]{:S(2)}, u32[]{:S(2)}) collective-permute-start(f32[256,768]{1,0:T(8,128)} %multiply_multiply_fusion.4), channel_id=1, source_target_pairs={{0,1},{1,0},{2,3},{3,2},{4,5},{5,4},{6,7},{7,6},{8,9},{9,8},{10,11... | collective-permute-start | bytes 2359304 | tf_op jit(solution)/shard_map/ppermute | solution.py:65
  277.4 234.5 %all-gather.11.cloned.1.call-start = ((), (), s32[]{:S(2)}) async-start(), calls=%async_computation.6 | async-start | bytes 29196288 | tf_op jit(solution)/shard_map/all_gather | solution.py:665
  297.1 4.9 collective-permute-start.20
  306.8 17.7 %collective-permute-start.26 = (f32[4,48,384]{2,1,0:T(8,128)}, f32[4,48,384]{2,1,0:T(8,128)S(1)}, u32[]{:S(2)}, u32[]{:S(2)}) collective-permute-start(f32[4,48,384]{2,1,0:T(8,128)} %get-tuple-element.226), channel_id=1, source_target_pairs={{0,64},{32,96},{64,0},{96,32},{1,65},{33,97},{65,1},{97,33},{2,66}... | collective-permute-start | bytes 884744 | tf_op jit(solution)/shard_map/ppermute | solution.py:83
  309.5 24.2 %collective-permute-start.25 = (f32[4,48,384]{2,1,0:T(8,128)S(1)}, f32[4,48,384]{2,1,0:T(8,128)S(1)}, u32[]{:S(2)}, u32[]{:S(2)}) collective-permute-start(f32[4,48,384]{2,1,0:T(8,128)S(1)} %get-tuple-element.227), channel_id=1, source_target_pairs={{0,96},{32,0},{64,32},{96,64},{1,97},{33,1},{65,33},{97,65},{2,98}... | collective-permute-start | bytes 884744 | tf_op jit(solution)/shard_map/ppermute | solution.py:83
  310.9 22.8 %collective-permute-start.24 = (f32[4,48,384]{2,1,0:T(8,128)S(1)}, f32[4,48,384]{2,1,0:T(8,128)S(1)}, u32[]{:S(2)}, u32[]{:S(2)}) collective-permute-start(f32[4,48,384]{2,1,0:T(8,128)S(1)} %get-tuple-element.228), channel_id=1, source_target_pairs={{0,32},{32,64},{64,96},{96,0},{1,33},{33,65},{65,97},{97,1},{2,34}... | collective-permute-start | bytes 884744 | tf_op jit(solution)/shard_map/ppermute | solution.py:83
  311.6 22.1 %collective-permute-start.23 = (f32[4,48,384]{2,1,0:T(8,128)S(1)}, f32[4,48,384]{2,1,0:T(8,128)S(1)}, u32[]{:S(2)}, u32[]{:S(2)}) collective-permute-start(f32[4,48,384]{2,1,0:T(8,128)S(1)} %get-tuple-element.230), channel_id=1, source_target_pairs={{0,8},{4,12},{8,0},{12,4},{1,9},{5,13},{9,1},{13,5},{2,10},{6,14},... | collective-permute-start | bytes 884744 | tf_op jit(solution)/shard_map/ppermute | solution.py:83
  313.2 21.0 %collective-permute-start.22 = (f32[4,48,384]{2,1,0:T(8,128)S(1)}, f32[4,48,384]{2,1,0:T(8,128)S(1)}, u32[]{:S(2)}, u32[]{:S(2)}) collective-permute-start(f32[4,48,384]{2,1,0:T(8,128)S(1)} %get-tuple-element.231), channel_id=1, source_target_pairs={{0,12},{4,0},{8,4},{12,8},{1,13},{5,1},{9,5},{13,9},{2,14},{6,2},{... | collective-permute-start | bytes 884744 | tf_op jit(solution)/shard_map/ppermute | solution.py:83
  324.5 15.3 %collective-permute-start.21 = (f32[4,48,384]{2,1,0:T(8,128)S(1)}, f32[4,48,384]{2,1,0:T(8,128)S(1)}, u32[]{:S(2)}, u32[]{:S(2)}) collective-permute-start(f32[4,48,384]{2,1,0:T(8,128)S(1)} %get-tuple-element.232), channel_id=1, source_target_pairs={{0,4},{4,8},{8,12},{12,0},{1,5},{5,9},{9,13},{13,1},{2,6},{6,10},{... | collective-permute-start | bytes 884744 | tf_op jit(solution)/shard_map/ppermute | solution.py:83
  339.9 7.6 %collective-permute-start.29 = (f32[48,384]{1,0:T(8,128)S(1)}, f32[48,384]{1,0:T(8,128)S(1)}, u32[]{:S(2)}, u32[]{:S(2)}) collective-permute-start(f32[48,384]{1,0:T(8,128)S(1)} %get-tuple-element.244), channel_id=1, source_target_pairs={{0,64},{32,96},{64,0},{96,32},{1,65},{33,97},{65,1},{97,33},{2,66}... | collective-permute-start | bytes 221192 | tf_op jit(solution)/shard_map/ppermute | solution.py:83
  342.5 7.2 %collective-permute-start.28 = (f32[48,384]{1,0:T(8,128)S(1)}, f32[48,384]{1,0:T(8,128)S(1)}, u32[]{:S(2)}, u32[]{:S(2)}) collective-permute-start(f32[48,384]{1,0:T(8,128)S(1)} %get-tuple-element.245), channel_id=1, source_target_pairs={{0,96},{32,0},{64,32},{96,64},{1,97},{33,1},{65,33},{97,65},{2,98}... | collective-permute-start | bytes 221192 | tf_op jit(solution)/shard_map/ppermute | solution.py:83
  344.2 8.4 %collective-permute-start.27 = (f32[48,384]{1,0:T(8,128)S(1)}, f32[48,384]{1,0:T(8,128)S(1)}, u32[]{:S(2)}, u32[]{:S(2)}) collective-permute-start(f32[48,384]{1,0:T(8,128)S(1)} %get-tuple-element.246), channel_id=1, source_target_pairs={{0,32},{32,64},{64,96},{96,0},{1,33},{33,65},{65,97},{97,1},{2,34}... | collective-permute-start | bytes 221192 | tf_op jit(solution)/shard_map/ppermute | solution.py:83
  344.9 9.8 %collective-permute-start.32 = (f32[48,384]{1,0:T(8,128)S(1)}, f32[48,384]{1,0:T(8,128)S(1)}, u32[]{:S(2)}, u32[]{:S(2)}) collective-permute-start(f32[48,384]{1,0:T(8,128)S(1)} %get-tuple-element.240), channel_id=1, source_target_pairs={{0,8},{4,12},{8,0},{12,4},{1,9},{5,13},{9,1},{13,5},{2,10},{6,14},... | collective-permute-start | bytes 221192 | tf_op jit(solution)/shard_map/ppermute | solution.py:83
  345.9 9.2 %collective-permute-start.31 = (f32[48,384]{1,0:T(8,128)S(1)}, f32[48,384]{1,0:T(8,128)S(1)}, u32[]{:S(2)}, u32[]{:S(2)}) collective-permute-start(f32[48,384]{1,0:T(8,128)S(1)} %get-tuple-element.241), channel_id=1, source_target_pairs={{0,12},{4,0},{8,4},{12,8},{1,13},{5,1},{9,5},{13,9},{2,14},{6,2},{... | collective-permute-start | bytes 221192 | tf_op jit(solution)/shard_map/ppermute | solution.py:83
  347.5 7.7 %collective-permute-start.30 = (f32[48,384]{1,0:T(8,128)S(1)}, f32[48,384]{1,0:T(8,128)S(1)}, u32[]{:S(2)}, u32[]{:S(2)}) collective-permute-start(f32[48,384]{1,0:T(8,128)S(1)} %get-tuple-element.242), channel_id=1, source_target_pairs={{0,4},{4,8},{8,12},{12,0},{1,5},{5,9},{9,13},{13,1},{2,6},{6,10},{... | collective-permute-start | bytes 221192 | tf_op jit(solution)/shard_map/ppermute | solution.py:83
  349.7 17.5 %collective-permute-start.19 = (f32[96,768]{1,0:T(8,128)S(1)}, f32[96,768]{1,0:T(8,128)S(1)}, u32[]{:S(2)}, u32[]{:S(2)}) collective-permute-start(f32[96,768]{1,0:T(8,128)S(1)} %get-tuple-element.237), channel_id=1, source_target_pairs={{0,17},{17,0},{1,16},{16,1},{2,19},{19,2},{3,18},{18,3},{4,21},{21... | collective-permute-start | bytes 884744 | tf_op jit(solution)/shard_map/ppermute | solution.py:655
  352.6 14.6 %collective-permute-start.18 = (f32[96,768]{1,0:T(8,128)S(1)}, f32[96,768]{1,0:T(8,128)S(1)}, u32[]{:S(2)}, u32[]{:S(2)}) collective-permute-start(f32[96,768]{1,0:T(8,128)S(1)} %get-tuple-element.237), channel_id=1, source_target_pairs={{0,1},{1,0},{2,3},{3,2},{4,5},{5,4},{6,7},{7,6},{8,9},{9,8},{10,11... | collective-permute-start | bytes 884744 | tf_op jit(solution)/shard_map/ppermute | solution.py:65
  354.7 12.5 %collective-permute-start.17 = (f32[96,768]{1,0:T(8,128)S(1)}, f32[96,768]{1,0:T(8,128)S(1)}, u32[]{:S(2)}, u32[]{:S(2)}) collective-permute-start(f32[96,768]{1,0:T(8,128)S(1)} %get-tuple-element.236), channel_id=1, source_target_pairs={{0,16},{16,0},{1,17},{17,1},{2,18},{18,2},{3,19},{19,3},{4,20},{20... | collective-permute-start | bytes 884744 | tf_op jit(solution)/shard_map/ppermute | solution.py:65
  355.3 13.5 %collective-permute-start.33 = (f32[96,384]{1,0:T(8,128)S(1)}, f32[96,384]{1,0:T(8,128)S(1)}, u32[]{:S(2)}, u32[]{:S(2)}) collective-permute-start(f32[96,384]{1,0:T(8,128)S(1)} %pad_maximum_fusion.2), channel_id=1, source_target_pairs={{0,16},{16,0},{1,17},{17,1},{2,18},{18,2},{3,19},{19,3},{4,20},{20... | collective-permute-start | bytes 442376 | tf_op jit(solution)/shard_map/ppermute | solution.py:65
  390.6 13.2 %collective-permute-start.34 = (f32[96,1152]{1,0:T(8,128)S(1)}, f32[96,1152]{1,0:T(8,128)S(1)}, u32[]{:S(2)}, u32[]{:S(2)}) collective-permute-start(f32[96,1152]{1,0:T(8,128)S(1)} %pad_maximum_fusion.1), channel_id=1, source_target_pairs={{0,16},{16,0},{1,17},{17,1},{2,18},{18,2},{3,19},{19,3},{4,20},{20... | collective-permute-start | bytes 1327112 | tf_op jit(solution)/shard_map/ppermute | solution.py:65
  392.2 11.6 %collective-permute-start.36 = (f32[96,768]{1,0:T(8,128)S(1)}, f32[96,768]{1,0:T(8,128)S(1)}, u32[]{:S(2)}, u32[]{:S(2)}) collective-permute-start(f32[96,768]{1,0:T(8,128)S(1)} %get-tuple-element.234), channel_id=1, source_target_pairs={{0,17},{17,0},{1,16},{16,1},{2,19},{19,2},{3,18},{18,3},{4,21},{21... | collective-permute-start | bytes 884744 | tf_op jit(solution)/shard_map/ppermute | solution.py:655
  394.4 16.6 %collective-permute-start.35 = (f32[96,768]{1,0:T(8,128)S(1)}, f32[96,768]{1,0:T(8,128)S(1)}, u32[]{:S(2)}, u32[]{:S(2)}) collective-permute-start(f32[96,768]{1,0:T(8,128)S(1)} %get-tuple-element.234), channel_id=1, source_target_pairs={{0,1},{1,0},{2,3},{3,2},{4,5},{5,4},{6,7},{7,6},{8,9},{9,8},{10,11... | collective-permute-start | bytes 884744 | tf_op jit(solution)/shard_map/ppermute | solution.py:65
  411.0 38.5 %copy-start.61 = (f32[256,768]{1,0:T(8,128)S(1)}, f32[256,768]{1,0:T(8,128)}, u32[]{:S(2)}) copy-start(f32[256,768]{1,0:T(8,128)} %copy-done.60) | copy-start | bytes 2359300
  411.1 38.5 %copy-start.59 = (f32[256,768]{1,0:T(8,128)S(1)}, f32[256,768]{1,0:T(8,128)}, u32[]{:S(2)}) copy-start(f32[256,768]{1,0:T(8,128)} %copy-done.58) | copy-start | bytes 2359300
  412.9 38.8 %copy-start.94 = (f32[768]{0:T(1024)S(1)}, f32[768]{0:T(1024)}, u32[]{:S(2)}) copy-start(f32[768]{0:T(1024)} %get-tuple-element.173) | copy-start | bytes 9220
  412.9 38.8 %copy-start.93 = (f32[768]{0:T(1024)S(1)}, f32[768]{0:T(1024)}, u32[]{:S(2)}) copy-start(f32[768]{0:T(1024)} %get-tuple-element.179) | copy-start | bytes 9220
  412.9 38.8 %copy-start.95 = (f32[768]{0:T(1024)S(1)}, f32[768]{0:T(1024)}, u32[]{:S(2)}) copy-start(f32[768]{0:T(1024)} %get-tuple-element.203) | copy-start | bytes 9220
  412.9 38.9 %copy-start.114 = (f32[1536]{0:T(1024)S(1)}, f32[1536]{0:T(1024)}, u32[]{:S(2)}) copy-start(f32[1536]{0:T(1024)} %get-tuple-element.277) | copy-start | bytes 18436
  412.9 38.9 %copy-start.113 = (f32[1536]{0:T(1024)S(1)}, f32[1536]{0:T(1024)}, u32[]{:S(2)}) copy-start(f32[1536]{0:T(1024)} %get-tuple-element.281) | copy-start | bytes 18436
  412.9 38.9 %copy-start.122 = (f32[768]{0:T(1024)S(1)}, f32[768]{0:T(1024)}, u32[]{:S(2)}) copy-start(f32[768]{0:T(1024)} %get-tuple-element.169) | copy-start | bytes 9220
  412.9 38.9 %copy-start.121 = (f32[768]{0:T(1024)S(1)}, f32[768]{0:T(1024)}, u32[]{:S(2)}) copy-start(f32[768]{0:T(1024)} %get-tuple-element.181) | copy-start | bytes 9220
  413.0 39.0 %copy-start.99 = (f32[768]{0:T(1024)S(1)}, f32[768]{0:T(1024)}, u32[]{:S(2)}) copy-start(f32[768]{0:T(1024)} %get-tuple-element.171) | copy-start | bytes 9220
  413.0 39.0 %copy-start.116 = (f32[1536]{0:T(1024)S(1)}, f32[1536]{0:T(1024)}, u32[]{:S(2)}) copy-start(f32[1536]{0:T(1024)} %get-tuple-element.279) | copy-start | bytes 18436
  413.0 39.0 %copy-start.97 = (f32[768]{0:T(1024)S(1)}, f32[768]{0:T(1024)}, u32[]{:S(2)}) copy-start(f32[768]{0:T(1024)} %get-tuple-element.205) | copy-start | bytes 9220
  413.0 39.0 %copy-start.98 = (f32[768]{0:T(1024)S(1)}, f32[768]{0:T(1024)}, u32[]{:S(2)}) copy-start(f32[768]{0:T(1024)} %get-tuple-element.182) | copy-start | bytes 9220
  413.0 39.0 %copy-start.123 = (f32[768]{0:T(1024)S(1)}, f32[768]{0:T(1024)}, u32[]{:S(2)}) copy-start(f32[768]{0:T(1024)} %get-tuple-element.168) | copy-start | bytes 9220
  413.0 42.0 %copy-start.96 = (f32[768]{0:T(1024)S(1)}, f32[768]{0:T(1024)}, u32[]{:S(2)}) copy-start(f32[768]{0:T(1024)} %get-tuple-element.199) | copy-start | bytes 9220
  413.0 42.1 %copy-start.115 = (f32[1536]{0:T(1024)S(1)}, f32[1536]{0:T(1024)}, u32[]{:S(2)}) copy-start(f32[1536]{0:T(1024)} %get-tuple-element.275) | copy-start | bytes 18436
  413.0 36.6 %collective-permute-start.15 = (f32[512,768]{1,0:T(8,128)S(1)}, f32[512,768]{1,0:T(8,128)S(1)}, u32[]{:S(2)}, u32[]{:S(2)}) collective-permute-start(f32[512,768]{1,0:T(8,128)S(1)} %copy-done.12), channel_id=1, source_target_pairs={{0,1},{1,0},{2,3},{3,2},{4,5},{5,4},{6,7},{7,6},{8,9},{9,8},{10,11... | collective-permute-start | bytes 4718600 | tf_op jit(solution)/shard_map/ppermute | solution.py:65
  451.1 20.1 %collective-permute-start.16 = (f32[256,768]{1,0:T(8,128)}, f32[256,768]{1,0:T(8,128)S(1)}, u32[]{:S(2)}, u32[]{:S(2)}) collective-permute-start(f32[256,768]{1,0:T(8,128)} %get-tuple-element.132), channel_id=1, source_target_pairs={{0,1},{1,0},{2,3},{3,2},{4,5},{5,4},{6,7},{7,6},{8,9},{9,8},{10,11... | collective-permute-start | bytes 2359304 | tf_op jit(solution)/shard_map/ppermute | solution.py:65
  452.1 18.9 %collective-permute-start.11 = (f32[14,768]{1,0:T(8,128)S(1)}, f32[14,768]{1,0:T(8,128)S(1)}, u32[]{:S(2)}, u32[]{:S(2)}) collective-permute-start(f32[14,768]{1,0:T(8,128)S(1)} %concatenate.45), channel_id=1, source_target_pairs={{0,1},{1,0},{2,3},{3,2},{4,5},{5,4},{6,7},{7,6},{8,9},{9,8},{10,11... | collective-permute-start | bytes 129032 | tf_op jit(solution)/shard_map/ppermute | solution.py:65
  473.5 1.3 collective-permute-start.37
  474.8 6.5 %collective-permute-start.38 = (f32[18,768]{1,0:T(8,128)S(1)}, f32[18,768]{1,0:T(8,128)S(1)}, u32[]{:S(2)}, u32[]{:S(2)}) collective-permute-start(f32[18,768]{1,0:T(8,128)S(1)} %add.533), channel_id=1, source_target_pairs={{0,4},{4,0},{8,12},{12,8},{1,5},{5,1},{9,13},{13,9},{2,6},{6,2},{1... | collective-permute-start | bytes 165896 | tf_op jit(solution)/shard_map/ppermute | solution.py:679
  481.3 7.4 %collective-permute-start.39 = (f32[18,768]{1,0:T(8,128)S(1)}, f32[18,768]{1,0:T(8,128)S(1)}, u32[]{:S(2)}, u32[]{:S(2)}) collective-permute-start(f32[18,768]{1,0:T(8,128)S(1)} %add.534), channel_id=1, source_target_pairs={{4,8},{8,4},{12,0},{0,12},{5,9},{9,5},{13,1},{1,13},{6,10},{10,6},... | collective-permute-start | bytes 165896 | tf_op jit(solution)/shard_map/ppermute | solution.py:679
  488.7 6.0 %collective-permute-start.40 = (f32[18,768]{1,0:T(8,128)S(1)}, f32[18,768]{1,0:T(8,128)S(1)}, u32[]{:S(2)}, u32[]{:S(2)}) collective-permute-start(f32[18,768]{1,0:T(8,128)S(1)} %add.535), channel_id=1, source_target_pairs={{0,32},{32,0},{64,96},{96,64},{1,33},{33,1},{65,97},{97,65},{2,34}... | collective-permute-start | bytes 165896 | tf_op jit(solution)/shard_map/ppermute | solution.py:679
  494.7 7.2 %collective-permute-start.41 = (f32[18,768]{1,0:T(8,128)S(1)}, f32[18,768]{1,0:T(8,128)S(1)}, u32[]{:S(2)}, u32[]{:S(2)}) collective-permute-start(f32[18,768]{1,0:T(8,128)S(1)} %add.536), channel_id=1, source_target_pairs={{32,64},{64,32},{96,0},{0,96},{33,65},{65,33},{97,1},{1,97},{34,66... | collective-permute-start | bytes 165896 | tf_op jit(solution)/shard_map/ppermute | solution.py:679
  502.0 4.4 collective-permute-start.42
  (121 other events, 647.1 us)
Sparse Core Ops, SparseCore 0:
  25.9 57.0 all-gather.6
  85.8 54.9 all-gather.8
  190.5 86.7 reduce-scatter.2
  281.1 107.3 reduce-scatter.4
  412.3 97.7 all-gather.10
